TPU v7x, 128 devices: a whole 4x4x4 slice. The times are simulated.
128 devices in a mesh: slab: 4 (over x), leaf: 32 (over y, z, core).
Axes of the slice: x: 4, y: 4, z: 4, core: 2. Of those that a mesh axis runs over, the one named last changes fastest.
Arguments:
- right_sides: bfloat16 [32, 524288], P(None, ('slab', 'leaf')), may hold values from -6 to 6
- left_sides: bfloat16 [32, 524288], P(None, ('slab', 'leaf')), may hold values from -6 to 6
- near_blocks: bfloat16 [4096, 8, 128, 128], P(('slab', 'leaf')), may hold values from -0.1875 to 0.1875
- near_columns: int32 [4096, 8], P(('slab', 'leaf')), may hold values from 0 to 4095, as said below
- cluster_points: int32 [4096], P(('slab', 'leaf')), may hold values from 64 to 128, as said below
- leaf_basis: bfloat16 [4096, 64, 128], P(('slab', 'leaf')), may hold values from -0.5 to 0.5
- transfer: float32 [4096, 64, 128], P(('slab', 'leaf')), may hold values from -0.625 to 0.625
- far_parents: int32 [128, 96], P(('slab', 'leaf')), may hold values from 0 to 127, as said below
- far_count: int32 [128], P(('slab', 'leaf')), may hold values from 48 to 96, as said below
- coupling: float32 [128, 96, 128, 128], P(('slab', 'leaf')), may hold values from -0.1875 to 0.1875
- slab_transfer: float32 [128, 128, 128], P(('slab', 'leaf')), may hold values from -0.5 to 0.5
- apex_coupling: float32 [4, 4, 128, 128], replicated, may hold values from -0.75 to 0.75
Outputs:
- product: float32 [32, 524288], P(None, ('slab', 'leaf'))
- adjoint_product: float32 [32, 524288], P(None, ('slab', 'leaf'))
Inputs may be any that keep to these rules, and one draw needn't show every extreme that they name: `near_columns`: row i holds 8 different clusters, i among them, all inside the window of 9 consecutive clusters centred on i, moved inward where it would pass an end of 0 to 4095. `cluster_points`: some cluster has exactly 128 points and some exactly 64. `far_parents`: row p holds 96 different parents, none equal to p; only the first far_count[p] are used. `far_count`: some parent uses all 96 slots and some exactly 48.
All inputs are finite; a program needn't handle non-finite values.
Results may differ from a plain program's by a relative error of at most 0.0024.
Values may be sent and summed in bfloat16 or wider, within the bound.
No kernel may reach another device: no remote copies, remote signals or barrier semaphores. Data moves between devices by JAX's collectives and lax.ppermute only.
A program may use at most 128 MiB of HBM per device.

v0:
```python
import jax
import jax.numpy as jnp
from jax import lax
from jax.sharding import PartitionSpec as P

B = 128
HW = 4


def extended_2(value, sides, width):
    for axis, dim in sides:
        size, length = (lax.axis_size(axis), value.shape[dim])
        up = [(i, (i + 1) % size) for i in range(size - 1)]
        down = [(j, i) for i, j in up]
        last = lax.slice_in_dim(value, length - width, length, axis=dim)
        first = lax.slice_in_dim(value, 0, width, axis=dim)
        before = lax.ppermute(last, axis, up)
        after = lax.ppermute(first, axis, down)
        value = jnp.concatenate([before, value, after], axis=dim)
    return value


def passed_along(block, axis, distance):
    devices = range(lax.axis_size(axis))
    route = [(i - distance, i) for i in devices if i - distance in devices]
    return lax.ppermute(block, axis, route)


def shards(
    right_sides,
    left_sides,
    near_blocks,
    near_columns,
    cluster_points,
    leaf_basis,
    transfer,
    far_parents,
    far_count,
    coupling,
    slab_transfer,
    apex_coupling,
):
    uppermost_level = lax.Precision.HIGHEST
    rhs_count = right_sides.shape[0]
    clusters = near_blocks.shape[0]
    device = lax.axis_index(("slab", "leaf"))
    devices_all = lax.axis_size(("slab", "leaf"))
    slab_index = lax.axis_index("slab")
    slab_count = lax.axis_size("slab")
    point_mask = jnp.arange(B, dtype=jnp.int32)[None, :] < cluster_points[:, None]
    zero_bf = jnp.zeros((), jnp.bfloat16)
    masked_right = jnp.where(point_mask[None], right_sides.reshape(rhs_count, clusters, B), zero_bf)
    masked_left = jnp.where(point_mask[None], left_sides.reshape(rhs_count, clusters, B), zero_bf)
    extended = extended_2(
        masked_right.reshape(rhs_count, clusters * B), ((("slab", "leaf"), 1),), HW * B
    )
    extended = extended.reshape(rhs_count, clusters + 2 * HW, B)
    offsets = near_columns - (device * clusters - HW)
    picked = jnp.take(extended, offsets, axis=1)
    near_out = jnp.einsum("csab,rcsb->rca", near_blocks, picked, preferred_element_type=jnp.float32)
    contrib = jnp.einsum(
        "csab,rca->csrb", near_blocks, masked_left, preferred_element_type=jnp.float32
    )
    collected = jax.ops.segment_sum(
        contrib.reshape(-1, rhs_count, B), offsets.reshape(-1), num_segments=clusters + 2 * HW
    )
    from_next = passed_along(collected[:HW].astype(jnp.bfloat16), ("slab", "leaf"), -1).astype(
        jnp.float32
    )
    from_prev = passed_along(
        collected[clusters + HW :].astype(jnp.bfloat16), ("slab", "leaf"), 1
    ).astype(jnp.float32)
    middle = collected[HW : clusters + HW]
    middle = middle.at[clusters - HW :].add(from_next).at[:HW].add(from_prev)
    near_back = jnp.transpose(middle, (1, 0, 2))
    leaf_right = jnp.einsum(
        "ckb,rcb->ckr", leaf_basis, masked_right, preferred_element_type=jnp.float32
    )
    leaf_left = jnp.einsum(
        "ckb,rcb->ckr", leaf_basis, masked_left, preferred_element_type=jnp.float32
    )
    parent_right = jnp.einsum("ckq,ckr->qr", transfer, leaf_right, precision=uppermost_level)
    parent_left = jnp.einsum("ckq,ckr->qr", transfer, leaf_left, precision=uppermost_level)
    targets = far_parents[0]
    live_slots = jnp.arange(targets.shape[0], dtype=jnp.int32) < far_count[0]
    couple = coupling[0]
    piece = lax.all_gather(parent_right[None], ("slab", "leaf"), axis=0, tiled=True)
    owners = jnp.arange(piece.shape[0], dtype=jnp.int32)
    select = ((targets[:, None] == owners[None, :]) & live_slots[:, None]).astype(jnp.float32)
    chosen = jnp.einsum("fn,nqr->fqr", select, piece, precision=uppermost_level)
    far_right = jnp.einsum("fab,fbr->ar", couple, chosen, precision=uppermost_level)
    outward = jnp.einsum("fab,ar->fbr", couple, parent_left, precision=uppermost_level)
    routing = (
        (targets[:, None] == jnp.arange(devices_all, dtype=jnp.int32)[None, :])
        & live_slots[:, None]
    ).astype(jnp.float32)
    spread = jnp.einsum("fp,fbr->pbr", routing, outward, precision=uppermost_level)
    far_left = lax.psum_scatter(spread, ("slab", "leaf"), scatter_dimension=0, tiled=True)[0]
    lift = slab_transfer[0]
    slab_share = jnp.stack(
        [
            jnp.einsum("qt,qr->tr", lift, parent_right, precision=uppermost_level),
            jnp.einsum("qt,qr->tr", lift, parent_left, precision=uppermost_level),
        ]
    )
    within = lax.psum(slab_share, "leaf")
    slab_sum_totals = lax.all_gather(within[None], "slab", axis=0, tiled=True)
    remaining_slabs = (jnp.arange(slab_count, dtype=jnp.int32) != slab_index).astype(jnp.float32)
    row_block_list = lax.dynamic_index_in_dim(apex_coupling, slab_index, 0, keepdims=False)
    column_blocks = lax.dynamic_index_in_dim(apex_coupling, slab_index, 1, keepdims=False)
    apex_right = jnp.einsum(
        "j,jiv,jvq->iq",
        remaining_slabs,
        row_block_list,
        slab_sum_totals[:, 0],
        precision=uppermost_level,
    )
    apex_left = jnp.einsum(
        "s,sab,sar->br",
        remaining_slabs,
        column_blocks,
        slab_sum_totals[:, 1],
        precision=uppermost_level,
    )
    hat_right = far_right + jnp.einsum("qt,tr->qr", lift, apex_right, precision=uppermost_level)
    hat_left = far_left + jnp.einsum("qt,tr->qr", lift, apex_left, precision=uppermost_level)
    down_right = jnp.einsum("ckq,qr->ckr", transfer, hat_right, precision=uppermost_level).astype(
        jnp.bfloat16
    )
    down_left = jnp.einsum("ckq,qr->ckr", transfer, hat_left, precision=uppermost_level).astype(
        jnp.bfloat16
    )
    far_out = jnp.einsum("ckb,ckr->rcb", leaf_basis, down_right, preferred_element_type=jnp.float32)
    far_back = jnp.einsum("ckb,ckr->rcb", leaf_basis, down_left, preferred_element_type=jnp.float32)
    zero_wide = jnp.zeros((), jnp.float32)
    product = jnp.where(point_mask[None], near_out + far_out, zero_wide).reshape(
        rhs_count, clusters * B
    )
    adjoint_product = jnp.where(point_mask[None], near_back + far_back, zero_wide).reshape(
        rhs_count, clusters * B
    )
    return (product, adjoint_product)


def solution(mesh):
    return jax.shard_map(
        shards,
        mesh=mesh,
        in_specs=(
            P(None, ("slab", "leaf")),
            P(None, ("slab", "leaf")),
            P(("slab", "leaf"), None, None, None),
            P(("slab", "leaf"), None),
            P(("slab", "leaf")),
            P(("slab", "leaf"), None, None),
            P(("slab", "leaf"), None, None),
            P(("slab", "leaf"), None),
            P(("slab", "leaf")),
            P(("slab", "leaf"), None, None, None),
            P(("slab", "leaf"), None, None),
            P(),
        ),
        out_specs=(P(None, ("slab", "leaf")), P(None, ("slab", "leaf"))),
        check_vma=False,
    )
```

profile of v0, /device:TPU:0, one launch (start us, length us, event | category | flops | bytes accessed | tf_op | source)
XLA Modules:
  0.0 732.9 jit_solution(6171635464661570695)
XLA Ops:
  7.2 0.8 iota_compare_fusion.1
  8.1 1.5 convolution_bitcast_fusion.1
  9.6 1.4 fusion.74
  11.0 0.1 copy.46
  11.1 0.1 reshape.132
  11.2 6.6 fusion.33
  17.8 0.1 broadcast_in_dim.78
  17.9 22.6 %scatter_fusion = f32[40,32,128]{2,1,0:T(8,128)S(1)} fusion(f32[40,32,128]{2,1,0:T(8,128)S(1)} %broadcast_in_dim.78, s32[256]{0:T(256)S(1)} %reshape.132, f32[256,32,128]{2,1,0:T(8,128)} %bitcast.170), kind=kCustom, calls=%fused_computation.1 | custom fusion | flops 1048576 | bytes 12583936 | tf_op jit(solution)/shard_map/scatter-add | solution.py:64
  40.5 0.1 convert.9
  40.5 0.6 fusion.72
  41.2 1.3 collective-permute-start.2
  42.4 3.6 collective-permute-start.3
  46.8 0.4 convolution_bitcast_fusion
  47.1 0.8 fusion.75
  47.9 5.4 fusion.11
  53.3 2.1 fusion.8
  55.4 2.5 copy.48
  58.0 0.6 copy-done.16
  58.6 0.1 lt.59
  58.7 0.2 copy-done.7
  59.0 2.9 collective-permute-start
  61.9 1.3 collective-permute-start.1
  63.2 0.1 copy.39
  63.3 0.1 reshape.124
  63.4 0.2 convolution_bitcast_fusion.5
  63.6 0.2 convolution_bitcast_fusion.6
  63.8 134.7 %psum.7 = f32[1,2,128,32]{2,3,1,0:T(8,128)S(1)} all-reduce(f32[1,2,128,32]{2,3,1,0:T(8,128)S(1)} %maximum_bitcast_fusion.1), channel_id=1, replica_groups=mesh['slab'=4,'leaf'=32] {'leaf'}, use_global_device_ids=true, to_apply=%region_0.1 | all-reduce | flops 8192 | bytes 65536 | tf_op jit(solution)/shard_map/psum | solution.py:106
  198.5 12.5 %all_gather.7 = f32[4,2,128,32]{2,3,1,0:T(8,128)S(1)} all-gather(f32[1,2,128,32]{2,3,1,0:T(8,128)S(1)} %psum.7), channel_id=1, replica_groups=mesh['slab'=4,'leaf'=32] {'slab'}, dimensions={0}, use_global_device_ids=true | all-gather | bytes 163840 | tf_op jit(solution)/shard_map/all_gather | solution.py:107
  211.0 1.8 convolution_bitcast_fusion.3
  212.8 2.0 convolution_bitcast_fusion.4
  214.8 0.1 copy.38
  215.0 0.8 copy-done.3
  215.7 0.1 copy_bitcast_fusion.2
  215.8 1.0 gather_fusion
  216.8 1.5 fusion.45
  218.3 6.0 fusion.14
  224.3 2.0 copy.58
  226.3 1.1 fusion.56
  227.4 8.8 %fusion.23 = f32[32,128]{1,0:T(8,128)S(1)} fusion(f32[1,96,128,128]{3,2,1,0:T(8,128)} %param.25, f32[96,128,32]{1,0,2:T(8,128)S(1)} %fusion.56), kind=kOutput, calls=%fused_computation.27 | convolution fusion | flops 603979776 | bytes 7880704 | tf_op jit(solution)/shard_map/fab,fbr->ar/dot_general | solution.py:91
  236.2 0.2 fusion.30
  236.4 2.9 fusion.21
  239.4 0.3 fusion.20
  239.7 0.8 copy.78
  240.5 480.5 %reduce-scatter.2.cloned.1.call-done = f32[1,128,32]{1,2,0:T(8,128)} async-done(((f32[128,128,32]{1,2,0:T(8,128)}), f32[1,128,32]{1,2,0:T(8,128)}) %reduce-scatter.2.cloned.1.call-update) | async-done | bytes 16400 | tf_op jit(solution)/shard_map/reduce_scatter | solution.py:98
  721.1 0.9 fusion.29
  722.0 2.9 fusion.22
  724.9 0.3 fusion.18
  725.2 0.8 copy.77
  (51 shorter events, 0.4 us)
Async XLA Ops:
  7.2 2.4 copy-start
  7.2 3.8 copy-start.12
  7.2 4.0 copy-start.6
  7.2 217.1 %all-gather.3.cloned.1.call-start = ((), (), s32[]{:S(2)}) async-start(), calls=%async_computation.2 | async-start | bytes 2113536 | tf_op jit(solution)/shard_map/all_gather | solution.py:87
  11.0 710.1 %reduce-scatter.2.cloned.1.call-start = ((), (), s32[]{:S(2)}) async-start(), calls=%async_computation.1 | async-start | bytes 2113536 | tf_op jit(solution)/shard_map/reduce_scatter | solution.py:98
  17.9 28.9 %copy-start.1 = (bf16[32,64,128]{2,1,0:T(8,128)(2,1)S(1)}, bf16[32,64,128]{2,1,0:T(8,128)(2,1)}, u32[]{:S(2)}) copy-start(bf16[32,64,128]{2,1,0:T(8,128)(2,1)} %param.21) | copy-start | bytes 1572868
  41.2 173.8 %collective-permute-start.2 = (bf16[4,32,128]{2,1,0:T(8,128)(2,1)S(1)}, bf16[4,32,128]{2,1,0:T(8,128)(2,1)S(1)}, u32[]{:S(2)}, u32[]{:S(2)}) collective-permute-start(bf16[4,32,128]{2,1,0:T(8,128)(2,1)S(1)} %get-tuple-element.29), channel_id=1, source_target_pairs={{1,0},{2,1},{3,2},{4,3},{5,4},{6,5},{7,6},{8,7},{9,8},{10,9},{11,1... | collective-permute-start | bytes 98312 | tf_op jit(solution)/shard_map/ppermute | solution.py:26
  42.4 174.4 %collective-permute-start.3 = (bf16[4,32,128]{2,1,0:T(8,128)(2,1)}, bf16[4,32,128]{2,1,0:T(8,128)(2,1)}, u32[]{:S(2)}, u32[]{:S(2)}) collective-permute-start(bf16[4,32,128]{2,1,0:T(8,128)(2,1)} %get-tuple-element.28), channel_id=1, source_target_pairs={{0,1},{1,2},{2,3},{3,4},{4,5},{5,6},{6,7},{7,8},{8,9},{9,10},{10,1... | collective-permute-start | bytes 98312 | tf_op jit(solution)/shard_map/ppermute | solution.py:26
  46.8 6.5 copy-start.14
  47.9 5.4 copy-start.13
  58.0 0.7 copy-start.16
  58.0 1.0 copy-start.7
  58.0 5.4 copy-start.8
  58.0 5.6 copy-start.9
  59.0 156.0 %collective-permute-start = (bf16[32,512]{1,0:T(8,128)(2,1)S(1)}, bf16[32,512]{1,0:T(8,128)(2,1)S(1)}, u32[]{:S(2)}, u32[]{:S(2)}) collective-permute-start(bf16[32,512]{1,0:T(8,128)(2,1)S(1)} %get-tuple-element.30), channel_id=1, source_target_pairs={{0,1},{1,2},{2,3},{3,4},{4,5},{5,6},{6,7},{7,8},{8,9},{9,10},{10,1... | collective-permute-start | bytes 98312 | tf_op jit(solution)/shard_map/ppermute | solution.py:17
  61.9 153.1 %collective-permute-start.1 = (bf16[32,512]{1,0:T(8,128)(2,1)S(1)}, bf16[32,512]{1,0:T(8,128)(2,1)S(1)}, u32[]{:S(2)}, u32[]{:S(2)}) collective-permute-start(bf16[32,512]{1,0:T(8,128)(2,1)S(1)} %get-tuple-element.31), channel_id=1, source_target_pairs={{1,0},{2,1},{3,2},{4,3},{5,4},{6,5},{7,6},{8,7},{9,8},{10,9},{11,1... | collective-permute-start | bytes 98312 | tf_op jit(solution)/shard_map/ppermute | solution.py:18
  215.0 0.8 copy-start.3
  224.3 2.0 copy-start.15
  227.4 8.8 %copy-start.11 = (f32[128,32]{0,1:T(8,128)S(1)}, f32[128,32]{0,1:T(8,128)}, u32[]{:S(2)}) copy-start(f32[128,32]{0,1:T(8,128)} %convolution_bitcast_fusion.4) | copy-start | bytes 49156
  227.4 12.0 %copy-start.2 = (bf16[32,64,128]{2,1,0:T(8,128)(2,1)S(1)}, bf16[32,64,128]{2,1,0:T(8,128)(2,1)}, u32[]{:S(2)}) copy-start(bf16[32,64,128]{2,1,0:T(8,128)(2,1)} %param.21) | copy-start | bytes 1572868
  227.4 12.0 %copy-start.5 = (f32[32,32,128]{2,1,0:T(8,128)S(1)}, f32[32,32,128]{2,1,0:T(8,128)}, u32[]{:S(2)}) copy-start(f32[32,32,128]{2,1,0:T(8,128)} %fusion.14) | copy-start | bytes 1572868
  236.4 484.6 %copy-start.10 = (f32[128,32]{0,1:T(8,128)S(1)}, f32[128,32]{0,1:T(8,128)}, u32[]{:S(2)}) copy-start(f32[128,32]{0,1:T(8,128)} %convolution_bitcast_fusion.3) | copy-start | bytes 49156
  239.4 485.5 %copy-start.4 = (f32[32,32,128]{2,1,0:T(8,128)S(1)}, f32[32,32,128]{2,1,0:T(8,128)}, u32[]{:S(2)}) copy-start(f32[32,32,128]{2,1,0:T(8,128)} %fusion.45) | copy-start | bytes 1572868
Sparse Core Ops, SparseCore 0:
  11.4 67.6 all-gather.2
  81.5 639.5 reduce-scatter.1
where the time goes:
time: 734 us; the launch traced here: 733 us
  waiting for transfers between devices  481 us (66%)
  blocking collectives  147 us (20%)
  matrix products  45.5 us (6%)
  other arithmetic  25.1 us (3%)
  between operations  15.1 us (2%)
  local copies, waits for them, and re-layouts  10.1 us (1%)
  starting transfers between devices  9.22 us (1%)
    reduce_scatter x1, waiting for transfers between devices, shards(): lax.psum_scatter(spread, ('slab', 'leaf'), scatter_dimension=0, tiled=True)  481 us
    psum x1, blocking collectives, shards(): within = lax.psum(slab_share, 'leaf')  135 us
    scatter-add x1, other arithmetic, shards(): jax.ops.segment_sum(contrib.reshape(-1, rhs_count, B), offsets.reshape(-1...  22.6 us
  transfers between devices with their start and end apart: 6, of which 1 were waited for; matrix products, arithmetic and copies ran while one was open for 10% of the time, Pallas kernels for 0%

commit v1 on v0

v1 whole, which is shorter than its diff:
```python
import jax
import jax.numpy as jnp
import numpy as np
from jax import lax
from jax.experimental import pallas as pl
from jax.experimental.pallas import tpu as pltpu
from jax.sharding import PartitionSpec as P

B = 128
HW = 4
AXES = ("slab", "leaf")
BF = jnp.bfloat16
F32 = jnp.float32

CORE, Z1, Z3, Y1, Y3, X1, X3 = 1, 2, 6, 8, 24, 32, 96
REDUCE_ORDER = (CORE, Y1, Y3, Z1, Z3, X1, X3)
GATHER_ORDER = (X1, X3, Z3, Z1, Y1, Y3, CORE)


def swapped(block, mask):
    route = [(i, i ^ mask) for i in range(lax.axis_size(AXES))]
    return lax.ppermute(block, AXES, route)


def passed_along(block, distance):
    devices = range(lax.axis_size(AXES))
    route = [(i - distance, i) for i in devices if i - distance in devices]
    return lax.ppermute(block, AXES, route)


def slot_of(difference, order, first_is_high):
    slot = jnp.zeros_like(difference)
    for step, mask in enumerate(order):
        if mask == CORE:
            bit = difference & 1
        else:
            shift = {Z1: 1, Z3: 1, Y1: 3, Y3: 3, X1: 5, X3: 5}[mask]
            low, high = (difference >> shift) & 1, (difference >> (shift + 1)) & 1
            bit = high if mask in (Z3, Y3, X3) else low ^ high
        place = len(order) - 1 - step if first_is_high else step
        slot = slot | (bit << place)
    return slot


def two(value):
    high = value.astype(BF)
    return high, (value - high.astype(F32)).astype(BF)


def two_outside(value):
    high = lax.reduce_precision(value, 8, 7)
    return high.astype(BF), (value - high).astype(BF)


NN = (((1,), (0,)), ((), ()))
NT = (((1,), (1,)), ((), ()))


def dot(a, b, how):
    return lax.dot_general(a, b, how, preferred_element_type=F32)


def dot3(a, b, how):
    (ah, al), (bh, bl) = two(a), two(b)
    left = jnp.concatenate([ah, al, ah], axis=1)
    right = jnp.concatenate([bh, bh, bl], axis=1 if how is NT else 0)
    return dot(left, right, how)


def up_kernel(
    points, right, left, basis, transfer, lift, mright, mleft, pright, pleft, shares
):
    clusters = basis.shape[0]
    rhs = right.shape[0]
    lane = lax.broadcasted_iota(jnp.int32, (rhs, B), 1)
    total = jnp.zeros((2 * rhs, B), F32)
    for c in range(clusters):
        mask = lane < points[c]
        xr = jnp.where(mask, right[:, c * B : (c + 1) * B].astype(F32), 0.0).astype(BF)
        xl = jnp.where(mask, left[:, c * B : (c + 1) * B].astype(F32), 0.0).astype(BF)
        mright[c] = xr
        mleft[c] = xl
        leaf = dot(jnp.concatenate([xr, xl], axis=0), basis[c], NT)
        total = total + dot3(leaf, transfer[c], NN)
    pright[...] = total[:rhs].astype(BF)
    pleft[...] = total[rhs:]
    shares[...] = dot3(total, lift[0], NN)


def outward_kernel(count, slots, pleft, coupling, keep, send):
    step = pl.program_id(0)
    per = coupling.shape[1]
    half = keep.shape[0]

    @pl.when(step == 0)
    def _():
        keep[...] = jnp.zeros_like(keep)
        send[...] = jnp.zeros_like(send)

    ph, plow = two(pleft[...])
    rhs = ph.shape[0]
    wide = jnp.concatenate([ph, plow], axis=0)
    for g in range(per):
        f = step * per + g
        ch, cl = two(coupling[0, g])
        main = dot(wide, ch, NN)
        value = main[:rhs] + main[rhs:] + dot(ph, cl, NN)
        slot = slots[0, f]
        live = f < count[0]

        @pl.when(live & (slot < half))
        def _():
            keep[slot] = value

        @pl.when(live & (slot >= half))
        def _():
            send[slot - half] = value


def near_kernel(offsets, first, extended, mleft, blocks, out, back):
    step = pl.program_id(0)
    per, slots = blocks.shape[:2]

    @pl.when(step == 0)
    def _():
        back[...] = jnp.zeros_like(back)

    for g in range(per):
        c = step * per + g
        xl = mleft[c]
        total = jnp.zeros((xl.shape[0], B), F32)
        for s in range(slots):
            place = offsets[c, s] - first[0]
            block = blocks[g, s]
            total = total + dot(extended[place], block, NT)
            back[place] += dot(xl, block, NN)
        out[c] = total


def forward_kernel(count, slots, gathered, coupling, out):
    step = pl.program_id(0)
    per = coupling.shape[1]

    @pl.when(step == 0)
    def _():
        out[...] = jnp.zeros_like(out)

    total = jnp.zeros_like(out)
    for g in range(per):
        f = step * per + g
        ch, cl = two(coupling[0, g])
        value = gathered[slots[0, f]]
        part = dot(
            jnp.concatenate([value, value], axis=1), jnp.concatenate([ch, cl], axis=1), NT
        )
        total = total + jnp.where(f < count[0], part, 0.0)
    out[...] += total


def down_kernel(
    points,
    far_right,
    far_left,
    slabs,
    apex_row,
    apex_column,
    lift,
    transfer,
    basis,
    near_out,
    near_back,
    from_prev,
    from_next,
    product,
    adjoint,
):
    rhs = far_right.shape[0]
    clusters = basis.shape[0]
    top_right = jnp.zeros((rhs, B), F32)
    top_left = jnp.zeros((rhs, B), F32)
    for t in range(3):
        top_right = top_right + dot3(slabs[2 * t], apex_row[t], NT)
        top_left = top_left + dot3(slabs[2 * t + 1], apex_column[t], NN)
    hats = jnp.concatenate([far_right[...], far_left[...]], axis=0) + dot3(
        jnp.concatenate([top_right, top_left], axis=0), lift[0], NT
    )
    hh, hl = two(hats)
    hat3 = jnp.concatenate([hh, hl, hh], axis=1)
    lane = lax.broadcasted_iota(jnp.int32, (rhs, B), 1)
    for c in range(clusters):
        th, tl = two(transfer[c])
        down = dot(hat3, jnp.concatenate([th, th, tl], axis=1), NT)
        dh, dl = two(down)
        far = dot(
            jnp.concatenate([dh, dl], axis=1),
            jnp.concatenate([basis[c], basis[c]], axis=0),
            NN,
        )
        mask = lane < points[c]
        back = near_back[HW + c]
        if c < HW:
            back = back + from_prev[c].astype(F32)
        if c >= clusters - HW:
            back = back + from_next[c - clusters + HW].astype(F32)
        product[:, c * B : (c + 1) * B] = jnp.where(mask, near_out[c] + far[:rhs], 0.0)
        adjoint[:, c * B : (c + 1) * B] = jnp.where(mask, back + far[rhs:], 0.0)


SMEM = pl.BlockSpec(memory_space=pltpu.SMEM)
VMEM = pl.BlockSpec(memory_space=pltpu.VMEM)
PARAMS = pltpu.CompilerParams(vmem_limit_bytes=48 * 1024 * 1024)


def shape(dims, kind):
    return jax.ShapeDtypeStruct(dims, kind)


def cost(flops, nbytes):
    return pl.CostEstimate(flops=int(flops), bytes_accessed=int(nbytes), transcendentals=0)


def shards(
    right_sides,
    left_sides,
    near_blocks,
    near_columns,
    cluster_points,
    leaf_basis,
    transfer,
    far_parents,
    far_count,
    coupling,
    slab_transfer,
    apex_coupling,
):
    rhs = right_sides.shape[0]
    clusters, near_slots = near_blocks.shape[:2]
    far_slots = coupling.shape[1]
    me = lax.axis_index(AXES)
    slab = lax.axis_index("slab")
    devices = lax.axis_size(AXES)
    block = (rhs, B)

    mright, mleft, pright, pleft, shares = pl.pallas_call(
        up_kernel,
        out_shape=(
            shape((clusters, *block), BF),
            shape((clusters, *block), BF),
            shape(block, BF),
            shape(block, F32),
            shape((2 * rhs, B), F32),
        ),
        in_specs=[SMEM] + [VMEM] * 5,
        out_specs=(VMEM,) * 5,
        compiler_params=PARAMS,
        cost_estimate=cost(2e8, 3e6),
        name="up",
    )(cluster_points, right_sides, left_sides, leaf_basis, transfer, slab_transfer)

    before = passed_along(mright[clusters - HW :], 1)
    after = passed_along(mright[:HW], -1)

    gathered = pright[None]
    for mask in GATHER_ORDER:
        gathered = jnp.concatenate([gathered, swapped(gathered, mask)], axis=0)

    difference = far_parents ^ me
    per = 16
    keep, send = pl.pallas_call(
        outward_kernel,
        grid=(far_slots // per,),
        out_shape=(shape((devices // 2, *block), F32),) * 2,
        in_specs=[
            SMEM,
            SMEM,
            pl.BlockSpec(block, lambda i: (0, 0)),
            pl.BlockSpec((1, per, B, B), lambda i: (0, i, 0, 0)),
        ],
        out_specs=(pl.BlockSpec((devices // 2, *block), lambda i: (0, 0, 0)),) * 2,
        compiler_params=PARAMS,
        cost_estimate=cost(3e8, 7e6),
        name="outward",
    )(far_count, slot_of(difference, REDUCE_ORDER, True), pleft, coupling)
    sums = shares.reshape(2, *block)
    partial = keep + swapped(send, CORE)
    sums = sums + swapped(sums, CORE)
    others = []
    for step, mask in enumerate(REDUCE_ORDER[1:]):
        n = partial.shape[0] // 2
        going = partial[n:]
        parts = [going.astype(BF)] if step < 2 else list(two_outside(going))
        sent = jnp.concatenate([sums, *others], axis=0) if mask == X3 else sums
        parts += list(two_outside(sent))
        came = swapped(jnp.concatenate(parts, axis=0), mask).astype(F32)
        if step < 2:
            partial = partial[:n] + came[:n]
        else:
            partial = partial[:n] + (came[:n] + came[n : 2 * n])
            n = 2 * n
        m = sent.shape[0]
        came_sums = came[n : n + m] + came[n + m : n + 2 * m]
        if mask in (X1, X3):
            others.append(came_sums)
        else:
            sums = sums + came_sums
    far_left = partial[0]
    slabs = jnp.concatenate(others, axis=0)

    extended = jnp.concatenate([before, mright, after], axis=0)
    per = 4
    near_out, near_back = pl.pallas_call(
        near_kernel,
        grid=(clusters // per,),
        out_shape=(
            shape((clusters, *block), F32),
            shape((clusters + 2 * HW, *block), F32),
        ),
        in_specs=[
            SMEM,
            SMEM,
            pl.BlockSpec((clusters + 2 * HW, *block), lambda i: (0, 0, 0)),
            pl.BlockSpec((clusters, *block), lambda i: (0, 0, 0)),
            pl.BlockSpec((per, near_slots, B, B), lambda i: (i, 0, 0, 0)),
        ],
        out_specs=(
            pl.BlockSpec((clusters, *block), lambda i: (0, 0, 0)),
            pl.BlockSpec((clusters + 2 * HW, *block), lambda i: (0, 0, 0)),
        ),
        compiler_params=PARAMS,
        cost_estimate=cost(6e8, 9e6),
        name="near",
    )(near_columns, (me * clusters - HW)[None], extended, mleft, near_blocks)
    from_next = passed_along(near_back[:HW].astype(BF), -1)
    from_prev = passed_along(near_back[clusters + HW :].astype(BF), 1)

    per = 16
    far_right = pl.pallas_call(
        forward_kernel,
        grid=(far_slots // per,),
        out_shape=shape(block, F32),
        in_specs=[
            SMEM,
            SMEM,
            pl.BlockSpec((devices, *block), lambda i: (0, 0, 0)),
            pl.BlockSpec((1, per, B, B), lambda i: (0, i, 0, 0)),
        ],
        out_specs=pl.BlockSpec(block, lambda i: (0, 0)),
        compiler_params=PARAMS,
        cost_estimate=cost(3e8, 7e6),
        name="forward",
    )(far_count, slot_of(difference, GATHER_ORDER, False), gathered, coupling)

    order = slab ^ jnp.array([1, 3, 2], jnp.int32)
    apex_row = jnp.take(lax.dynamic_index_in_dim(apex_coupling, slab, 0, False), order, axis=0)
    apex_column = jnp.take(lax.dynamic_index_in_dim(apex_coupling, slab, 1, False), order, axis=0)
    return pl.pallas_call(
        down_kernel,
        out_shape=(shape((rhs, clusters * B), F32),) * 2,
        in_specs=[SMEM] + [VMEM] * 12,
        out_specs=(VMEM,) * 2,
        compiler_params=PARAMS,
        cost_estimate=cost(4e8, 5e6),
        name="down",
    )(
        cluster_points,
        far_right,
        far_left,
        slabs,
        apex_row,
        apex_column,
        slab_transfer,
        transfer,
        leaf_basis,
        near_out,
        near_back,
        from_prev,
        from_next,
    )


def solution(mesh):
    return jax.shard_map(
        shards,
        mesh=mesh,
        in_specs=(
            P(None, AXES),
            P(None, AXES),
            P(AXES, None, None, None),
            P(AXES, None),
            P(AXES),
            P(AXES, None, None),
            P(AXES, None, None),
            P(AXES, None),
            P(AXES),
            P(AXES, None, None, None),
            P(AXES, None, None),
            P(),
        ),
        out_specs=(P(None, AXES), P(None, AXES)),
        check_vma=False,
    )
```

time: 734 us -> 113 us (0.15)
  waiting for transfers between devices: 481 us -> 7.27 us
  blocking collectives: 147 us -> 0 us
  matrix products: 45.5 us -> 0 us
  Pallas kernels: 0 us -> 44.4 us
  starting transfers between devices: 9.22 us -> 36.9 us
  other arithmetic: 25.1 us -> 6.79 us
  between operations: 15.1 us -> 1.91 us
    reduce_scatter x1 -> x0, waiting for transfers between devices: 481 us -> none  [shards(): lax.psum_scatter(spread, ('slab', 'leaf'), scatter_dimension=0, tiled=True)]
    psum x1 -> x0, blocking collectives: 135 us -> none  [shards(): within = lax.psum(slab_share, 'leaf')]
    dot_general x20 -> x0, matrix products: 45.5 us -> none  [the longest x1 8.76 us: shards(): jnp.einsum('fab,fbr->ar', couple, chosen, precision=uppermost_level)]
    pallas_call x0 -> x5, Pallas kernels: none -> 44.4 us  [the longest x1 16.9 us: shards(): pl.pallas_call(outward_kernel, grid=(far_slots // per,), out_shape=(shape...]
    ppermute x4 -> x19, starting transfers between devices: 9.14 us -> 36.9 us  [the longest x15 26.5 us: swapped(): return lax.ppermute(block, AXES, route)]
    scatter-add x3 -> x0, other arithmetic: 24.1 us -> none  [the longest x1 22.6 us: shards(): jax.ops.segment_sum(contrib.reshape(-1, rhs_count, B), offsets.reshape(-1...]
    all_gather x1 -> x0, blocking collectives: 12.5 us -> none  [shards(): slab_sum_totals = lax.all_gather(within[None], 'slab', axis=0, tiled=True)]
    unnamed x35 -> x47, local copies, waits for them, and re-layouts: 3.66 us -> 11.6 us
  transfers between devices with their start and end apart: 6 -> 19, of which waited for: 1 -> 6; matrix products, arithmetic and copies ran while one was open for 10% -> 11% of each run, Pallas kernels for 0% -> 29%
where the time goes in v1:
time: 113 us; the launch traced here: 111 us
  Pallas kernels  44.4 us (39%)
  starting transfers between devices  36.9 us (33%)
  local copies, waits for them, and re-layouts  13.6 us (12%)
  waiting for transfers between devices  7.27 us (6%)
  other arithmetic  6.79 us (6%)
  between operations  1.91 us (2%)
    ppermute x15, starting transfers between devices, swapped(): return lax.ppermute(block, AXES, route)  26.5 us
    pallas_call x1, Pallas kernels, shards(): pl.pallas_call(outward_kernel, grid=(far_slots // per,), out_shape=(shape...  16.9 us
    unnamed x47, local copies, waits for them, and re-layouts  11.6 us
    ppermute x4, starting transfers between devices, passed_along(): return lax.ppermute(block, AXES, route)  10.3 us
    pallas_call x1, Pallas kernels, shards(): pl.pallas_call(near_kernel, grid=(clusters // per,), out_shape=(shape((cl...  9.97 us
    pallas_call x1, Pallas kernels, shards(): pl.pallas_call(down_kernel, out_shape=(shape((rhs, clusters * B), F32),)...  8.57 us
    ppermute x15, waiting for transfers between devices, swapped(): return lax.ppermute(block, AXES, route)  7.26 us
    pallas_call x1, Pallas kernels, shards(): pl.pallas_call(forward_kernel, grid=(far_slots // per,), out_shape=shape(...  5.76 us
  transfers between devices with their start and end apart: 19, of which 6 were waited for; matrix products, arithmetic and copies ran while one was open for 11% of the time, Pallas kernels for 29%

profile of v1, /device:TPU:0, one launch (start us, length us, event | category | flops | bytes accessed | tf_op | source)
XLA Modules:
  0.0 110.8 jit_solution(13031497148762032400)
XLA Ops:
  0.7 1.3 %copy-done.1 = f32[32,64,128]{2,1,0:T(8,128)S(1)} copy-done((f32[32,64,128]{2,1,0:T(8,128)S(1)}, f32[32,64,128]{2,1,0:T(8,128)}, u32[]{:S(2)}) %copy-start.1) | copy-done | bytes 1048600
  2.0 1.0 copy-done.3
  3.0 0.9 copy-done.6
  4.0 0.9 copy-done.7
  4.9 0.8 copy-done.10
  5.8 0.7 copy-done.13
  6.4 3.2 %up.1 = (bf16[32,32,128]{2,1,0:T(8,128)(2,1)S(1)}, bf16[32,32,128]{2,1,0:T(8,128)(2,1)S(1)}, bf16[32,128]{1,0:T(8,128)(2,1)S(1)}, f32[32,128]{1,0:T(8,128)S(1)}, f32[64,128]{1,0:T(8,128)}) custom-call(s32[32]{0:T(128)S(1)} %copy-done.13, bf16[32,4096]{1,0:T(8,128)(2,1)S(1)} %copy-done.6, bf16[32,4096]{1,0:T(8,128)(2,1)S(1)} %copy-done.7, ...), custom_call_target="tpu_custom_call" | custom-call | flops 200000000 | bytes 3000000 | tf_op jit(solution)/shard_map/up/pallas_call | solution.py:244
  9.6 0.7 copy-done.8
  10.3 1.6 %collective-permute-start = (bf16[1,32,128]{2,1,0:T(8,128)(2,1)S(1)}, bf16[1,32,128]{2,1,0:T(8,128)(2,1)}, u32[]{:S(2)}, u32[]{:S(2)}) collective-permute-start(bf16[1,32,128]{2,1,0:T(8,128)(2,1)S(1)} %bitcast.13), channel_id=1, source_target_pairs={{0,32},{1,33},{2,34},{3,35},{4,36},{5,37},{6,38},{7,39},{8,40},{9,... | collective-permute-start | bytes 24584 | tf_op jit(solution)/shard_map/ppermute | solution.py:22
  12.5 0.7 shift-left_or_fusion
  13.2 16.9 %outward.1 = (f32[64,32,128]{2,1,0:T(8,128)S(1)}, f32[64,32,128]{2,1,0:T(8,128)}) custom-call(s32[1]{0:T(128)S(6)} %copy.38.count, s32[1,96]{1,0:T(1,128)S(1)} %get-tuple-element.76.slots, f32[32,128]{1,0:T(8,128)S(1)} %get-tuple-element.13.pleft, f32[1,96,128,128]{3,2,1,0:T(8,128)} %coupling.3), custom_call_target="tpu_custom_call" | custom-call | flops 300000000 | bytes 7000000 | tf_op jit(solution)/shard_map/outward/pallas_call | solution.py:269
  30.1 0.5 collective-permute-start.7
  30.6 0.6 fusion.25
  31.3 1.3 %collective-permute-start.16 = (bf16[4,32,128]{2,1,0:T(8,128)(2,1)}, bf16[4,32,128]{2,1,0:T(8,128)(2,1)}, u32[]{:S(2)}, u32[]{:S(2)}) collective-permute-start(bf16[4,32,128]{2,1,0:T(8,128)(2,1)} %get-tuple-element.36), channel_id=1, source_target_pairs={{1,0},{2,1},{3,2},{4,3},{5,4},{6,5},{7,6},{8,7},{9,8},{10,9},{11,1... | collective-permute-start | bytes 98312 | tf_op jit(solution)/shard_map/ppermute | solution.py:28
  32.5 3.6 %collective-permute-start.15 = (bf16[4,32,128]{2,1,0:T(8,128)(2,1)}, bf16[4,32,128]{2,1,0:T(8,128)(2,1)}, u32[]{:S(2)}, u32[]{:S(2)}) collective-permute-start(bf16[4,32,128]{2,1,0:T(8,128)(2,1)} %get-tuple-element.35), channel_id=1, source_target_pairs={{0,1},{1,2},{2,3},{3,4},{4,5},{5,6},{6,7},{7,8},{8,9},{9,10},{10,1... | collective-permute-start | bytes 98312 | tf_op jit(solution)/shard_map/ppermute | solution.py:28
  36.3 0.6 gather_fusion.1
  36.8 0.6 gather_fusion
  37.5 0.6 constant_dynamic-update-slice_fusion.17
  38.1 0.7 copy.15.offsets
  38.8 0.7 pad_maximum_fusion.11
  39.5 7.8 %collective-permute-start.1 = (bf16[2,32,128]{2,1,0:T(8,128)(2,1)S(1)}, bf16[2,32,128]{2,1,0:T(8,128)(2,1)S(1)}, u32[]{:S(2)}, u32[]{:S(2)}) collective-permute-start(bf16[2,32,128]{2,1,0:T(8,128)(2,1)S(1)} %pad_maximum_fusion.11), channel_id=1, source_target_pairs={{0,96},{1,97},{2,98},{3,99},{4,100},{5,101},{6,102},{7,103},{8,104... | collective-permute-start | bytes 49160 | tf_op jit(solution)/shard_map/ppermute | solution.py:22
  47.3 1.3 %constant_dynamic-update-slice_fusion.16 = (bf16[64,32,128]{2,1,0:T(8,128)(2,1)}, bf16[128,32,128]{2,1,0:T(8,128)(2,1)S(1)}, bf16[32,32,128]{2,1,0:T(8,128)(2,1)}, bf16[16,32,128]{2,1,0:T(8,128)(2,1)}) fusion(bf16[64,32,128]{2,1,0:T(8,128)(2,1)} %get-tuple-element.70, bf16[1,32,128]{2,1,0:T(8,128)(2,1)} %collective-permute-done, ...), kind=kLoop, calls=%fused_computation.50 | loop fusion | bytes 40960
  48.6 0.8 reduce-precision_convert_fusion.8
  49.4 1.4 %add.80 = f32[64,32,128]{2,1,0:T(8,128)S(1)} add(f32[64,32,128]{2,1,0:T(8,128)S(1)} %get-tuple-element.14, f32[64,32,128]{2,1,0:T(8,128)} %collective-permute-done.7) | non-fusion elementwise | flops 262144 | bytes 3145728 | tf_op jit(solution)/shard_map/add | solution.py:285
  51.0 0.7 pad_maximum_fusion.10
  51.7 0.6 constant_dynamic-update-slice_fusion.15
  52.3 1.1 pad_maximum_fusion.extended
  53.4 0.9 copy-done.9
  54.3 0.7 copy-done.12
  55.1 10.0 %near.1 = (f32[32,32,128]{2,1,0:T(8,128)S(1)}, f32[40,32,128]{2,1,0:T(8,128)S(1)}) custom-call(s32[32,8]{1,0:T(8,128)S(1)} %copy-done.12, s32[1]{0:T(128)} %bitcast.5.first, bf16[40,32,128]{2,1,0:T(8,128)(2,1)S(1)} %pad_maximum_fusion.extended, bf16[32,32,128]{2,1,0:T(8,128)(2,1)S(1)} %copy-done.9, bf16[32,8,128,128]{3,2,1,0:T(8,128)(2,1)} %blocks.1), custom_call_target="tpu_custom_call" | custom-call | flops 600000000 | bytes 9000000 | tf_op jit(solution)/shard_map/near/pallas_call | solution.py:311
  65.4 1.6 %collective-permute-start.10 = (bf16[20,32,128]{2,1,0:T(8,128)(2,1)S(1)}, bf16[20,32,128]{2,1,0:T(8,128)(2,1)S(1)}, u32[]{:S(2)}, u32[]{:S(2)}) collective-permute-start(bf16[20,32,128]{2,1,0:T(8,128)(2,1)S(1)} %pad_maximum_fusion.2), channel_id=1, source_target_pairs={{0,24},{1,25},{2,26},{3,27},{4,28},{5,29},{6,30},{7,31},{8,16},{9,... | collective-permute-start | bytes 491528 | tf_op jit(solution)/shard_map/ppermute | solution.py:22
  67.0 4.1 %collective-permute-start.17 = (bf16[4,32,128]{2,1,0:T(8,128)(2,1)S(1)}, bf16[4,32,128]{2,1,0:T(8,128)(2,1)S(1)}, u32[]{:S(2)}, u32[]{:S(2)}) collective-permute-start(bf16[4,32,128]{2,1,0:T(8,128)(2,1)S(1)} %get-tuple-element.34), channel_id=1, source_target_pairs={{0,1},{1,2},{2,3},{3,4},{4,5},{5,6},{6,7},{7,8},{8,9},{9,10},{10,1... | collective-permute-start | bytes 98312 | tf_op jit(solution)/shard_map/ppermute | solution.py:28
  71.1 1.3 %collective-permute-start.18 = (bf16[4,32,128]{2,1,0:T(8,128)(2,1)S(1)}, bf16[4,32,128]{2,1,0:T(8,128)(2,1)S(1)}, u32[]{:S(2)}, u32[]{:S(2)}) collective-permute-start(bf16[4,32,128]{2,1,0:T(8,128)(2,1)S(1)} %get-tuple-element.33), channel_id=1, source_target_pairs={{1,0},{2,1},{3,2},{4,3},{5,4},{6,5},{7,6},{8,7},{9,8},{10,9},{11,1... | collective-permute-start | bytes 98312 | tf_op jit(solution)/shard_map/ppermute | solution.py:28
  72.5 0.7 pad_maximum_fusion.7
  73.2 2.3 %collective-permute-start.3 = (bf16[8,32,128]{2,1,0:T(8,128)(2,1)S(1)}, bf16[8,32,128]{2,1,0:T(8,128)(2,1)S(1)}, u32[]{:S(2)}, u32[]{:S(2)}) collective-permute-start(bf16[8,32,128]{2,1,0:T(8,128)(2,1)S(1)} %pad_maximum_fusion.7), channel_id=1, source_target_pairs={{0,2},{1,3},{2,0},{3,1},{4,6},{5,7},{6,4},{7,5},{8,10},{9,11},{10,... | collective-permute-start | bytes 196616 | tf_op jit(solution)/shard_map/ppermute | solution.py:22
  75.8 2.6 %collective-permute-done.3 = bf16[8,32,128]{2,1,0:T(8,128)(2,1)S(1)} collective-permute-done((bf16[8,32,128]{2,1,0:T(8,128)(2,1)S(1)}, bf16[8,32,128]{2,1,0:T(8,128)(2,1)S(1)}, u32[]{:S(2)}, u32[]{:S(2)}) %collective-permute-start.3) | collective-permute-done | bytes 65568 | tf_op jit(solution)/shard_map/ppermute | solution.py:22
  78.5 2.7 %collective-permute-start.4 = (bf16[16,32,128]{2,1,0:T(8,128)(2,1)S(1)}, bf16[16,32,128]{2,1,0:T(8,128)(2,1)S(1)}, u32[]{:S(2)}, u32[]{:S(2)}) collective-permute-start(bf16[16,32,128]{2,1,0:T(8,128)(2,1)S(1)} %get-tuple-element.55), channel_id=1, source_target_pairs={{0,8},{1,9},{2,10},{3,11},{4,12},{5,13},{6,14},{7,15},{8,0},{9,1},... | collective-permute-start | bytes 393224 | tf_op jit(solution)/shard_map/ppermute | solution.py:22
  81.3 0.6 collective-permute-done.11
  82.0 1.4 %collective-permute-start.12 = (bf16[12,32,128]{2,1,0:T(8,128)(2,1)S(1)}, bf16[12,32,128]{2,1,0:T(8,128)(2,1)S(1)}, u32[]{:S(2)}, u32[]{:S(2)}) collective-permute-start(bf16[12,32,128]{2,1,0:T(8,128)(2,1)S(1)} %pad_maximum_fusion.4), channel_id=1, source_target_pairs={{0,6},{1,7},{2,4},{3,5},{4,2},{5,3},{6,0},{7,1},{8,14},{9,15},{10,... | collective-permute-start | bytes 294920 | tf_op jit(solution)/shard_map/ppermute | solution.py:22
  83.4 0.8 collective-permute-done.4
  84.3 2.5 %collective-permute-start.5 = (bf16[32,32,128]{2,1,0:T(8,128)(2,1)S(1)}, bf16[32,32,128]{2,1,0:T(8,128)(2,1)S(1)}, u32[]{:S(2)}, u32[]{:S(2)}) collective-permute-start(bf16[32,32,128]{2,1,0:T(8,128)(2,1)S(1)} %get-tuple-element.47), channel_id=1, source_target_pairs={{0,24},{1,25},{2,26},{3,27},{4,28},{5,29},{6,30},{7,31},{8,16},{9,... | collective-permute-start | bytes 786440 | tf_op jit(solution)/shard_map/ppermute | solution.py:22
  86.7 1.2 %collective-permute-done.12 = bf16[12,32,128]{2,1,0:T(8,128)(2,1)S(1)} collective-permute-done((bf16[12,32,128]{2,1,0:T(8,128)(2,1)S(1)}, bf16[12,32,128]{2,1,0:T(8,128)(2,1)S(1)}, u32[]{:S(2)}, u32[]{:S(2)}) %collective-permute-start.12) | collective-permute-done | bytes 98336 | tf_op jit(solution)/shard_map/ppermute | solution.py:22
  88.0 2.4 %collective-permute-start.13 = (bf16[8,32,128]{2,1,0:T(8,128)(2,1)S(1)}, bf16[8,32,128]{2,1,0:T(8,128)(2,1)S(1)}, u32[]{:S(2)}, u32[]{:S(2)}) collective-permute-start(bf16[8,32,128]{2,1,0:T(8,128)(2,1)S(1)} %pad_maximum_fusion.8), channel_id=1, source_target_pairs={{0,32},{1,33},{2,34},{3,35},{4,36},{5,37},{6,38},{7,39},{8,40},{9,... | collective-permute-start | bytes 196616 | tf_op jit(solution)/shard_map/ppermute | solution.py:22
  90.4 1.5 %collective-permute-done.5 = bf16[32,32,128]{2,1,0:T(8,128)(2,1)S(1)} collective-permute-done((bf16[32,32,128]{2,1,0:T(8,128)(2,1)S(1)}, bf16[32,32,128]{2,1,0:T(8,128)(2,1)S(1)}, u32[]{:S(2)}, u32[]{:S(2)}) %collective-permute-start.5) | collective-permute-done | bytes 262176 | tf_op jit(solution)/shard_map/ppermute | solution.py:22
  92.2 0.5 collective-permute-done.13
  92.8 3.5 %collective-permute-start.14 = (bf16[10,32,128]{2,1,0:T(8,128)(2,1)S(1)}, bf16[10,32,128]{2,1,0:T(8,128)(2,1)S(1)}, u32[]{:S(2)}, u32[]{:S(2)}) collective-permute-start(bf16[10,32,128]{2,1,0:T(8,128)(2,1)S(1)} %pad_maximum_fusion.6), channel_id=1, source_target_pairs={{0,96},{1,97},{2,98},{3,99},{4,100},{5,101},{6,102},{7,103},{8,104... | collective-permute-start | bytes 245768 | tf_op jit(solution)/shard_map/ppermute | solution.py:22
  96.3 5.8 %forward.1.far_right = f32[32,128]{1,0:T(8,128)S(1)} custom-call(s32[1]{0:T(128)S(6)} %copy.38.count, s32[1,96]{1,0:T(1,128)S(1)} %get-tuple-element.77.slots, bf16[128,32,128]{2,1,0:T(8,128)(2,1)S(1)} %constant_dynamic-update-slice_fusion.18.gathered, f32[1,96,128,128]{3,2,1,0:T(8,128)} %coupling.3), custom_call_target="tpu_custom_call" | custom-call | flops 300000000 | bytes 7000000 | tf_op jit(solution)/shard_map/forward/pallas_call | solution.py:337
  102.3 8.6 %down.1 = (f32[32,4096]{1,0:T(8,128)}, f32[32,4096]{1,0:T(8,128)}) custom-call(s32[32]{0:T(128)S(1)} %copy-done.14, f32[32,128]{1,0:T(8,128)S(1)} %forward.1.far_right, f32[32,128]{1,0:T(8,128)S(1)} %fusion.18.far_left, f32[6,32,128]{2,1,0:T(8,128)S(1)} %pad_maximum_fusion.5.slabs, f32[3,128,128]{2,1,0:T(8,128)S(1)} %get-tuple-element.75.apex_row, ...), custom_call_target="tpu_custom_call" | custom-call | flops 400000000 | bytes 5000000 | tf_op jit(solution)/shard_map/down/pallas_call | solution.py:356
  (96 shorter events, 1.7 us)
Async XLA Ops:
  0.6 35.6 %copy-start = (f32[4,4,128,128]{3,2,1,0:T(8,128)S(1)}, f32[4,4,128,128]{3,2,1,0:T(8,128)}, u32[]{:S(2)}) copy-start(f32[4,4,128,128]{3,2,1,0:T(8,128)} %param.26) | copy-start | bytes 3145732
  0.6 35.6 %copy-start.17 = (s32[3]{0:T(128)S(1)}, s32[3]{0:T(128)}, u32[]{:S(2)}) copy-start(s32[3]{0:T(128)} %constant.48.clone) | copy-start | bytes 40
  0.7 1.3 %copy-start.1 = (f32[32,64,128]{2,1,0:T(8,128)S(1)}, f32[32,64,128]{2,1,0:T(8,128)}, u32[]{:S(2)}) copy-start(f32[32,64,128]{2,1,0:T(8,128)} %transfer.3) | copy-start | bytes 3145732
  2.0 1.0 copy-start.3
  3.0 0.9 copy-start.6
  4.0 0.9 copy-start.7
  4.9 0.8 copy-start.10
  5.8 0.7 copy-start.13
  6.4 31.7 %copy-start.15 = (s32[32,8]{0,1:T(8,128)S(1)}, s32[32,8]{0,1:T(8,128)}, u32[]{:S(2)}) copy-start(s32[32,8]{0,1:T(8,128)} %param.18) | copy-start | bytes 3076
  9.6 0.7 copy-start.8
  10.3 27.1 %copy-start.5 = (bf16[32,32,128]{2,1,0:T(8,128)(2,1)}, bf16[32,32,128]{2,1,0:T(8,128)(2,1)S(1)}, u32[]{:S(2)}) copy-start(bf16[32,32,128]{2,1,0:T(8,128)(2,1)S(1)} %get-tuple-element.17) | copy-start | bytes 786436
  10.3 28.5 %collective-permute-start = (bf16[1,32,128]{2,1,0:T(8,128)(2,1)S(1)}, bf16[1,32,128]{2,1,0:T(8,128)(2,1)}, u32[]{:S(2)}, u32[]{:S(2)}) collective-permute-start(bf16[1,32,128]{2,1,0:T(8,128)(2,1)S(1)} %bitcast.13), channel_id=1, source_target_pairs={{0,32},{1,33},{2,34},{3,35},{4,36},{5,37},{6,38},{7,39},{8,40},{9,... | collective-permute-start | bytes 24584 | tf_op jit(solution)/shard_map/ppermute | solution.py:22
  11.9 36.7 %collective-permute-start.8 = (f32[2,32,128]{2,1,0:T(8,128)}, f32[2,32,128]{2,1,0:T(8,128)}, u32[]{:S(2)}, u32[]{:S(2)}) collective-permute-start(f32[2,32,128]{2,1,0:T(8,128)} %bitcast.1), channel_id=1, source_target_pairs={{0,1},{1,0},{2,3},{3,2},{4,5},{5,4},{6,7},{7,6},{8,9},{9,8},{10,11... | collective-permute-start | bytes 98312 | tf_op jit(solution)/shard_map/ppermute | solution.py:22
  30.1 19.3 %collective-permute-start.7 = (f32[64,32,128]{2,1,0:T(8,128)}, f32[64,32,128]{2,1,0:T(8,128)}, u32[]{:S(2)}, u32[]{:S(2)}) collective-permute-start(f32[64,32,128]{2,1,0:T(8,128)} %get-tuple-element.15), channel_id=1, source_target_pairs={{0,1},{1,0},{2,3},{3,2},{4,5},{5,4},{6,7},{7,6},{8,9},{9,8},{10,11... | collective-permute-start | bytes 3145736 | tf_op jit(solution)/shard_map/ppermute | solution.py:22
  31.3 21.0 %collective-permute-start.16 = (bf16[4,32,128]{2,1,0:T(8,128)(2,1)}, bf16[4,32,128]{2,1,0:T(8,128)(2,1)}, u32[]{:S(2)}, u32[]{:S(2)}) collective-permute-start(bf16[4,32,128]{2,1,0:T(8,128)(2,1)} %get-tuple-element.36), channel_id=1, source_target_pairs={{1,0},{2,1},{3,2},{4,3},{5,4},{6,5},{7,6},{8,7},{9,8},{10,9},{11,1... | collective-permute-start | bytes 98312 | tf_op jit(solution)/shard_map/ppermute | solution.py:28
  32.5 19.8 %collective-permute-start.15 = (bf16[4,32,128]{2,1,0:T(8,128)(2,1)}, bf16[4,32,128]{2,1,0:T(8,128)(2,1)}, u32[]{:S(2)}, u32[]{:S(2)}) collective-permute-start(bf16[4,32,128]{2,1,0:T(8,128)(2,1)} %get-tuple-element.35), channel_id=1, source_target_pairs={{0,1},{1,2},{2,3},{3,4},{4,5},{5,6},{6,7},{7,8},{8,9},{9,10},{10,1... | collective-permute-start | bytes 98312 | tf_op jit(solution)/shard_map/ppermute | solution.py:28
  39.5 11.4 %collective-permute-start.1 = (bf16[2,32,128]{2,1,0:T(8,128)(2,1)S(1)}, bf16[2,32,128]{2,1,0:T(8,128)(2,1)S(1)}, u32[]{:S(2)}, u32[]{:S(2)}) collective-permute-start(bf16[2,32,128]{2,1,0:T(8,128)(2,1)S(1)} %pad_maximum_fusion.11), channel_id=1, source_target_pairs={{0,96},{1,97},{2,98},{3,99},{4,100},{5,101},{6,102},{7,103},{8,104... | collective-permute-start | bytes 49160 | tf_op jit(solution)/shard_map/ppermute | solution.py:22
  50.9 14.2 %collective-permute-start.9 = (bf16[36,32,128]{2,1,0:T(8,128)(2,1)S(1)}, bf16[36,32,128]{2,1,0:T(8,128)(2,1)S(1)}, u32[]{:S(2)}, u32[]{:S(2)}) collective-permute-start(bf16[36,32,128]{2,1,0:T(8,128)(2,1)S(1)} %pad_maximum_fusion.1), channel_id=1, source_target_pairs={{0,8},{1,9},{2,10},{3,11},{4,12},{5,13},{6,14},{7,15},{8,0},{9,1},... | collective-permute-start | bytes 884744 | tf_op jit(solution)/shard_map/ppermute | solution.py:22
  51.7 20.8 %collective-permute-start.2 = (bf16[4,32,128]{2,1,0:T(8,128)(2,1)S(1)}, bf16[4,32,128]{2,1,0:T(8,128)(2,1)S(1)}, u32[]{:S(2)}, u32[]{:S(2)}) collective-permute-start(bf16[4,32,128]{2,1,0:T(8,128)(2,1)S(1)} %pad_maximum_fusion.10), channel_id=1, source_target_pairs={{0,6},{1,7},{2,4},{3,5},{4,2},{5,3},{6,0},{7,1},{8,14},{9,15},{10,... | collective-permute-start | bytes 98312 | tf_op jit(solution)/shard_map/ppermute | solution.py:22
  52.3 23.5 %copy-start.16 = (bf16[16,32,128]{2,1,0:T(8,128)(2,1)S(1)}, bf16[16,32,128]{2,1,0:T(8,128)(2,1)}, u32[]{:S(2)}) copy-start(bf16[16,32,128]{2,1,0:T(8,128)(2,1)} %get-tuple-element.65) | copy-start | bytes 393220
  52.3 23.5 %copy-start.18 = (bf16[32,32,128]{2,1,0:T(8,128)(2,1)S(1)}, bf16[32,32,128]{2,1,0:T(8,128)(2,1)}, u32[]{:S(2)}) copy-start(bf16[32,32,128]{2,1,0:T(8,128)(2,1)} %get-tuple-element.64) | copy-start | bytes 786436
  53.4 1.0 copy-start.9
  54.3 0.7 copy-start.12
  55.1 20.7 %copy-start.19 = (bf16[64,32,128]{2,1,0:T(8,128)(2,1)S(1)}, bf16[64,32,128]{2,1,0:T(8,128)(2,1)}, u32[]{:S(2)}) copy-start(bf16[64,32,128]{2,1,0:T(8,128)(2,1)} %get-tuple-element.62) | copy-start | bytes 1572868
  65.3 36.9 %copy-start.2 = (f32[32,64,128]{2,1,0:T(8,128)S(1)}, f32[32,64,128]{2,1,0:T(8,128)}, u32[]{:S(2)}) copy-start(f32[32,64,128]{2,1,0:T(8,128)} %transfer.3) | copy-start | bytes 3145732
  65.3 36.9 %copy-start.4 = (bf16[32,64,128]{2,1,0:T(8,128)(2,1)S(1)}, bf16[32,64,128]{2,1,0:T(8,128)(2,1)}, u32[]{:S(2)}) copy-start(bf16[32,64,128]{2,1,0:T(8,128)(2,1)} %basis.3) | copy-start | bytes 1572868
  65.3 36.9 %copy-start.11 = (f32[1,128,128]{2,1,0:T(8,128)S(1)}, f32[1,128,128]{2,1,0:T(8,128)}, u32[]{:S(2)}) copy-start(f32[1,128,128]{2,1,0:T(8,128)} %lift.3) | copy-start | bytes 196612
  65.4 36.9 %copy-start.14 = (s32[32]{0:T(128)S(1)}, s32[32]{0:T(128)}, u32[]{:S(2)}) copy-start(s32[32]{0:T(128)} %points.3) | copy-start | bytes 388
  65.4 10.1 %collective-permute-start.10 = (bf16[20,32,128]{2,1,0:T(8,128)(2,1)S(1)}, bf16[20,32,128]{2,1,0:T(8,128)(2,1)S(1)}, u32[]{:S(2)}, u32[]{:S(2)}) collective-permute-start(bf16[20,32,128]{2,1,0:T(8,128)(2,1)S(1)} %pad_maximum_fusion.2), channel_id=1, source_target_pairs={{0,24},{1,25},{2,26},{3,27},{4,28},{5,29},{6,30},{7,31},{8,16},{9,... | collective-permute-start | bytes 491528 | tf_op jit(solution)/shard_map/ppermute | solution.py:22
  67.0 35.2 %collective-permute-start.17 = (bf16[4,32,128]{2,1,0:T(8,128)(2,1)S(1)}, bf16[4,32,128]{2,1,0:T(8,128)(2,1)S(1)}, u32[]{:S(2)}, u32[]{:S(2)}) collective-permute-start(bf16[4,32,128]{2,1,0:T(8,128)(2,1)S(1)} %get-tuple-element.34), channel_id=1, source_target_pairs={{0,1},{1,2},{2,3},{3,4},{4,5},{5,6},{6,7},{7,8},{8,9},{9,10},{10,1... | collective-permute-start | bytes 98312 | tf_op jit(solution)/shard_map/ppermute | solution.py:28
  71.1 31.1 %collective-permute-start.18 = (bf16[4,32,128]{2,1,0:T(8,128)(2,1)S(1)}, bf16[4,32,128]{2,1,0:T(8,128)(2,1)S(1)}, u32[]{:S(2)}, u32[]{:S(2)}) collective-permute-start(bf16[4,32,128]{2,1,0:T(8,128)(2,1)S(1)} %get-tuple-element.33), channel_id=1, source_target_pairs={{1,0},{2,1},{3,2},{4,3},{5,4},{6,5},{7,6},{8,7},{9,8},{10,9},{11,1... | collective-permute-start | bytes 98312 | tf_op jit(solution)/shard_map/ppermute | solution.py:28
  73.2 5.3 %collective-permute-start.3 = (bf16[8,32,128]{2,1,0:T(8,128)(2,1)S(1)}, bf16[8,32,128]{2,1,0:T(8,128)(2,1)S(1)}, u32[]{:S(2)}, u32[]{:S(2)}) collective-permute-start(bf16[8,32,128]{2,1,0:T(8,128)(2,1)S(1)} %pad_maximum_fusion.7), channel_id=1, source_target_pairs={{0,2},{1,3},{2,0},{3,1},{4,6},{5,7},{6,4},{7,5},{8,10},{9,11},{10,... | collective-permute-start | bytes 196616 | tf_op jit(solution)/shard_map/ppermute | solution.py:22
  75.7 6.2 %collective-permute-start.11 = (bf16[20,32,128]{2,1,0:T(8,128)(2,1)S(1)}, bf16[20,32,128]{2,1,0:T(8,128)(2,1)S(1)}, u32[]{:S(2)}, u32[]{:S(2)}) collective-permute-start(bf16[20,32,128]{2,1,0:T(8,128)(2,1)S(1)} %pad_maximum_fusion.3), channel_id=1, source_target_pairs={{0,2},{1,3},{2,0},{3,1},{4,6},{5,7},{6,4},{7,5},{8,10},{9,11},{10,... | collective-permute-start | bytes 491528 | tf_op jit(solution)/shard_map/ppermute | solution.py:22
  78.5 5.7 %collective-permute-start.4 = (bf16[16,32,128]{2,1,0:T(8,128)(2,1)S(1)}, bf16[16,32,128]{2,1,0:T(8,128)(2,1)S(1)}, u32[]{:S(2)}, u32[]{:S(2)}) collective-permute-start(bf16[16,32,128]{2,1,0:T(8,128)(2,1)S(1)} %get-tuple-element.55), channel_id=1, source_target_pairs={{0,8},{1,9},{2,10},{3,11},{4,12},{5,13},{6,14},{7,15},{8,0},{9,1},... | collective-permute-start | bytes 393224 | tf_op jit(solution)/shard_map/ppermute | solution.py:22
  82.0 5.9 %collective-permute-start.12 = (bf16[12,32,128]{2,1,0:T(8,128)(2,1)S(1)}, bf16[12,32,128]{2,1,0:T(8,128)(2,1)S(1)}, u32[]{:S(2)}, u32[]{:S(2)}) collective-permute-start(bf16[12,32,128]{2,1,0:T(8,128)(2,1)S(1)} %pad_maximum_fusion.4), channel_id=1, source_target_pairs={{0,6},{1,7},{2,4},{3,5},{4,2},{5,3},{6,0},{7,1},{8,14},{9,15},{10,... | collective-permute-start | bytes 294920 | tf_op jit(solution)/shard_map/ppermute | solution.py:22
  84.3 7.7 %collective-permute-start.5 = (bf16[32,32,128]{2,1,0:T(8,128)(2,1)S(1)}, bf16[32,32,128]{2,1,0:T(8,128)(2,1)S(1)}, u32[]{:S(2)}, u32[]{:S(2)}) collective-permute-start(bf16[32,32,128]{2,1,0:T(8,128)(2,1)S(1)} %get-tuple-element.47), channel_id=1, source_target_pairs={{0,24},{1,25},{2,26},{3,27},{4,28},{5,29},{6,30},{7,31},{8,16},{9,... | collective-permute-start | bytes 786440 | tf_op jit(solution)/shard_map/ppermute | solution.py:22
  88.0 4.6 %collective-permute-start.13 = (bf16[8,32,128]{2,1,0:T(8,128)(2,1)S(1)}, bf16[8,32,128]{2,1,0:T(8,128)(2,1)S(1)}, u32[]{:S(2)}, u32[]{:S(2)}) collective-permute-start(bf16[8,32,128]{2,1,0:T(8,128)(2,1)S(1)} %pad_maximum_fusion.8), channel_id=1, source_target_pairs={{0,32},{1,33},{2,34},{3,35},{4,36},{5,37},{6,38},{7,39},{8,40},{9,... | collective-permute-start | bytes 196616 | tf_op jit(solution)/shard_map/ppermute | solution.py:22
  92.1 4.2 %collective-permute-start.6 = (bf16[64,32,128]{2,1,0:T(8,128)(2,1)S(1)}, bf16[64,32,128]{2,1,0:T(8,128)(2,1)S(1)}, u32[]{:S(2)}, u32[]{:S(2)}) collective-permute-start(bf16[64,32,128]{2,1,0:T(8,128)(2,1)S(1)} %get-tuple-element.39), channel_id=1, source_target_pairs={{0,1},{1,0},{2,3},{3,2},{4,5},{5,4},{6,7},{7,6},{8,9},{9,8},{10,11... | collective-permute-start | bytes 1572872 | tf_op jit(solution)/shard_map/ppermute | solution.py:22
  92.8 9.3 %collective-permute-start.14 = (bf16[10,32,128]{2,1,0:T(8,128)(2,1)S(1)}, bf16[10,32,128]{2,1,0:T(8,128)(2,1)S(1)}, u32[]{:S(2)}, u32[]{:S(2)}) collective-permute-start(bf16[10,32,128]{2,1,0:T(8,128)(2,1)S(1)} %pad_maximum_fusion.6), channel_id=1, source_target_pairs={{0,96},{1,97},{2,98},{3,99},{4,100},{5,101},{6,102},{7,103},{8,104... | collective-permute-start | bytes 245768 | tf_op jit(solution)/shard_map/ppermute | solution.py:22

commit v2 on v1

v2 whole, which is shorter than its diff:
```python
import functools

import jax
import jax.numpy as jnp
from jax import lax
from jax.experimental import pallas as pl
from jax.experimental.pallas import tpu as pltpu
from jax.sharding import PartitionSpec as P

B = 128
HW = 4
AXES = ("slab", "leaf")
BF = jnp.bfloat16
F32 = jnp.float32

CORE, Z1, Z3, Y1, Y3, X1, X3 = 1, 2, 6, 8, 24, 32, 96
REDUCE_ORDER = (CORE, Y1, Y3, Z1, Z3, X1, X3)
GATHER_ORDER = (X1, X3, Z3, Z1, Y1, Y3, CORE)


def swapped(block, mask):
    route = [(i, i ^ mask) for i in range(lax.axis_size(AXES))]
    return lax.ppermute(block, AXES, route)


def passed_along(block, distance):
    devices = range(lax.axis_size(AXES))
    route = [(i - distance, i) for i in devices if i - distance in devices]
    return lax.ppermute(block, AXES, route)


def slot_of(difference, order, first_is_high):
    slot = jnp.zeros_like(difference)
    for step, mask in enumerate(order):
        if mask == CORE:
            bit = difference & 1
        else:
            shift = {Z1: 1, Z3: 1, Y1: 3, Y3: 3, X1: 5, X3: 5}[mask]
            low, high = (difference >> shift) & 1, (difference >> (shift + 1)) & 1
            bit = high if mask in (Z3, Y3, X3) else low ^ high
        place = len(order) - 1 - step if first_is_high else step
        slot = slot | (bit << place)
    return slot


def two(value):
    high = value.astype(BF)
    return high, (value - high.astype(F32)).astype(BF)


NN = (((1,), (0,)), ((), ()))
NT = (((1,), (1,)), ((), ()))


def dot(a, b, how):
    return lax.dot_general(a, b, how, preferred_element_type=F32)


def dot3(a, b, how):
    (ah, al), (bh, bl) = two(a), two(b)
    left = jnp.concatenate([ah, al, ah], axis=1)
    right = jnp.concatenate([bh, bh, bl], axis=1 if how is NT else 0)
    return dot(left, right, how)


def stacked(value):
    high, low = two(value)
    upper = jnp.concatenate([high, high], axis=1)
    return jnp.concatenate([upper, jnp.concatenate([low, jnp.zeros_like(low)], axis=1)], axis=0)


def both(value):
    half = value.shape[0] // 2
    return value[:half] + value[half:]


def diagonal(a, b):
    upper = jnp.concatenate([a, jnp.zeros_like(a)], axis=1)
    return jnp.concatenate([upper, jnp.concatenate([jnp.zeros_like(b), b], axis=1)], axis=0)


def pair_mask(points, c, rows):
    lane = lax.broadcasted_iota(jnp.int32, (rows, 2 * B), 1)
    return lane < jnp.where(lane < B, points[c], B + points[c + 1])


def up_kernel(
    points, right, left, basis, transfer, lift, mright, mleft, pright, pleft, shares, total
):
    step = pl.program_id(0)
    per = basis.shape[0]
    rhs = right.shape[0]
    part = jnp.zeros((4 * rhs, B), F32)
    for g in range(0, per, 2):
        mask = pair_mask(points, step * per + g, rhs)
        columns = slice(g * B, (g + 2) * B)
        xr = jnp.where(mask, right[:, columns].astype(F32), 0.0).astype(BF)
        xl = jnp.where(mask, left[:, columns].astype(F32), 0.0).astype(BF)
        for q in range(2):
            mright[g + q] = xr[:, q * B : (q + 1) * B]
            mleft[g + q] = xl[:, q * B : (q + 1) * B]
        leaf = dot(jnp.concatenate([xr, xl], axis=0), diagonal(basis[g], basis[g + 1]), NT)
        high, low = two(jnp.concatenate([transfer[g], transfer[g + 1]], axis=0))
        part = part + dot(stacked(leaf), jnp.concatenate([high, low], axis=0), NN)
    part = both(part)

    @pl.when(step == 0)
    def _():
        total[...] = part

    @pl.when(step > 0)
    def _():
        total[...] += part

    @pl.when(step == pl.num_programs(0) - 1)
    def _():
        pright[0] = total[:rhs].astype(BF)
        pleft[...] = total[rhs:]
        shares[...] = dot3(total[...], lift[0], NN)


def outward_kernel(count, slots, pleft, shares, coupling, keep, send, sums):
    step = pl.program_id(0)
    per = coupling.shape[1]
    rhs = pleft.shape[0]
    half = keep.shape[0] - 1

    @pl.when(step == 0)
    def _():
        keep[...] = jnp.zeros_like(keep)
        send[...] = jnp.zeros_like(send)
        for q in range(2):
            value = shares[q * rhs : (q + 1) * rhs]
            send[half + 1 + q] = value
            sums[q] = value

    wide = stacked(pleft[...])
    group = 8
    for start in range(0, per, group):
        values = []
        for g in range(start, start + group, 2):
            (ah, al), (bh, bl) = two(coupling[0, g]), two(coupling[0, g + 1])
            high, low = (jnp.concatenate(pair, axis=1) for pair in ((ah, bh), (al, bl)))
            value = both(dot(wide, jnp.concatenate([high, low], axis=0), NN))
            values += [value[:, :B], value[:, B:]]
        for q, value in enumerate(values):
            f = step * per + start + q
            slot = jnp.where(f < count[0], slots[0, f], half)
            other = jnp.where(f < count[0], slots[0, f] - half, -1)
            keep[jnp.minimum(slot, half)] = value
            send[jnp.where(other >= 0, other, half)] = value


def fold_kernel(exact, exact_next, add, came, partial, sums, payload, keep, sums_next):
    n = 2 * keep.shape[0]
    m = sums.shape[0]
    if came.dtype == F32:
        total = partial[:n] + came[:n]
        got = came[n + 1 : n + 1 + m]
    else:
        total = partial[...] + came[:n].astype(F32)
        start = n
        if exact:
            total = total + came[n : 2 * n].astype(F32)
            start = 2 * n
        got = came[start : start + m].astype(F32) + came[start + m : start + 2 * m].astype(F32)
    if add:
        sums_next[...] = sums[...] + got
    else:
        sums_next[:m] = sums[...]
        sums_next[m:] = got
    keep[...] = total[: n // 2]
    high, low = two(total[n // 2 :])
    place = n // 2
    payload[:place] = high
    if exact_next:
        payload[place : 2 * place] = low
        place = 2 * place
    high, low = two(sums_next[...])
    k = high.shape[0]
    payload[place : place + k] = high
    payload[place + k :] = low


def grow_kernel(gathered, came, out):
    n = gathered.shape[0]
    out[:n] = gathered[...]
    out[n:] = came[...]


def near_kernel(columns, first, mright, mleft, blocks, out, back, to_prev, to_next):
    step = pl.program_id(0)
    per, slots = blocks.shape[:2]
    clusters, rhs = mright.shape[:2]

    @pl.when(step == 0)
    def _():
        back[...] = jnp.zeros_like(back)

    group = 4
    for start in range(0, per, group):
        done = []
        for g in range(start, start + group):
            c = step * per + g
            row = jnp.concatenate([blocks[g, s] for s in range(slots)], axis=1)
            places = [columns[s, c] - first[0] for s in range(slots)]
            inside = []
            for place in places:
                own = place - HW
                value = mright[jnp.clip(own, 0, clusters - 1)]
                is_own = (own >= 0) & (own < clusters)
                inside.append(jnp.where(is_own, value, jnp.zeros_like(value)))
            out[c] = dot(row, jnp.concatenate(inside, axis=1), NT).T
            done.append((places, dot(mleft[c], row, NN)))
        for places, value in done:
            held = [back[place] for place in places]
            for s, place in enumerate(places):
                back[place] = held[s] + value[:, s * B : (s + 1) * B]

    @pl.when(step == pl.num_programs(0) - 1)
    def _():
        to_prev[:HW] = mright[:HW]
        to_prev[HW:] = back[:HW].astype(BF)
        to_next[:HW] = mright[clusters - HW :]
        to_next[HW:] = back[clusters + HW :].astype(BF)


def edge_kernel(columns, first, from_prev, from_next, low_blocks, high_blocks, out):
    slots = low_blocks.shape[1]
    clusters = columns.shape[1]
    for g in range(2 * HW):
        low = g < HW
        c = g if low else clusters - 2 * HW + g
        blocks, halo = (low_blocks, from_prev) if low else (high_blocks, from_next)
        row = jnp.concatenate([blocks[g % HW, s] for s in range(slots)], axis=1)
        values = []
        for s in range(slots):
            place = columns[s, c] - first[0]
            place = place if low else place - (clusters + HW)
            value = halo[jnp.clip(place, 0, HW - 1)]
            is_there = (place >= 0) & (place < HW)
            values.append(jnp.where(is_there, value, jnp.zeros_like(value)))
        out[g] = dot(row, jnp.concatenate(values, axis=1), NT).T


def forward_kernel(count, slots, own, came, coupling, out, total):
    step = pl.program_id(0)
    per = coupling.shape[1]
    half = own.shape[0]
    rows, values = [], []
    for g in range(per):
        f = step * per + g
        slot = slots[0, f]
        a = own[jnp.minimum(slot, half - 1)]
        b = came[jnp.maximum(slot - half, 0)]
        value = jnp.where(slot < half, a, b)
        value = jnp.where(f < count[0], value, jnp.zeros_like(value))
        values += [value, value]
        rows += two(coupling[0, g])
    part = dot(jnp.concatenate(rows, axis=1), jnp.concatenate(values, axis=1), NT)

    @pl.when(step == 0)
    def _():
        total[...] = part

    @pl.when(step > 0)
    def _():
        total[...] += part

    @pl.when(step == pl.num_programs(0) - 1)
    def _():
        out[...] = total[...].T


def down_kernel(
    points,
    place,
    far_right,
    partial,
    sums,
    came,
    apex,
    lift,
    transfer,
    basis,
    near_out,
    near_back,
    edge_out,
    from_prev,
    from_next,
    product,
    adjoint,
    hats,
):
    step = pl.program_id(0)
    per = basis.shape[0]
    clusters, rhs = near_out.shape[:2]

    @pl.when(step == 0)
    def _():
        slab = place[0]
        got = came[2:6].astype(F32) + came[6:10].astype(F32)
        slabs = [sums[2], sums[3], got[0], got[1], got[2], got[3]]
        top_right = jnp.zeros((rhs, B), F32)
        top_left = jnp.zeros((rhs, B), F32)
        for t, mask in enumerate((1, 3, 2)):
            top_right = top_right + dot3(slabs[2 * t], apex[slab, slab ^ mask], NT)
            top_left = top_left + dot3(slabs[2 * t + 1], apex[slab ^ mask, slab], NN)
        far_left = partial[0] + (came[0].astype(F32) + came[1].astype(F32))
        hats[...] = stacked(
            jnp.concatenate([far_right[...], far_left], axis=0)
            + dot3(jnp.concatenate([top_right, top_left], axis=0), lift[0], NT)
        )

    for g in range(0, per, 2):
        c = step * per + g
        high, low = two(jnp.concatenate([transfer[g], transfer[g + 1]], axis=0))
        down = both(dot(hats[...], jnp.concatenate([high, low], axis=1), NT))
        high, low = two(down)
        two_bases = diagonal(basis[g], basis[g + 1])
        far = dot(
            jnp.concatenate([high, low], axis=1),
            jnp.concatenate([two_bases, two_bases], axis=0),
            NN,
        )
        mask = pair_mask(points, c, rhs)
        columns = slice(g * B, (g + 2) * B)
        near = jnp.concatenate([near_out[c], near_out[c + 1]], axis=1)
        back = jnp.concatenate([near_back[HW + c], near_back[HW + c + 1]], axis=1)
        product[:, columns] = jnp.where(mask, near + far[:rhs], 0.0)
        adjoint[:, columns] = jnp.where(mask, back + far[rhs:], 0.0)

    def edge(g, c, halo):
        mask = lax.broadcasted_iota(jnp.int32, (rhs, B), 1) < points[c]
        columns = slice((c % per) * B, (c % per + 1) * B)
        product[:, columns] += jnp.where(mask, edge_out[g], 0.0)
        adjoint[:, columns] += jnp.where(mask, halo[HW + g % HW].astype(F32), 0.0)

    @pl.when(step == 0)
    def _():
        for g in range(HW):
            edge(g, g, from_prev)

    @pl.when(step == pl.num_programs(0) - 1)
    def _():
        for g in range(HW):
            edge(HW + g, clusters - HW + g, from_next)


SMEM = pl.BlockSpec(memory_space=pltpu.SMEM)
VMEM = pl.BlockSpec(memory_space=pltpu.VMEM)
MIB = 1024 * 1024


def shape(dims, kind):
    return jax.ShapeDtypeStruct(dims, kind)


def whole(*dims):
    return pl.BlockSpec(dims, lambda *_: (0,) * len(dims))


def call(kernel, name, grid, ins, outs, args, us, scratch=(), vmem=20):
    results = pl.pallas_call(
        kernel,
        grid=grid,
        out_shape=tuple(shape(dims, kind) for _, dims, kind in outs),
        in_specs=ins,
        out_specs=tuple(spec for spec, _, _ in outs),
        scratch_shapes=list(scratch),
        compiler_params=pltpu.CompilerParams(vmem_limit_bytes=vmem * MIB),
        cost_estimate=pl.CostEstimate(
            flops=1000, bytes_accessed=int(us * 3.6e6), transcendentals=0
        ),
        name=name,
    )(*args)
    return results


def shards(
    right_sides,
    left_sides,
    near_blocks,
    near_columns,
    cluster_points,
    leaf_basis,
    transfer,
    far_parents,
    far_count,
    coupling,
    slab_transfer,
    apex_coupling,
):
    rhs = right_sides.shape[0]
    clusters, near_slots = near_blocks.shape[:2]
    far_slots = coupling.shape[1]
    rank = leaf_basis.shape[1]
    me = lax.axis_index(AXES)
    slab = lax.axis_index("slab")
    devices = lax.axis_size(AXES)
    block = (rhs, B)
    all_clusters = (clusters, *block)
    half = devices // 2

    per = 16
    sides = pl.BlockSpec((rhs, per * B), lambda i: (0, i))
    bases = pl.BlockSpec((per, rank, B), lambda i: (i, 0, 0))
    some_clusters = pl.BlockSpec((per, *block), lambda i: (i, 0, 0))
    mright, mleft, pright, pleft, shares = call(
        up_kernel,
        "up",
        (clusters // per,),
        [SMEM, sides, sides, bases, bases, whole(1, B, B)],
        [
            (some_clusters, all_clusters, BF),
            (some_clusters, all_clusters, BF),
            (whole(1, *block), (1, *block), BF),
            (whole(*block), block, F32),
            (whole(2 * rhs, B), (2 * rhs, B), F32),
        ],
        (cluster_points, right_sides, left_sides, leaf_basis, transfer, slab_transfer),
        us=3,
        scratch=[pltpu.VMEM((2 * rhs, B), F32)],
        vmem=60,
    )

    difference = far_parents ^ me
    reduce_slots = slot_of(difference, REDUCE_ORDER, True)
    gather_slots = slot_of(difference, GATHER_ORDER, False)

    gathered = pright
    for mask in GATHER_ORDER[:-1]:
        came = swapped(gathered, mask)
        n = gathered.shape[0]
        dims = (2 * n, *block)
        (gathered,) = call(
            grow_kernel, "grow", (), [VMEM] * 2, [(VMEM, dims, BF)], (gathered, came), us=0.6
        )
    gathered_came = swapped(gathered, CORE)

    per = 48
    couplings = pl.BlockSpec((1, per, B, B), lambda i: (0, i, 0, 0))
    partial, sent, sums = call(
        outward_kernel,
        "outward",
        (far_slots // per,),
        [SMEM, SMEM, whole(*block), whole(2 * rhs, B), couplings],
        [
            (whole(half + 1, *block), (half + 1, *block), F32),
            (whole(half + 3, *block), (half + 3, *block), F32),
            (whole(2, *block), (2, *block), F32),
        ],
        (far_count, reduce_slots, pleft, shares, coupling),
        us=5,
    )
    came = swapped(sent, CORE)
    n = half
    for step, mask in enumerate(REDUCE_ORDER[1:]):
        exact_next = step >= 2
        add = REDUCE_ORDER[step] not in (X1, X3)
        m = 2 if add else 4
        rows = n // 2 * (2 if exact_next else 1) + 2 * m
        payload, partial, sums = call(
            functools.partial(fold_kernel, step >= 3, exact_next, add),
            "fold",
            (),
            [VMEM] * 3,
            [
                (VMEM, (rows, *block), BF),
                (VMEM, (n // 2, *block), F32),
                (VMEM, (m, *block), F32),
            ],
            (came, partial, sums),
            us=0.8,
        )
        came = swapped(payload, mask)
        n = n // 2

    columns = near_columns.T
    first = (me * clusters - HW)[None]
    per = 16
    halo = (2 * HW, *block)
    near_out, near_back, to_prev, to_next = call(
        near_kernel,
        "near",
        (clusters // per,),
        [
            SMEM,
            SMEM,
            whole(*all_clusters),
            whole(*all_clusters),
            pl.BlockSpec((per, near_slots, B, B), lambda i: (i, 0, 0, 0)),
        ],
        [
            (whole(*all_clusters), all_clusters, F32),
            (whole(clusters + 2 * HW, *block), (clusters + 2 * HW, *block), F32),
            (whole(*halo), halo, BF),
            (whole(*halo), halo, BF),
        ],
        (columns, first, mright, mleft, near_blocks),
        us=7,
    )
    from_next = passed_along(to_prev, -1)
    from_prev = passed_along(to_next, 1)
    last = clusters // HW - 1
    (edge_out,) = call(
        edge_kernel,
        "edge",
        (1,),
        [
            SMEM,
            SMEM,
            whole(*halo),
            whole(*halo),
            pl.BlockSpec((HW, near_slots, B, B), lambda i: (0, 0, 0, 0)),
            pl.BlockSpec((HW, near_slots, B, B), lambda i: (last, 0, 0, 0)),
        ],
        [(whole(*halo), halo, F32)],
        (columns, first, from_prev, from_next, near_blocks, near_blocks),
        us=2.5,
    )

    per = 48
    (far_right,) = call(
        forward_kernel,
        "forward",
        (far_slots // per,),
        [SMEM, SMEM, whole(half, *block), whole(half, *block), couplings],
        [(whole(*block), block, F32)],
        (far_count, gather_slots, gathered, gathered_came, coupling),
        us=5,
        scratch=[pltpu.VMEM((B, rhs), F32)],
    )

    per = 16
    sides = pl.BlockSpec((rhs, per * B), lambda i: (0, i))
    return call(
        down_kernel,
        "down",
        (clusters // per,),
        [
            SMEM,
            SMEM,
            whole(*block),
            whole(1, *block),
            whole(4, *block),
            whole(10, *block),
            whole(*apex_coupling.shape),
            whole(1, B, B),
            bases,
            bases,
            whole(*all_clusters),
            whole(clusters + 2 * HW, *block),
            whole(*halo),
            whole(*halo),
            whole(*halo),
        ],
        [(sides, (rhs, clusters * B), F32)] * 2,
        (
            cluster_points,
            slab[None],
            far_right,
            partial,
            sums,
            came,
            apex_coupling,
            slab_transfer,
            transfer,
            leaf_basis,
            near_out,
            near_back,
            edge_out,
            from_prev,
            from_next,
        ),
        us=4,
        scratch=[pltpu.VMEM((4 * rhs, 2 * B), BF)],
    )


def solution(mesh):
    return jax.shard_map(
        shards,
        mesh=mesh,
        in_specs=(
            P(None, AXES),
            P(None, AXES),
            P(AXES, None, None, None),
            P(AXES, None),
            P(AXES),
            P(AXES, None, None),
            P(AXES, None, None),
            P(AXES, None),
            P(AXES),
            P(AXES, None, None, None),
            P(AXES, None, None),
            P(),
        ),
        out_specs=(P(None, AXES), P(None, AXES)),
        check_vma=False,
    )
```

time: 113 us -> 89.8 us (0.79)
  the two profiles are of different devices: /device:TPU:0 before, /device:TPU:121 now
where the time goes in v2:
time: 89.8 us; the launch traced here: 89.4 us
  waiting for transfers between devices  36.9 us (41%)
  starting transfers between devices  25.3 us (28%)
  Pallas kernels  17.2 us (19%)
  local copies, waits for them, and re-layouts  7.72 us (9%)
  between operations  1.58 us (2%)
    ppermute x14, waiting for transfers between devices, swapped(): return lax.ppermute(block, AXES, route)  30.6 us
    pallas_call x18, Pallas kernels, call(): pl.pallas_call(kernel, grid=grid, out_shape=tuple((shape(dims, kind) for...  17.2 us
    ppermute x14, starting transfers between devices, swapped(): return lax.ppermute(block, AXES, route)  15.8 us
    ppermute x2, starting transfers between devices, passed_along(): return lax.ppermute(block, AXES, route)  9.47 us
    unnamed x32, local copies, waits for them, and re-layouts  7.72 us
    ppermute x2, waiting for transfers between devices, passed_along(): return lax.ppermute(block, AXES, route)  6.35 us
  transfers between devices with their start and end apart: 16, of which 11 were waited for; matrix products, arithmetic and copies ran while one was open for 0% of the time, Pallas kernels for 10%

profile of v2, /device:TPU:121, one launch (start us, length us, event | category | flops | bytes accessed | tf_op | source)
XLA Modules:
  0.0 89.4 jit_solution(8841900663048866600)
XLA Ops:
  1.3 0.7 shift-left_or_fusion
  2.0 3.6 %up.1 = (bf16[32,32,128]{2,1,0:T(8,128)(2,1)}, bf16[32,32,128]{2,1,0:T(8,128)(2,1)}, bf16[1,32,128]{2,1,0:T(8,128)(2,1)}, f32[32,128]{1,0:T(8,128)}, f32[64,128]{1,0:T(8,128)}) custom-call(s32[32]{0:T(128)} %points.3, bf16[32,4096]{1,0:T(8,128)(2,1)} %right.1, bf16[32,4096]{1,0:T(8,128)(2,1)} %left.1, bf16[32,64,128]{2,1,0:T(8,128)(2,1)} %basis.3, ...), custom_call_target="tpu_custom_call" | custom-call | flops 1000 | bytes 10800000 | tf_op jit(solution)/shard_map/up/pallas_call | solution.py:364
  5.5 2.8 %copy-done.2 = f32[1,96,128,128]{3,2,1,0:T(8,128)S(1)} copy-done((f32[1,96,128,128]{3,2,1,0:T(8,128)S(1)}, f32[1,96,128,128]{3,2,1,0:T(8,128)}, u32[]{:S(2)}) %copy-start.2) | copy-done | bytes 6291480
  8.3 0.8 copy-done.9
  9.1 0.7 copy-done.10
  9.8 2.1 %outward.1 = (f32[65,32,128]{2,1,0:T(8,128)S(1)}, f32[67,32,128]{2,1,0:T(8,128)S(1)}, f32[2,32,128]{2,1,0:T(8,128)S(1)}) custom-call(s32[1]{0:T(128)S(6)} %copy.14.count, s32[1,96]{1,0:T(1,128)S(1)} %get-tuple-element.62.slots, f32[32,128]{1,0:T(8,128)S(1)} %copy-done.10, f32[64,128]{1,0:T(8,128)S(1)} %copy-done.9, f32[1,96,128,128]{3,2,1,0:T(8,128)S(1)} %copy-done.2), custom_call_target="tpu_custom_call" | custom-call | flops 1000 | bytes 18000000 | tf_op jit(solution)/shard_map/outward/pallas_call | solution.py:364
  11.9 0.8 collective-permute-start.7
  12.6 1.2 %collective-permute-start = (bf16[1,32,128]{2,1,0:T(8,128)(2,1)S(1)}, bf16[1,32,128]{2,1,0:T(8,128)(2,1)S(1)}, u32[]{:S(2)}, u32[]{:S(2)}) collective-permute-start(bf16[1,32,128]{2,1,0:T(8,128)(2,1)S(1)} %copy-done.12), channel_id=1, source_target_pairs={{0,32},{1,33},{2,34},{3,35},{4,36},{5,37},{6,38},{7,39},{8,40},{9,... | collective-permute-start | bytes 24584 | tf_op jit(solution)/shard_map/ppermute | solution.py:23
  13.8 1.3 %collective-permute-done.came = bf16[1,32,128]{2,1,0:T(8,128)(2,1)S(1)} collective-permute-done((bf16[1,32,128]{2,1,0:T(8,128)(2,1)S(1)}, bf16[1,32,128]{2,1,0:T(8,128)(2,1)S(1)}, u32[]{:S(2)}, u32[]{:S(2)}) %collective-permute-start) | collective-permute-done | bytes 8224 | tf_op jit(solution)/shard_map/ppermute | solution.py:23
  15.1 2.5 %collective-permute-start.1 = (bf16[2,32,128]{2,1,0:T(8,128)(2,1)S(1)}, bf16[2,32,128]{2,1,0:T(8,128)(2,1)S(1)}, u32[]{:S(2)}, u32[]{:S(2)}) collective-permute-start(bf16[2,32,128]{2,1,0:T(8,128)(2,1)S(1)} %grow.6.gathered), channel_id=1, source_target_pairs={{0,96},{1,97},{2,98},{3,99},{4,100},{5,101},{6,102},{7,103},{8,104... | collective-permute-start | bytes 49160 | tf_op jit(solution)/shard_map/ppermute | solution.py:23
  17.6 1.3 %collective-permute-done.1.came = bf16[2,32,128]{2,1,0:T(8,128)(2,1)S(1)} collective-permute-done((bf16[2,32,128]{2,1,0:T(8,128)(2,1)S(1)}, bf16[2,32,128]{2,1,0:T(8,128)(2,1)S(1)}, u32[]{:S(2)}, u32[]{:S(2)}) %collective-permute-start.1) | collective-permute-done | bytes 16416 | tf_op jit(solution)/shard_map/ppermute | solution.py:23
  19.0 4.0 %collective-permute-done.2.came = bf16[4,32,128]{2,1,0:T(8,128)(2,1)S(1)} collective-permute-done((bf16[4,32,128]{2,1,0:T(8,128)(2,1)S(1)}, bf16[4,32,128]{2,1,0:T(8,128)(2,1)S(1)}, u32[]{:S(2)}, u32[]{:S(2)}) %collective-permute-start.2) | collective-permute-done | bytes 32800 | tf_op jit(solution)/shard_map/ppermute | solution.py:23
  22.9 3.1 %collective-permute-done.3.came = bf16[8,32,128]{2,1,0:T(8,128)(2,1)S(1)} collective-permute-done((bf16[8,32,128]{2,1,0:T(8,128)(2,1)S(1)}, bf16[8,32,128]{2,1,0:T(8,128)(2,1)S(1)}, u32[]{:S(2)}, u32[]{:S(2)}) %collective-permute-start.3) | collective-permute-done | bytes 65568 | tf_op jit(solution)/shard_map/ppermute | solution.py:23
  26.1 0.5 collective-permute-start.4
  26.6 0.1 fold.6
  26.7 1.1 %collective-permute-start.8 = (bf16[36,32,128]{2,1,0:T(8,128)(2,1)S(1)}, bf16[36,32,128]{2,1,0:T(8,128)(2,1)S(1)}, u32[]{:S(2)}, u32[]{:S(2)}) collective-permute-start(bf16[36,32,128]{2,1,0:T(8,128)(2,1)S(1)} %get-tuple-element.38), channel_id=1, source_target_pairs={{0,8},{1,9},{2,10},{3,11},{4,12},{5,13},{6,14},{7,15},{8,0},{9,1},... | collective-permute-start | bytes 884744 | tf_op jit(solution)/shard_map/ppermute | solution.py:23
  27.8 2.5 %collective-permute-done.4.came = bf16[16,32,128]{2,1,0:T(8,128)(2,1)S(1)} collective-permute-done((bf16[16,32,128]{2,1,0:T(8,128)(2,1)S(1)}, bf16[16,32,128]{2,1,0:T(8,128)(2,1)S(1)}, u32[]{:S(2)}, u32[]{:S(2)}) %collective-permute-start.4) | collective-permute-done | bytes 131104 | tf_op jit(solution)/shard_map/ppermute | solution.py:23
  30.3 0.1 collective-permute-start.5
  30.4 2.8 %collective-permute-done.8.came = bf16[36,32,128]{2,1,0:T(8,128)(2,1)S(1)} collective-permute-done((bf16[36,32,128]{2,1,0:T(8,128)(2,1)S(1)}, bf16[36,32,128]{2,1,0:T(8,128)(2,1)S(1)}, u32[]{:S(2)}, u32[]{:S(2)}) %collective-permute-start.8) | collective-permute-done | bytes 294944 | tf_op jit(solution)/shard_map/ppermute | solution.py:23
  33.1 0.1 fold.7
  33.2 0.0 copy-start.7
  33.2 0.0 copy-start.8
  33.2 0.0 copy-start.11
  33.2 0.1 collective-permute-start.9
  33.3 3.5 %collective-permute-done.5.came = bf16[32,32,128]{2,1,0:T(8,128)(2,1)S(1)} collective-permute-done((bf16[32,32,128]{2,1,0:T(8,128)(2,1)S(1)}, bf16[32,32,128]{2,1,0:T(8,128)(2,1)S(1)}, u32[]{:S(2)}, u32[]{:S(2)}) %collective-permute-start.5) | collective-permute-done | bytes 262176 | tf_op jit(solution)/shard_map/ppermute | solution.py:23
  36.8 6.8 %collective-permute-start.6 = (bf16[64,32,128]{2,1,0:T(8,128)(2,1)S(1)}, bf16[64,32,128]{2,1,0:T(8,128)(2,1)S(1)}, u32[]{:S(2)}, u32[]{:S(2)}) collective-permute-start(bf16[64,32,128]{2,1,0:T(8,128)(2,1)S(1)} %grow.11.own), channel_id=1, source_target_pairs={{0,1},{1,0},{2,3},{3,2},{4,5},{5,4},{6,7},{7,6},{8,9},{9,8},{10,11... | collective-permute-start | bytes 1572872 | tf_op jit(solution)/shard_map/ppermute | solution.py:23
  43.6 0.1 collective-permute-start.10
  43.7 4.2 %collective-permute-done.10.came = bf16[20,32,128]{2,1,0:T(8,128)(2,1)S(1)} collective-permute-done((bf16[20,32,128]{2,1,0:T(8,128)(2,1)S(1)}, bf16[20,32,128]{2,1,0:T(8,128)(2,1)S(1)}, u32[]{:S(2)}, u32[]{:S(2)}) %collective-permute-start.10) | collective-permute-done | bytes 163872 | tf_op jit(solution)/shard_map/ppermute | solution.py:23
  47.9 0.1 collective-permute-start.11
  48.0 4.7 %collective-permute-done.11.came = bf16[12,32,128]{2,1,0:T(8,128)(2,1)S(1)} collective-permute-done((bf16[12,32,128]{2,1,0:T(8,128)(2,1)S(1)}, bf16[12,32,128]{2,1,0:T(8,128)(2,1)S(1)}, u32[]{:S(2)}, u32[]{:S(2)}) %collective-permute-start.11) | collective-permute-done | bytes 98336 | tf_op jit(solution)/shard_map/ppermute | solution.py:23
  52.7 0.1 collective-permute-start.12
  52.8 3.4 %collective-permute-done.12.came = bf16[8,32,128]{2,1,0:T(8,128)(2,1)S(1)} collective-permute-done((bf16[8,32,128]{2,1,0:T(8,128)(2,1)S(1)}, bf16[8,32,128]{2,1,0:T(8,128)(2,1)S(1)}, u32[]{:S(2)}, u32[]{:S(2)}) %collective-permute-start.12) | collective-permute-done | bytes 65568 | tf_op jit(solution)/shard_map/ppermute | solution.py:23
  56.2 2.6 %collective-permute-start.13 = (bf16[10,32,128]{2,1,0:T(8,128)(2,1)S(1)}, bf16[10,32,128]{2,1,0:T(8,128)(2,1)S(1)}, u32[]{:S(2)}, u32[]{:S(2)}) collective-permute-start(bf16[10,32,128]{2,1,0:T(8,128)(2,1)S(1)} %get-tuple-element.55), channel_id=1, source_target_pairs={{0,96},{1,97},{2,98},{3,99},{4,100},{5,101},{6,102},{7,103},{8,104... | collective-permute-start | bytes 245768 | tf_op jit(solution)/shard_map/ppermute | solution.py:23
  58.8 3.4 %copy-done = bf16[32,8,128,128]{3,2,1,0:T(8,128)(2,1)S(1)} copy-done((bf16[32,8,128,128]{3,2,1,0:T(8,128)(2,1)S(1)}, bf16[32,8,128,128]{3,2,1,0:T(8,128)(2,1)}, u32[]{:S(2)}) %copy-start) | copy-done | bytes 8388632
  62.2 4.2 %near.1 = (f32[32,32,128]{2,1,0:T(8,128)S(1)}, f32[40,32,128]{2,1,0:T(8,128)S(1)}, bf16[8,32,128]{2,1,0:T(8,128)(2,1)S(1)}, bf16[8,32,128]{2,1,0:T(8,128)(2,1)S(1)}) custom-call(s32[8,32]{1,0:T(8,128)S(1)} %bitcast.5, s32[1]{0:T(128)} %bitcast.2.first, bf16[32,32,128]{2,1,0:T(8,128)(2,1)S(1)} %copy-done.7, bf16[32,32,128]{2,1,0:T(8,128)(2,1)S(1)} %copy-done.8, ...), custom_call_target="tpu_custom_call" | custom-call | flops 1000 | bytes 25200000 | tf_op jit(solution)/shard_map/near/pallas_call | solution.py:364
  66.4 5.9 %collective-permute-start.14 = (bf16[8,32,128]{2,1,0:T(8,128)(2,1)S(1)}, bf16[8,32,128]{2,1,0:T(8,128)(2,1)S(1)}, u32[]{:S(2)}, u32[]{:S(2)}) collective-permute-start(bf16[8,32,128]{2,1,0:T(8,128)(2,1)S(1)} %get-tuple-element.60), channel_id=1, source_target_pairs={{0,1},{1,2},{2,3},{3,4},{4,5},{5,6},{6,7},{7,8},{8,9},{9,10},{10,1... | collective-permute-start | bytes 196616 | tf_op jit(solution)/shard_map/ppermute | solution.py:29
  72.3 0.0 slice-start.1
  72.4 3.6 %collective-permute-start.15 = (bf16[8,32,128]{2,1,0:T(8,128)(2,1)S(1)}, bf16[8,32,128]{2,1,0:T(8,128)(2,1)S(1)}, u32[]{:S(2)}, u32[]{:S(2)}) collective-permute-start(bf16[8,32,128]{2,1,0:T(8,128)(2,1)S(1)} %get-tuple-element.61), channel_id=1, source_target_pairs={{1,0},{2,1},{3,2},{4,3},{5,4},{6,5},{7,6},{8,7},{9,8},{10,9},{11,1... | collective-permute-start | bytes 196616 | tf_op jit(solution)/shard_map/ppermute | solution.py:29
  75.9 6.3 %collective-permute-done.15.from_next = bf16[8,32,128]{2,1,0:T(8,128)(2,1)S(1)} collective-permute-done((bf16[8,32,128]{2,1,0:T(8,128)(2,1)S(1)}, bf16[8,32,128]{2,1,0:T(8,128)(2,1)S(1)}, u32[]{:S(2)}, u32[]{:S(2)}) %collective-permute-start.15) | collective-permute-done | bytes 65568 | tf_op jit(solution)/shard_map/ppermute | solution.py:29
  82.3 1.3 %edge.1.edge_out = f32[8,32,128]{2,1,0:T(8,128)S(1)} custom-call(s32[8,32]{1,0:T(8,128)S(1)} %bitcast.6, s32[1]{0:T(128)} %bitcast.2.first, bf16[8,32,128]{2,1,0:T(8,128)(2,1)S(1)} %collective-permute-done.14.from_prev, bf16[8,32,128]{2,1,0:T(8,128)(2,1)S(1)} %collective-permute-done.15.from_next, bf16[32,8,128,128]{3,2,1,0:T(8,128)(2,1)S(1)} %copy-done.1, ...), custom_call_target="tpu_custom_call" | custom-call | flops 1000 | bytes 9000000 | tf_op jit(solution)/shard_map/edge/pallas_call | solution.py:364
  83.7 0.0 copy-start.3
  83.7 0.0 copy-start.4
  83.7 0.0 copy-start.5
  83.7 0.0 copy-start.6
  83.7 0.0 copy-start.13
  83.7 2.6 %forward.1.far_right = f32[32,128]{1,0:T(8,128)S(1)} custom-call(s32[1]{0:T(128)S(6)} %copy.14.count, s32[1,96]{1,0:T(1,128)S(1)} %get-tuple-element.63.slots, bf16[64,32,128]{2,1,0:T(8,128)(2,1)S(1)} %grow.11.own, bf16[64,32,128]{2,1,0:T(8,128)(2,1)S(1)} %collective-permute-done.6.came, f32[1,96,128,128]{3,2,1,0:T(8,128)S(1)} %bitcast.4), custom_call_target="tpu_custom_call" | custom-call | flops 1000 | bytes 18000000 | tf_op jit(solution)/shard_map/forward/pallas_call | solution.py:364
  86.3 0.0 copy-done.3
  86.4 3.0 %down.1 = (f32[32,4096]{1,0:T(8,128)}, f32[32,4096]{1,0:T(8,128)}) custom-call(s32[32]{0:T(128)S(1)} %copy-done.13, s32[1]{0:T(128)} %bitcast.place, f32[32,128]{1,0:T(8,128)S(1)} %forward.1.far_right, f32[1,32,128]{2,1,0:T(8,128)S(1)} %get-tuple-element.53.partial, f32[4,32,128]{2,1,0:T(8,128)S(1)} %get-tuple-element.54.sums, ...), custom_call_target="tpu_custom_call" | custom-call | flops 1000 | bytes 14400000 | tf_op jit(solution)/shard_map/down/pallas_call | solution.py:364
  (36 shorter events, 0.3 us)
Async XLA Ops:
  5.5 2.8 %copy-start.2 = (f32[1,96,128,128]{3,2,1,0:T(8,128)S(1)}, f32[1,96,128,128]{3,2,1,0:T(8,128)}, u32[]{:S(2)}) copy-start(f32[1,96,128,128]{3,2,1,0:T(8,128)} %coupling.3) | copy-start | bytes 18874372
  8.3 0.8 copy-start.9
  9.1 0.7 copy-start.10
  9.8 2.8 %copy-start.12 = (bf16[1,32,128]{2,1,0:T(8,128)(2,1)S(1)}, bf16[1,32,128]{2,1,0:T(8,128)(2,1)}, u32[]{:S(2)}) copy-start(bf16[1,32,128]{2,1,0:T(8,128)(2,1)} %get-tuple-element.32.gathered) | copy-start | bytes 24580
  11.9 14.8 %collective-permute-start.7 = (f32[67,32,128]{2,1,0:T(8,128)S(1)}, f32[67,32,128]{2,1,0:T(8,128)S(1)}, u32[]{:S(2)}, u32[]{:S(2)}) collective-permute-start(f32[67,32,128]{2,1,0:T(8,128)S(1)} %get-tuple-element.35), channel_id=1, source_target_pairs={{0,1},{1,0},{2,3},{3,2},{4,5},{5,4},{6,7},{7,6},{8,9},{9,8},{10,11... | collective-permute-start | bytes 3293192 | tf_op jit(solution)/shard_map/ppermute | solution.py:23
  12.6 2.5 %collective-permute-start = (bf16[1,32,128]{2,1,0:T(8,128)(2,1)S(1)}, bf16[1,32,128]{2,1,0:T(8,128)(2,1)S(1)}, u32[]{:S(2)}, u32[]{:S(2)}) collective-permute-start(bf16[1,32,128]{2,1,0:T(8,128)(2,1)S(1)} %copy-done.12), channel_id=1, source_target_pairs={{0,32},{1,33},{2,34},{3,35},{4,36},{5,37},{6,38},{7,39},{8,40},{9,... | collective-permute-start | bytes 24584 | tf_op jit(solution)/shard_map/ppermute | solution.py:23
  15.1 3.8 %collective-permute-start.1 = (bf16[2,32,128]{2,1,0:T(8,128)(2,1)S(1)}, bf16[2,32,128]{2,1,0:T(8,128)(2,1)S(1)}, u32[]{:S(2)}, u32[]{:S(2)}) collective-permute-start(bf16[2,32,128]{2,1,0:T(8,128)(2,1)S(1)} %grow.6.gathered), channel_id=1, source_target_pairs={{0,96},{1,97},{2,98},{3,99},{4,100},{5,101},{6,102},{7,103},{8,104... | collective-permute-start | bytes 49160 | tf_op jit(solution)/shard_map/ppermute | solution.py:23
  18.9 4.0 %collective-permute-start.2 = (bf16[4,32,128]{2,1,0:T(8,128)(2,1)S(1)}, bf16[4,32,128]{2,1,0:T(8,128)(2,1)S(1)}, u32[]{:S(2)}, u32[]{:S(2)}) collective-permute-start(bf16[4,32,128]{2,1,0:T(8,128)(2,1)S(1)} %grow.7.gathered), channel_id=1, source_target_pairs={{0,6},{1,7},{2,4},{3,5},{4,2},{5,3},{6,0},{7,1},{8,14},{9,15},{10,... | collective-permute-start | bytes 98312 | tf_op jit(solution)/shard_map/ppermute | solution.py:23
  22.9 3.1 %collective-permute-start.3 = (bf16[8,32,128]{2,1,0:T(8,128)(2,1)S(1)}, bf16[8,32,128]{2,1,0:T(8,128)(2,1)S(1)}, u32[]{:S(2)}, u32[]{:S(2)}) collective-permute-start(bf16[8,32,128]{2,1,0:T(8,128)(2,1)S(1)} %grow.8.gathered), channel_id=1, source_target_pairs={{0,2},{1,3},{2,0},{3,1},{4,6},{5,7},{6,4},{7,5},{8,10},{9,11},{10,... | collective-permute-start | bytes 196616 | tf_op jit(solution)/shard_map/ppermute | solution.py:23
  26.1 4.2 %collective-permute-start.4 = (bf16[16,32,128]{2,1,0:T(8,128)(2,1)S(1)}, bf16[16,32,128]{2,1,0:T(8,128)(2,1)S(1)}, u32[]{:S(2)}, u32[]{:S(2)}) collective-permute-start(bf16[16,32,128]{2,1,0:T(8,128)(2,1)S(1)} %grow.9.gathered), channel_id=1, source_target_pairs={{0,8},{1,9},{2,10},{3,11},{4,12},{5,13},{6,14},{7,15},{8,0},{9,1},... | collective-permute-start | bytes 393224 | tf_op jit(solution)/shard_map/ppermute | solution.py:23
  26.7 6.4 %collective-permute-start.8 = (bf16[36,32,128]{2,1,0:T(8,128)(2,1)S(1)}, bf16[36,32,128]{2,1,0:T(8,128)(2,1)S(1)}, u32[]{:S(2)}, u32[]{:S(2)}) collective-permute-start(bf16[36,32,128]{2,1,0:T(8,128)(2,1)S(1)} %get-tuple-element.38), channel_id=1, source_target_pairs={{0,8},{1,9},{2,10},{3,11},{4,12},{5,13},{6,14},{7,15},{8,0},{9,1},... | collective-permute-start | bytes 884744 | tf_op jit(solution)/shard_map/ppermute | solution.py:23
  30.3 6.5 %collective-permute-start.5 = (bf16[32,32,128]{2,1,0:T(8,128)(2,1)S(1)}, bf16[32,32,128]{2,1,0:T(8,128)(2,1)S(1)}, u32[]{:S(2)}, u32[]{:S(2)}) collective-permute-start(bf16[32,32,128]{2,1,0:T(8,128)(2,1)S(1)} %grow.10.gathered), channel_id=1, source_target_pairs={{0,24},{1,25},{2,26},{3,27},{4,28},{5,29},{6,30},{7,31},{8,16},{9,... | collective-permute-start | bytes 786440 | tf_op jit(solution)/shard_map/ppermute | solution.py:23
  33.2 25.6 %copy-start.7 = (bf16[32,32,128]{2,1,0:T(8,128)(2,1)S(1)}, bf16[32,32,128]{2,1,0:T(8,128)(2,1)}, u32[]{:S(2)}) copy-start(bf16[32,32,128]{2,1,0:T(8,128)(2,1)} %get-tuple-element.56.mright) | copy-start | bytes 786436
  33.2 25.6 %copy-start.8 = (bf16[32,32,128]{2,1,0:T(8,128)(2,1)S(1)}, bf16[32,32,128]{2,1,0:T(8,128)(2,1)}, u32[]{:S(2)}) copy-start(bf16[32,32,128]{2,1,0:T(8,128)(2,1)} %get-tuple-element.57.mleft) | copy-start | bytes 786436
  33.2 25.6 %copy-start.11 = (s32[32,8]{0,1:T(8,128)S(1)}, s32[32,8]{0,1:T(8,128)}, u32[]{:S(2)}) copy-start(s32[32,8]{0,1:T(8,128)} %param.15) | copy-start | bytes 3076
  33.2 10.3 %collective-permute-start.9 = (bf16[20,32,128]{2,1,0:T(8,128)(2,1)S(1)}, bf16[20,32,128]{2,1,0:T(8,128)(2,1)S(1)}, u32[]{:S(2)}, u32[]{:S(2)}) collective-permute-start(bf16[20,32,128]{2,1,0:T(8,128)(2,1)S(1)} %get-tuple-element.41), channel_id=1, source_target_pairs={{0,24},{1,25},{2,26},{3,27},{4,28},{5,29},{6,30},{7,31},{8,16},{9,... | collective-permute-start | bytes 491528 | tf_op jit(solution)/shard_map/ppermute | solution.py:23
  36.8 46.8 %collective-permute-start.6 = (bf16[64,32,128]{2,1,0:T(8,128)(2,1)S(1)}, bf16[64,32,128]{2,1,0:T(8,128)(2,1)S(1)}, u32[]{:S(2)}, u32[]{:S(2)}) collective-permute-start(bf16[64,32,128]{2,1,0:T(8,128)(2,1)S(1)} %grow.11.own), channel_id=1, source_target_pairs={{0,1},{1,0},{2,3},{3,2},{4,5},{5,4},{6,7},{7,6},{8,9},{9,8},{10,11... | collective-permute-start | bytes 1572872 | tf_op jit(solution)/shard_map/ppermute | solution.py:23
  43.6 4.2 %collective-permute-start.10 = (bf16[20,32,128]{2,1,0:T(8,128)(2,1)S(1)}, bf16[20,32,128]{2,1,0:T(8,128)(2,1)S(1)}, u32[]{:S(2)}, u32[]{:S(2)}) collective-permute-start(bf16[20,32,128]{2,1,0:T(8,128)(2,1)S(1)} %get-tuple-element.44), channel_id=1, source_target_pairs={{0,2},{1,3},{2,0},{3,1},{4,6},{5,7},{6,4},{7,5},{8,10},{9,11},{10,... | collective-permute-start | bytes 491528 | tf_op jit(solution)/shard_map/ppermute | solution.py:23
  47.9 4.8 %collective-permute-start.11 = (bf16[12,32,128]{2,1,0:T(8,128)(2,1)S(1)}, bf16[12,32,128]{2,1,0:T(8,128)(2,1)S(1)}, u32[]{:S(2)}, u32[]{:S(2)}) collective-permute-start(bf16[12,32,128]{2,1,0:T(8,128)(2,1)S(1)} %get-tuple-element.47), channel_id=1, source_target_pairs={{0,6},{1,7},{2,4},{3,5},{4,2},{5,3},{6,0},{7,1},{8,14},{9,15},{10,... | collective-permute-start | bytes 294920 | tf_op jit(solution)/shard_map/ppermute | solution.py:23
  52.7 3.5 %collective-permute-start.12 = (bf16[8,32,128]{2,1,0:T(8,128)(2,1)S(1)}, bf16[8,32,128]{2,1,0:T(8,128)(2,1)S(1)}, u32[]{:S(2)}, u32[]{:S(2)}) collective-permute-start(bf16[8,32,128]{2,1,0:T(8,128)(2,1)S(1)} %get-tuple-element.50), channel_id=1, source_target_pairs={{0,32},{1,33},{2,34},{3,35},{4,36},{5,37},{6,38},{7,39},{8,40},{9,... | collective-permute-start | bytes 196616 | tf_op jit(solution)/shard_map/ppermute | solution.py:23
  56.2 30.1 %collective-permute-start.13 = (bf16[10,32,128]{2,1,0:T(8,128)(2,1)S(1)}, bf16[10,32,128]{2,1,0:T(8,128)(2,1)S(1)}, u32[]{:S(2)}, u32[]{:S(2)}) collective-permute-start(bf16[10,32,128]{2,1,0:T(8,128)(2,1)S(1)} %get-tuple-element.55), channel_id=1, source_target_pairs={{0,96},{1,97},{2,98},{3,99},{4,100},{5,101},{6,102},{7,103},{8,104... | collective-permute-start | bytes 245768 | tf_op jit(solution)/shard_map/ppermute | solution.py:23
  58.8 3.4 %copy-start = (bf16[32,8,128,128]{3,2,1,0:T(8,128)(2,1)S(1)}, bf16[32,8,128,128]{3,2,1,0:T(8,128)(2,1)}, u32[]{:S(2)}) copy-start(bf16[32,8,128,128]{3,2,1,0:T(8,128)(2,1)} %high_blocks.1) | copy-start | bytes 25165828
  62.2 20.1 %copy-start.1 = (bf16[32,8,128,128]{3,2,1,0:T(8,128)(2,1)S(1)}, bf16[32,8,128,128]{3,2,1,0:T(8,128)(2,1)}, u32[]{:S(2)}) copy-start(bf16[32,8,128,128]{3,2,1,0:T(8,128)(2,1)} %high_blocks.1) | copy-start | bytes 25165828
  62.2 21.5 %slice-start = ((s8[6291456]{0:T(1024)(128)(4,1)}), s8[4194304]{0:T(1024)(128)(4,1)S(1)}, s32[]{:S(2)}) async-start(s8[6291456]{0:T(1024)(128)(4,1)} %bitcast.3), calls=%async_computation | async-start | bytes 8388608
  66.4 9.5 %collective-permute-start.14 = (bf16[8,32,128]{2,1,0:T(8,128)(2,1)S(1)}, bf16[8,32,128]{2,1,0:T(8,128)(2,1)S(1)}, u32[]{:S(2)}, u32[]{:S(2)}) collective-permute-start(bf16[8,32,128]{2,1,0:T(8,128)(2,1)S(1)} %get-tuple-element.60), channel_id=1, source_target_pairs={{0,1},{1,2},{2,3},{3,4},{4,5},{5,6},{6,7},{7,8},{8,9},{9,10},{10,1... | collective-permute-start | bytes 196616 | tf_op jit(solution)/shard_map/ppermute | solution.py:29
  72.3 11.3 %slice-start.1 = ((s8[6291456]{0:T(1024)(128)(4,1)}), s8[2097152]{0:T(1024)(128)(4,1)S(1)}, s32[]{:S(2)}) async-start(s8[6291456]{0:T(1024)(128)(4,1)} %bitcast.3), calls=%async_computation.1 | async-start | bytes 4194304
  72.4 9.9 %collective-permute-start.15 = (bf16[8,32,128]{2,1,0:T(8,128)(2,1)S(1)}, bf16[8,32,128]{2,1,0:T(8,128)(2,1)S(1)}, u32[]{:S(2)}, u32[]{:S(2)}) collective-permute-start(bf16[8,32,128]{2,1,0:T(8,128)(2,1)S(1)} %get-tuple-element.61), channel_id=1, source_target_pairs={{1,0},{2,1},{3,2},{4,3},{5,4},{6,5},{7,6},{8,7},{9,8},{10,9},{11,1... | collective-permute-start | bytes 196616 | tf_op jit(solution)/shard_map/ppermute | solution.py:29
  83.7 2.7 %copy-start.3 = (f32[32,64,128]{2,1,0:T(8,128)S(1)}, f32[32,64,128]{2,1,0:T(8,128)}, u32[]{:S(2)}) copy-start(f32[32,64,128]{2,1,0:T(8,128)} %transfer.3) | copy-start | bytes 3145732
  83.7 2.7 %copy-start.4 = (bf16[32,64,128]{2,1,0:T(8,128)(2,1)S(1)}, bf16[32,64,128]{2,1,0:T(8,128)(2,1)}, u32[]{:S(2)}) copy-start(bf16[32,64,128]{2,1,0:T(8,128)(2,1)} %basis.3) | copy-start | bytes 1572868
  83.7 2.7 %copy-start.5 = (f32[4,4,128,128]{3,2,1,0:T(8,128)S(1)}, f32[4,4,128,128]{3,2,1,0:T(8,128)}, u32[]{:S(2)}) copy-start(f32[4,4,128,128]{3,2,1,0:T(8,128)} %apex.1) | copy-start | bytes 3145732
  83.7 2.7 %copy-start.6 = (f32[1,128,128]{2,1,0:T(8,128)S(1)}, f32[1,128,128]{2,1,0:T(8,128)}, u32[]{:S(2)}) copy-start(f32[1,128,128]{2,1,0:T(8,128)} %lift.3) | copy-start | bytes 196612
  83.7 2.7 %copy-start.13 = (s32[32]{0:T(128)S(1)}, s32[32]{0:T(128)}, u32[]{:S(2)}) copy-start(s32[32]{0:T(128)} %points.3) | copy-start | bytes 388

commit v3 on v2

v3 whole, which is shorter than its diff:
```python
import functools

import jax
import jax.numpy as jnp
import numpy as np
from jax import lax
from jax.experimental import pallas as pl
from jax.experimental.pallas import tpu as pltpu
from jax.sharding import PartitionSpec as P

B = 128
HW = 4
AXES = ("slab", "leaf")
BF = jnp.bfloat16
F32 = jnp.float32

Z, Y, X = 1, 3, 5
STEPS = ((Y, 0), (Y, 1), (Z, 0), (Z, 1), (X, 0), (X, 1))


def routed(block, step):
    axis, turn = step
    route = []
    for i in range(lax.axis_size(AXES)):
        pairing = 1 if (i & 1) == turn else 3
        route.append((i, i ^ (pairing << axis)))
    return lax.ppermute(block, AXES, route)


def to_other_core(block):
    return lax.ppermute(block, AXES, [(i, i ^ 1) for i in range(lax.axis_size(AXES))])


def passed_along(block, distance):
    devices = range(lax.axis_size(AXES))
    route = [(i - distance, i) for i in devices if i - distance in devices]
    return lax.ppermute(block, AXES, route)


def slot_tables(devices):
    reduce = np.zeros((2, devices), np.int32)
    gather = np.zeros((2, devices), np.int32)
    for core in range(2):
        for difference in range(devices):
            other = difference & 1
            for place, (axis, turn) in enumerate(STEPS):
                low, high = (difference >> axis) & 1, (difference >> (axis + 1)) & 1
                by_one = turn == core ^ other
                bit = low ^ high if by_one else high
                reduce[core, difference] |= bit << (len(STEPS) - 1 - place)
                gather[core, difference] |= bit << place
            reduce[core, difference] |= other << len(STEPS)
            gather[core, difference] |= other << len(STEPS)
    return reduce.reshape(-1), gather.reshape(-1)


def slot_in(table, parents, f, me, devices):
    return table[(me & 1) * devices + (parents[0, f] ^ me)]


def two(value):
    high = value.astype(BF)
    return high, (value - high.astype(F32)).astype(BF)


NN = (((1,), (0,)), ((), ()))
NT = (((1,), (1,)), ((), ()))


def dot(a, b, how):
    return lax.dot_general(a, b, how, preferred_element_type=F32)


def dot3(a, b, how):
    (ah, al), (bh, bl) = two(a), two(b)
    left = jnp.concatenate([ah, al, ah], axis=1)
    right = jnp.concatenate([bh, bh, bl], axis=1 if how is NT else 0)
    return dot(left, right, how)


def stacked(value):
    high, low = two(value)
    upper = jnp.concatenate([high, high], axis=1)
    return jnp.concatenate([upper, jnp.concatenate([low, jnp.zeros_like(low)], axis=1)], axis=0)


def both(value):
    half = value.shape[0] // 2
    return value[:half] + value[half:]


def diagonal(a, b):
    upper = jnp.concatenate([a, jnp.zeros_like(a)], axis=1)
    return jnp.concatenate([upper, jnp.concatenate([jnp.zeros_like(b), b], axis=1)], axis=0)


def pair_mask(points, c, rows):
    lane = lax.broadcasted_iota(jnp.int32, (rows, 2 * B), 1)
    return lane < jnp.where(lane < B, points[c], B + points[c + 1])


def rise_kernel(
    place,
    count,
    points_hbm,
    parents_hbm,
    table_hbm,
    right_hbm,
    left_hbm,
    basis_hbm,
    transfer_hbm,
    lift_hbm,
    coupling_hbm,
    mright,
    mleft,
    pright,
    keep,
    send,
    sums,
    points,
    parents,
    table,
    right,
    left,
    basis,
    transfer,
    lift,
    coupling,
    done,
):
    rhs = right.shape[0]
    clusters = basis.shape[0]
    far_slots = coupling.shape[1]
    half = keep.shape[0] - 1
    pieces, far_pieces = 2, 4
    count_of = iter(range(done.shape[0]))

    def fetch(source, target, index):
        return pltpu.make_async_copy(source.at[index], target.at[index], done.at[next(count_of)])

    per = clusters // pieces
    early = []
    for j in range(pieces):
        some = pl.ds(j * per, per)
        columns = (slice(None), pl.ds(j * per * B, per * B))
        early.append(
            [
                fetch(right_hbm, right, columns),
                fetch(left_hbm, left, columns),
                fetch(basis_hbm, basis, some),
                fetch(transfer_hbm, transfer, some),
            ]
        )
    early[0].append(fetch(points_hbm, points, slice(None)))
    early[1].append(fetch(parents_hbm, parents, slice(None)))
    early[1].append(fetch(table_hbm, table, slice(None)))
    early[1].append(fetch(lift_hbm, lift, slice(None)))
    far_per = far_slots // far_pieces
    late = [
        fetch(coupling_hbm, coupling, (slice(None), pl.ds(j * far_per, far_per)))
        for j in range(far_pieces)
    ]
    for copy in [*early[0], *early[1]]:
        copy.start()
    keep[...] = jnp.zeros_like(keep)
    send[...] = jnp.zeros_like(send)

    part = jnp.zeros((4 * rhs, B), F32)
    for j in range(pieces):
        for copy in early[j]:
            copy.wait()
        if j == 0:
            for copy in late:
                copy.start()
        for c in range(j * per, (j + 1) * per, 2):
            mask = pair_mask(points, c, rhs)
            columns = slice(c * B, (c + 2) * B)
            xr = jnp.where(mask, right[:, columns].astype(F32), 0.0).astype(BF)
            xl = jnp.where(mask, left[:, columns].astype(F32), 0.0).astype(BF)
            for q in range(2):
                mright[c + q] = xr[:, q * B : (q + 1) * B]
                mleft[c + q] = xl[:, q * B : (q + 1) * B]
            leaf = dot(jnp.concatenate([xr, xl], axis=0), diagonal(basis[c], basis[c + 1]), NT)
            high, low = two(jnp.concatenate([transfer[c], transfer[c + 1]], axis=0))
            part = part + dot(stacked(leaf), jnp.concatenate([high, low], axis=0), NN)
    total = both(part)
    pright[0] = total[:rhs].astype(BF)
    shares = dot3(total, lift[0], NN)
    for q in range(2):
        value = shares[q * rhs : (q + 1) * rhs]
        send[half + 1 + q] = value
        sums[q] = value

    wide = stacked(total[rhs:])
    me = place[0]
    group = 8
    for j in range(far_pieces):
        late[j].wait()
        for start in range(j * far_per, (j + 1) * far_per, group):
            values = []
            for f in range(start, start + group, 2):
                (ah, al), (bh, bl) = two(coupling[0, f]), two(coupling[0, f + 1])
                high, low = (jnp.concatenate(pair, axis=1) for pair in ((ah, bh), (al, bl)))
                value = both(dot(wide, jnp.concatenate([high, low], axis=0), NN))
                values += [value[:, :B], value[:, B:]]
            for q, value in enumerate(values):
                f = start + q
                slot = slot_in(table, parents, f, me, 2 * half)
                live = f < count[0]
                own = jnp.where(live & (slot < half), slot, half)
                other = jnp.where(live & (slot >= half), slot - half, half)
                keep[own] = value
                send[other] = value


def fold_kernel(exact, exact_next, add, cores, came, partial, sums, gathered, *rest):
    payload, keep, sums_next, gathered_next = rest[-4:]
    n = 2 * keep.shape[0]
    m = sums.shape[0]
    a = gathered.shape[0]
    if cores:
        total = partial[:n] + came[:n]
        got = came[n + 1 : n + 1 + m]
        gathered_next[...] = gathered[...]
    else:
        total = partial[...] + came[:n].astype(F32)
        start = n
        if exact:
            total = total + came[n : 2 * n].astype(F32)
            start = 2 * n
        got = came[start : start + m].astype(F32) + came[start + m : start + 2 * m].astype(F32)
        gathered_next[:a] = gathered[...]
        gathered_next[a:] = came[start + 2 * m :]
    if add:
        sums_next[...] = sums[...] + got
    else:
        sums_next[:m] = sums[...]
        sums_next[m:] = got
    keep[...] = total[: n // 2]
    high, low = two(total[n // 2 :])
    start = n // 2
    payload[:start] = high
    if exact_next:
        payload[start : 2 * start] = low
        start = 2 * start
    high, low = two(sums_next[...])
    k = high.shape[0]
    payload[start : start + k] = high
    payload[start + k : start + 2 * k] = low
    payload[start + 2 * k :] = gathered_next[...]


def tail_kernel(start, came, out):
    out[...] = came[start:]


def near_kernel(columns, first, mright, mleft, blocks, _, out, back, to_prev, to_next):
    step = pl.program_id(0)
    per, slots = blocks.shape[:2]
    clusters, rhs = mright.shape[:2]

    @pl.when(step == 0)
    def _():
        back[...] = jnp.zeros_like(back)

    group = 4
    for start in range(0, per, group):
        done = []
        for g in range(start, start + group):
            c = step * per + g
            row = jnp.concatenate([blocks[g, s] for s in range(slots)], axis=1)
            places = [columns[s, c] - first[0] for s in range(slots)]
            inside = []
            for place in places:
                own = place - HW
                value = mright[jnp.clip(own, 0, clusters - 1)]
                is_own = (own >= 0) & (own < clusters)
                inside.append(jnp.where(is_own, value, jnp.zeros_like(value)))
            out[c] = dot(row, jnp.concatenate(inside, axis=1), NT).T
            done.append((places, dot(mleft[c], row, NN)))
        for places, value in done:
            held = [back[place] for place in places]
            for s, place in enumerate(places):
                back[place] = held[s] + value[:, s * B : (s + 1) * B]

    @pl.when(step == pl.num_programs(0) - 1)
    def _():
        to_prev[:HW] = mright[:HW]
        to_prev[HW:] = back[:HW].astype(BF)
        to_next[:HW] = mright[clusters - HW :]
        to_next[HW:] = back[clusters + HW :].astype(BF)


def edge_kernel(columns, first, from_prev, from_next, low_blocks, high_blocks, out):
    slots = low_blocks.shape[1]
    clusters = columns.shape[1]
    for g in range(2 * HW):
        low = g < HW
        c = g if low else clusters - 2 * HW + g
        blocks, halo = (low_blocks, from_prev) if low else (high_blocks, from_next)
        row = jnp.concatenate([blocks[g % HW, s] for s in range(slots)], axis=1)
        values = []
        for s in range(slots):
            place = columns[s, c] - first[0]
            place = place if low else place - (clusters + HW)
            value = halo[jnp.clip(place, 0, HW - 1)]
            is_there = (place >= 0) & (place < HW)
            values.append(jnp.where(is_there, value, jnp.zeros_like(value)))
        out[g] = dot(row, jnp.concatenate(values, axis=1), NT).T


def forward_kernel(place, count, parents, table, own, came, own_other, other, coupling, out, all_of):
    far_slots = coupling.shape[1]
    quarter = own.shape[0]
    all_of[:quarter] = own[...]
    all_of[quarter : 2 * quarter] = came[came.shape[0] - quarter :]
    all_of[2 * quarter : 3 * quarter] = own_other[...]
    all_of[3 * quarter :] = other[...]
    me = place[0]
    total = jnp.zeros((B, own.shape[1]), F32)
    group = 48
    for start in range(0, far_slots, group):
        rows, values = [], []
        for f in range(start, start + group):
            value = all_of[slot_in(table, parents, f, me, 4 * quarter)]
            value = jnp.where(f < count[0], value, jnp.zeros_like(value))
            values += [value, value]
            rows += two(coupling[0, f])
        total = total + dot(
            jnp.concatenate(rows, axis=1), jnp.concatenate(values, axis=1), NT
        )
    out[...] = total.T


def down_kernel(
    points,
    place,
    far_right,
    partial,
    sums,
    came,
    apex,
    lift,
    transfer,
    basis,
    near_out,
    near_back,
    edge_out,
    from_prev,
    from_next,
    product,
    adjoint,
    hats,
):
    step = pl.program_id(0)
    per = basis.shape[0]
    clusters, rhs = near_out.shape[:2]

    @pl.when(step == 0)
    def _():
        core = place[0] & 1
        slab = place[0] >> X
        got = came[2:6].astype(F32) + came[6:10].astype(F32)
        slabs = [sums[2], sums[3], got[0], got[1], got[2], got[3]]
        top_right = jnp.zeros((rhs, B), F32)
        top_left = jnp.zeros((rhs, B), F32)
        for t, mask in enumerate((1 + 2 * core, 3 - 2 * core, 2)):
            top_right = top_right + dot3(slabs[2 * t], apex[slab, slab ^ mask], NT)
            top_left = top_left + dot3(slabs[2 * t + 1], apex[slab ^ mask, slab], NN)
        far_left = partial[0] + (came[0].astype(F32) + came[1].astype(F32))
        hats[...] = stacked(
            jnp.concatenate([far_right[...], far_left], axis=0)
            + dot3(jnp.concatenate([top_right, top_left], axis=0), lift[0], NT)
        )

    for g in range(0, per, 2):
        c = step * per + g
        high, low = two(jnp.concatenate([transfer[g], transfer[g + 1]], axis=0))
        down = both(dot(hats[...], jnp.concatenate([high, low], axis=1), NT))
        high, low = two(down)
        two_bases = diagonal(basis[g], basis[g + 1])
        far = dot(
            jnp.concatenate([high, low], axis=1),
            jnp.concatenate([two_bases, two_bases], axis=0),
            NN,
        )
        mask = pair_mask(points, c, rhs)
        columns = slice(g * B, (g + 2) * B)
        near = jnp.concatenate([near_out[c], near_out[c + 1]], axis=1)
        back = jnp.concatenate([near_back[HW + c], near_back[HW + c + 1]], axis=1)
        product[:, columns] = jnp.where(mask, near + far[:rhs], 0.0)
        adjoint[:, columns] = jnp.where(mask, back + far[rhs:], 0.0)

    def edge(g, c, halo):
        mask = lax.broadcasted_iota(jnp.int32, (rhs, B), 1) < points[c]
        columns = slice((c % per) * B, (c % per + 1) * B)
        product[:, columns] += jnp.where(mask, edge_out[g], 0.0)
        adjoint[:, columns] += jnp.where(mask, halo[HW + g % HW].astype(F32), 0.0)

    @pl.when(step == 0)
    def _():
        for g in range(HW):
            edge(g, g, from_prev)

    @pl.when(step == pl.num_programs(0) - 1)
    def _():
        for g in range(HW):
            edge(HW + g, clusters - HW + g, from_next)


SMEM = pl.BlockSpec(memory_space=pltpu.SMEM)
HBM = pl.BlockSpec(memory_space=pltpu.HBM)
ANY = pl.BlockSpec(memory_space=pl.ANY)
VMEM = pl.BlockSpec(memory_space=pltpu.VMEM)
MIB = 1024 * 1024


def shape(dims, kind):
    return jax.ShapeDtypeStruct(dims, kind)


def whole(*dims):
    return pl.BlockSpec(dims, lambda *_: (0,) * len(dims))


def call(kernel, name, grid, ins, outs, args, us, scratch=(), vmem=20):
    results = pl.pallas_call(
        kernel,
        grid=grid,
        out_shape=tuple(shape(dims, kind) for _, dims, kind in outs),
        in_specs=ins,
        out_specs=tuple(spec for spec, _, _ in outs),
        scratch_shapes=list(scratch),
        compiler_params=pltpu.CompilerParams(vmem_limit_bytes=vmem * MIB),
        cost_estimate=pl.CostEstimate(
            flops=1000, bytes_accessed=int(us * 3.6e6), transcendentals=0
        ),
        name=name,
    )(*args)
    return results


def shards(
    right_sides,
    left_sides,
    near_blocks,
    near_columns,
    cluster_points,
    leaf_basis,
    transfer,
    far_parents,
    far_count,
    coupling,
    slab_transfer,
    apex_coupling,
):
    rhs = right_sides.shape[0]
    clusters, near_slots = near_blocks.shape[:2]
    far_slots = coupling.shape[1]
    rank = leaf_basis.shape[1]
    me = lax.axis_index(AXES)
    devices = lax.axis_size(AXES)
    block = (rhs, B)
    all_clusters = (clusters, *block)
    half = devices // 2
    place = me.astype(jnp.int32)[None]
    reduce_table, gather_table = (jnp.asarray(table) for table in slot_tables(devices))

    mright, mleft, gathered, partial, sent, sums = call(
        rise_kernel,
        "rise",
        (),
        [SMEM] * 2 + [HBM] * 9,
        [
            (VMEM, all_clusters, BF),
            (VMEM, all_clusters, BF),
            (VMEM, (1, *block), BF),
            (VMEM, (half + 1, *block), F32),
            (VMEM, (half + 3, *block), F32),
            (VMEM, (2, *block), F32),
        ],
        (
            place,
            far_count,
            *(
                pltpu.with_memory_space_constraint(value, pltpu.HBM)
                for value in (
                    cluster_points,
                    far_parents,
                    reduce_table,
                    right_sides,
                    left_sides,
                    leaf_basis,
                    transfer,
                    slab_transfer,
                    coupling,
                )
            ),
        ),
        us=5,
        scratch=[
            pltpu.SMEM(cluster_points.shape, jnp.int32),
            pltpu.SMEM(far_parents.shape, jnp.int32),
            pltpu.SMEM(reduce_table.shape, jnp.int32),
            pltpu.VMEM(right_sides.shape, BF),
            pltpu.VMEM(left_sides.shape, BF),
            pltpu.VMEM(leaf_basis.shape, BF),
            pltpu.VMEM(transfer.shape, F32),
            pltpu.VMEM(slab_transfer.shape, F32),
            pltpu.VMEM(coupling.shape, F32),
            pltpu.SemaphoreType.DMA((16,)),
        ],
    )

    def fold(step, came, partial, sums, gathered, after=()):
        n = half >> step
        exact_next = step >= 2
        add = step == 0 or STEPS[step - 1][0] != X
        m = 2 if add else 4
        a = 1 << step
        rows = n // 2 * (2 if exact_next else 1) + 2 * m + a
        return call(
            functools.partial(fold_kernel, step >= 3, exact_next, add, step == 0),
            "fold",
            (),
            [VMEM] * 4 + [ANY] * len(after),
            [
                (VMEM, (rows, *block), BF),
                (VMEM, (n // 2, *block), F32),
                (VMEM, (m, *block), F32),
                (VMEM, (a, *block), BF),
            ],
            (came, partial, sums, gathered, *after),
            us=0.3,
        )

    came = to_other_core(sent)
    payload, partial, sums, gathered = fold(0, came, partial, sums, gathered)
    came = routed(payload, STEPS[0])

    columns = near_columns.T
    first = place * clusters - HW
    per = 16
    halo = (2 * HW, *block)
    near_out, near_back, to_prev, to_next = call(
        near_kernel,
        "near",
        (clusters // per,),
        [
            SMEM,
            SMEM,
            whole(*all_clusters),
            whole(*all_clusters),
            pl.BlockSpec((per, near_slots, B, B), lambda i: (i, 0, 0, 0)),
            ANY,
        ],
        [
            (whole(*all_clusters), all_clusters, F32),
            (whole(clusters + 2 * HW, *block), (clusters + 2 * HW, *block), F32),
            (whole(*halo), halo, BF),
            (whole(*halo), halo, BF),
        ],
        (columns, first, mright, mleft, near_blocks, payload),
        us=5,
    )
    payload, partial, sums, gathered = fold(1, came, partial, sums, gathered, (near_out,))
    came = routed(payload, STEPS[1])
    from_next = passed_along(to_prev, -1)
    from_prev = passed_along(to_next, 1)
    payload, partial, sums, gathered = fold(2, came, partial, sums, gathered)
    came = routed(payload, STEPS[2])
    payload, partial, sums, gathered = fold(3, came, partial, sums, gathered)
    came = routed(payload, STEPS[3])
    last = clusters // HW - 1
    (edge_out,) = call(
        edge_kernel,
        "edge",
        (1,),
        [
            SMEM,
            SMEM,
            whole(*halo),
            whole(*halo),
            pl.BlockSpec((HW, near_slots, B, B), lambda i: (0, 0, 0, 0)),
            pl.BlockSpec((HW, near_slots, B, B), lambda i: (last, 0, 0, 0)),
        ],
        [(whole(*halo), halo, F32)],
        (columns, first, from_prev, from_next, near_blocks, near_blocks),
        us=2,
    )
    payload, partial, sums, gathered = fold(4, came, partial, sums, gathered, (edge_out,))
    came = routed(payload, STEPS[4])
    payload, partial, sums, gathered = fold(5, came, partial, sums, gathered)
    came = routed(payload, STEPS[5])
    gathered_other = to_other_core(gathered)
    quarter = (half // 2, *block)
    (came_last,) = call(
        functools.partial(tail_kernel, 10),
        "tail",
        (),
        [VMEM],
        [(VMEM, quarter, BF)],
        (came,),
        us=0.3,
    )
    other = to_other_core(came_last)

    (far_right,) = call(
        forward_kernel,
        "forward",
        (),
        [SMEM] * 4 + [VMEM] * 5,
        [(VMEM, block, F32)],
        (
            place,
            far_count,
            far_parents,
            gather_table,
            gathered,
            came,
            gathered_other,
            other,
            coupling,
        ),
        us=3,
        scratch=[pltpu.VMEM((devices, *block), BF)],
    )

    per = 16
    sides = pl.BlockSpec((rhs, per * B), lambda i: (0, i))
    bases = pl.BlockSpec((per, rank, B), lambda i: (i, 0, 0))
    return call(
        down_kernel,
        "down",
        (clusters // per,),
        [
            SMEM,
            SMEM,
            whole(*block),
            whole(1, *block),
            whole(4, *block),
            whole(42, *block),
            whole(*apex_coupling.shape),
            whole(1, B, B),
            bases,
            bases,
            whole(*all_clusters),
            whole(clusters + 2 * HW, *block),
            whole(*halo),
            whole(*halo),
            whole(*halo),
        ],
        [(sides, (rhs, clusters * B), F32)] * 2,
        (
            cluster_points,
            place,
            far_right,
            partial,
            sums,
            came,
            apex_coupling,
            slab_transfer,
            transfer,
            leaf_basis,
            near_out,
            near_back,
            edge_out,
            from_prev,
            from_next,
        ),
        us=4,
        scratch=[pltpu.VMEM((4 * rhs, 2 * B), BF)],
    )


def solution(mesh):
    return jax.shard_map(
        shards,
        mesh=mesh,
        in_specs=(
            P(None, AXES),
            P(None, AXES),
            P(AXES, None, None, None),
            P(AXES, None),
            P(AXES),
            P(AXES, None, None),
            P(AXES, None, None),
            P(AXES, None),
            P(AXES),
            P(AXES, None, None, None),
            P(AXES, None, None),
            P(),
        ),
        out_specs=(P(None, AXES), P(None, AXES)),
        check_vma=False,
    )
```

time: 89.8 us -> 70.1 us (0.78)
  the two profiles are of different devices: /device:TPU:121 before, /device:TPU:0 now
where the time goes in v3:
time: 70.1 us; the launch traced here: 68.8 us
  starting transfers between devices  26.1 us (37%)
  waiting for transfers between devices  24.6 us (35%)
  Pallas kernels  16.5 us (24%)
  between operations  1.52 us (2%)
    ppermute x6, starting transfers between devices, routed(): return lax.ppermute(block, AXES, route)  23.1 us
    ppermute x6, waiting for transfers between devices, routed(): return lax.ppermute(block, AXES, route)  18.4 us
    pallas_call x12, Pallas kernels, call(): pl.pallas_call(kernel, grid=grid, out_shape=tuple((shape(dims, kind) for...  16.5 us
    ppermute x3, waiting for transfers between devices, to_other_core(): lax.ppermute(block, AXES, [(i, i ^ 1) for i in range(lax.axis_size(AXES))])  4.23 us
    ppermute x2, starting transfers between devices, passed_along(): return lax.ppermute(block, AXES, route)  2.84 us
    ppermute x2, waiting for transfers between devices, passed_along(): return lax.ppermute(block, AXES, route)  2 us
  transfers between devices with their start and end apart: 11, of which 8 were waited for; matrix products, arithmetic and copies ran while one was open for 0% of the time, Pallas kernels for 8%

profile of v3, /device:TPU:0, one launch (start us, length us, event | category | flops | bytes accessed | tf_op | source)
XLA Modules:
  0.0 68.8 jit_solution(5561106653827672409)
XLA Ops:
  1.3 0.0 copy-start
  1.3 5.1 %rise.1 = (bf16[32,32,128]{2,1,0:T(8,128)(2,1)S(1)}, bf16[32,32,128]{2,1,0:T(8,128)(2,1)S(1)}, bf16[1,32,128]{2,1,0:T(8,128)(2,1)S(1)}, f32[65,32,128]{2,1,0:T(8...) custom-call(s32[1]{0:T(128)} %bitcast.place, s32[1]{0:T(128)S(6)} %copy.16.count, s32[32]{0:T(128)} %points.1, ...), custom_call_target="tpu_custom_call" | custom-call | flops 1000 | bytes 18000000 | tf_op jit(solution)/shard_map/rise/pallas_call | solution.py:427
  6.4 0.1 collective-permute-start
  6.5 2.7 %collective-permute-done.came = f32[67,32,128]{2,1,0:T(8,128)S(1)} collective-permute-done((f32[67,32,128]{2,1,0:T(8,128)S(1)}, f32[67,32,128]{2,1,0:T(8,128)S(1)}, u32[]{:S(2)}, u32[]{:S(2)}) %collective-permute-start) | collective-permute-done | bytes 1097760 | tf_op jit(solution)/shard_map/ppermute | solution.py:31
  9.2 0.1 fold.6
  9.3 1.7 %collective-permute-start.1 = (bf16[37,32,128]{2,1,0:T(8,128)(2,1)S(1)}, bf16[37,32,128]{2,1,0:T(8,128)(2,1)S(1)}, u32[]{:S(2)}, u32[]{:S(2)}) collective-permute-start(bf16[37,32,128]{2,1,0:T(8,128)(2,1)S(1)} %get-tuple-element.40._), channel_id=1, source_target_pairs={{0,8},{1,25},{2,10},{3,27},{4,12},{5,29},{6,14},{7,31},{8,0},{9,17... | collective-permute-start | bytes 909320 | tf_op jit(solution)/shard_map/ppermute | solution.py:27
  11.1 0.0 copy-done
  11.1 0.0 copy-done.5
  11.1 4.3 %near.1 = (f32[32,32,128]{2,1,0:T(8,128)S(1)}, f32[40,32,128]{2,1,0:T(8,128)S(1)}, bf16[8,32,128]{2,1,0:T(8,128)(2,1)S(1)}, bf16[8,32,128]{2,1,0:T(8,128)(2,1)S(1)}) custom-call(s32[8,32]{1,0:T(8,128)S(1)} %bitcast.4, s32[1]{0:T(128)S(6)} %sub.3.first, bf16[32,32,128]{2,1,0:T(8,128)(2,1)S(1)} %get-tuple-element.44.mright, ...), custom_call_target="tpu_custom_call" | custom-call | flops 1000 | bytes 18000000 | tf_op jit(solution)/shard_map/near/pallas_call | solution.py:427
  15.3 0.9 %collective-permute-done.1.came = bf16[37,32,128]{2,1,0:T(8,128)(2,1)S(1)} collective-permute-done((bf16[37,32,128]{2,1,0:T(8,128)(2,1)S(1)}, bf16[37,32,128]{2,1,0:T(8,128)(2,1)S(1)}, u32[]{:S(2)}, u32[]{:S(2)}) %collective-permute-start.1) | collective-permute-done | bytes 303136 | tf_op jit(solution)/shard_map/ppermute | solution.py:27
  16.2 0.1 fold.7
  16.3 3.2 %collective-permute-start.2 = (bf16[22,32,128]{2,1,0:T(8,128)(2,1)S(1)}, bf16[22,32,128]{2,1,0:T(8,128)(2,1)S(1)}, u32[]{:S(2)}, u32[]{:S(2)}) collective-permute-start(bf16[22,32,128]{2,1,0:T(8,128)(2,1)S(1)} %get-tuple-element.47), channel_id=1, source_target_pairs={{0,24},{1,9},{2,26},{3,11},{4,28},{5,13},{6,30},{7,15},{8,16},{9,1... | collective-permute-start | bytes 540680 | tf_op jit(solution)/shard_map/ppermute | solution.py:27
  19.5 3.6 %collective-permute-done.2.came = bf16[22,32,128]{2,1,0:T(8,128)(2,1)S(1)} collective-permute-done((bf16[22,32,128]{2,1,0:T(8,128)(2,1)S(1)}, bf16[22,32,128]{2,1,0:T(8,128)(2,1)S(1)}, u32[]{:S(2)}, u32[]{:S(2)}) %collective-permute-start.2) | collective-permute-done | bytes 180256 | tf_op jit(solution)/shard_map/ppermute | solution.py:27
  23.1 0.1 fold.8
  23.1 2.1 %collective-permute-start.3 = (bf16[24,32,128]{2,1,0:T(8,128)(2,1)S(1)}, bf16[24,32,128]{2,1,0:T(8,128)(2,1)S(1)}, u32[]{:S(2)}, u32[]{:S(2)}) collective-permute-start(bf16[24,32,128]{2,1,0:T(8,128)(2,1)S(1)} %get-tuple-element.51), channel_id=1, source_target_pairs={{0,2},{1,7},{2,0},{3,5},{4,6},{5,3},{6,4},{7,1},{8,10},{9,15},{10,... | collective-permute-start | bytes 589832 | tf_op jit(solution)/shard_map/ppermute | solution.py:27
  25.2 3.7 %collective-permute-done.3.came = bf16[24,32,128]{2,1,0:T(8,128)(2,1)S(1)} collective-permute-done((bf16[24,32,128]{2,1,0:T(8,128)(2,1)S(1)}, bf16[24,32,128]{2,1,0:T(8,128)(2,1)S(1)}, u32[]{:S(2)}, u32[]{:S(2)}) %collective-permute-start.3) | collective-permute-done | bytes 196640 | tf_op jit(solution)/shard_map/ppermute | solution.py:27
  28.9 4.2 %collective-permute-start.4 = (bf16[20,32,128]{2,1,0:T(8,128)(2,1)S(1)}, bf16[20,32,128]{2,1,0:T(8,128)(2,1)S(1)}, u32[]{:S(2)}, u32[]{:S(2)}) collective-permute-start(bf16[20,32,128]{2,1,0:T(8,128)(2,1)S(1)} %get-tuple-element.55), channel_id=1, source_target_pairs={{0,6},{1,3},{2,4},{3,1},{4,2},{5,7},{6,0},{7,5},{8,14},{9,11},{10,... | collective-permute-start | bytes 491528 | tf_op jit(solution)/shard_map/ppermute | solution.py:27
  33.1 1.3 %collective-permute-start.5 = (bf16[8,32,128]{2,1,0:T(8,128)(2,1)S(1)}, bf16[8,32,128]{2,1,0:T(8,128)(2,1)S(1)}, u32[]{:S(2)}, u32[]{:S(2)}) collective-permute-start(bf16[8,32,128]{2,1,0:T(8,128)(2,1)S(1)} %get-tuple-element.59), channel_id=1, source_target_pairs={{0,1},{1,2},{2,3},{3,4},{4,5},{5,6},{6,7},{7,8},{8,9},{9,10},{10,1... | collective-permute-start | bytes 196616 | tf_op jit(solution)/shard_map/ppermute | solution.py:37
  34.4 0.0 slice-start
  34.4 0.0 slice-start.1
  34.4 1.6 %collective-permute-start.6 = (bf16[8,32,128]{2,1,0:T(8,128)(2,1)S(1)}, bf16[8,32,128]{2,1,0:T(8,128)(2,1)S(1)}, u32[]{:S(2)}, u32[]{:S(2)}) collective-permute-start(bf16[8,32,128]{2,1,0:T(8,128)(2,1)S(1)} %get-tuple-element.60), channel_id=1, source_target_pairs={{1,0},{2,1},{3,2},{4,3},{5,4},{6,5},{7,6},{8,7},{9,8},{10,9},{11,1... | collective-permute-start | bytes 196616 | tf_op jit(solution)/shard_map/ppermute | solution.py:37
  36.0 0.0 collective-permute-done.5.from_prev
  36.0 2.0 %collective-permute-done.6.from_next = bf16[8,32,128]{2,1,0:T(8,128)(2,1)S(1)} collective-permute-done((bf16[8,32,128]{2,1,0:T(8,128)(2,1)S(1)}, bf16[8,32,128]{2,1,0:T(8,128)(2,1)S(1)}, u32[]{:S(2)}, u32[]{:S(2)}) %collective-permute-start.6) | collective-permute-done | bytes 65568 | tf_op jit(solution)/shard_map/ppermute | solution.py:37
  38.0 1.3 %edge.1.rest_0_.edge_out = f32[8,32,128]{2,1,0:T(8,128)S(1)} custom-call(s32[8,32]{1,0:T(8,128)S(1)} %bitcast.5, s32[1]{0:T(128)S(6)} %sub.3.first, bf16[8,32,128]{2,1,0:T(8,128)(2,1)S(1)} %collective-permute-done.5.from_prev, bf16[8,32,128]{2,1,0:T(8,128)(2,1)S(1)} %collective-permute-done.6.from_next, bf16[32,8,128,128]{3,2,1,0:T(8,128)(2,1)S(1)} %copy-done, ...), custom_call_target="tpu_custom_call" | custom-call | flops 1000 | bytes 7200000 | tf_op jit(solution)/shard_map/edge/pallas_call | solution.py:427
  39.4 0.0 copy-start.6
  39.4 0.0 copy-start.8
  39.4 0.0 collective-permute-done.4.came
  39.4 8.6 %collective-permute-start.7 = (bf16[24,32,128]{2,1,0:T(8,128)(2,1)S(1)}, bf16[24,32,128]{2,1,0:T(8,128)(2,1)S(1)}, u32[]{:S(2)}, u32[]{:S(2)}) collective-permute-start(bf16[24,32,128]{2,1,0:T(8,128)(2,1)S(1)} %get-tuple-element.61), channel_id=1, source_target_pairs={{0,32},{1,97},{2,34},{3,99},{4,36},{5,101},{6,38},{7,103},{8,40},{... | collective-permute-start | bytes 589832 | tf_op jit(solution)/shard_map/ppermute | solution.py:27
  48.1 5.0 %collective-permute-done.7.came = bf16[24,32,128]{2,1,0:T(8,128)(2,1)S(1)} collective-permute-done((bf16[24,32,128]{2,1,0:T(8,128)(2,1)S(1)}, bf16[24,32,128]{2,1,0:T(8,128)(2,1)S(1)}, u32[]{:S(2)}, u32[]{:S(2)}) %collective-permute-start.7) | collective-permute-done | bytes 196640 | tf_op jit(solution)/shard_map/ppermute | solution.py:27
  53.1 3.2 %collective-permute-start.8 = (bf16[42,32,128]{2,1,0:T(8,128)(2,1)S(1)}, bf16[42,32,128]{2,1,0:T(8,128)(2,1)S(1)}, u32[]{:S(2)}, u32[]{:S(2)}) collective-permute-start(bf16[42,32,128]{2,1,0:T(8,128)(2,1)S(1)} %get-tuple-element.66), channel_id=1, source_target_pairs={{0,96},{1,33},{2,98},{3,35},{4,100},{5,37},{6,102},{7,39},{8,104},... | collective-permute-start | bytes 1032200 | tf_op jit(solution)/shard_map/ppermute | solution.py:27
  56.3 0.0 collective-permute-start.9
  56.3 5.3 %collective-permute-done.8.came = bf16[42,32,128]{2,1,0:T(8,128)(2,1)S(1)} collective-permute-done((bf16[42,32,128]{2,1,0:T(8,128)(2,1)S(1)}, bf16[42,32,128]{2,1,0:T(8,128)(2,1)S(1)}, u32[]{:S(2)}, u32[]{:S(2)}) %collective-permute-start.8) | collective-permute-done | bytes 344096 | tf_op jit(solution)/shard_map/ppermute | solution.py:27
  61.7 0.0 copy-start.1
  61.7 0.0 copy-start.2
  61.7 0.0 copy-start.3
  61.7 0.0 copy-start.4
  61.7 0.0 copy-start.7
  61.7 0.1 collective-permute-start.10
  61.8 0.0 collective-permute-done.9.own_other
  61.8 1.5 %collective-permute-done.10.other = bf16[32,32,128]{2,1,0:T(8,128)(2,1)S(1)} collective-permute-done((bf16[32,32,128]{2,1,0:T(8,128)(2,1)S(1)}, bf16[32,32,128]{2,1,0:T(8,128)(2,1)S(1)}, u32[]{:S(2)}, u32[]{:S(2)}) %collective-permute-start.10) | collective-permute-done | bytes 262176 | tf_op jit(solution)/shard_map/ppermute | solution.py:31
  63.3 0.0 slice-done
  63.3 0.0 slice-done.1
  63.3 0.0 copy-done.6
  63.3 0.0 copy-done.8
  63.4 2.4 %forward.1.far_right = f32[32,128]{1,0:T(8,128)S(1)} custom-call(s32[1]{0:T(128)} %bitcast.place, s32[1]{0:T(128)S(6)} %copy.16.count, s32[1,96]{1,0:T(1,128)S(1)} %copy-done.6, s32[256]{0:T(256)S(1)} %copy-done.8, bf16[32,32,128]{2,1,0:T(8,128)(2,1)S(1)} %get-tuple-element.65.own, bf16[42,32,128]{2,1,0:T(8,128)(2,1)S(1)} %collective-permute-done.8.came, ...), custom_call_target="tpu_custom_call" | custom-call | flops 1000 | bytes 10800000 | tf_op jit(solution)/shard_map/forward/pallas_call | solution.py:427
  65.8 0.0 copy-done.1
  65.8 0.0 copy-done.2
  65.8 3.0 %down.1 = (f32[32,4096]{1,0:T(8,128)}, f32[32,4096]{1,0:T(8,128)}) custom-call(s32[32]{0:T(128)S(1)} %copy-done.7, s32[1]{0:T(128)} %bitcast.place, f32[32,128]{1,0:T(8,128)S(1)} %forward.1.far_right, f32[1,32,128]{2,1,0:T(8,128)S(1)} %get-tuple-element.67.partial, f32[4,32,128]{2,1,0:T(8,128)S(1)} %get-tuple-element.68.sums, ...), custom_call_target="tpu_custom_call" | custom-call | flops 1000 | bytes 14400000 | tf_op jit(solution)/shard_map/down/pallas_call | solution.py:427
  (9 shorter events, 0.2 us)
Async XLA Ops:
  1.3 9.8 %copy-start = (bf16[32,8,128,128]{3,2,1,0:T(8,128)(2,1)S(1)}, bf16[32,8,128,128]{3,2,1,0:T(8,128)(2,1)}, u32[]{:S(2)}) copy-start(bf16[32,8,128,128]{3,2,1,0:T(8,128)(2,1)} %high_blocks.1) | copy-start | bytes 25165828
  6.4 2.8 %collective-permute-start = (f32[67,32,128]{2,1,0:T(8,128)S(1)}, f32[67,32,128]{2,1,0:T(8,128)S(1)}, u32[]{:S(2)}, u32[]{:S(2)}) collective-permute-start(f32[67,32,128]{2,1,0:T(8,128)S(1)} %get-tuple-element.36), channel_id=1, source_target_pairs={{0,1},{1,0},{2,3},{3,2},{4,5},{5,4},{6,7},{7,6},{8,9},{9,8},{10,11... | collective-permute-start | bytes 3293192 | tf_op jit(solution)/shard_map/ppermute | solution.py:31
  9.2 1.9 %copy-start.5 = (s32[32,8]{0,1:T(8,128)S(1)}, s32[32,8]{0,1:T(8,128)}, u32[]{:S(2)}) copy-start(s32[32,8]{0,1:T(8,128)} %param.17) | copy-start | bytes 3076
  9.3 6.9 %collective-permute-start.1 = (bf16[37,32,128]{2,1,0:T(8,128)(2,1)S(1)}, bf16[37,32,128]{2,1,0:T(8,128)(2,1)S(1)}, u32[]{:S(2)}, u32[]{:S(2)}) collective-permute-start(bf16[37,32,128]{2,1,0:T(8,128)(2,1)S(1)} %get-tuple-element.40._), channel_id=1, source_target_pairs={{0,8},{1,25},{2,10},{3,27},{4,12},{5,29},{6,14},{7,31},{8,0},{9,17... | collective-permute-start | bytes 909320 | tf_op jit(solution)/shard_map/ppermute | solution.py:27
  16.3 6.8 %collective-permute-start.2 = (bf16[22,32,128]{2,1,0:T(8,128)(2,1)S(1)}, bf16[22,32,128]{2,1,0:T(8,128)(2,1)S(1)}, u32[]{:S(2)}, u32[]{:S(2)}) collective-permute-start(bf16[22,32,128]{2,1,0:T(8,128)(2,1)S(1)} %get-tuple-element.47), channel_id=1, source_target_pairs={{0,24},{1,9},{2,26},{3,11},{4,28},{5,13},{6,30},{7,15},{8,16},{9,1... | collective-permute-start | bytes 540680 | tf_op jit(solution)/shard_map/ppermute | solution.py:27
  23.1 5.8 %collective-permute-start.3 = (bf16[24,32,128]{2,1,0:T(8,128)(2,1)S(1)}, bf16[24,32,128]{2,1,0:T(8,128)(2,1)S(1)}, u32[]{:S(2)}, u32[]{:S(2)}) collective-permute-start(bf16[24,32,128]{2,1,0:T(8,128)(2,1)S(1)} %get-tuple-element.51), channel_id=1, source_target_pairs={{0,2},{1,7},{2,0},{3,5},{4,6},{5,3},{6,4},{7,1},{8,10},{9,15},{10,... | collective-permute-start | bytes 589832 | tf_op jit(solution)/shard_map/ppermute | solution.py:27
  28.9 10.5 %collective-permute-start.4 = (bf16[20,32,128]{2,1,0:T(8,128)(2,1)S(1)}, bf16[20,32,128]{2,1,0:T(8,128)(2,1)S(1)}, u32[]{:S(2)}, u32[]{:S(2)}) collective-permute-start(bf16[20,32,128]{2,1,0:T(8,128)(2,1)S(1)} %get-tuple-element.55), channel_id=1, source_target_pairs={{0,6},{1,3},{2,4},{3,1},{4,2},{5,7},{6,0},{7,5},{8,14},{9,11},{10,... | collective-permute-start | bytes 491528 | tf_op jit(solution)/shard_map/ppermute | solution.py:27
  33.1 2.9 %collective-permute-start.5 = (bf16[8,32,128]{2,1,0:T(8,128)(2,1)S(1)}, bf16[8,32,128]{2,1,0:T(8,128)(2,1)S(1)}, u32[]{:S(2)}, u32[]{:S(2)}) collective-permute-start(bf16[8,32,128]{2,1,0:T(8,128)(2,1)S(1)} %get-tuple-element.59), channel_id=1, source_target_pairs={{0,1},{1,2},{2,3},{3,4},{4,5},{5,6},{6,7},{7,8},{8,9},{9,10},{10,1... | collective-permute-start | bytes 196616 | tf_op jit(solution)/shard_map/ppermute | solution.py:37
  34.4 28.9 %slice-start = ((s8[6291456]{0:T(1024)(128)(4,1)}), s8[4194304]{0:T(1024)(128)(4,1)S(1)}, s32[]{:S(2)}) async-start(s8[6291456]{0:T(1024)(128)(4,1)} %bitcast.2), calls=%async_computation | async-start | bytes 8388608
  34.4 28.9 %slice-start.1 = ((s8[6291456]{0:T(1024)(128)(4,1)}), s8[2097152]{0:T(1024)(128)(4,1)S(1)}, s32[]{:S(2)}) async-start(s8[6291456]{0:T(1024)(128)(4,1)} %bitcast.2), calls=%async_computation.1 | async-start | bytes 4194304
  34.4 3.6 %collective-permute-start.6 = (bf16[8,32,128]{2,1,0:T(8,128)(2,1)S(1)}, bf16[8,32,128]{2,1,0:T(8,128)(2,1)S(1)}, u32[]{:S(2)}, u32[]{:S(2)}) collective-permute-start(bf16[8,32,128]{2,1,0:T(8,128)(2,1)S(1)} %get-tuple-element.60), channel_id=1, source_target_pairs={{1,0},{2,1},{3,2},{4,3},{5,4},{6,5},{7,6},{8,7},{9,8},{10,9},{11,1... | collective-permute-start | bytes 196616 | tf_op jit(solution)/shard_map/ppermute | solution.py:37
  39.4 24.0 %copy-start.6 = (s32[1,96]{1,0:T(1,128)S(1)}, s32[1,96]{1,0:T(1,128)}, u32[]{:S(2)}) copy-start(s32[1,96]{1,0:T(1,128)} %parents.1) | copy-start | bytes 1156
  39.4 24.0 %copy-start.8 = (s32[256]{0:T(256)S(1)}, s32[256]{0:T(256)}, u32[]{:S(2)}) copy-start(s32[256]{0:T(256)} %constant.21.clone.table) | copy-start | bytes 3076
  39.4 13.6 %collective-permute-start.7 = (bf16[24,32,128]{2,1,0:T(8,128)(2,1)S(1)}, bf16[24,32,128]{2,1,0:T(8,128)(2,1)S(1)}, u32[]{:S(2)}, u32[]{:S(2)}) collective-permute-start(bf16[24,32,128]{2,1,0:T(8,128)(2,1)S(1)} %get-tuple-element.61), channel_id=1, source_target_pairs={{0,32},{1,97},{2,34},{3,99},{4,36},{5,101},{6,38},{7,103},{8,40},{... | collective-permute-start | bytes 589832 | tf_op jit(solution)/shard_map/ppermute | solution.py:27
  53.1 8.5 %collective-permute-start.8 = (bf16[42,32,128]{2,1,0:T(8,128)(2,1)S(1)}, bf16[42,32,128]{2,1,0:T(8,128)(2,1)S(1)}, u32[]{:S(2)}, u32[]{:S(2)}) collective-permute-start(bf16[42,32,128]{2,1,0:T(8,128)(2,1)S(1)} %get-tuple-element.66), channel_id=1, source_target_pairs={{0,96},{1,33},{2,98},{3,35},{4,100},{5,37},{6,102},{7,39},{8,104},... | collective-permute-start | bytes 1032200 | tf_op jit(solution)/shard_map/ppermute | solution.py:27
  56.3 5.5 %collective-permute-start.9 = (bf16[32,32,128]{2,1,0:T(8,128)(2,1)S(1)}, bf16[32,32,128]{2,1,0:T(8,128)(2,1)S(1)}, u32[]{:S(2)}, u32[]{:S(2)}) collective-permute-start(bf16[32,32,128]{2,1,0:T(8,128)(2,1)S(1)} %get-tuple-element.65.own), channel_id=1, source_target_pairs={{0,1},{1,0},{2,3},{3,2},{4,5},{5,4},{6,7},{7,6},{8,9},{9,8},{10,11... | collective-permute-start | bytes 786440 | tf_op jit(solution)/shard_map/ppermute | solution.py:31
  61.7 4.1 %copy-start.1 = (f32[32,64,128]{2,1,0:T(8,128)S(1)}, f32[32,64,128]{2,1,0:T(8,128)}, u32[]{:S(2)}) copy-start(f32[32,64,128]{2,1,0:T(8,128)} %transfer.1) | copy-start | bytes 3145732
  61.7 4.1 %copy-start.2 = (bf16[32,64,128]{2,1,0:T(8,128)(2,1)S(1)}, bf16[32,64,128]{2,1,0:T(8,128)(2,1)}, u32[]{:S(2)}) copy-start(bf16[32,64,128]{2,1,0:T(8,128)(2,1)} %basis.1) | copy-start | bytes 1572868
  61.7 4.1 %copy-start.3 = (f32[4,4,128,128]{3,2,1,0:T(8,128)S(1)}, f32[4,4,128,128]{3,2,1,0:T(8,128)}, u32[]{:S(2)}) copy-start(f32[4,4,128,128]{3,2,1,0:T(8,128)} %apex.1) | copy-start | bytes 3145732
  61.7 4.1 %copy-start.4 = (f32[1,128,128]{2,1,0:T(8,128)S(1)}, f32[1,128,128]{2,1,0:T(8,128)}, u32[]{:S(2)}) copy-start(f32[1,128,128]{2,1,0:T(8,128)} %lift.1) | copy-start | bytes 196612
  61.7 4.1 %copy-start.7 = (s32[32]{0:T(128)S(1)}, s32[32]{0:T(128)}, u32[]{:S(2)}) copy-start(s32[32]{0:T(128)} %points.1) | copy-start | bytes 388
  61.7 1.6 %collective-permute-start.10 = (bf16[32,32,128]{2,1,0:T(8,128)(2,1)S(1)}, bf16[32,32,128]{2,1,0:T(8,128)(2,1)S(1)}, u32[]{:S(2)}, u32[]{:S(2)}) collective-permute-start(bf16[32,32,128]{2,1,0:T(8,128)(2,1)S(1)} %tail.1), channel_id=1, source_target_pairs={{0,1},{1,0},{2,3},{3,2},{4,5},{5,4},{6,7},{7,6},{8,9},{9,8},{10,11... | collective-permute-start | bytes 786440 | tf_op jit(solution)/shard_map/ppermute | solution.py:31

commit v4 on v3

v4 whole, which is shorter than its diff:
```python
import functools

import jax
import jax.numpy as jnp
import numpy as np
from jax import lax
from jax.experimental import pallas as pl
from jax.experimental.pallas import tpu as pltpu
from jax.sharding import PartitionSpec as P

B = 128
HW = 4
AXES = ("slab", "leaf")
BF = jnp.bfloat16
F32 = jnp.float32

Z, Y, X = 1, 3, 5
STEPS = ((Y, 0), (Y, 1), (Z, 0), (Z, 1), (X, 0), (X, 1))
GATHER_STEPS = (*STEPS[4:], *STEPS[:4])


def routed(block, step):
    axis, turn = step
    route = []
    for i in range(lax.axis_size(AXES)):
        pairing = 1 if (i & 1) == turn else 3
        route.append((i, i ^ (pairing << axis)))
    return lax.ppermute(block, AXES, route)


def to_other_core(block):
    return lax.ppermute(block, AXES, [(i, i ^ 1) for i in range(lax.axis_size(AXES))])


def passed_along(block, distance):
    devices = range(lax.axis_size(AXES))
    route = [(i - distance, i) for i in devices if i - distance in devices]
    return lax.ppermute(block, AXES, route)


def slot_tables(devices):
    def table(order):
        slots = np.zeros((2, devices), np.int32)
        for core in range(2):
            for difference in range(devices):
                other = difference & 1
                for place, (axis, turn) in enumerate(order):
                    low, high = (difference >> axis) & 1, (difference >> (axis + 1)) & 1
                    by_one = turn == core ^ other
                    slots[core, difference] |= (low ^ high if by_one else high) << place
                slots[core, difference] |= other << len(order)
        return jnp.asarray(slots.reshape(-1))

    return table(STEPS[::-1]), table(GATHER_STEPS)


def slot_in(table, parents, f, me, devices):
    return table[(me & 1) * devices + (parents[0, f] ^ me)]


def two(value):
    high = value.astype(BF)
    return high, (value - high.astype(F32)).astype(BF)


NN = (((1,), (0,)), ((), ()))
NT = (((1,), (1,)), ((), ()))


def dot(a, b, how):
    return lax.dot_general(a, b, how, preferred_element_type=F32)


def dot3(a, b, how):
    (ah, al), (bh, bl) = two(a), two(b)
    left = jnp.concatenate([ah, al, ah], axis=1)
    right = jnp.concatenate([bh, bh, bl], axis=1 if how is NT else 0)
    return dot(left, right, how)


def stacked(value):
    high, low = two(value)
    upper = jnp.concatenate([high, high], axis=1)
    return jnp.concatenate([upper, jnp.concatenate([low, jnp.zeros_like(low)], axis=1)], axis=0)


def both(value):
    half = value.shape[0] // 2
    return value[:half] + value[half:]


def diagonal(a, b):
    upper = jnp.concatenate([a, jnp.zeros_like(a)], axis=1)
    return jnp.concatenate([upper, jnp.concatenate([jnp.zeros_like(b), b], axis=1)], axis=0)


def pair_mask(points, c, rows):
    lane = lax.broadcasted_iota(jnp.int32, (rows, 2 * B), 1)
    return lane < jnp.where(lane < B, points[c], B + points[c + 1])


def moved(place, axis, first_sends_odd, x_first, held, at_first, at_second):
    me = place[0]
    up = (me & 1) == (1 if x_first else 0)
    y, z = (me >> Y) & 3, (me >> Z) & 3
    last = jnp.where(up, 3, 0)
    if axis == Z:
        moves = z >= 0
    elif axis == Y:
        moves = z == last
    else:
        where = last if x_first else 3 - last
        moves = (y == where) & (z == where)
    odd = ((me >> axis) & 1) == 1
    by_first = ~odd if first_sends_odd else odd
    return jnp.where(moves, jnp.where(by_first, at_first, at_second), held)


def leaf_kernel(
    place,
    points_hbm,
    right_hbm,
    left_hbm,
    basis_hbm,
    transfer_hbm,
    lift_hbm,
    mright,
    mleft,
    pleft,
    sums,
    ahead,
    inchip,
    points,
    right,
    left,
    basis,
    transfer,
    lift,
    done,
):
    rhs = right.shape[0]
    clusters = basis.shape[0]
    pieces = 2
    count_of = iter(range(done.shape[0]))

    def fetch(source, target, index):
        return pltpu.make_async_copy(source.at[index], target.at[index], done.at[next(count_of)])

    per = clusters // pieces
    copies = []
    for j in range(pieces):
        some = pl.ds(j * per, per)
        columns = (slice(None), pl.ds(j * per * B, per * B))
        copies.append(
            [
                fetch(right_hbm, right, columns),
                fetch(left_hbm, left, columns),
                fetch(basis_hbm, basis, some),
                fetch(transfer_hbm, transfer, some),
            ]
        )
    copies[0].append(fetch(points_hbm, points, slice(None)))
    copies[1].append(fetch(lift_hbm, lift, slice(None)))
    for copy in [*copies[0], *copies[1]]:
        copy.start()
    part = jnp.zeros((4 * rhs, B), F32)
    for j in range(pieces):
        for copy in copies[j]:
            copy.wait()
        for c in range(j * per, (j + 1) * per, 2):
            mask = pair_mask(points, c, rhs)
            columns = slice(c * B, (c + 2) * B)
            xr = jnp.where(mask, right[:, columns].astype(F32), 0.0).astype(BF)
            xl = jnp.where(mask, left[:, columns].astype(F32), 0.0).astype(BF)
            for q in range(2):
                mright[c + q] = xr[:, q * B : (q + 1) * B]
                mleft[c + q] = xl[:, q * B : (q + 1) * B]
            leaf = dot(jnp.concatenate([xr, xl], axis=0), diagonal(basis[c], basis[c + 1]), NT)
            high, low = two(jnp.concatenate([transfer[c], transfer[c + 1]], axis=0))
            part = part + dot(stacked(leaf), jnp.concatenate([high, low], axis=0), NN)
    total = both(part)
    pleft[...] = total[rhs:]
    shares = dot3(total, lift[0], NN)
    sums[0] = shares[:rhs]
    sums[1] = shares[rhs:]
    ahead[0] = total[:rhs].astype(BF)
    core = place[0] & 1
    ahead[1:] = mright[pl.ds(core * (clusters - HW), HW)]
    inchip[...] = mright[pl.ds((1 - core) * (clusters - HW), HW)]


def outward_kernel(place, count, parents, table, pleft, sums, coupling, keep, send):
    far_slots = coupling.shape[1]
    half = keep.shape[0] - 1
    keep[...] = jnp.zeros_like(keep)
    send[: half + 1] = jnp.zeros((half + 1, *send.shape[1:]), F32)
    send[half + 1 :] = sums[...]
    wide = stacked(pleft[...])
    me = place[0]
    group = 8
    for start in range(0, far_slots, group):
        values = []
        for f in range(start, start + group, 2):
            (ah, al), (bh, bl) = two(coupling[0, f]), two(coupling[0, f + 1])
            high, low = (jnp.concatenate(pair, axis=1) for pair in ((ah, bh), (al, bl)))
            value = both(dot(wide, jnp.concatenate([high, low], axis=0), NN))
            values += [value[:, :B], value[:, B:]]
        for q, value in enumerate(values):
            f = start + q
            slot = slot_in(table, parents, f, me, 2 * half)
            live = f < count[0]
            keep[jnp.where(live & (slot < half), slot, half)] = value
            send[jnp.where(live & (slot >= half), slot - half, half)] = value


def grow_kernel(ahead, came, out):
    out[0] = ahead[0]
    out[1] = came[0]
    out[2:] = ahead[1:]


def lay_out(payload, going, exact, sums, *rest):
    high, low = two(going)
    start = going.shape[0]
    payload[:start] = high
    if exact:
        payload[start : 2 * start] = low
        start = 2 * start
    for part in (*two(sums), *rest):
        payload[start : start + part.shape[0]] = part
        start = start + part.shape[0]


def first_fold_kernel(
    place, came, partial, sums, ahead, came_ahead, grown, came_grown, back,
    payload, keep, sums_next, gathered, halo, tail,
):
    n = 2 * keep.shape[0]
    total = partial[:n] + came[:n]
    keep[...] = total[: n // 2]
    sums_next[...] = sums[...] + came[n + 1 :]
    gathered[:2] = grown[:2]
    gathered[2:] = came_grown[:2]
    halo[...] = moved(place, X, True, True, ahead[1:], came_ahead[1:], came_grown[2:])
    tail[...] = back[pl.ds((1 - (place[0] & 1)) * HW, HW)]
    lay_out(payload, total[n // 2 :], False, sums_next[...], gathered[...], halo[...], tail[...])


def fold_kernel(step, *refs):
    refs = iter(refs)
    place, came, partial, sums = (next(refs) for _ in range(4))
    axis, turn = STEPS[step - 1]
    gathers = axis != X
    gathers_next = STEPS[step][0] != X
    gathered, halo = (next(refs), next(refs)) if gathers else (None, None)
    tail = next(refs)
    before = next(refs) if turn else None
    inchip = next(refs) if gathers and not gathers_next else None
    next(refs)
    payload, keep, sums_next = (next(refs) for _ in range(3))
    n = partial.shape[0]
    m = sums.shape[0]
    total = partial[...] + came[:n].astype(F32)
    start = n
    if step >= 3:
        total = total + came[n : 2 * n].astype(F32)
        start = 2 * n
    got = came[start : start + m].astype(F32) + came[start + m : start + 2 * m].astype(F32)
    start = start + 2 * m
    if gathers:
        sums_next[...] = sums[...] + got
    else:
        sums_next[:m] = sums[...]
        sums_next[m:] = got
    keep[...] = total[: n // 2]
    end = came.shape[0]
    parts = []
    if gathers:
        a = gathered.shape[0]
        gathered_next = next(refs)
        gathered_next[:a] = gathered[...]
        gathered_next[a : 2 * a] = came[start : start + a]
        halo_now = halo[...]
    tail_now = tail[...]
    if turn:
        last = before.shape[0]
        halo_now = moved(
            place, axis, True, True, halo_now,
            before[last - 2 * HW : last - HW], came[end - 2 * HW : end - HW],
        )
        tail_now = moved(
            place, axis, False, False, tail_now, before[last - HW :], came[end - HW :]
        )
        if gathers_next:
            next(refs)[...] = halo_now
        next(refs)[...] = tail_now
    if gathers_next:
        parts = [gathered_next[...], halo_now]
    elif gathers:
        gathered_next[2 * a : 2 * a + HW] = halo_now
        gathered_next[2 * a + HW :] = inchip[...]
    lay_out(payload, total[n // 2 :], step >= 2, sums_next[...], *parts, tail_now)


def rows_of(blocks, c):
    return jnp.concatenate([blocks[c, s] for s in range(blocks.shape[1])], axis=1)


def add_back(columns, first, mleft, blocks, clusters, back):
    done = []
    for c in clusters:
        places = [columns[s, c] - first[0] for s in range(blocks.shape[1])]
        done.append((places, dot(mleft[c], rows_of(blocks, c), NN)))
    for places, value in done:
        held = [back[place] for place in places]
        for s, place in enumerate(places):
            back[place] = held[s] + value[:, s * B : (s + 1) * B]


def near_outer_kernel(columns, first, mleft, blocks, back, sent):
    clusters = mleft.shape[0]
    back[...] = jnp.zeros_like(back)
    add_back(columns, first, mleft, blocks, range(HW), back)
    add_back(columns, first, mleft, blocks, range(clusters - HW, clusters), back)
    sent[:HW] = back[:HW].astype(BF)
    sent[HW:] = back[clusters + HW :].astype(BF)


def near_kernel(columns, first, mright, mleft, blocks, back_outer, _, out, back):
    clusters = mright.shape[0]
    slots = blocks.shape[1]
    back[...] = back_outer[...]
    for start in range(0, clusters, 4):
        group = range(start, start + 4)
        for c in group:
            inside = []
            for s in range(slots):
                own = columns[s, c] - first[0] - HW
                value = mright[jnp.clip(own, 0, clusters - 1)]
                is_own = (own >= 0) & (own < clusters)
                inside.append(jnp.where(is_own, value, jnp.zeros_like(value)))
            out[c] = dot(rows_of(blocks, c), jnp.concatenate(inside, axis=1), NT).T
        if HW <= start < clusters - HW:
            add_back(columns, first, mleft, blocks, group, back)


def edge_kernel(place, columns, first, other, blocks, _, out):
    slots = blocks.shape[1]
    clusters = columns.shape[1]
    core = place[0] & 1
    start = other.shape[0] - 2 * HW
    for g in range(2 * HW):
        low = g < HW
        c = g if low else clusters - 2 * HW + g
        halo = start + HW * (core if low else 1 - core)
        values = []
        for s in range(slots):
            row = columns[s, c] - first[0] - (0 if low else clusters + HW)
            value = other[halo + jnp.clip(row, 0, HW - 1)]
            is_there = (row >= 0) & (row < HW)
            values.append(jnp.where(is_there, value, jnp.zeros_like(value)))
        out[g] = dot(rows_of(blocks, c), jnp.concatenate(values, axis=1), NT).T


def forward_kernel(place, count, parents, table, own, other, coupling, out, all_of):
    far_slots = coupling.shape[1]
    half = all_of.shape[0] // 2
    all_of[:half] = own[:half]
    all_of[half:] = other[:half]
    me = place[0]
    total = jnp.zeros((B, own.shape[1]), F32)
    group = 48
    for start in range(0, far_slots, group):
        rows, values = [], []
        for f in range(start, start + group):
            value = all_of[slot_in(table, parents, f, me, 2 * half)]
            value = jnp.where(f < count[0], value, jnp.zeros_like(value))
            values += [value, value]
            rows += two(coupling[0, f])
        total = total + dot(
            jnp.concatenate(rows, axis=1), jnp.concatenate(values, axis=1), NT
        )
    out[...] = total.T


def down_kernel(
    points,
    place,
    far_right,
    partial,
    sums,
    came,
    apex,
    lift,
    transfer,
    basis,
    near_out,
    near_back,
    edge_out,
    back_came,
    tail,
    before,
    product,
    adjoint,
    hats,
):
    step = pl.program_id(0)
    per = basis.shape[0]
    clusters, rhs = near_out.shape[:2]

    @pl.when(step == 0)
    def _():
        core = place[0] & 1
        slab = place[0] >> X
        got = came[2:6].astype(F32) + came[6:10].astype(F32)
        slabs = [sums[2], sums[3], got[0], got[1], got[2], got[3]]
        top_right = jnp.zeros((rhs, B), F32)
        top_left = jnp.zeros((rhs, B), F32)
        for t, mask in enumerate((1 + 2 * core, 3 - 2 * core, 2)):
            top_right = top_right + dot3(slabs[2 * t], apex[slab, slab ^ mask], NT)
            top_left = top_left + dot3(slabs[2 * t + 1], apex[slab ^ mask, slab], NN)
        far_left = partial[0] + (came[0].astype(F32) + came[1].astype(F32))
        hats[...] = stacked(
            jnp.concatenate([far_right[...], far_left], axis=0)
            + dot3(jnp.concatenate([top_right, top_left], axis=0), lift[0], NT)
        )

    for g in range(0, per, 2):
        c = step * per + g
        high, low = two(jnp.concatenate([transfer[g], transfer[g + 1]], axis=0))
        down = both(dot(hats[...], jnp.concatenate([high, low], axis=1), NT))
        high, low = two(down)
        two_bases = diagonal(basis[g], basis[g + 1])
        far = dot(
            jnp.concatenate([high, low], axis=1),
            jnp.concatenate([two_bases, two_bases], axis=0),
            NN,
        )
        mask = pair_mask(points, c, rhs)
        columns = slice(g * B, (g + 2) * B)
        near = jnp.concatenate([near_out[c], near_out[c + 1]], axis=1)
        back = jnp.concatenate([near_back[HW + c], near_back[HW + c + 1]], axis=1)
        product[:, columns] = jnp.where(mask, near + far[:rhs], 0.0)
        adjoint[:, columns] = jnp.where(mask, back + far[rhs:], 0.0)

    core = place[0] & 1
    rows = before.shape[0]
    far_tail = moved(place, X, False, False, tail[...], before[rows - HW :], came[10:])
    near_tail = back_came[pl.ds(core * HW, HW)]

    def edge(g, c, low):
        mask = lax.broadcasted_iota(jnp.int32, (rhs, B), 1) < points[c]
        columns = slice((c % per) * B, (c % per + 1) * B)
        product[:, columns] += jnp.where(mask, edge_out[g], 0.0)
        tail_is_far = (core == 0) if low else (core == 1)
        value = jnp.where(tail_is_far, far_tail[g % HW], near_tail[g % HW]).astype(F32)
        adjoint[:, columns] += jnp.where(mask, value, 0.0)

    @pl.when(step == 0)
    def _():
        for g in range(HW):
            edge(g, g, True)

    @pl.when(step == pl.num_programs(0) - 1)
    def _():
        for g in range(HW):
            edge(HW + g, clusters - HW + g, False)


SMEM = pl.BlockSpec(memory_space=pltpu.SMEM)
HBM = pl.BlockSpec(memory_space=pltpu.HBM)
ANY = pl.BlockSpec(memory_space=pl.ANY)
VMEM = pl.BlockSpec(memory_space=pltpu.VMEM)
MIB = 1024 * 1024


def shape(dims, kind):
    return jax.ShapeDtypeStruct(dims, kind)


def whole(*dims):
    return pl.BlockSpec(dims, lambda *_: (0,) * len(dims))


def call(kernel, name, grid, ins, outs, args, us, scratch=(), vmem=20):
    results = pl.pallas_call(
        kernel,
        grid=grid,
        out_shape=tuple(shape(dims, kind) for _, dims, kind in outs),
        in_specs=ins,
        out_specs=tuple(spec for spec, _, _ in outs),
        scratch_shapes=list(scratch),
        compiler_params=pltpu.CompilerParams(vmem_limit_bytes=vmem * MIB),
        cost_estimate=pl.CostEstimate(
            flops=1000, bytes_accessed=int(us * 3.6e6), transcendentals=0
        ),
        name=name,
    )(*args)
    return results


def shards(
    right_sides,
    left_sides,
    near_blocks,
    near_columns,
    cluster_points,
    leaf_basis,
    transfer,
    far_parents,
    far_count,
    coupling,
    slab_transfer,
    apex_coupling,
):
    rhs = right_sides.shape[0]
    clusters = near_blocks.shape[0]
    rank = leaf_basis.shape[1]
    me = lax.axis_index(AXES)
    devices = lax.axis_size(AXES)
    block = (rhs, B)
    all_clusters = (clusters, *block)
    half = devices // 2
    place = me.astype(jnp.int32)[None]
    first = place * clusters - HW
    columns = near_columns.T
    reduce_table, gather_table = slot_tables(devices)

    def rows(n, kind=BF):
        return (VMEM, (n, *block), kind)

    mright, mleft, pleft, sums, ahead, inchip = call(
        leaf_kernel,
        "leaf",
        (),
        [SMEM] + [HBM] * 6,
        [rows(clusters), rows(clusters), (VMEM, block, F32), rows(2, F32), rows(1 + HW), rows(HW)],
        (
            place,
            *(
                pltpu.with_memory_space_constraint(value, pltpu.HBM)
                for value in (
                    cluster_points,
                    right_sides,
                    left_sides,
                    leaf_basis,
                    transfer,
                    slab_transfer,
                )
            ),
        ),
        us=3,
        scratch=[
            pltpu.SMEM(cluster_points.shape, jnp.int32),
            pltpu.VMEM(right_sides.shape, BF),
            pltpu.VMEM(left_sides.shape, BF),
            pltpu.VMEM(leaf_basis.shape, BF),
            pltpu.VMEM(transfer.shape, F32),
            pltpu.VMEM(slab_transfer.shape, F32),
            pltpu.SemaphoreType.DMA((10,)),
        ],
    )
    came_ahead = routed(ahead, GATHER_STEPS[0])

    partial, sent = call(
        outward_kernel,
        "outward",
        (),
        [SMEM] * 4 + [VMEM] * 3,
        [rows(half + 1, F32), rows(half + 3, F32)],
        (place, far_count, far_parents, reduce_table, pleft, sums, coupling),
        us=2,
    )
    came = to_other_core(sent)
    (grown,) = call(
        grow_kernel, "grow", (), [VMEM] * 2, [rows(2 + HW)], (ahead, came_ahead), us=0.2
    )
    came_grown = routed(grown, GATHER_STEPS[1])
    back_outer, back_sent = call(
        near_outer_kernel,
        "near_outer",
        (),
        [SMEM] * 2 + [VMEM] * 2,
        [rows(clusters + 2 * HW, F32), rows(2 * HW)],
        (columns, first, mleft, near_blocks),
        us=1,
    )
    back_came = to_other_core(back_sent)

    payload, partial, sums, gathered, halo, tail = call(
        first_fold_kernel,
        "first_fold",
        (),
        [SMEM] + [VMEM] * 8,
        [
            rows(half // 2 + 4 + 4 + 2 * HW),
            rows(half // 2, F32),
            rows(2, F32),
            rows(4),
            rows(HW),
            rows(HW),
        ],
        (place, came, partial, sums, ahead, came_ahead, grown, came_grown, back_came),
        us=0.3,
    )
    came = routed(payload, STEPS[0])
    before = None
    after = payload
    for step in range(1, len(STEPS)):
        axis, turn = STEPS[step - 1]
        gathers, gathers_next = axis != X, STEPS[step][0] != X
        if step == 1:
            near_out, near_back = call(
                near_kernel,
                "near",
                (),
                [SMEM] * 2 + [VMEM] * 4 + [ANY],
                [rows(clusters, F32), rows(clusters + 2 * HW, F32)],
                (columns, first, mright, mleft, near_blocks, back_outer, payload),
                us=4,
            )
            after = near_out
        if step == 5:
            gathered_other = to_other_core(gathered)
            (far_right,) = call(
                forward_kernel,
                "forward",
                (),
                [SMEM] * 4 + [VMEM] * 3,
                [(VMEM, block, F32)],
                (
                    place,
                    far_count,
                    far_parents,
                    gather_table,
                    gathered,
                    gathered_other,
                    coupling,
                ),
                us=2.5,
                scratch=[pltpu.VMEM((devices, *block), BF)],
            )
            after = far_right
        n = half >> step
        m = 2 if gathers else 4
        a = 4 << (step - 1)
        size = n // 2 * (2 if step >= 2 else 1) + 2 * m + HW
        args = [place, came, partial, sums]
        outs = [None, rows(n // 2, F32), rows(m, F32)]
        if gathers:
            args += [gathered, halo]
            outs.append(rows(2 * a if gathers_next else 2 * a + 2 * HW))
        args.append(tail)
        if turn:
            args.append(before)
            outs += [rows(HW)] * (2 if gathers_next else 1)
        if gathers and not gathers_next:
            args.append(inchip)
        if gathers_next:
            size += 2 * a + HW
        outs[0] = rows(size)
        made = call(
            functools.partial(fold_kernel, step),
            "fold",
            (),
            [SMEM] + [VMEM] * (len(args) - 1) + [ANY],
            outs,
            (*args, after),
            us=0.3,
        )
        payload, partial, sums, *made = made
        if gathers:
            gathered, *made = made
        if turn and gathers_next:
            halo, *made = made
        if turn:
            (tail,) = made
        before = came
        came = routed(payload, STEPS[step])

    (edge_out,) = call(
        edge_kernel,
        "edge",
        (),
        [SMEM] * 3 + [VMEM] * 2 + [ANY],
        [rows(2 * HW, F32)],
        (place, columns, first, gathered_other, near_blocks, payload),
        us=1.5,
    )

    per = 16
    sides = pl.BlockSpec((rhs, per * B), lambda i: (0, i))
    bases = pl.BlockSpec((per, rank, B), lambda i: (i, 0, 0))
    return call(
        down_kernel,
        "down",
        (clusters // per,),
        [
            SMEM,
            SMEM,
            whole(*block),
            whole(1, *block),
            whole(4, *block),
            whole(*came.shape),
            whole(*apex_coupling.shape),
            whole(1, B, B),
            bases,
            bases,
            whole(*all_clusters),
            whole(clusters + 2 * HW, *block),
            whole(*edge_out.shape),
            whole(*back_came.shape),
            whole(*tail.shape),
            whole(*before.shape),
        ],
        [(sides, (rhs, clusters * B), F32)] * 2,
        (
            cluster_points,
            place,
            far_right,
            partial,
            sums,
            came,
            apex_coupling,
            slab_transfer,
            transfer,
            leaf_basis,
            near_out,
            near_back,
            edge_out,
            back_came,
            tail,
            before,
        ),
        us=4,
        scratch=[pltpu.VMEM((4 * rhs, 2 * B), BF)],
    )


def solution(mesh):
    return jax.shard_map(
        shards,
        mesh=mesh,
        in_specs=(
            P(None, AXES),
            P(None, AXES),
            P(AXES, None, None, None),
            P(AXES, None),
            P(AXES),
            P(AXES, None, None),
            P(AXES, None, None),
            P(AXES, None),
            P(AXES),
            P(AXES, None, None, None),
            P(AXES, None, None),
            P(),
        ),
        out_specs=(P(None, AXES), P(None, AXES)),
        check_vma=False,
    )
```

time: 70.1 us -> 68.5 us (0.977); the launches traced: 68.8 us -> 68.3 us
  starting transfers between devices: 26.1 us -> 19.6 us
  local copies, waits for them, and re-layouts: 0.07 us -> 3.02 us
  waiting for transfers between devices: 24.6 us -> 27.2 us
    ppermute x6 -> x8, waiting for transfers between devices: 18.4 us -> 25.3 us  [routed(): return lax.ppermute(block, AXES, route)]
    ppermute x6 -> x8, starting transfers between devices: 23.1 us -> 17.9 us  [routed(): return lax.ppermute(block, AXES, route)]
    unnamed x22 -> x26, local copies, waits for them, and re-layouts: 0.07 us -> 3.02 us
    ppermute x2 -> x0, starting transfers between devices: 2.84 us -> none  [passed_along(): return lax.ppermute(block, AXES, route)]
    ppermute x3, waiting for transfers between devices: 4.23 us -> 1.88 us  [to_other_core(): lax.ppermute(block, AXES, [(i, i ^ 1) for i in range(lax.axis_size(AXES))])]
    ppermute x2 -> x0, waiting for transfers between devices: 2 us -> none  [passed_along(): return lax.ppermute(block, AXES, route)]
    ppermute x3, starting transfers between devices: 0.17 us -> 1.66 us  [to_other_core(): lax.ppermute(block, AXES, [(i, i ^ 1) for i in range(lax.axis_size(AXES))])]
    pallas_call x12 -> x14, Pallas kernels: 16.5 us -> 17 us  [call(): pl.pallas_call(kernel, grid=grid, out_shape=tuple((shape(dims, kind) for...]
  transfers between devices with their start and end apart: 11 -> 11, of which waited for: 8 -> 8; matrix products, arithmetic and copies ran while one was open for 0% -> 0% of each run, Pallas kernels for 8% -> 13%
where the time goes in v4:
time: 68.5 us; the launch traced here: 68.3 us
  waiting for transfers between devices  27.2 us (40%)
  starting transfers between devices  19.6 us (29%)
  Pallas kernels  17 us (25%)
  local copies, waits for them, and re-layouts  3.02 us (4%)
  between operations  1.5 us (2%)
    ppermute x8, waiting for transfers between devices, routed(): return lax.ppermute(block, AXES, route)  25.3 us
    ppermute x8, starting transfers between devices, routed(): return lax.ppermute(block, AXES, route)  17.9 us
    pallas_call x14, Pallas kernels, call(): pl.pallas_call(kernel, grid=grid, out_shape=tuple((shape(dims, kind) for...  17 us
    unnamed x26, local copies, waits for them, and re-layouts  3.02 us
    ppermute x3, waiting for transfers between devices, to_other_core(): lax.ppermute(block, AXES, [(i, i ^ 1) for i in range(lax.axis_size(AXES))])  1.88 us
    ppermute x3, starting transfers between devices, to_other_core(): lax.ppermute(block, AXES, [(i, i ^ 1) for i in range(lax.axis_size(AXES))])  1.66 us
  transfers between devices with their start and end apart: 11, of which 8 were waited for; matrix products, arithmetic and copies ran while one was open for 0% of the time, Pallas kernels for 13%

profile of v4, /device:TPU:0, one launch (start us, length us, event | category | flops | bytes accessed | tf_op | source)
XLA Modules:
  0.0 68.3 jit_solution(7594638112512535445)
XLA Ops:
  0.6 0.0 copy-start.10
  0.6 0.0 copy-start.7
  1.3 2.9 %leaf.1 = (bf16[32,32,128]{2,1,0:T(8,128)(2,1)S(1)}, bf16[32,32,128]{2,1,0:T(8,128)(2,1)S(1)}, f32[32,128]{1,0:T(8,128)S(1)}, f32[2,32,128]{2,1,0:T(8,128)S(1)},...) custom-call(s32[1]{0:T(128)} %bitcast.place.refs_0_, s32[32]{0:T(128)} %points.1, ...), custom_call_target="tpu_custom_call" | custom-call | flops 1000 | bytes 10800000 | tf_op jit(solution)/shard_map/leaf/pallas_call | solution.py:486
  4.2 0.0 copy-start.1
  4.2 3.0 %copy-done.1 = f32[1,96,128,128]{3,2,1,0:T(8,128)S(1)} copy-done((f32[1,96,128,128]{3,2,1,0:T(8,128)S(1)}, f32[1,96,128,128]{3,2,1,0:T(8,128)}, u32[]{:S(2)}) %copy-start.1) | copy-done | bytes 6291480
  7.2 2.0 %outward.1 = (f32[65,32,128]{2,1,0:T(8,128)S(1)}, f32[67,32,128]{2,1,0:T(8,128)S(1)}) custom-call(s32[1]{0:T(128)} %bitcast.place.refs_0_, s32[1]{0:T(128)S(6)} %copy.16.count, s32[1,96]{1,0:T(1,128)S(1)} %copy-done.7, s32[256]{0:T(256)S(1)} %copy-done.10, f32[32,128]{1,0:T(8,128)S(1)} %get-tuple-element.42.pleft, f32[2,32,128]{2,1,0:T(8,128)S(1)} %get-tuple-element.43.sums, ...), custom_call_target="tpu_custom_call" | custom-call | flops 1000 | bytes 7200000 | tf_op jit(solution)/shard_map/outward/pallas_call | solution.py:486
  9.2 0.1 collective-permute-start
  9.3 1.7 %collective-permute-start.1 = (bf16[5,32,128]{2,1,0:T(8,128)(2,1)S(1)}, bf16[5,32,128]{2,1,0:T(8,128)(2,1)S(1)}, u32[]{:S(2)}, u32[]{:S(2)}) collective-permute-start(bf16[5,32,128]{2,1,0:T(8,128)(2,1)S(1)} %get-tuple-element.46.ahead), channel_id=1, source_target_pairs={{0,32},{1,97},{2,34},{3,99},{4,36},{5,101},{6,38},{7,103},{8,40},{... | collective-permute-start | bytes 122888 | tf_op jit(solution)/shard_map/ppermute | solution.py:28
  10.9 0.0 copy-done.6
  10.9 1.1 %near_outer.1 = (f32[40,32,128]{2,1,0:T(8,128)S(1)}, bf16[8,32,128]{2,1,0:T(8,128)(2,1)S(1)}) custom-call(s32[8,32]{1,0:T(8,128)S(1)} %bitcast.4, s32[1]{0:T(128)S(6)} %sub.3.first, bf16[32,32,128]{2,1,0:T(8,128)(2,1)S(1)} %get-tuple-element.47.mleft, bf16[32,8,128,128]{3,2,1,0:T(8,128)(2,1)S(1)} %copy-done), custom_call_target="tpu_custom_call" | custom-call | flops 1000 | bytes 3600000 | tf_op jit(solution)/shard_map/near_outer/pallas_call | solution.py:486
  12.0 1.5 %collective-permute-start.3 = (bf16[8,32,128]{2,1,0:T(8,128)(2,1)S(1)}, bf16[8,32,128]{2,1,0:T(8,128)(2,1)S(1)}, u32[]{:S(2)}, u32[]{:S(2)}) collective-permute-start(bf16[8,32,128]{2,1,0:T(8,128)(2,1)S(1)} %get-tuple-element.48), channel_id=1, source_target_pairs={{0,1},{1,0},{2,3},{3,2},{4,5},{5,4},{6,7},{7,6},{8,9},{9,8},{10,11... | collective-permute-start | bytes 196616 | tf_op jit(solution)/shard_map/ppermute | solution.py:32
  13.5 0.0 collective-permute-done.1.came.came_ahead
  13.5 2.7 %collective-permute-start.2 = (bf16[6,32,128]{2,1,0:T(8,128)(2,1)S(1)}, bf16[6,32,128]{2,1,0:T(8,128)(2,1)S(1)}, u32[]{:S(2)}, u32[]{:S(2)}) collective-permute-start(bf16[6,32,128]{2,1,0:T(8,128)(2,1)S(1)} %grow.1.grown), channel_id=1, source_target_pairs={{0,96},{1,33},{2,98},{3,35},{4,100},{5,37},{6,102},{7,39},{8,104},... | collective-permute-start | bytes 147464 | tf_op jit(solution)/shard_map/ppermute | solution.py:28
  16.2 0.0 collective-permute-done.3.back.back_came
  16.2 2.7 %collective-permute-done.2.came_grown = bf16[6,32,128]{2,1,0:T(8,128)(2,1)S(1)} collective-permute-done((bf16[6,32,128]{2,1,0:T(8,128)(2,1)S(1)}, bf16[6,32,128]{2,1,0:T(8,128)(2,1)S(1)}, u32[]{:S(2)}, u32[]{:S(2)}) %collective-permute-start.2) | collective-permute-done | bytes 49184 | tf_op jit(solution)/shard_map/ppermute | solution.py:28
  18.9 0.0 collective-permute-done.came
  18.9 0.1 first_fold.1
  19.0 1.6 %collective-permute-start.4 = (bf16[48,32,128]{2,1,0:T(8,128)(2,1)S(1)}, bf16[48,32,128]{2,1,0:T(8,128)(2,1)S(1)}, u32[]{:S(2)}, u32[]{:S(2)}) collective-permute-start(bf16[48,32,128]{2,1,0:T(8,128)(2,1)S(1)} %get-tuple-element.49._), channel_id=1, source_target_pairs={{0,8},{1,25},{2,10},{3,27},{4,12},{5,29},{6,14},{7,31},{8,0},{9,17... | collective-permute-start | bytes 1179656 | tf_op jit(solution)/shard_map/ppermute | solution.py:28
  20.7 3.8 %near.1 = (f32[32,32,128]{2,1,0:T(8,128)S(1)}, f32[40,32,128]{2,1,0:T(8,128)S(1)}) custom-call(s32[8,32]{1,0:T(8,128)S(1)} %bitcast.5, s32[1]{0:T(128)S(6)} %sub.3.first, bf16[32,32,128]{2,1,0:T(8,128)(2,1)S(1)} %get-tuple-element.55.mright, bf16[32,32,128]{2,1,0:T(8,128)(2,1)S(1)} %get-tuple-element.47.mleft, bf16[32,8,128,128]{3,2,1,0:T(8,128)(2,1)S(1)} %copy-done, ...), custom_call_target="tpu_custom_call" | custom-call | flops 1000 | bytes 14400000 | tf_op jit(solution)/shard_map/near/pallas_call | solution.py:486
  24.5 2.4 %collective-permute-done.4.refs_1_.refs_7_ = bf16[48,32,128]{2,1,0:T(8,128)(2,1)S(1)} collective-permute-done((bf16[48,32,128]{2,1,0:T(8,128)(2,1)S(1)}, bf16[48,32,128]{2,1,0:T(8,128)(2,1)S(1)}, u32[]{:S(2)}, u32[]{:S(2)}) %collective-permute-start.4) | collective-permute-done | bytes 393248 | tf_op jit(solution)/shard_map/ppermute | solution.py:28
  26.9 0.1 fold.5
  27.0 3.1 %collective-permute-start.5 = (bf16[36,32,128]{2,1,0:T(8,128)(2,1)S(1)}, bf16[36,32,128]{2,1,0:T(8,128)(2,1)S(1)}, u32[]{:S(2)}, u32[]{:S(2)}) collective-permute-start(bf16[36,32,128]{2,1,0:T(8,128)(2,1)S(1)} %get-tuple-element.58), channel_id=1, source_target_pairs={{0,24},{1,9},{2,26},{3,11},{4,28},{5,13},{6,30},{7,15},{8,16},{9,1... | collective-permute-start | bytes 884744 | tf_op jit(solution)/shard_map/ppermute | solution.py:28
  30.1 4.9 %collective-permute-done.5.refs_1_ = bf16[36,32,128]{2,1,0:T(8,128)(2,1)S(1)} collective-permute-done((bf16[36,32,128]{2,1,0:T(8,128)(2,1)S(1)}, bf16[36,32,128]{2,1,0:T(8,128)(2,1)S(1)}, u32[]{:S(2)}, u32[]{:S(2)}) %collective-permute-start.5) | collective-permute-done | bytes 294944 | tf_op jit(solution)/shard_map/ppermute | solution.py:28
  35.0 0.1 fold.6
  35.1 2.0 %collective-permute-start.6 = (bf16[44,32,128]{2,1,0:T(8,128)(2,1)S(1)}, bf16[44,32,128]{2,1,0:T(8,128)(2,1)S(1)}, u32[]{:S(2)}, u32[]{:S(2)}) collective-permute-start(bf16[44,32,128]{2,1,0:T(8,128)(2,1)S(1)} %get-tuple-element.62), channel_id=1, source_target_pairs={{0,2},{1,7},{2,0},{3,5},{4,6},{5,3},{6,4},{7,1},{8,10},{9,15},{10,... | collective-permute-start | bytes 1081352 | tf_op jit(solution)/shard_map/ppermute | solution.py:28
  37.1 6.8 %collective-permute-done.6.refs_1_.refs_7_ = bf16[44,32,128]{2,1,0:T(8,128)(2,1)S(1)} collective-permute-done((bf16[44,32,128]{2,1,0:T(8,128)(2,1)S(1)}, bf16[44,32,128]{2,1,0:T(8,128)(2,1)S(1)}, u32[]{:S(2)}, u32[]{:S(2)}) %collective-permute-start.6) | collective-permute-done | bytes 360480 | tf_op jit(solution)/shard_map/ppermute | solution.py:28
  43.9 0.1 fold.7
  44.0 0.0 copy-start.9
  44.0 4.1 %collective-permute-start.7 = (bf16[52,32,128]{2,1,0:T(8,128)(2,1)S(1)}, bf16[52,32,128]{2,1,0:T(8,128)(2,1)S(1)}, u32[]{:S(2)}, u32[]{:S(2)}) collective-permute-start(bf16[52,32,128]{2,1,0:T(8,128)(2,1)S(1)} %get-tuple-element.68), channel_id=1, source_target_pairs={{0,6},{1,3},{2,4},{3,1},{4,2},{5,7},{6,0},{7,5},{8,14},{9,11},{10,... | collective-permute-start | bytes 1277960 | tf_op jit(solution)/shard_map/ppermute | solution.py:28
  48.1 6.1 %collective-permute-done.7.refs_1_ = bf16[52,32,128]{2,1,0:T(8,128)(2,1)S(1)} collective-permute-done((bf16[52,32,128]{2,1,0:T(8,128)(2,1)S(1)}, bf16[52,32,128]{2,1,0:T(8,128)(2,1)S(1)}, u32[]{:S(2)}, u32[]{:S(2)}) %collective-permute-start.7) | collective-permute-done | bytes 426016 | tf_op jit(solution)/shard_map/ppermute | solution.py:28
  54.2 0.1 fold.8
  54.3 0.1 collective-permute-start.8
  54.4 0.1 collective-permute-start.9
  54.5 1.9 %collective-permute-done.8.other = bf16[72,32,128]{2,1,0:T(8,128)(2,1)S(1)} collective-permute-done((bf16[72,32,128]{2,1,0:T(8,128)(2,1)S(1)}, bf16[72,32,128]{2,1,0:T(8,128)(2,1)S(1)}, u32[]{:S(2)}, u32[]{:S(2)}) %collective-permute-start.8) | collective-permute-done | bytes 589856 | tf_op jit(solution)/shard_map/ppermute | solution.py:32
  56.4 0.0 slice-done.1
  56.4 2.4 %forward.1.refs_5_.far_right = f32[32,128]{1,0:T(8,128)S(1)} custom-call(s32[1]{0:T(128)} %bitcast.place.refs_0_, s32[1]{0:T(128)S(6)} %copy.16.count, s32[1,96]{1,0:T(1,128)S(1)} %copy-done.7, s32[256]{0:T(256)S(1)} %copy-done.9, bf16[72,32,128]{2,1,0:T(8,128)(2,1)S(1)} %get-tuple-element.73.own, bf16[72,32,128]{2,1,0:T(8,128)(2,1)S(1)} %collective-permute-done.8.other, ...), custom_call_target="tpu_custom_call" | custom-call | flops 1000 | bytes 9000000 | tf_op jit(solution)/shard_map/forward/pallas_call | solution.py:486
  58.8 0.3 collective-permute-done.9.refs_1_.before
  59.1 0.0 copy-start.2
  59.1 0.0 copy-start.3
  59.2 0.0 copy-start.4
  59.2 0.0 copy-start.5
  59.2 0.0 copy-start.8
  59.2 2.6 %collective-permute-start.10 = (bf16[14,32,128]{2,1,0:T(8,128)(2,1)S(1)}, bf16[14,32,128]{2,1,0:T(8,128)(2,1)S(1)}, u32[]{:S(2)}, u32[]{:S(2)}) collective-permute-start(bf16[14,32,128]{2,1,0:T(8,128)(2,1)S(1)} %get-tuple-element.80._), channel_id=1, source_target_pairs={{0,96},{1,33},{2,98},{3,35},{4,100},{5,37},{6,102},{7,39},{8,104},... | collective-permute-start | bytes 344072 | tf_op jit(solution)/shard_map/ppermute | solution.py:28
  61.8 1.3 %edge.1.edge_out = f32[8,32,128]{2,1,0:T(8,128)S(1)} custom-call(s32[1]{0:T(128)} %bitcast.place.refs_0_, s32[8,32]{1,0:T(8,128)S(1)} %bitcast.6, s32[1]{0:T(128)S(6)} %sub.3.first, bf16[72,32,128]{2,1,0:T(8,128)(2,1)S(1)} %collective-permute-done.8.other, bf16[32,8,128,128]{3,2,1,0:T(8,128)(2,1)S(1)} %copy-done, bf16[14,32,128]{2,1,0:T(8,128)(2,1)S(1)} %get-tuple-element.80._), custom_call_target="tpu_custom_call" | custom-call | flops 1000 | bytes 5400000 | tf_op jit(solution)/shard_map/edge/pallas_call | solution.py:486
  63.1 2.1 %collective-permute-done.10.came = bf16[14,32,128]{2,1,0:T(8,128)(2,1)S(1)} collective-permute-done((bf16[14,32,128]{2,1,0:T(8,128)(2,1)S(1)}, bf16[14,32,128]{2,1,0:T(8,128)(2,1)S(1)}, u32[]{:S(2)}, u32[]{:S(2)}) %collective-permute-start.10) | collective-permute-done | bytes 114720 | tf_op jit(solution)/shard_map/ppermute | solution.py:28
  65.3 0.0 copy-done.2
  65.3 0.0 copy-done.4
  65.3 3.0 %down.1 = (f32[32,4096]{1,0:T(8,128)}, f32[32,4096]{1,0:T(8,128)}) custom-call(s32[32]{0:T(128)S(1)} %copy-done.8, s32[1]{0:T(128)} %bitcast.place.refs_0_, f32[32,128]{1,0:T(8,128)S(1)} %forward.1.refs_5_.far_right, f32[1,32,128]{2,1,0:T(8,128)S(1)} %get-tuple-element.78.partial, f32[4,32,128]{2,1,0:T(8,128)S(1)} %get-tuple-element.79.sums, ...), custom_call_target="tpu_custom_call" | custom-call | flops 1000 | bytes 14400000 | tf_op jit(solution)/shard_map/down/pallas_call | solution.py:486
  (15 shorter events, 0.0 us)
Async XLA Ops:
  0.6 3.6 %copy-start.10 = (s32[256]{0:T(256)S(1)}, s32[256]{0:T(256)}, u32[]{:S(2)}) copy-start(s32[256]{0:T(256)} %constant.20.clone.table) | copy-start | bytes 3076
  0.6 3.6 %copy-start.7 = (s32[1,96]{1,0:T(1,128)S(1)}, s32[1,96]{1,0:T(1,128)}, u32[]{:S(2)}) copy-start(s32[1,96]{1,0:T(1,128)} %parents.3) | copy-start | bytes 1156
  1.3 9.6 %copy-start = (bf16[32,8,128,128]{3,2,1,0:T(8,128)(2,1)S(1)}, bf16[32,8,128,128]{3,2,1,0:T(8,128)(2,1)}, u32[]{:S(2)}) copy-start(bf16[32,8,128,128]{3,2,1,0:T(8,128)(2,1)} %blocks.5) | copy-start | bytes 25165828
  4.2 3.0 %copy-start.1 = (f32[1,96,128,128]{3,2,1,0:T(8,128)S(1)}, f32[1,96,128,128]{3,2,1,0:T(8,128)}, u32[]{:S(2)}) copy-start(f32[1,96,128,128]{3,2,1,0:T(8,128)} %coupling.3) | copy-start | bytes 18874372
  7.2 3.8 %copy-start.6 = (s32[32,8]{0,1:T(8,128)S(1)}, s32[32,8]{0,1:T(8,128)}, u32[]{:S(2)}) copy-start(s32[32,8]{0,1:T(8,128)} %param.17) | copy-start | bytes 3076
  9.2 9.7 %collective-permute-start = (f32[67,32,128]{2,1,0:T(8,128)S(1)}, f32[67,32,128]{2,1,0:T(8,128)S(1)}, u32[]{:S(2)}, u32[]{:S(2)}) collective-permute-start(f32[67,32,128]{2,1,0:T(8,128)S(1)} %get-tuple-element.44), channel_id=1, source_target_pairs={{0,1},{1,0},{2,3},{3,2},{4,5},{5,4},{6,7},{7,6},{8,9},{9,8},{10,11... | collective-permute-start | bytes 3293192 | tf_op jit(solution)/shard_map/ppermute | solution.py:32
  9.3 4.2 %collective-permute-start.1 = (bf16[5,32,128]{2,1,0:T(8,128)(2,1)S(1)}, bf16[5,32,128]{2,1,0:T(8,128)(2,1)S(1)}, u32[]{:S(2)}, u32[]{:S(2)}) collective-permute-start(bf16[5,32,128]{2,1,0:T(8,128)(2,1)S(1)} %get-tuple-element.46.ahead), channel_id=1, source_target_pairs={{0,32},{1,97},{2,34},{3,99},{4,36},{5,101},{6,38},{7,103},{8,40},{... | collective-permute-start | bytes 122888 | tf_op jit(solution)/shard_map/ppermute | solution.py:28
  12.0 4.2 %collective-permute-start.3 = (bf16[8,32,128]{2,1,0:T(8,128)(2,1)S(1)}, bf16[8,32,128]{2,1,0:T(8,128)(2,1)S(1)}, u32[]{:S(2)}, u32[]{:S(2)}) collective-permute-start(bf16[8,32,128]{2,1,0:T(8,128)(2,1)S(1)} %get-tuple-element.48), channel_id=1, source_target_pairs={{0,1},{1,0},{2,3},{3,2},{4,5},{5,4},{6,7},{7,6},{8,9},{9,8},{10,11... | collective-permute-start | bytes 196616 | tf_op jit(solution)/shard_map/ppermute | solution.py:32
  13.5 5.4 %collective-permute-start.2 = (bf16[6,32,128]{2,1,0:T(8,128)(2,1)S(1)}, bf16[6,32,128]{2,1,0:T(8,128)(2,1)S(1)}, u32[]{:S(2)}, u32[]{:S(2)}) collective-permute-start(bf16[6,32,128]{2,1,0:T(8,128)(2,1)S(1)} %grow.1.grown), channel_id=1, source_target_pairs={{0,96},{1,33},{2,98},{3,35},{4,100},{5,37},{6,102},{7,39},{8,104},... | collective-permute-start | bytes 147464 | tf_op jit(solution)/shard_map/ppermute | solution.py:28
  18.9 37.5 %slice-start = ((s8[6291456]{0:T(1024)(128)(4,1)}), s8[4194304]{0:T(1024)(128)(4,1)S(1)}, s32[]{:S(2)}) async-start(s8[6291456]{0:T(1024)(128)(4,1)} %bitcast.2), calls=%async_computation | async-start | bytes 8388608
  19.0 7.9 %collective-permute-start.4 = (bf16[48,32,128]{2,1,0:T(8,128)(2,1)S(1)}, bf16[48,32,128]{2,1,0:T(8,128)(2,1)S(1)}, u32[]{:S(2)}, u32[]{:S(2)}) collective-permute-start(bf16[48,32,128]{2,1,0:T(8,128)(2,1)S(1)} %get-tuple-element.49._), channel_id=1, source_target_pairs={{0,8},{1,25},{2,10},{3,27},{4,12},{5,29},{6,14},{7,31},{8,0},{9,17... | collective-permute-start | bytes 1179656 | tf_op jit(solution)/shard_map/ppermute | solution.py:28
  20.7 35.7 %slice-start.1 = ((s8[6291456]{0:T(1024)(128)(4,1)}), s8[2097152]{0:T(1024)(128)(4,1)S(1)}, s32[]{:S(2)}) async-start(s8[6291456]{0:T(1024)(128)(4,1)} %bitcast.2), calls=%async_computation.1 | async-start | bytes 4194304
  27.0 8.0 %collective-permute-start.5 = (bf16[36,32,128]{2,1,0:T(8,128)(2,1)S(1)}, bf16[36,32,128]{2,1,0:T(8,128)(2,1)S(1)}, u32[]{:S(2)}, u32[]{:S(2)}) collective-permute-start(bf16[36,32,128]{2,1,0:T(8,128)(2,1)S(1)} %get-tuple-element.58), channel_id=1, source_target_pairs={{0,24},{1,9},{2,26},{3,11},{4,28},{5,13},{6,30},{7,15},{8,16},{9,1... | collective-permute-start | bytes 884744 | tf_op jit(solution)/shard_map/ppermute | solution.py:28
  35.1 8.8 %collective-permute-start.6 = (bf16[44,32,128]{2,1,0:T(8,128)(2,1)S(1)}, bf16[44,32,128]{2,1,0:T(8,128)(2,1)S(1)}, u32[]{:S(2)}, u32[]{:S(2)}) collective-permute-start(bf16[44,32,128]{2,1,0:T(8,128)(2,1)S(1)} %get-tuple-element.62), channel_id=1, source_target_pairs={{0,2},{1,7},{2,0},{3,5},{4,6},{5,3},{6,4},{7,1},{8,10},{9,15},{10,... | collective-permute-start | bytes 1081352 | tf_op jit(solution)/shard_map/ppermute | solution.py:28
  44.0 12.4 %copy-start.9 = (s32[256]{0:T(256)S(1)}, s32[256]{0:T(256)}, u32[]{:S(2)}) copy-start(s32[256]{0:T(256)} %constant.21.clone.table) | copy-start | bytes 3076
  44.0 10.2 %collective-permute-start.7 = (bf16[52,32,128]{2,1,0:T(8,128)(2,1)S(1)}, bf16[52,32,128]{2,1,0:T(8,128)(2,1)S(1)}, u32[]{:S(2)}, u32[]{:S(2)}) collective-permute-start(bf16[52,32,128]{2,1,0:T(8,128)(2,1)S(1)} %get-tuple-element.68), channel_id=1, source_target_pairs={{0,6},{1,3},{2,4},{3,1},{4,2},{5,7},{6,0},{7,5},{8,14},{9,11},{10,... | collective-permute-start | bytes 1277960 | tf_op jit(solution)/shard_map/ppermute | solution.py:28
  54.3 2.1 %collective-permute-start.8 = (bf16[72,32,128]{2,1,0:T(8,128)(2,1)S(1)}, bf16[72,32,128]{2,1,0:T(8,128)(2,1)S(1)}, u32[]{:S(2)}, u32[]{:S(2)}) collective-permute-start(bf16[72,32,128]{2,1,0:T(8,128)(2,1)S(1)} %get-tuple-element.73.own), channel_id=1, source_target_pairs={{0,1},{1,0},{2,3},{3,2},{4,5},{5,4},{6,7},{7,6},{8,9},{9,8},{10,11... | collective-permute-start | bytes 1769480 | tf_op jit(solution)/shard_map/ppermute | solution.py:32
  54.4 4.7 %collective-permute-start.9 = (bf16[12,32,128]{2,1,0:T(8,128)(2,1)S(1)}, bf16[12,32,128]{2,1,0:T(8,128)(2,1)S(1)}, u32[]{:S(2)}, u32[]{:S(2)}) collective-permute-start(bf16[12,32,128]{2,1,0:T(8,128)(2,1)S(1)} %get-tuple-element.74), channel_id=1, source_target_pairs={{0,32},{1,97},{2,34},{3,99},{4,36},{5,101},{6,38},{7,103},{8,40},{... | collective-permute-start | bytes 294920 | tf_op jit(solution)/shard_map/ppermute | solution.py:28
  59.1 6.1 %copy-start.2 = (f32[32,64,128]{2,1,0:T(8,128)S(1)}, f32[32,64,128]{2,1,0:T(8,128)}, u32[]{:S(2)}) copy-start(f32[32,64,128]{2,1,0:T(8,128)} %transfer.1) | copy-start | bytes 3145732
  59.1 6.1 %copy-start.3 = (bf16[32,64,128]{2,1,0:T(8,128)(2,1)S(1)}, bf16[32,64,128]{2,1,0:T(8,128)(2,1)}, u32[]{:S(2)}) copy-start(bf16[32,64,128]{2,1,0:T(8,128)(2,1)} %basis.1) | copy-start | bytes 1572868
  59.2 6.1 %copy-start.4 = (f32[4,4,128,128]{3,2,1,0:T(8,128)S(1)}, f32[4,4,128,128]{3,2,1,0:T(8,128)}, u32[]{:S(2)}) copy-start(f32[4,4,128,128]{3,2,1,0:T(8,128)} %apex.1) | copy-start | bytes 3145732
  59.2 6.1 %copy-start.5 = (f32[1,128,128]{2,1,0:T(8,128)S(1)}, f32[1,128,128]{2,1,0:T(8,128)}, u32[]{:S(2)}) copy-start(f32[1,128,128]{2,1,0:T(8,128)} %lift.1) | copy-start | bytes 196612
  59.2 6.1 %copy-start.8 = (s32[32]{0:T(128)S(1)}, s32[32]{0:T(128)}, u32[]{:S(2)}) copy-start(s32[32]{0:T(128)} %points.1) | copy-start | bytes 388
  59.2 6.1 %collective-permute-start.10 = (bf16[14,32,128]{2,1,0:T(8,128)(2,1)S(1)}, bf16[14,32,128]{2,1,0:T(8,128)(2,1)S(1)}, u32[]{:S(2)}, u32[]{:S(2)}) collective-permute-start(bf16[14,32,128]{2,1,0:T(8,128)(2,1)S(1)} %get-tuple-element.80._), channel_id=1, source_target_pairs={{0,96},{1,33},{2,98},{3,35},{4,100},{5,37},{6,102},{7,39},{8,104},... | collective-permute-start | bytes 344072 | tf_op jit(solution)/shard_map/ppermute | solution.py:28

commit v5 on v3

--- a/solution.py
+++ b/solution.py
@@ -16,6 +16,7 @@
 
 Z, Y, X = 1, 3, 5
 STEPS = ((Y, 0), (Y, 1), (Z, 0), (Z, 1), (X, 0), (X, 1))
+GATHER_STEPS = (STEPS[5], *STEPS[:5])
 
 
 def routed(block, step):
@@ -38,20 +39,19 @@
 
 
 def slot_tables(devices):
-    reduce = np.zeros((2, devices), np.int32)
-    gather = np.zeros((2, devices), np.int32)
-    for core in range(2):
-        for difference in range(devices):
-            other = difference & 1
-            for place, (axis, turn) in enumerate(STEPS):
-                low, high = (difference >> axis) & 1, (difference >> (axis + 1)) & 1
-                by_one = turn == core ^ other
-                bit = low ^ high if by_one else high
-                reduce[core, difference] |= bit << (len(STEPS) - 1 - place)
-                gather[core, difference] |= bit << place
-            reduce[core, difference] |= other << len(STEPS)
-            gather[core, difference] |= other << len(STEPS)
-    return reduce.reshape(-1), gather.reshape(-1)
+    def table(order):
+        slots = np.zeros((2, devices), np.int32)
+        for core in range(2):
+            for difference in range(devices):
+                other = difference & 1
+                for place, (axis, turn) in enumerate(order):
+                    low, high = (difference >> axis) & 1, (difference >> (axis + 1)) & 1
+                    by_one = turn == core ^ other
+                    slots[core, difference] |= (low ^ high if by_one else high) << place
+                slots[core, difference] |= other << len(order)
+        return jnp.asarray(slots.reshape(-1))
+
+    return table(STEPS[::-1]), table(GATHER_STEPS)
 
 
 def slot_in(table, parents, f, me, devices):
@@ -97,6 +97,20 @@
 def pair_mask(points, c, rows):
     lane = lax.broadcasted_iota(jnp.int32, (rows, 2 * B), 1)
     return lane < jnp.where(lane < B, points[c], B + points[c + 1])
+
+
+def moved(place, axis, held, at_first, at_second):
+    me = place[0]
+    y, z = (me >> Y) & 3, (me >> Z) & 3
+    last = 3 * (1 - (me & 1))
+    if axis == Z:
+        moves = z >= 0
+    elif axis == Y:
+        moves = z == last
+    else:
+        moves = (y == 3 - last) & (z == 3 - last)
+    odd = ((me >> axis) & 1) == 1
+    return jnp.where(moves, jnp.where(odd, at_first, at_second), held)
 
 
 def rise_kernel(
@@ -212,117 +226,156 @@
                 keep[own] = value
                 send[other] = value
 
-
-def fold_kernel(exact, exact_next, add, cores, came, partial, sums, gathered, *rest):
-    payload, keep, sums_next, gathered_next = rest[-4:]
+def lay_out(payload, going, exact, sums, *rest):
+    high, low = two(going)
+    start = going.shape[0]
+    payload[:start] = high
+    if exact:
+        payload[start : 2 * start] = low
+        start = 2 * start
+    for part in (*two(sums), *rest):
+        payload[start : start + part.shape[0]] = part
+        start = start + part.shape[0]
+
+
+def fold_kernel(step, *refs):
+    refs = list(refs)
+    place, came, partial, sums = refs[:4]
+    del refs[:4]
+    payload, keep, sums_next = refs[-5:-2]
+    gathered_next, halo_next = refs[-2:]
+    gathered = refs[0]
+    a = gathered.shape[0]
     n = 2 * keep.shape[0]
     m = sums.shape[0]
-    a = gathered.shape[0]
-    if cores:
+    gathered_next[:a] = gathered[...]
+    if step == 0:
+        came_own, pair = refs[1:3]
         total = partial[:n] + came[:n]
-        got = came[n + 1 : n + 1 + m]
-        gathered_next[...] = gathered[...]
+        got = came[n + 1 :]
+        gathered_next[a:] = came_own[...]
+        other = HW * (1 - (place[0] & 1))
+        halo_next[:HW] = pair[pl.ds(other, HW)]
+        halo_next[HW:] = pair[pl.ds(2 * HW + other, HW)]
     else:
+        halo = refs[1]
         total = partial[...] + came[:n].astype(F32)
         start = n
-        if exact:
+        if step >= 3:
             total = total + came[n : 2 * n].astype(F32)
             start = 2 * n
         got = came[start : start + m].astype(F32) + came[start + m : start + 2 * m].astype(F32)
-        gathered_next[:a] = gathered[...]
-        gathered_next[a:] = came[start + 2 * m :]
-    if add:
+        start = start + 2 * m
+        gathered_next[a:] = came[start : start + a]
+        axis, turn = STEPS[step - 1]
+        if turn:
+            before = refs[2]
+            halo_next[...] = moved(
+                place, axis, halo[...], before[before.shape[0] - 2 * HW :], came[start + a :]
+            )
+        else:
+            halo_next[...] = halo[...]
+    if sums_next.shape[0] == m:
         sums_next[...] = sums[...] + got
     else:
         sums_next[:m] = sums[...]
         sums_next[m:] = got
     keep[...] = total[: n // 2]
-    high, low = two(total[n // 2 :])
-    start = n // 2
-    payload[:start] = high
-    if exact_next:
-        payload[start : 2 * start] = low
-        start = 2 * start
-    high, low = two(sums_next[...])
-    k = high.shape[0]
-    payload[start : start + k] = high
-    payload[start + k : start + 2 * k] = low
-    payload[start + 2 * k :] = gathered_next[...]
-
-
-def tail_kernel(start, came, out):
-    out[...] = came[start:]
-
-
-def near_kernel(columns, first, mright, mleft, blocks, _, out, back, to_prev, to_next):
-    step = pl.program_id(0)
-    per, slots = blocks.shape[:2]
-    clusters, rhs = mright.shape[:2]
-
-    @pl.when(step == 0)
-    def _():
-        back[...] = jnp.zeros_like(back)
-
-    group = 4
-    for start in range(0, per, group):
-        done = []
-        for g in range(start, start + group):
-            c = step * per + g
-            row = jnp.concatenate([blocks[g, s] for s in range(slots)], axis=1)
-            places = [columns[s, c] - first[0] for s in range(slots)]
+    parts = [halo_next[...]]
+    if step < 5:
+        parts = [gathered_next[...], *parts]
+    lay_out(payload, total[n // 2 :], step >= 2, sums_next[...], *parts)
+
+
+def rows_of(blocks, c):
+    return jnp.concatenate([blocks[c, s] for s in range(blocks.shape[1])], axis=1)
+
+
+def add_back(columns, first, mleft, blocks, clusters, back):
+    done = []
+    for c in clusters:
+        places = [columns[s, c] - first[0] for s in range(blocks.shape[1])]
+        done.append((places, dot(mleft[c], rows_of(blocks, c), NN)))
+    for places, value in done:
+        held = [back[place] for place in places]
+        for s, place in enumerate(places):
+            back[place] = held[s] + value[:, s * B : (s + 1) * B]
+
+
+def near_outer_kernel(columns, first, mright, mleft, blocks, back, sent):
+    clusters = mleft.shape[0]
+    back[...] = jnp.zeros_like(back)
+    add_back(columns, first, mleft, blocks, range(HW), back)
+    add_back(columns, first, mleft, blocks, range(clusters - HW, clusters), back)
+    sent[:HW] = mright[:HW]
+    sent[HW : 2 * HW] = mright[clusters - HW :]
+    sent[2 * HW : 3 * HW] = back[:HW].astype(BF)
+    sent[3 * HW :] = back[clusters + HW :].astype(BF)
+
+
+def near_kernel(columns, first, mright, mleft, blocks, back_outer, _, out, back):
+    clusters = mright.shape[0]
+    slots = blocks.shape[1]
+    back[...] = back_outer[...]
+    for start in range(0, clusters, 4):
+        group = range(start, start + 4)
+        for c in group:
             inside = []
-            for place in places:
-                own = place - HW
+            for s in range(slots):
+                own = columns[s, c] - first[0] - HW
                 value = mright[jnp.clip(own, 0, clusters - 1)]
                 is_own = (own >= 0) & (own < clusters)
                 inside.append(jnp.where(is_own, value, jnp.zeros_like(value)))
-            out[c] = dot(row, jnp.concatenate(inside, axis=1), NT).T
-            done.append((places, dot(mleft[c], row, NN)))
-        for places, value in done:
-            held = [back[place] for place in places]
-            for s, place in enumerate(places):
-                back[place] = held[s] + value[:, s * B : (s + 1) * B]
-
-    @pl.when(step == pl.num_programs(0) - 1)
-    def _():
-        to_prev[:HW] = mright[:HW]
-        to_prev[HW:] = back[:HW].astype(BF)
-        to_next[:HW] = mright[clusters - HW :]
-        to_next[HW:] = back[clusters + HW :].astype(BF)
-
-
-def edge_kernel(columns, first, from_prev, from_next, low_blocks, high_blocks, out):
-    slots = low_blocks.shape[1]
+            out[c] = dot(rows_of(blocks, c), jnp.concatenate(inside, axis=1), NT).T
+        if HW <= start < clusters - HW:
+            add_back(columns, first, mleft, blocks, group, back)
+
+
+def edge(low, columns, first, halo, blocks, out):
+    slots = blocks.shape[1]
     clusters = columns.shape[1]
-    for g in range(2 * HW):
-        low = g < HW
-        c = g if low else clusters - 2 * HW + g
-        blocks, halo = (low_blocks, from_prev) if low else (high_blocks, from_next)
-        row = jnp.concatenate([blocks[g % HW, s] for s in range(slots)], axis=1)
+    start = jnp.where(low, 0, clusters - HW)
+    row_start = first[0] + jnp.where(low, 0, clusters + HW)
+    for g in range(HW):
+        c = start + g
         values = []
         for s in range(slots):
-            place = columns[s, c] - first[0]
-            place = place if low else place - (clusters + HW)
-            value = halo[jnp.clip(place, 0, HW - 1)]
-            is_there = (place >= 0) & (place < HW)
+            row = columns[s, c] - row_start
+            value = halo[jnp.clip(row, 0, HW - 1)]
+            is_there = (row >= 0) & (row < HW)
             values.append(jnp.where(is_there, value, jnp.zeros_like(value)))
-        out[g] = dot(row, jnp.concatenate(values, axis=1), NT).T
-
-
-def forward_kernel(place, count, parents, table, own, came, own_other, other, coupling, out, all_of):
+        out[g] = dot(rows_of(blocks, c), jnp.concatenate(values, axis=1), NT).T
+
+
+def edge_pair_kernel(place, columns, first, pair, blocks, _, out, back, halo):
+    core = place[0] & 1
+    halo[...] = pair[pl.ds(HW * core, HW)]
+    edge(core == 1, columns, first, halo, blocks, out)
+    back[...] = pair[pl.ds(2 * HW + HW * core, HW)].astype(F32)
+
+
+def edge_chain_kernel(place, columns, first, held, before, came, blocks, _, out, back, halo):
+    core = place[0] & 1
+    value = moved(
+        place, X, held[...], before[before.shape[0] - 2 * HW :], came[came.shape[0] - 2 * HW :]
+    )
+    halo[...] = value[:HW]
+    edge(core == 0, columns, first, halo, blocks, out)
+    back[...] = value[HW:].astype(F32)
+
+
+def forward_kernel(place, count, parents, table, own, other, coupling, _, out, all_of):
     far_slots = coupling.shape[1]
-    quarter = own.shape[0]
-    all_of[:quarter] = own[...]
-    all_of[quarter : 2 * quarter] = came[came.shape[0] - quarter :]
-    all_of[2 * quarter : 3 * quarter] = own_other[...]
-    all_of[3 * quarter :] = other[...]
+    half = all_of.shape[0] // 2
+    all_of[:half] = own[:half]
+    all_of[half:] = other[:half]
     me = place[0]
     total = jnp.zeros((B, own.shape[1]), F32)
     group = 48
     for start in range(0, far_slots, group):
         rows, values = [], []
         for f in range(start, start + group):
-            value = all_of[slot_in(table, parents, f, me, 4 * quarter)]
+            value = all_of[slot_in(table, parents, f, me, 2 * half)]
             value = jnp.where(f < count[0], value, jnp.zeros_like(value))
             values += [value, value]
             rows += two(coupling[0, f])
@@ -345,9 +398,10 @@
     basis,
     near_out,
     near_back,
-    edge_out,
-    from_prev,
-    from_next,
+    pair_out,
+    pair_back,
+    chain_out,
+    chain_back,
     product,
     adjoint,
     hats,
@@ -391,21 +445,25 @@
         product[:, columns] = jnp.where(mask, near + far[:rhs], 0.0)
         adjoint[:, columns] = jnp.where(mask, back + far[rhs:], 0.0)
 
-    def edge(g, c, halo):
+    def add_edge(c, low):
         mask = lax.broadcasted_iota(jnp.int32, (rhs, B), 1) < points[c]
         columns = slice((c % per) * B, (c % per + 1) * B)
-        product[:, columns] += jnp.where(mask, edge_out[g], 0.0)
-        adjoint[:, columns] += jnp.where(mask, halo[HW + g % HW].astype(F32), 0.0)
+        g = c % HW
+        in_chip = (place[0] & 1) == (1 if low else 0)
+        out = jnp.where(in_chip, pair_out[g], chain_out[g])
+        back = jnp.where(in_chip, pair_back[g], chain_back[g])
+        product[:, columns] += jnp.where(mask, out, 0.0)
+        adjoint[:, columns] += jnp.where(mask, back, 0.0)
 
     @pl.when(step == 0)
     def _():
-        for g in range(HW):
-            edge(g, g, from_prev)
+        for c in range(HW):
+            add_edge(c, True)
 
     @pl.when(step == pl.num_programs(0) - 1)
     def _():
-        for g in range(HW):
-            edge(HW + g, clusters - HW + g, from_next)
+        for c in range(clusters - HW, clusters):
+            add_edge(c, False)
 
 
 SMEM = pl.BlockSpec(memory_space=pltpu.SMEM)
@@ -455,8 +513,7 @@
     apex_coupling,
 ):
     rhs = right_sides.shape[0]
-    clusters, near_slots = near_blocks.shape[:2]
-    far_slots = coupling.shape[1]
+    clusters = near_blocks.shape[0]
     rank = leaf_basis.shape[1]
     me = lax.axis_index(AXES)
     devices = lax.axis_size(AXES)
@@ -464,37 +521,42 @@
     all_clusters = (clusters, *block)
     half = devices // 2
     place = me.astype(jnp.int32)[None]
-    reduce_table, gather_table = (jnp.asarray(table) for table in slot_tables(devices))
-
-    mright, mleft, gathered, partial, sent, sums = call(
+    first = place * clusters - HW
+    columns = near_columns.T
+    reduce_table, gather_table = slot_tables(devices)
+
+    def rows(n, kind=BF):
+        return (VMEM, (n, *block), kind)
+
+    def at_rest(*values):
+        return [pltpu.with_memory_space_constraint(value, pltpu.HBM) for value in values]
+
+    mright, mleft, own, partial, sent, sums = call(
         rise_kernel,
         "rise",
         (),
         [SMEM] * 2 + [HBM] * 9,
         [
-            (VMEM, all_clusters, BF),
-            (VMEM, all_clusters, BF),
-            (VMEM, (1, *block), BF),
-            (VMEM, (half + 1, *block), F32),
-            (VMEM, (half + 3, *block), F32),
-            (VMEM, (2, *block), F32),
+            rows(clusters),
+            rows(clusters),
+            rows(1),
+            rows(half + 1, F32),
+            rows(half + 3, F32),
+            rows(2, F32),
         ],
         (
             place,
             far_count,
-            *(
-                pltpu.with_memory_space_constraint(value, pltpu.HBM)
-                for value in (
-                    cluster_points,
-                    far_parents,
-                    reduce_table,
-                    right_sides,
-                    left_sides,
-                    leaf_basis,
-                    transfer,
-                    slab_transfer,
-                    coupling,
-                )
+            *at_rest(
+                cluster_points,
+                far_parents,
+                reduce_table,
+                right_sides,
+                left_sides,
+                leaf_basis,
+                transfer,
+                slab_transfer,
+                coupling,
             ),
         ),
         us=5,
@@ -511,105 +573,76 @@
             pltpu.SemaphoreType.DMA((16,)),
         ],
     )
-
-    def fold(step, came, partial, sums, gathered, after=()):
+    came = to_other_core(sent)
+    came_own = routed(own, GATHER_STEPS[0])
+    back_outer, pair_sent = call(
+        near_outer_kernel,
+        "near_outer",
+        (),
+        [SMEM] * 2 + [VMEM] * 3,
+        [rows(clusters + 2 * HW, F32), rows(4 * HW)],
+        (columns, first, mright, mleft, near_blocks),
+        us=1,
+    )
+    pair = to_other_core(pair_sent)
+
+    def fold(step, came, partial, sums, gathered, *rest, after):
         n = half >> step
-        exact_next = step >= 2
-        add = step == 0 or STEPS[step - 1][0] != X
-        m = 2 if add else 4
-        a = 1 << step
-        rows = n // 2 * (2 if exact_next else 1) + 2 * m + a
+        m = 2 if step == 0 or STEPS[step - 1][0] != X else 4
+        a = 2 << step
+        size = n // 2 * (2 if step >= 2 else 1) + 2 * m + 2 * HW + (a if step < 5 else 0)
+        args = (place, came, partial, sums, gathered, *rest)
         return call(
-            functools.partial(fold_kernel, step >= 3, exact_next, add, step == 0),
+            lambda *refs: fold_kernel(step, *refs[: len(args)], *refs[len(args) + 1 :]),
             "fold",
             (),
-            [VMEM] * 4 + [ANY] * len(after),
-            [
-                (VMEM, (rows, *block), BF),
-                (VMEM, (n // 2, *block), F32),
-                (VMEM, (m, *block), F32),
-                (VMEM, (a, *block), BF),
-            ],
-            (came, partial, sums, gathered, *after),
+            [SMEM] + [VMEM] * (len(args) - 1) + [ANY],
+            [rows(size), rows(n // 2, F32), rows(m, F32), rows(a), rows(2 * HW)],
+            (*args, after),
             us=0.3,
         )
 
-    came = to_other_core(sent)
-    payload, partial, sums, gathered = fold(0, came, partial, sums, gathered)
+    payload, partial, sums, gathered, halo = fold(
+        0, came, partial, sums, own, came_own, pair, after=back_outer
+    )
     came = routed(payload, STEPS[0])
-
-    columns = near_columns.T
-    first = place * clusters - HW
-    per = 16
-    halo = (2 * HW, *block)
-    near_out, near_back, to_prev, to_next = call(
+    near_out, near_back = call(
         near_kernel,
         "near",
-        (clusters // per,),
-        [
-            SMEM,
-            SMEM,
-            whole(*all_clusters),
-            whole(*all_clusters),
-            pl.BlockSpec((per, near_slots, B, B), lambda i: (i, 0, 0, 0)),
-            ANY,
-        ],
-        [
-            (whole(*all_clusters), all_clusters, F32),
-            (whole(clusters + 2 * HW, *block), (clusters + 2 * HW, *block), F32),
-            (whole(*halo), halo, BF),
-            (whole(*halo), halo, BF),
-        ],
-        (columns, first, mright, mleft, near_blocks, payload),
-        us=5,
-    )
-    payload, partial, sums, gathered = fold(1, came, partial, sums, gathered, (near_out,))
-    came = routed(payload, STEPS[1])
-    from_next = passed_along(to_prev, -1)
-    from_prev = passed_along(to_next, 1)
-    payload, partial, sums, gathered = fold(2, came, partial, sums, gathered)
-    came = routed(payload, STEPS[2])
-    payload, partial, sums, gathered = fold(3, came, partial, sums, gathered)
-    came = routed(payload, STEPS[3])
-    last = clusters // HW - 1
-    (edge_out,) = call(
-        edge_kernel,
-        "edge",
-        (1,),
-        [
-            SMEM,
-            SMEM,
-            whole(*halo),
-            whole(*halo),
-            pl.BlockSpec((HW, near_slots, B, B), lambda i: (0, 0, 0, 0)),
-            pl.BlockSpec((HW, near_slots, B, B), lambda i: (last, 0, 0, 0)),
-        ],
-        [(whole(*halo), halo, F32)],
-        (columns, first, from_prev, from_next, near_blocks, near_blocks),
-        us=2,
-    )
-    payload, partial, sums, gathered = fold(4, came, partial, sums, gathered, (edge_out,))
-    came = routed(payload, STEPS[4])
-    payload, partial, sums, gathered = fold(5, came, partial, sums, gathered)
-    came = routed(payload, STEPS[5])
+        (),
+        [SMEM] * 2 + [VMEM] * 4 + [ANY],
+        [rows(clusters, F32), rows(clusters + 2 * HW, F32)],
+        (columns, first, mright, mleft, near_blocks, back_outer, payload),
+        us=4,
+    )
+    after = near_out
+    before = came
+    for step in range(1, len(STEPS)):
+        rest = (halo, before) if STEPS[step - 1][1] else (halo,)
+        before = came
+        payload, partial, sums, gathered, halo = fold(
+            step, came, partial, sums, gathered, *rest, after=after
+        )
+        came = routed(payload, STEPS[step])
+        after = payload
+        if step == 1:
+            pair_out, pair_back = call(
+                edge_pair_kernel,
+                "edge_pair",
+                (),
+                [SMEM] * 3 + [VMEM] * 2 + [ANY],
+                [rows(HW, F32)] * 2,
+                (place, columns, first, pair, near_blocks, payload),
+                us=0.8,
+                scratch=[pltpu.VMEM((HW, *block), BF)],
+            )
+            after = pair_out
     gathered_other = to_other_core(gathered)
-    quarter = (half // 2, *block)
-    (came_last,) = call(
-        functools.partial(tail_kernel, 10),
-        "tail",
-        (),
-        [VMEM],
-        [(VMEM, quarter, BF)],
-        (came,),
-        us=0.3,
-    )
-    other = to_other_core(came_last)
-
     (far_right,) = call(
         forward_kernel,
         "forward",
         (),
-        [SMEM] * 4 + [VMEM] * 5,
+        [SMEM] * 4 + [VMEM] * 3 + [ANY],
         [(VMEM, block, F32)],
         (
             place,
@@ -617,13 +650,22 @@
             far_parents,
             gather_table,
             gathered,
-            came,
             gathered_other,
-            other,
             coupling,
+            payload,
         ),
-        us=3,
+        us=2.5,
         scratch=[pltpu.VMEM((devices, *block), BF)],
+    )
+    chain_out, chain_back = call(
+        edge_chain_kernel,
+        "edge_chain",
+        (),
+        [SMEM] * 3 + [VMEM] * 4 + [ANY],
+        [rows(HW, F32)] * 2,
+        (place, columns, first, halo, before, came, near_blocks, far_right),
+        us=0.8,
+        scratch=[pltpu.VMEM((HW, *block), BF)],
     )
 
     per = 16
@@ -639,16 +681,14 @@
             whole(*block),
             whole(1, *block),
             whole(4, *block),
-            whole(42, *block),
+            whole(*came.shape),
             whole(*apex_coupling.shape),
             whole(1, B, B),
             bases,
             bases,
             whole(*all_clusters),
             whole(clusters + 2 * HW, *block),
-            whole(*halo),
-            whole(*halo),
-            whole(*halo),
+            *[whole(HW, *block)] * 4,
         ],
         [(sides, (rhs, clusters * B), F32)] * 2,
         (
@@ -664,9 +704,10 @@
             leaf_basis,
             near_out,
             near_back,
-            edge_out,
-            from_prev,
-            from_next,
+            pair_out,
+            pair_back,
+            chain_out,
+            chain_back,
         ),
         us=4,
         scratch=[pltpu.VMEM((4 * rhs, 2 * B), BF)],

time: 70.1 us -> 66.2 us (0.944); the launches traced: 68.8 us -> 66 us
  starting transfers between devices: 26.1 us -> 17.6 us
  waiting for transfers between devices: 24.6 us -> 27.5 us
  Pallas kernels: 16.5 us -> 18.7 us
  local copies, waits for them, and re-layouts: 0.07 us -> 0.79 us
    ppermute x6 -> x7, waiting for transfers between devices: 18.4 us -> 27.5 us  [routed(): return lax.ppermute(block, AXES, route)]
    ppermute x6 -> x7, starting transfers between devices: 23.1 us -> 17 us  [routed(): return lax.ppermute(block, AXES, route)]
    ppermute x3, waiting for transfers between devices: 4.23 us -> 0.01 us  [to_other_core(): lax.ppermute(block, AXES, [(i, i ^ 1) for i in range(lax.axis_size(AXES))])]
    ppermute x2 -> x0, starting transfers between devices: 2.84 us -> none  [passed_along(): return lax.ppermute(block, AXES, route)]
    pallas_call x12 -> x13, Pallas kernels: 16.5 us -> 18.7 us  [call(): pl.pallas_call(kernel, grid=grid, out_shape=tuple((shape(dims, kind) for...]
    ppermute x2 -> x0, waiting for transfers between devices: 2 us -> none  [passed_along(): return lax.ppermute(block, AXES, route)]
    unnamed x22, local copies, waits for them, and re-layouts: 0.07 us -> 0.79 us
  transfers between devices with their start and end apart: 11 -> 10, of which waited for: 8 -> 7; matrix products, arithmetic and copies ran while one was open for 0% -> 0% of each run, Pallas kernels for 8% -> 13%
where the time goes in v5:
time: 66.2 us; the launch traced here: 66 us
  waiting for transfers between devices  27.5 us (42%)
  Pallas kernels  18.7 us (28%)
  starting transfers between devices  17.6 us (27%)
  between operations  1.42 us (2%)
  local copies, waits for them, and re-layouts  0.79 us (1%)
    ppermute x7, waiting for transfers between devices, routed(): return lax.ppermute(block, AXES, route)  27.5 us
    pallas_call x13, Pallas kernels, call(): pl.pallas_call(kernel, grid=grid, out_shape=tuple((shape(dims, kind) for...  18.7 us
    ppermute x7, starting transfers between devices, routed(): return lax.ppermute(block, AXES, route)  17 us
  transfers between devices with their start and end apart: 10, of which 7 were waited for; matrix products, arithmetic and copies ran while one was open for 0% of the time, Pallas kernels for 13%

profile of v5, /device:TPU:0, one launch (start us, length us, event | category | flops | bytes accessed | tf_op | source)
XLA Modules:
  0.0 66.0 jit_solution(17118459677710558055)
XLA Ops:
  1.3 0.0 copy-start
  1.3 0.0 copy-start.5
  1.3 5.6 %rise.1 = (bf16[32,32,128]{2,1,0:T(8,128)(2,1)S(1)}, bf16[32,32,128]{2,1,0:T(8,128)(2,1)S(1)}, bf16[1,32,128]{2,1,0:T(8,128)(2,1)S(1)}, f32[65,32,128]{2,1,0:T(8...) custom-call(s32[1]{0:T(128)} %bitcast.place.refs_0_, s32[1]{0:T(128)S(6)} %copy.16.count, s32[32]{0:T(128)} %points.1, ...), custom_call_target="tpu_custom_call" | custom-call | flops 1000 | bytes 18000000 | tf_op jit(solution)/shard_map/rise/pallas_call | solution.py:485
  6.9 0.1 collective-permute-start
  7.0 0.2 copy-done
  7.2 0.0 copy-done.5
  7.2 1.1 %near_outer.1 = (f32[40,32,128]{2,1,0:T(8,128)S(1)}, bf16[16,32,128]{2,1,0:T(8,128)(2,1)S(1)}) custom-call(s32[8,32]{1,0:T(8,128)S(1)} %bitcast.4, s32[1]{0:T(128)S(6)} %sub.3.first, bf16[32,32,128]{2,1,0:T(8,128)(2,1)S(1)} %get-tuple-element.50.mright, bf16[32,32,128]{2,1,0:T(8,128)(2,1)S(1)} %get-tuple-element.51.mleft, bf16[32,8,128,128]{3,2,1,0:T(8,128)(2,1)S(1)} %copy-done), custom_call_target="tpu_custom_call" | custom-call | flops 1000 | bytes 3600000 | tf_op jit(solution)/shard_map/near_outer/pallas_call | solution.py:485
  8.3 0.4 collective-permute-start.2
  8.7 2.8 %collective-permute-start.1 = (bf16[1,32,128]{2,1,0:T(8,128)(2,1)S(1)}, bf16[1,32,128]{2,1,0:T(8,128)(2,1)S(1)}, u32[]{:S(2)}, u32[]{:S(2)}) collective-permute-start(bf16[1,32,128]{2,1,0:T(8,128)(2,1)S(1)} %get-tuple-element.49.refs_4_), channel_id=1, source_target_pairs={{0,96},{1,33},{2,98},{3,35},{4,100},{5,37},{6,102},{7,39},{8,104},... | collective-permute-start | bytes 24584 | tf_op jit(solution)/shard_map/ppermute | solution.py:28
  11.5 2.0 %collective-permute-done.1.refs_5_ = bf16[1,32,128]{2,1,0:T(8,128)(2,1)S(1)} collective-permute-done((bf16[1,32,128]{2,1,0:T(8,128)(2,1)S(1)}, bf16[1,32,128]{2,1,0:T(8,128)(2,1)S(1)}, u32[]{:S(2)}, u32[]{:S(2)}) %collective-permute-start.1) | collective-permute-done | bytes 8224 | tf_op jit(solution)/shard_map/ppermute | solution.py:28
  13.5 0.0 collective-permute-done.2.refs_6_.pair
  13.6 0.0 collective-permute-done.refs_1_
  13.6 0.1 fold.6
  13.7 1.7 %collective-permute-start.3 = (bf16[46,32,128]{2,1,0:T(8,128)(2,1)S(1)}, bf16[46,32,128]{2,1,0:T(8,128)(2,1)S(1)}, u32[]{:S(2)}, u32[]{:S(2)}) collective-permute-start(bf16[46,32,128]{2,1,0:T(8,128)(2,1)S(1)} %get-tuple-element.54._), channel_id=1, source_target_pairs={{0,8},{1,25},{2,10},{3,27},{4,12},{5,29},{6,14},{7,31},{8,0},{9,17... | collective-permute-start | bytes 1130504 | tf_op jit(solution)/shard_map/ppermute | solution.py:28
  15.4 3.9 %near.1 = (f32[32,32,128]{2,1,0:T(8,128)S(1)}, f32[40,32,128]{2,1,0:T(8,128)S(1)}) custom-call(s32[8,32]{1,0:T(8,128)S(1)} %bitcast.5, s32[1]{0:T(128)S(6)} %sub.3.first, bf16[32,32,128]{2,1,0:T(8,128)(2,1)S(1)} %get-tuple-element.50.mright, bf16[32,32,128]{2,1,0:T(8,128)(2,1)S(1)} %get-tuple-element.51.mleft, bf16[32,8,128,128]{3,2,1,0:T(8,128)(2,1)S(1)} %copy-done, ...), custom_call_target="tpu_custom_call" | custom-call | flops 1000 | bytes 14400000 | tf_op jit(solution)/shard_map/near/pallas_call | solution.py:485
  19.3 2.1 %collective-permute-done.3.refs_1_.refs_6_ = bf16[46,32,128]{2,1,0:T(8,128)(2,1)S(1)} collective-permute-done((bf16[46,32,128]{2,1,0:T(8,128)(2,1)S(1)}, bf16[46,32,128]{2,1,0:T(8,128)(2,1)S(1)}, u32[]{:S(2)}, u32[]{:S(2)}) %collective-permute-start.3) | collective-permute-done | bytes 376864 | tf_op jit(solution)/shard_map/ppermute | solution.py:28
  21.4 0.1 fold.7
  21.5 0.0 slice-start.1
  21.5 3.2 %collective-permute-start.4 = (bf16[32,32,128]{2,1,0:T(8,128)(2,1)S(1)}, bf16[32,32,128]{2,1,0:T(8,128)(2,1)S(1)}, u32[]{:S(2)}, u32[]{:S(2)}) collective-permute-start(bf16[32,32,128]{2,1,0:T(8,128)(2,1)S(1)} %get-tuple-element.60._), channel_id=1, source_target_pairs={{0,24},{1,9},{2,26},{3,11},{4,28},{5,13},{6,30},{7,15},{8,16},{9,1... | collective-permute-start | bytes 786440 | tf_op jit(solution)/shard_map/ppermute | solution.py:28
  24.7 1.1 %edge_pair.1 = (f32[4,32,128]{2,1,0:T(8,128)S(1)}, f32[4,32,128]{2,1,0:T(8,128)S(1)}) custom-call(s32[1]{0:T(128)} %bitcast.place.refs_0_, s32[8,32]{1,0:T(8,128)S(1)} %bitcast.6, s32[1]{0:T(128)S(6)} %sub.3.first, bf16[16,32,128]{2,1,0:T(8,128)(2,1)S(1)} %collective-permute-done.2.refs_6_.pair, bf16[32,8,128,128]{3,2,1,0:T(8,128)(2,1)S(1)} %copy-done, ...), custom_call_target="tpu_custom_call" | custom-call | flops 1000 | bytes 2880000 | tf_op jit(solution)/shard_map/edge_pair/pallas_call | solution.py:485
  25.7 3.4 %collective-permute-done.4.refs_1_ = bf16[32,32,128]{2,1,0:T(8,128)(2,1)S(1)} collective-permute-done((bf16[32,32,128]{2,1,0:T(8,128)(2,1)S(1)}, bf16[32,32,128]{2,1,0:T(8,128)(2,1)S(1)}, u32[]{:S(2)}, u32[]{:S(2)}) %collective-permute-start.4) | collective-permute-done | bytes 262176 | tf_op jit(solution)/shard_map/ppermute | solution.py:28
  29.2 0.1 fold.8
  29.3 2.1 %collective-permute-start.5 = (bf16[36,32,128]{2,1,0:T(8,128)(2,1)S(1)}, bf16[36,32,128]{2,1,0:T(8,128)(2,1)S(1)}, u32[]{:S(2)}, u32[]{:S(2)}) collective-permute-start(bf16[36,32,128]{2,1,0:T(8,128)(2,1)S(1)} %get-tuple-element.66.refs_6_), channel_id=1, source_target_pairs={{0,2},{1,7},{2,0},{3,5},{4,6},{5,3},{6,4},{7,1},{8,10},{9,15},{10,... | collective-permute-start | bytes 884744 | tf_op jit(solution)/shard_map/ppermute | solution.py:28
  31.3 6.4 %collective-permute-done.5.refs_1_.refs_6_ = bf16[36,32,128]{2,1,0:T(8,128)(2,1)S(1)} collective-permute-done((bf16[36,32,128]{2,1,0:T(8,128)(2,1)S(1)}, bf16[36,32,128]{2,1,0:T(8,128)(2,1)S(1)}, u32[]{:S(2)}, u32[]{:S(2)}) %collective-permute-start.5) | collective-permute-done | bytes 294944 | tf_op jit(solution)/shard_map/ppermute | solution.py:28
  37.7 0.1 fold.9
  37.8 4.1 %collective-permute-start.6 = (bf16[36,32,128]{2,1,0:T(8,128)(2,1)S(1)}, bf16[36,32,128]{2,1,0:T(8,128)(2,1)S(1)}, u32[]{:S(2)}, u32[]{:S(2)}) collective-permute-start(bf16[36,32,128]{2,1,0:T(8,128)(2,1)S(1)} %get-tuple-element.71.refs_7_), channel_id=1, source_target_pairs={{0,6},{1,3},{2,4},{3,1},{4,2},{5,7},{6,0},{7,5},{8,14},{9,11},{10,... | collective-permute-start | bytes 884744 | tf_op jit(solution)/shard_map/ppermute | solution.py:28
  41.9 4.7 %collective-permute-done.6.refs_1_ = bf16[36,32,128]{2,1,0:T(8,128)(2,1)S(1)} collective-permute-done((bf16[36,32,128]{2,1,0:T(8,128)(2,1)S(1)}, bf16[36,32,128]{2,1,0:T(8,128)(2,1)S(1)}, u32[]{:S(2)}, u32[]{:S(2)}) %collective-permute-start.6) | collective-permute-done | bytes 294944 | tf_op jit(solution)/shard_map/ppermute | solution.py:28
  46.6 0.1 fold.10
  46.7 0.1 collective-permute-start.7
  46.8 7.8 %collective-permute-done.7.refs_1_.before = bf16[48,32,128]{2,1,0:T(8,128)(2,1)S(1)} collective-permute-done((bf16[48,32,128]{2,1,0:T(8,128)(2,1)S(1)}, bf16[48,32,128]{2,1,0:T(8,128)(2,1)S(1)}, u32[]{:S(2)}, u32[]{:S(2)}) %collective-permute-start.7) | collective-permute-done | bytes 393248 | tf_op jit(solution)/shard_map/ppermute | solution.py:28
  54.5 0.1 fold.11
  54.6 0.1 collective-permute-start.8
  54.7 3.0 %collective-permute-start.9 = (bf16[18,32,128]{2,1,0:T(8,128)(2,1)S(1)}, bf16[18,32,128]{2,1,0:T(8,128)(2,1)S(1)}, u32[]{:S(2)}, u32[]{:S(2)}) collective-permute-start(bf16[18,32,128]{2,1,0:T(8,128)(2,1)S(1)} %get-tuple-element.82._), channel_id=1, source_target_pairs={{0,96},{1,33},{2,98},{3,35},{4,100},{5,37},{6,102},{7,39},{8,104},... | collective-permute-start | bytes 442376 | tf_op jit(solution)/shard_map/ppermute | solution.py:28
  57.7 0.0 collective-permute-done.8.other
  57.7 0.0 slice-done
  57.7 0.0 slice-done.1
  57.7 0.0 copy-done.6
  57.7 0.0 copy-done.8
  57.7 2.4 %forward.1._.far_right = f32[32,128]{1,0:T(8,128)S(1)} custom-call(s32[1]{0:T(128)} %bitcast.place.refs_0_, s32[1]{0:T(128)S(6)} %copy.16.count, s32[1,96]{1,0:T(1,128)S(1)} %copy-done.6, s32[256]{0:T(256)S(1)} %copy-done.8, bf16[64,32,128]{2,1,0:T(8,128)(2,1)S(1)} %get-tuple-element.81.own, bf16[64,32,128]{2,1,0:T(8,128)(2,1)S(1)} %collective-permute-done.8.other, ...), custom_call_target="tpu_custom_call" | custom-call | flops 1000 | bytes 9000000 | tf_op jit(solution)/shard_map/forward/pallas_call | solution.py:485
  60.1 1.1 %collective-permute-done.9.came = bf16[18,32,128]{2,1,0:T(8,128)(2,1)S(1)} collective-permute-done((bf16[18,32,128]{2,1,0:T(8,128)(2,1)S(1)}, bf16[18,32,128]{2,1,0:T(8,128)(2,1)S(1)}, u32[]{:S(2)}, u32[]{:S(2)}) %collective-permute-start.9) | collective-permute-done | bytes 147488 | tf_op jit(solution)/shard_map/ppermute | solution.py:28
  61.3 0.0 copy-start.7
  61.3 1.1 %edge_chain.1 = (f32[4,32,128]{2,1,0:T(8,128)S(1)}, f32[4,32,128]{2,1,0:T(8,128)S(1)}) custom-call(s32[1]{0:T(128)} %bitcast.place.refs_0_, s32[8,32]{1,0:T(8,128)S(1)} %bitcast.7, s32[1]{0:T(128)S(6)} %sub.3.first, bf16[8,32,128]{2,1,0:T(8,128)(2,1)S(1)} %get-tuple-element.87.held, bf16[48,32,128]{2,1,0:T(8,128)(2,1)S(1)} %collective-permute-done.7.refs_1_.before, ...), custom_call_target="tpu_custom_call" | custom-call | flops 1000 | bytes 2880000 | tf_op jit(solution)/shard_map/edge_chain/pallas_call | solution.py:485
  62.4 0.1 copy-done.1
  62.5 0.1 copy-done.2
  62.6 0.3 copy-done.3
  63.0 0.0 copy-done.4
  63.0 0.0 copy-done.7
  63.0 3.0 %down.1 = (f32[32,4096]{1,0:T(8,128)}, f32[32,4096]{1,0:T(8,128)}) custom-call(s32[32]{0:T(128)S(1)} %copy-done.7, s32[1]{0:T(128)} %bitcast.place.refs_0_, f32[32,128]{1,0:T(8,128)S(1)} %forward.1._.far_right, f32[1,32,128]{2,1,0:T(8,128)S(1)} %get-tuple-element.83.partial, f32[4,32,128]{2,1,0:T(8,128)S(1)} %get-tuple-element.84.sums, ...), custom_call_target="tpu_custom_call" | custom-call | flops 1000 | bytes 14400000 | tf_op jit(solution)/shard_map/down/pallas_call | solution.py:485
  (8 shorter events, 0.0 us)
Async XLA Ops:
  1.3 5.9 %copy-start = (bf16[32,8,128,128]{3,2,1,0:T(8,128)(2,1)S(1)}, bf16[32,8,128,128]{3,2,1,0:T(8,128)(2,1)}, u32[]{:S(2)}) copy-start(bf16[32,8,128,128]{3,2,1,0:T(8,128)(2,1)} %blocks.7) | copy-start | bytes 25165828
  1.3 5.9 %copy-start.5 = (s32[32,8]{0,1:T(8,128)S(1)}, s32[32,8]{0,1:T(8,128)}, u32[]{:S(2)}) copy-start(s32[32,8]{0,1:T(8,128)} %param.17) | copy-start | bytes 3076
  6.9 6.6 %collective-permute-start = (f32[67,32,128]{2,1,0:T(8,128)S(1)}, f32[67,32,128]{2,1,0:T(8,128)S(1)}, u32[]{:S(2)}, u32[]{:S(2)}) collective-permute-start(f32[67,32,128]{2,1,0:T(8,128)S(1)} %get-tuple-element.46), channel_id=1, source_target_pairs={{0,1},{1,0},{2,3},{3,2},{4,5},{5,4},{6,7},{7,6},{8,9},{9,8},{10,11... | collective-permute-start | bytes 3293192 | tf_op jit(solution)/shard_map/ppermute | solution.py:32
  8.3 5.3 %collective-permute-start.2 = (bf16[16,32,128]{2,1,0:T(8,128)(2,1)S(1)}, bf16[16,32,128]{2,1,0:T(8,128)(2,1)S(1)}, u32[]{:S(2)}, u32[]{:S(2)}) collective-permute-start(bf16[16,32,128]{2,1,0:T(8,128)(2,1)S(1)} %get-tuple-element.52), channel_id=1, source_target_pairs={{0,1},{1,0},{2,3},{3,2},{4,5},{5,4},{6,7},{7,6},{8,9},{9,8},{10,11... | collective-permute-start | bytes 393224 | tf_op jit(solution)/shard_map/ppermute | solution.py:32
  8.7 4.9 %collective-permute-start.1 = (bf16[1,32,128]{2,1,0:T(8,128)(2,1)S(1)}, bf16[1,32,128]{2,1,0:T(8,128)(2,1)S(1)}, u32[]{:S(2)}, u32[]{:S(2)}) collective-permute-start(bf16[1,32,128]{2,1,0:T(8,128)(2,1)S(1)} %get-tuple-element.49.refs_4_), channel_id=1, source_target_pairs={{0,96},{1,33},{2,98},{3,35},{4,100},{5,37},{6,102},{7,39},{8,104},... | collective-permute-start | bytes 24584 | tf_op jit(solution)/shard_map/ppermute | solution.py:28
  13.7 7.7 %collective-permute-start.3 = (bf16[46,32,128]{2,1,0:T(8,128)(2,1)S(1)}, bf16[46,32,128]{2,1,0:T(8,128)(2,1)S(1)}, u32[]{:S(2)}, u32[]{:S(2)}) collective-permute-start(bf16[46,32,128]{2,1,0:T(8,128)(2,1)S(1)} %get-tuple-element.54._), channel_id=1, source_target_pairs={{0,8},{1,25},{2,10},{3,27},{4,12},{5,29},{6,14},{7,31},{8,0},{9,17... | collective-permute-start | bytes 1130504 | tf_op jit(solution)/shard_map/ppermute | solution.py:28
  21.4 36.3 %slice-start = ((s8[6291456]{0:T(1024)(128)(4,1)}), s8[4194304]{0:T(1024)(128)(4,1)S(1)}, s32[]{:S(2)}) async-start(s8[6291456]{0:T(1024)(128)(4,1)} %bitcast.2), calls=%async_computation | async-start | bytes 8388608
  21.5 36.2 %slice-start.1 = ((s8[6291456]{0:T(1024)(128)(4,1)}), s8[2097152]{0:T(1024)(128)(4,1)S(1)}, s32[]{:S(2)}) async-start(s8[6291456]{0:T(1024)(128)(4,1)} %bitcast.2), calls=%async_computation.1 | async-start | bytes 4194304
  21.5 7.7 %collective-permute-start.4 = (bf16[32,32,128]{2,1,0:T(8,128)(2,1)S(1)}, bf16[32,32,128]{2,1,0:T(8,128)(2,1)S(1)}, u32[]{:S(2)}, u32[]{:S(2)}) collective-permute-start(bf16[32,32,128]{2,1,0:T(8,128)(2,1)S(1)} %get-tuple-element.60._), channel_id=1, source_target_pairs={{0,24},{1,9},{2,26},{3,11},{4,28},{5,13},{6,30},{7,15},{8,16},{9,1... | collective-permute-start | bytes 786440 | tf_op jit(solution)/shard_map/ppermute | solution.py:28
  29.3 8.5 %collective-permute-start.5 = (bf16[36,32,128]{2,1,0:T(8,128)(2,1)S(1)}, bf16[36,32,128]{2,1,0:T(8,128)(2,1)S(1)}, u32[]{:S(2)}, u32[]{:S(2)}) collective-permute-start(bf16[36,32,128]{2,1,0:T(8,128)(2,1)S(1)} %get-tuple-element.66.refs_6_), channel_id=1, source_target_pairs={{0,2},{1,7},{2,0},{3,5},{4,6},{5,3},{6,4},{7,1},{8,10},{9,15},{10,... | collective-permute-start | bytes 884744 | tf_op jit(solution)/shard_map/ppermute | solution.py:28
  37.8 8.8 %collective-permute-start.6 = (bf16[36,32,128]{2,1,0:T(8,128)(2,1)S(1)}, bf16[36,32,128]{2,1,0:T(8,128)(2,1)S(1)}, u32[]{:S(2)}, u32[]{:S(2)}) collective-permute-start(bf16[36,32,128]{2,1,0:T(8,128)(2,1)S(1)} %get-tuple-element.71.refs_7_), channel_id=1, source_target_pairs={{0,6},{1,3},{2,4},{3,1},{4,2},{5,7},{6,0},{7,5},{8,14},{9,11},{10,... | collective-permute-start | bytes 884744 | tf_op jit(solution)/shard_map/ppermute | solution.py:28
  46.6 11.1 %copy-start.6 = (s32[1,96]{1,0:T(1,128)S(1)}, s32[1,96]{1,0:T(1,128)}, u32[]{:S(2)}) copy-start(s32[1,96]{1,0:T(1,128)} %parents.1) | copy-start | bytes 1156
  46.6 11.1 %copy-start.8 = (s32[256]{0:T(256)S(1)}, s32[256]{0:T(256)}, u32[]{:S(2)}) copy-start(s32[256]{0:T(256)} %constant.21.clone.table) | copy-start | bytes 3076
  46.7 7.9 %collective-permute-start.7 = (bf16[48,32,128]{2,1,0:T(8,128)(2,1)S(1)}, bf16[48,32,128]{2,1,0:T(8,128)(2,1)S(1)}, u32[]{:S(2)}, u32[]{:S(2)}) collective-permute-start(bf16[48,32,128]{2,1,0:T(8,128)(2,1)S(1)} %get-tuple-element.76.refs_6_), channel_id=1, source_target_pairs={{0,32},{1,97},{2,34},{3,99},{4,36},{5,101},{6,38},{7,103},{8,40},{... | collective-permute-start | bytes 1179656 | tf_op jit(solution)/shard_map/ppermute | solution.py:28
  54.6 3.1 %collective-permute-start.8 = (bf16[64,32,128]{2,1,0:T(8,128)(2,1)S(1)}, bf16[64,32,128]{2,1,0:T(8,128)(2,1)S(1)}, u32[]{:S(2)}, u32[]{:S(2)}) collective-permute-start(bf16[64,32,128]{2,1,0:T(8,128)(2,1)S(1)} %get-tuple-element.81.own), channel_id=1, source_target_pairs={{0,1},{1,0},{2,3},{3,2},{4,5},{5,4},{6,7},{7,6},{8,9},{9,8},{10,11... | collective-permute-start | bytes 1572872 | tf_op jit(solution)/shard_map/ppermute | solution.py:32
  54.7 6.6 %collective-permute-start.9 = (bf16[18,32,128]{2,1,0:T(8,128)(2,1)S(1)}, bf16[18,32,128]{2,1,0:T(8,128)(2,1)S(1)}, u32[]{:S(2)}, u32[]{:S(2)}) collective-permute-start(bf16[18,32,128]{2,1,0:T(8,128)(2,1)S(1)} %get-tuple-element.82._), channel_id=1, source_target_pairs={{0,96},{1,33},{2,98},{3,35},{4,100},{5,37},{6,102},{7,39},{8,104},... | collective-permute-start | bytes 442376 | tf_op jit(solution)/shard_map/ppermute | solution.py:28
  61.3 1.2 %copy-start.1 = (f32[32,64,128]{2,1,0:T(8,128)S(1)}, f32[32,64,128]{2,1,0:T(8,128)}, u32[]{:S(2)}) copy-start(f32[32,64,128]{2,1,0:T(8,128)} %transfer.1) | copy-start | bytes 3145732
  61.3 1.4 %copy-start.2 = (bf16[32,64,128]{2,1,0:T(8,128)(2,1)S(1)}, bf16[32,64,128]{2,1,0:T(8,128)(2,1)}, u32[]{:S(2)}) copy-start(bf16[32,64,128]{2,1,0:T(8,128)(2,1)} %basis.1) | copy-start | bytes 1572868
  61.3 1.7 %copy-start.3 = (f32[4,4,128,128]{3,2,1,0:T(8,128)S(1)}, f32[4,4,128,128]{3,2,1,0:T(8,128)}, u32[]{:S(2)}) copy-start(f32[4,4,128,128]{3,2,1,0:T(8,128)} %apex.1) | copy-start | bytes 3145732
  61.3 1.7 %copy-start.4 = (f32[1,128,128]{2,1,0:T(8,128)S(1)}, f32[1,128,128]{2,1,0:T(8,128)}, u32[]{:S(2)}) copy-start(f32[1,128,128]{2,1,0:T(8,128)} %lift.1) | copy-start | bytes 196612
  61.3 1.7 %copy-start.7 = (s32[32]{0:T(128)S(1)}, s32[32]{0:T(128)}, u32[]{:S(2)}) copy-start(s32[32]{0:T(128)} %points.1) | copy-start | bytes 388

commit v6 on v5

--- a/solution.py
+++ b/solution.py
@@ -15,6 +15,7 @@
 F32 = jnp.float32
 
 Z, Y, X = 1, 3, 5
+CORE_1 = {Y: Z, Z: Y, X: X}
 STEPS = ((Y, 0), (Y, 1), (Z, 0), (Z, 1), (X, 0), (X, 1))
 GATHER_STEPS = (STEPS[5], *STEPS[:5])
 
@@ -24,7 +25,7 @@
     route = []
     for i in range(lax.axis_size(AXES)):
         pairing = 1 if (i & 1) == turn else 3
-        route.append((i, i ^ (pairing << axis)))
+        route.append((i, i ^ (pairing << (CORE_1[axis] if i & 1 else axis))))
     return lax.ppermute(block, AXES, route)
 
 
@@ -45,6 +46,7 @@
             for difference in range(devices):
                 other = difference & 1
                 for place, (axis, turn) in enumerate(order):
+                    axis = CORE_1[axis] if core ^ other else axis
                     low, high = (difference >> axis) & 1, (difference >> (axis + 1)) & 1
                     by_one = turn == core ^ other
                     slots[core, difference] |= (low ^ high if by_one else high) << place
@@ -101,15 +103,16 @@
 
 def moved(place, axis, held, at_first, at_second):
     me = place[0]
+    core_0 = (me & 1) == 0
     y, z = (me >> Y) & 3, (me >> Z) & 3
-    last = 3 * (1 - (me & 1))
-    if axis == Z:
-        moves = z >= 0
-    elif axis == Y:
-        moves = z == last
+    if axis == Y:
+        moves = ~core_0 | (z == 3)
+    elif axis == Z:
+        moves = core_0 | (z == 3)
     else:
-        moves = (y == 3 - last) & (z == 3 - last)
-    odd = ((me >> axis) & 1) == 1
+        end = jnp.where(core_0, 0, 3)
+        moves = (y == end) & (z == end)
+    odd = ((me >> jnp.where(core_0, axis, CORE_1[axis])) & 1) == 1
     return jnp.where(moves, jnp.where(odd, at_first, at_second), held)
 
 
@@ -354,17 +357,8 @@
     back[...] = pair[pl.ds(2 * HW + HW * core, HW)].astype(F32)
 
 
-def edge_chain_kernel(place, columns, first, held, before, came, blocks, _, out, back, halo):
-    core = place[0] & 1
-    value = moved(
-        place, X, held[...], before[before.shape[0] - 2 * HW :], came[came.shape[0] - 2 * HW :]
-    )
-    halo[...] = value[:HW]
-    edge(core == 0, columns, first, halo, blocks, out)
-    back[...] = value[HW:].astype(F32)
-
-
-def forward_kernel(place, count, parents, table, own, other, coupling, _, out, all_of):
+def forward_kernel(place, count, parents, table, own, other, coupling, *rest):
+    out, all_of = rest[-2:]
     far_slots = coupling.shape[1]
     half = all_of.shape[0] // 2
     all_of[:half] = own[:half]
@@ -386,8 +380,10 @@
 
 
 def down_kernel(
+    place,
     points,
-    place,
+    columns,
+    first,
     far_right,
     partial,
     sums,
@@ -400,70 +396,73 @@
     near_back,
     pair_out,
     pair_back,
-    chain_out,
-    chain_back,
+    held,
+    before,
+    blocks,
+    product_hbm,
+    adjoint_hbm,
     product,
     adjoint,
-    hats,
+    halo,
+    chain_out,
+    done,
 ):
-    step = pl.program_id(0)
-    per = basis.shape[0]
     clusters, rhs = near_out.shape[:2]
-
-    @pl.when(step == 0)
-    def _():
-        core = place[0] & 1
-        slab = place[0] >> X
-        got = came[2:6].astype(F32) + came[6:10].astype(F32)
-        slabs = [sums[2], sums[3], got[0], got[1], got[2], got[3]]
-        top_right = jnp.zeros((rhs, B), F32)
-        top_left = jnp.zeros((rhs, B), F32)
-        for t, mask in enumerate((1 + 2 * core, 3 - 2 * core, 2)):
-            top_right = top_right + dot3(slabs[2 * t], apex[slab, slab ^ mask], NT)
-            top_left = top_left + dot3(slabs[2 * t + 1], apex[slab ^ mask, slab], NN)
-        far_left = partial[0] + (came[0].astype(F32) + came[1].astype(F32))
-        hats[...] = stacked(
-            jnp.concatenate([far_right[...], far_left], axis=0)
-            + dot3(jnp.concatenate([top_right, top_left], axis=0), lift[0], NT)
-        )
-
-    for g in range(0, per, 2):
-        c = step * per + g
-        high, low = two(jnp.concatenate([transfer[g], transfer[g + 1]], axis=0))
-        down = both(dot(hats[...], jnp.concatenate([high, low], axis=1), NT))
-        high, low = two(down)
-        two_bases = diagonal(basis[g], basis[g + 1])
-        far = dot(
-            jnp.concatenate([high, low], axis=1),
-            jnp.concatenate([two_bases, two_bases], axis=0),
-            NN,
-        )
-        mask = pair_mask(points, c, rhs)
-        columns = slice(g * B, (g + 2) * B)
-        near = jnp.concatenate([near_out[c], near_out[c + 1]], axis=1)
-        back = jnp.concatenate([near_back[HW + c], near_back[HW + c + 1]], axis=1)
-        product[:, columns] = jnp.where(mask, near + far[:rhs], 0.0)
-        adjoint[:, columns] = jnp.where(mask, back + far[rhs:], 0.0)
-
-    def add_edge(c, low):
-        mask = lax.broadcasted_iota(jnp.int32, (rhs, B), 1) < points[c]
-        columns = slice((c % per) * B, (c % per + 1) * B)
-        g = c % HW
-        in_chip = (place[0] & 1) == (1 if low else 0)
-        out = jnp.where(in_chip, pair_out[g], chain_out[g])
-        back = jnp.where(in_chip, pair_back[g], chain_back[g])
-        product[:, columns] += jnp.where(mask, out, 0.0)
-        adjoint[:, columns] += jnp.where(mask, back, 0.0)
-
-    @pl.when(step == 0)
-    def _():
-        for c in range(HW):
-            add_edge(c, True)
-
-    @pl.when(step == pl.num_programs(0) - 1)
-    def _():
-        for c in range(clusters - HW, clusters):
-            add_edge(c, False)
+    core = place[0] & 1
+    slab = place[0] >> X
+    got = came[2:6].astype(F32) + came[6:10].astype(F32)
+    slabs = [sums[2], sums[3], got[0], got[1], got[2], got[3]]
+    top_right = jnp.zeros((rhs, B), F32)
+    top_left = jnp.zeros((rhs, B), F32)
+    for t, mask in enumerate((1 + 2 * core, 3 - 2 * core, 2)):
+        top_right = top_right + dot3(slabs[2 * t], apex[slab, slab ^ mask], NT)
+        top_left = top_left + dot3(slabs[2 * t + 1], apex[slab ^ mask, slab], NN)
+    far_left = partial[0] + (came[0].astype(F32) + came[1].astype(F32))
+    hats = stacked(
+        jnp.concatenate([far_right[...], far_left], axis=0)
+        + dot3(jnp.concatenate([top_right, top_left], axis=0), lift[0], NT)
+    )
+
+    message = moved(
+        place, X, held[...], before[before.shape[0] - 2 * HW :], came[came.shape[0] - 2 * HW :]
+    )
+    halo[...] = message[:HW]
+    chain_back = message[HW:].astype(F32)
+    edge(core == 0, columns, first, halo, blocks, chain_out)
+
+    pieces = done.shape[0] // 2
+    per = clusters // pieces
+    copies = []
+    for j in range(pieces):
+        for c in range(j * per, (j + 1) * per, 2):
+            high, low = two(jnp.concatenate([transfer[c], transfer[c + 1]], axis=0))
+            down = both(dot(hats, jnp.concatenate([high, low], axis=1), NT))
+            high, low = two(down)
+            two_bases = diagonal(basis[c], basis[c + 1])
+            far = dot(
+                jnp.concatenate([high, low], axis=1),
+                jnp.concatenate([two_bases, two_bases], axis=0),
+                NN,
+            )
+            for q in range(2):
+                k, g = c + q, (c + q) % HW
+                out, back = near_out[k], near_back[HW + k]
+                if k < HW or k >= clusters - HW:
+                    in_chip = core == (1 if k < HW else 0)
+                    out = out + jnp.where(in_chip, pair_out[g], chain_out[g])
+                    back = back + jnp.where(in_chip, pair_back[g], chain_back[g])
+                mask = lax.broadcasted_iota(jnp.int32, (rhs, B), 1) < points[k]
+                lanes = slice(q * B, (q + 1) * B)
+                place_of = slice(k * B, (k + 1) * B)
+                product[:, place_of] = jnp.where(mask, out + far[:rhs, lanes], 0.0)
+                adjoint[:, place_of] = jnp.where(mask, back + far[rhs:, lanes], 0.0)
+        index = (slice(None), pl.ds(j * per * B, per * B))
+        for q, (source, target) in enumerate(((product, product_hbm), (adjoint, adjoint_hbm))):
+            copy = pltpu.make_async_copy(source.at[index], target.at[index], done.at[2 * j + q])
+            copy.start()
+            copies.append(copy)
+    for copy in copies:
+        copy.wait()
 
 
 SMEM = pl.BlockSpec(memory_space=pltpu.SMEM)
@@ -514,7 +513,6 @@
 ):
     rhs = right_sides.shape[0]
     clusters = near_blocks.shape[0]
-    rank = leaf_basis.shape[1]
     me = lax.axis_index(AXES)
     devices = lax.axis_size(AXES)
     block = (rhs, B)
@@ -642,7 +640,7 @@
         forward_kernel,
         "forward",
         (),
-        [SMEM] * 4 + [VMEM] * 3 + [ANY],
+        [SMEM] * 4 + [VMEM] * 7 + [ANY],
         [(VMEM, block, F32)],
         (
             place,
@@ -652,48 +650,27 @@
             gathered,
             gathered_other,
             coupling,
+            apex_coupling,
+            slab_transfer,
+            transfer,
+            leaf_basis,
             payload,
         ),
         us=2.5,
         scratch=[pltpu.VMEM((devices, *block), BF)],
     )
-    chain_out, chain_back = call(
-        edge_chain_kernel,
-        "edge_chain",
-        (),
-        [SMEM] * 3 + [VMEM] * 4 + [ANY],
-        [rows(HW, F32)] * 2,
-        (place, columns, first, halo, before, came, near_blocks, far_right),
-        us=0.8,
-        scratch=[pltpu.VMEM((HW, *block), BF)],
-    )
-
-    per = 16
-    sides = pl.BlockSpec((rhs, per * B), lambda i: (0, i))
-    bases = pl.BlockSpec((per, rank, B), lambda i: (i, 0, 0))
+    wide = (rhs, clusters * B)
     return call(
         down_kernel,
         "down",
-        (clusters // per,),
-        [
-            SMEM,
-            SMEM,
-            whole(*block),
-            whole(1, *block),
-            whole(4, *block),
-            whole(*came.shape),
-            whole(*apex_coupling.shape),
-            whole(1, B, B),
-            bases,
-            bases,
-            whole(*all_clusters),
-            whole(clusters + 2 * HW, *block),
-            *[whole(HW, *block)] * 4,
-        ],
-        [(sides, (rhs, clusters * B), F32)] * 2,
+        (),
+        [SMEM] * 4 + [VMEM] * 15,
+        [(HBM, wide, F32)] * 2,
         (
+            place,
             cluster_points,
-            place,
+            columns,
+            first,
             far_right,
             partial,
             sums,
@@ -706,11 +683,18 @@
             near_back,
             pair_out,
             pair_back,
-            chain_out,
-            chain_back,
+            halo,
+            before,
+            near_blocks,
         ),
         us=4,
-        scratch=[pltpu.VMEM((4 * rhs, 2 * B), BF)],
+        scratch=[
+            pltpu.VMEM(wide, F32),
+            pltpu.VMEM(wide, F32),
+            pltpu.VMEM((HW, *block), BF),
+            pltpu.VMEM((HW, *block), F32),
+            pltpu.SemaphoreType.DMA((8,)),
+        ],
     )
 
 

time: 66.2 us -> 63.2 us (0.955)
  waiting for transfers between devices: 27.5 us -> 25.8 us
  Pallas kernels: 18.7 us -> 17.4 us
    ppermute x7, waiting for transfers between devices: 27.5 us -> 25.8 us  [routed(): return lax.ppermute(block, AXES, route)]
    pallas_call x13 -> x12, Pallas kernels: 18.7 us -> 17.4 us  [call(): pl.pallas_call(kernel, grid=grid, out_shape=tuple((shape(dims, kind) for...]
where the time goes in v6:
time: 63.2 us; the launch traced here: 63.1 us
  waiting for transfers between devices  25.8 us (41%)
  starting transfers between devices  18.1 us (29%)
  Pallas kernels  17.4 us (28%)
  between operations  1.62 us (3%)
    ppermute x7, waiting for transfers between devices, routed(): return lax.ppermute(block, AXES, route)  25.8 us
    ppermute x7, starting transfers between devices, routed(): return lax.ppermute(block, AXES, route)  17.5 us
    pallas_call x12, Pallas kernels, call(): pl.pallas_call(kernel, grid=grid, out_shape=tuple((shape(dims, kind) for...  17.4 us
  transfers between devices with their start and end apart: 10, of which 7 were waited for; matrix products, arithmetic and copies ran while one was open for 0% of the time, Pallas kernels for 13%

profile of v6, /device:TPU:0, one launch (start us, length us, event | category | flops | bytes accessed | tf_op | source)
XLA Modules:
  0.0 63.1 jit_solution(4680990525197345266)
XLA Ops:
  1.3 0.0 copy-start
  1.3 0.0 copy-start.5
  1.3 5.6 %rise.1 = (bf16[32,32,128]{2,1,0:T(8,128)(2,1)S(1)}, bf16[32,32,128]{2,1,0:T(8,128)(2,1)S(1)}, bf16[1,32,128]{2,1,0:T(8,128)(2,1)S(1)}, f32[65,32,128]{2,1,0:T(8...) custom-call(s32[1]{0:T(128)} %bitcast.place.refs_0_, s32[1]{0:T(128)S(6)} %copy.16.count, s32[32]{0:T(128)} %points.1, ...), custom_call_target="tpu_custom_call" | custom-call | flops 1000 | bytes 18000000 | tf_op jit(solution)/shard_map/rise/pallas_call | solution.py:484
  6.9 0.1 collective-permute-start
  7.0 0.2 copy-done
  7.2 0.0 copy-done.5
  7.2 1.1 %near_outer.1 = (f32[40,32,128]{2,1,0:T(8,128)S(1)}, bf16[16,32,128]{2,1,0:T(8,128)(2,1)S(1)}) custom-call(s32[8,32]{1,0:T(8,128)S(1)} %bitcast.4, s32[1]{0:T(128)S(6)} %sub.3.first, bf16[32,32,128]{2,1,0:T(8,128)(2,1)S(1)} %get-tuple-element.48.mright, bf16[32,32,128]{2,1,0:T(8,128)(2,1)S(1)} %get-tuple-element.49.mleft, bf16[32,8,128,128]{3,2,1,0:T(8,128)(2,1)S(1)} %copy-done), custom_call_target="tpu_custom_call" | custom-call | flops 1000 | bytes 3600000 | tf_op jit(solution)/shard_map/near_outer/pallas_call | solution.py:484
  8.3 0.4 collective-permute-start.2
  8.7 2.8 %collective-permute-start.1 = (bf16[1,32,128]{2,1,0:T(8,128)(2,1)S(1)}, bf16[1,32,128]{2,1,0:T(8,128)(2,1)S(1)}, u32[]{:S(2)}, u32[]{:S(2)}) collective-permute-start(bf16[1,32,128]{2,1,0:T(8,128)(2,1)S(1)} %get-tuple-element.47.refs_4_), channel_id=1, source_target_pairs={{0,96},{1,33},{2,98},{3,35},{4,100},{5,37},{6,102},{7,39},{8,104},... | collective-permute-start | bytes 24584 | tf_op jit(solution)/shard_map/ppermute | solution.py:29
  11.5 2.0 %collective-permute-done.1.refs_5_ = bf16[1,32,128]{2,1,0:T(8,128)(2,1)S(1)} collective-permute-done((bf16[1,32,128]{2,1,0:T(8,128)(2,1)S(1)}, bf16[1,32,128]{2,1,0:T(8,128)(2,1)S(1)}, u32[]{:S(2)}, u32[]{:S(2)}) %collective-permute-start.1) | collective-permute-done | bytes 8224 | tf_op jit(solution)/shard_map/ppermute | solution.py:29
  13.5 0.0 collective-permute-done.2.refs_6_.pair
  13.6 0.0 collective-permute-done.refs_1_
  13.6 0.1 fold.6
  13.7 1.7 %collective-permute-start.3 = (bf16[46,32,128]{2,1,0:T(8,128)(2,1)S(1)}, bf16[46,32,128]{2,1,0:T(8,128)(2,1)S(1)}, u32[]{:S(2)}, u32[]{:S(2)}) collective-permute-start(bf16[46,32,128]{2,1,0:T(8,128)(2,1)S(1)} %get-tuple-element.52._), channel_id=1, source_target_pairs={{0,8},{1,7},{2,10},{3,5},{4,12},{5,3},{6,14},{7,1},{8,0},{9,15},{1... | collective-permute-start | bytes 1130504 | tf_op jit(solution)/shard_map/ppermute | solution.py:29
  15.4 3.9 %near.1 = (f32[32,32,128]{2,1,0:T(8,128)S(1)}, f32[40,32,128]{2,1,0:T(8,128)S(1)}) custom-call(s32[8,32]{1,0:T(8,128)S(1)} %bitcast.5, s32[1]{0:T(128)S(6)} %sub.3.first, bf16[32,32,128]{2,1,0:T(8,128)(2,1)S(1)} %get-tuple-element.48.mright, bf16[32,32,128]{2,1,0:T(8,128)(2,1)S(1)} %get-tuple-element.49.mleft, bf16[32,8,128,128]{3,2,1,0:T(8,128)(2,1)S(1)} %copy-done, ...), custom_call_target="tpu_custom_call" | custom-call | flops 1000 | bytes 14400000 | tf_op jit(solution)/shard_map/near/pallas_call | solution.py:484
  19.3 2.1 %collective-permute-done.3.refs_1_.refs_6_ = bf16[46,32,128]{2,1,0:T(8,128)(2,1)S(1)} collective-permute-done((bf16[46,32,128]{2,1,0:T(8,128)(2,1)S(1)}, bf16[46,32,128]{2,1,0:T(8,128)(2,1)S(1)}, u32[]{:S(2)}, u32[]{:S(2)}) %collective-permute-start.3) | collective-permute-done | bytes 376864 | tf_op jit(solution)/shard_map/ppermute | solution.py:29
  21.4 0.1 fold.7
  21.5 0.0 slice-start.1
  21.5 3.2 %collective-permute-start.4 = (bf16[32,32,128]{2,1,0:T(8,128)(2,1)S(1)}, bf16[32,32,128]{2,1,0:T(8,128)(2,1)S(1)}, u32[]{:S(2)}, u32[]{:S(2)}) collective-permute-start(bf16[32,32,128]{2,1,0:T(8,128)(2,1)S(1)} %get-tuple-element.58._), channel_id=1, source_target_pairs={{0,24},{1,3},{2,26},{3,1},{4,28},{5,7},{6,30},{7,5},{8,16},{9,11},... | collective-permute-start | bytes 786440 | tf_op jit(solution)/shard_map/ppermute | solution.py:29
  24.6 1.1 %edge_pair.1 = (f32[4,32,128]{2,1,0:T(8,128)S(1)}, f32[4,32,128]{2,1,0:T(8,128)S(1)}) custom-call(s32[1]{0:T(128)} %bitcast.place.refs_0_, s32[8,32]{1,0:T(8,128)S(1)} %bitcast.6, s32[1]{0:T(128)S(6)} %sub.3.first, bf16[16,32,128]{2,1,0:T(8,128)(2,1)S(1)} %collective-permute-done.2.refs_6_.pair, bf16[32,8,128,128]{3,2,1,0:T(8,128)(2,1)S(1)} %copy-done, ...), custom_call_target="tpu_custom_call" | custom-call | flops 1000 | bytes 2880000 | tf_op jit(solution)/shard_map/edge_pair/pallas_call | solution.py:484
  25.7 3.4 %collective-permute-done.4.refs_1_ = bf16[32,32,128]{2,1,0:T(8,128)(2,1)S(1)} collective-permute-done((bf16[32,32,128]{2,1,0:T(8,128)(2,1)S(1)}, bf16[32,32,128]{2,1,0:T(8,128)(2,1)S(1)}, u32[]{:S(2)}, u32[]{:S(2)}) %collective-permute-start.4) | collective-permute-done | bytes 262176 | tf_op jit(solution)/shard_map/ppermute | solution.py:29
  29.1 0.1 fold.8
  29.2 3.0 %collective-permute-start.5 = (bf16[36,32,128]{2,1,0:T(8,128)(2,1)S(1)}, bf16[36,32,128]{2,1,0:T(8,128)(2,1)S(1)}, u32[]{:S(2)}, u32[]{:S(2)}) collective-permute-start(bf16[36,32,128]{2,1,0:T(8,128)(2,1)S(1)} %get-tuple-element.64.refs_6_), channel_id=1, source_target_pairs={{0,2},{1,25},{2,0},{3,27},{4,6},{5,29},{6,4},{7,31},{8,10},{9,17},... | collective-permute-start | bytes 884744 | tf_op jit(solution)/shard_map/ppermute | solution.py:29
  32.2 4.7 %collective-permute-done.5.refs_1_.refs_6_ = bf16[36,32,128]{2,1,0:T(8,128)(2,1)S(1)} collective-permute-done((bf16[36,32,128]{2,1,0:T(8,128)(2,1)S(1)}, bf16[36,32,128]{2,1,0:T(8,128)(2,1)S(1)}, u32[]{:S(2)}, u32[]{:S(2)}) %collective-permute-start.5) | collective-permute-done | bytes 294944 | tf_op jit(solution)/shard_map/ppermute | solution.py:29
  36.9 0.1 fold.9
  37.0 3.7 %collective-permute-start.6 = (bf16[36,32,128]{2,1,0:T(8,128)(2,1)S(1)}, bf16[36,32,128]{2,1,0:T(8,128)(2,1)S(1)}, u32[]{:S(2)}, u32[]{:S(2)}) collective-permute-start(bf16[36,32,128]{2,1,0:T(8,128)(2,1)S(1)} %get-tuple-element.69.refs_7_), channel_id=1, source_target_pairs={{0,6},{1,9},{2,4},{3,11},{4,2},{5,13},{6,0},{7,15},{8,14},{9,1},{1... | collective-permute-start | bytes 884744 | tf_op jit(solution)/shard_map/ppermute | solution.py:29
  40.6 4.7 %collective-permute-done.6.refs_1_ = bf16[36,32,128]{2,1,0:T(8,128)(2,1)S(1)} collective-permute-done((bf16[36,32,128]{2,1,0:T(8,128)(2,1)S(1)}, bf16[36,32,128]{2,1,0:T(8,128)(2,1)S(1)}, u32[]{:S(2)}, u32[]{:S(2)}) %collective-permute-start.6) | collective-permute-done | bytes 294944 | tf_op jit(solution)/shard_map/ppermute | solution.py:29
  45.4 0.0 copy-start.8
  45.4 0.1 fold.10
  45.5 0.1 collective-permute-start.7
  45.6 7.8 %collective-permute-done.7.refs_1_.before = bf16[48,32,128]{2,1,0:T(8,128)(2,1)S(1)} collective-permute-done((bf16[48,32,128]{2,1,0:T(8,128)(2,1)S(1)}, bf16[48,32,128]{2,1,0:T(8,128)(2,1)S(1)}, u32[]{:S(2)}, u32[]{:S(2)}) %collective-permute-start.7) | collective-permute-done | bytes 393248 | tf_op jit(solution)/shard_map/ppermute | solution.py:29
  53.3 0.1 fold.11
  53.4 0.1 collective-permute-start.8
  53.5 0.0 copy-start.7
  53.5 3.0 %collective-permute-start.9 = (bf16[18,32,128]{2,1,0:T(8,128)(2,1)S(1)}, bf16[18,32,128]{2,1,0:T(8,128)(2,1)S(1)}, u32[]{:S(2)}, u32[]{:S(2)}) collective-permute-start(bf16[18,32,128]{2,1,0:T(8,128)(2,1)S(1)} %get-tuple-element.80.rest_4_), channel_id=1, source_target_pairs={{0,96},{1,33},{2,98},{3,35},{4,100},{5,37},{6,102},{7,39},{8,104},... | collective-permute-start | bytes 442376 | tf_op jit(solution)/shard_map/ppermute | solution.py:29
  56.5 0.0 collective-permute-done.8.other
  56.5 0.0 slice-done
  56.5 0.0 slice-done.1
  56.5 0.0 copy-done.3
  56.5 0.0 copy-done.1
  56.5 0.0 copy-done.2
  56.6 0.0 copy-done.4
  56.6 0.0 copy-done.6
  56.6 0.0 copy-done.8
  56.6 2.4 %forward.1.far_right = f32[32,128]{1,0:T(8,128)S(1)} custom-call(s32[1]{0:T(128)} %bitcast.place.refs_0_, s32[1]{0:T(128)S(6)} %copy.16.count, s32[1,96]{1,0:T(1,128)S(1)} %copy-done.6, s32[256]{0:T(256)S(1)} %copy-done.8, bf16[64,32,128]{2,1,0:T(8,128)(2,1)S(1)} %get-tuple-element.79.own, bf16[64,32,128]{2,1,0:T(8,128)(2,1)S(1)} %collective-permute-done.8.other, ...), custom_call_target="tpu_custom_call" | custom-call | flops 1000 | bytes 9000000 | tf_op jit(solution)/shard_map/forward/pallas_call | solution.py:484
  59.0 1.1 %collective-permute-done.9.came = bf16[18,32,128]{2,1,0:T(8,128)(2,1)S(1)} collective-permute-done((bf16[18,32,128]{2,1,0:T(8,128)(2,1)S(1)}, bf16[18,32,128]{2,1,0:T(8,128)(2,1)S(1)}, u32[]{:S(2)}, u32[]{:S(2)}) %collective-permute-start.9) | collective-permute-done | bytes 147488 | tf_op jit(solution)/shard_map/ppermute | solution.py:29
  60.1 0.0 copy-done.7
  60.1 2.8 %down.1 = (f32[32,4096]{1,0:T(8,128)}, f32[32,4096]{1,0:T(8,128)}) custom-call(s32[1]{0:T(128)} %bitcast.place.refs_0_, s32[32]{0:T(128)S(1)} %copy-done.7, s32[8,32]{1,0:T(8,128)S(1)} %bitcast.7, s32[1]{0:T(128)S(6)} %sub.3.first, f32[32,128]{1,0:T(8,128)S(1)} %forward.1.far_right, f32[1,32,128]{2,1,0:T(8,128)S(1)} %get-tuple-element.81.partial, ...), custom_call_target="tpu_custom_call" | custom-call | flops 1000 | bytes 14400000 | tf_op jit(solution)/shard_map/down/pallas_call | solution.py:484
  (7 shorter events, 0.0 us)
Async XLA Ops:
  1.3 5.9 %copy-start = (bf16[32,8,128,128]{3,2,1,0:T(8,128)(2,1)S(1)}, bf16[32,8,128,128]{3,2,1,0:T(8,128)(2,1)}, u32[]{:S(2)}) copy-start(bf16[32,8,128,128]{3,2,1,0:T(8,128)(2,1)} %blocks.7) | copy-start | bytes 25165828
  1.3 5.9 %copy-start.5 = (s32[32,8]{0,1:T(8,128)S(1)}, s32[32,8]{0,1:T(8,128)}, u32[]{:S(2)}) copy-start(s32[32,8]{0,1:T(8,128)} %param.17) | copy-start | bytes 3076
  6.9 6.6 %collective-permute-start = (f32[67,32,128]{2,1,0:T(8,128)S(1)}, f32[67,32,128]{2,1,0:T(8,128)S(1)}, u32[]{:S(2)}, u32[]{:S(2)}) collective-permute-start(f32[67,32,128]{2,1,0:T(8,128)S(1)} %get-tuple-element.44), channel_id=1, source_target_pairs={{0,1},{1,0},{2,3},{3,2},{4,5},{5,4},{6,7},{7,6},{8,9},{9,8},{10,11... | collective-permute-start | bytes 3293192 | tf_op jit(solution)/shard_map/ppermute | solution.py:33
  8.3 5.3 %collective-permute-start.2 = (bf16[16,32,128]{2,1,0:T(8,128)(2,1)S(1)}, bf16[16,32,128]{2,1,0:T(8,128)(2,1)S(1)}, u32[]{:S(2)}, u32[]{:S(2)}) collective-permute-start(bf16[16,32,128]{2,1,0:T(8,128)(2,1)S(1)} %get-tuple-element.50), channel_id=1, source_target_pairs={{0,1},{1,0},{2,3},{3,2},{4,5},{5,4},{6,7},{7,6},{8,9},{9,8},{10,11... | collective-permute-start | bytes 393224 | tf_op jit(solution)/shard_map/ppermute | solution.py:33
  8.7 4.9 %collective-permute-start.1 = (bf16[1,32,128]{2,1,0:T(8,128)(2,1)S(1)}, bf16[1,32,128]{2,1,0:T(8,128)(2,1)S(1)}, u32[]{:S(2)}, u32[]{:S(2)}) collective-permute-start(bf16[1,32,128]{2,1,0:T(8,128)(2,1)S(1)} %get-tuple-element.47.refs_4_), channel_id=1, source_target_pairs={{0,96},{1,33},{2,98},{3,35},{4,100},{5,37},{6,102},{7,39},{8,104},... | collective-permute-start | bytes 24584 | tf_op jit(solution)/shard_map/ppermute | solution.py:29
  13.7 7.7 %collective-permute-start.3 = (bf16[46,32,128]{2,1,0:T(8,128)(2,1)S(1)}, bf16[46,32,128]{2,1,0:T(8,128)(2,1)S(1)}, u32[]{:S(2)}, u32[]{:S(2)}) collective-permute-start(bf16[46,32,128]{2,1,0:T(8,128)(2,1)S(1)} %get-tuple-element.52._), channel_id=1, source_target_pairs={{0,8},{1,7},{2,10},{3,5},{4,12},{5,3},{6,14},{7,1},{8,0},{9,15},{1... | collective-permute-start | bytes 1130504 | tf_op jit(solution)/shard_map/ppermute | solution.py:29
  21.4 35.2 %slice-start = ((s8[6291456]{0:T(1024)(128)(4,1)}), s8[4194304]{0:T(1024)(128)(4,1)S(1)}, s32[]{:S(2)}) async-start(s8[6291456]{0:T(1024)(128)(4,1)} %bitcast.2), calls=%async_computation | async-start | bytes 8388608
  21.5 35.1 %slice-start.1 = ((s8[6291456]{0:T(1024)(128)(4,1)}), s8[2097152]{0:T(1024)(128)(4,1)S(1)}, s32[]{:S(2)}) async-start(s8[6291456]{0:T(1024)(128)(4,1)} %bitcast.2), calls=%async_computation.1 | async-start | bytes 4194304
  21.5 7.7 %collective-permute-start.4 = (bf16[32,32,128]{2,1,0:T(8,128)(2,1)S(1)}, bf16[32,32,128]{2,1,0:T(8,128)(2,1)S(1)}, u32[]{:S(2)}, u32[]{:S(2)}) collective-permute-start(bf16[32,32,128]{2,1,0:T(8,128)(2,1)S(1)} %get-tuple-element.58._), channel_id=1, source_target_pairs={{0,24},{1,3},{2,26},{3,1},{4,28},{5,7},{6,30},{7,5},{8,16},{9,11},... | collective-permute-start | bytes 786440 | tf_op jit(solution)/shard_map/ppermute | solution.py:29
  29.2 7.7 %collective-permute-start.5 = (bf16[36,32,128]{2,1,0:T(8,128)(2,1)S(1)}, bf16[36,32,128]{2,1,0:T(8,128)(2,1)S(1)}, u32[]{:S(2)}, u32[]{:S(2)}) collective-permute-start(bf16[36,32,128]{2,1,0:T(8,128)(2,1)S(1)} %get-tuple-element.64.refs_6_), channel_id=1, source_target_pairs={{0,2},{1,25},{2,0},{3,27},{4,6},{5,29},{6,4},{7,31},{8,10},{9,17},... | collective-permute-start | bytes 884744 | tf_op jit(solution)/shard_map/ppermute | solution.py:29
  36.9 19.6 %copy-start.3 = (f32[4,4,128,128]{3,2,1,0:T(8,128)S(1)}, f32[4,4,128,128]{3,2,1,0:T(8,128)}, u32[]{:S(2)}) copy-start(f32[4,4,128,128]{3,2,1,0:T(8,128)} %apex.1) | copy-start | bytes 3145732
  37.0 8.4 %collective-permute-start.6 = (bf16[36,32,128]{2,1,0:T(8,128)(2,1)S(1)}, bf16[36,32,128]{2,1,0:T(8,128)(2,1)S(1)}, u32[]{:S(2)}, u32[]{:S(2)}) collective-permute-start(bf16[36,32,128]{2,1,0:T(8,128)(2,1)S(1)} %get-tuple-element.69.refs_7_), channel_id=1, source_target_pairs={{0,6},{1,9},{2,4},{3,11},{4,2},{5,13},{6,0},{7,15},{8,14},{9,1},{1... | collective-permute-start | bytes 884744 | tf_op jit(solution)/shard_map/ppermute | solution.py:29
  45.4 11.2 %copy-start.1 = (f32[32,64,128]{2,1,0:T(8,128)S(1)}, f32[32,64,128]{2,1,0:T(8,128)}, u32[]{:S(2)}) copy-start(f32[32,64,128]{2,1,0:T(8,128)} %transfer.1) | copy-start | bytes 3145732
  45.4 11.2 %copy-start.2 = (bf16[32,64,128]{2,1,0:T(8,128)(2,1)S(1)}, bf16[32,64,128]{2,1,0:T(8,128)(2,1)}, u32[]{:S(2)}) copy-start(bf16[32,64,128]{2,1,0:T(8,128)(2,1)} %basis.1) | copy-start | bytes 1572868
  45.4 11.2 %copy-start.4 = (f32[1,128,128]{2,1,0:T(8,128)S(1)}, f32[1,128,128]{2,1,0:T(8,128)}, u32[]{:S(2)}) copy-start(f32[1,128,128]{2,1,0:T(8,128)} %lift.1) | copy-start | bytes 196612
  45.4 11.2 %copy-start.6 = (s32[1,96]{1,0:T(1,128)S(1)}, s32[1,96]{1,0:T(1,128)}, u32[]{:S(2)}) copy-start(s32[1,96]{1,0:T(1,128)} %parents.1) | copy-start | bytes 1156
  45.4 11.2 %copy-start.8 = (s32[256]{0:T(256)S(1)}, s32[256]{0:T(256)}, u32[]{:S(2)}) copy-start(s32[256]{0:T(256)} %constant.21.clone.table) | copy-start | bytes 3076
  45.5 7.9 %collective-permute-start.7 = (bf16[48,32,128]{2,1,0:T(8,128)(2,1)S(1)}, bf16[48,32,128]{2,1,0:T(8,128)(2,1)S(1)}, u32[]{:S(2)}, u32[]{:S(2)}) collective-permute-start(bf16[48,32,128]{2,1,0:T(8,128)(2,1)S(1)} %get-tuple-element.74.refs_6_), channel_id=1, source_target_pairs={{0,32},{1,97},{2,34},{3,99},{4,36},{5,101},{6,38},{7,103},{8,40},{... | collective-permute-start | bytes 1179656 | tf_op jit(solution)/shard_map/ppermute | solution.py:29
  53.4 3.1 %collective-permute-start.8 = (bf16[64,32,128]{2,1,0:T(8,128)(2,1)S(1)}, bf16[64,32,128]{2,1,0:T(8,128)(2,1)S(1)}, u32[]{:S(2)}, u32[]{:S(2)}) collective-permute-start(bf16[64,32,128]{2,1,0:T(8,128)(2,1)S(1)} %get-tuple-element.79.own), channel_id=1, source_target_pairs={{0,1},{1,0},{2,3},{3,2},{4,5},{5,4},{6,7},{7,6},{8,9},{9,8},{10,11... | collective-permute-start | bytes 1572872 | tf_op jit(solution)/shard_map/ppermute | solution.py:33
  53.5 6.6 %copy-start.7 = (s32[32]{0:T(128)S(1)}, s32[32]{0:T(128)}, u32[]{:S(2)}) copy-start(s32[32]{0:T(128)} %points.1) | copy-start | bytes 388
  53.5 6.6 %collective-permute-start.9 = (bf16[18,32,128]{2,1,0:T(8,128)(2,1)S(1)}, bf16[18,32,128]{2,1,0:T(8,128)(2,1)S(1)}, u32[]{:S(2)}, u32[]{:S(2)}) collective-permute-start(bf16[18,32,128]{2,1,0:T(8,128)(2,1)S(1)} %get-tuple-element.80.rest_4_), channel_id=1, source_target_pairs={{0,96},{1,33},{2,98},{3,35},{4,100},{5,37},{6,102},{7,39},{8,104},... | collective-permute-start | bytes 442376 | tf_op jit(solution)/shard_map/ppermute | solution.py:29

commit v7 on v6

--- a/solution.py
+++ b/solution.py
@@ -17,7 +17,7 @@
 Z, Y, X = 1, 3, 5
 CORE_1 = {Y: Z, Z: Y, X: X}
 STEPS = ((Y, 0), (Y, 1), (Z, 0), (Z, 1), (X, 0), (X, 1))
-GATHER_STEPS = (STEPS[5], *STEPS[:5])
+GATHER_STEPS = (STEPS[4], *STEPS[:4], STEPS[5])
 
 
 def routed(block, step):
@@ -33,10 +33,10 @@
     return lax.ppermute(block, AXES, [(i, i ^ 1) for i in range(lax.axis_size(AXES))])
 
 
-def passed_along(block, distance):
+def to_other_chips(block):
     devices = range(lax.axis_size(AXES))
-    route = [(i - distance, i) for i in devices if i - distance in devices]
-    return lax.ppermute(block, AXES, route)
+    route = [(i, i + 2 - 4 * (i & 1)) for i in devices]
+    return lax.ppermute(block, AXES, [(i, j) for i, j in route if j in devices])
 
 
 def slot_tables(devices):
@@ -99,21 +99,6 @@
 def pair_mask(points, c, rows):
     lane = lax.broadcasted_iota(jnp.int32, (rows, 2 * B), 1)
     return lane < jnp.where(lane < B, points[c], B + points[c + 1])
-
-
-def moved(place, axis, held, at_first, at_second):
-    me = place[0]
-    core_0 = (me & 1) == 0
-    y, z = (me >> Y) & 3, (me >> Z) & 3
-    if axis == Y:
-        moves = ~core_0 | (z == 3)
-    elif axis == Z:
-        moves = core_0 | (z == 3)
-    else:
-        end = jnp.where(core_0, 0, 3)
-        moves = (y == end) & (z == end)
-    odd = ((me >> jnp.where(core_0, axis, CORE_1[axis])) & 1) == 1
-    return jnp.where(moves, jnp.where(odd, at_first, at_second), held)
 
 
 def rise_kernel(
@@ -241,53 +226,48 @@
         start = start + part.shape[0]
 
 
-def fold_kernel(step, *refs):
-    refs = list(refs)
-    place, came, partial, sums = refs[:4]
-    del refs[:4]
-    payload, keep, sums_next = refs[-5:-2]
-    gathered_next, halo_next = refs[-2:]
-    gathered = refs[0]
-    a = gathered.shape[0]
+def fold_kernel(step, place, came, partial, sums, *refs):
+    if step == 0:
+        gathered, came_own, pair, _, payload, keep, sums_next, gathered_next, halo = refs
+    elif step < 5:
+        gathered, _, payload, keep, sums_next, gathered_next = refs
+    else:
+        gathered, _, payload, keep, sums_next = refs
     n = 2 * keep.shape[0]
     m = sums.shape[0]
-    gathered_next[:a] = gathered[...]
     if step == 0:
-        came_own, pair = refs[1:3]
         total = partial[:n] + came[:n]
         got = came[n + 1 :]
-        gathered_next[a:] = came_own[...]
         other = HW * (1 - (place[0] & 1))
-        halo_next[:HW] = pair[pl.ds(other, HW)]
-        halo_next[HW:] = pair[pl.ds(2 * HW + other, HW)]
+        halo[:HW] = pair[pl.ds(other, HW)]
+        halo[HW:] = pair[pl.ds(2 * HW + other, HW)]
+        more = came_own[...]
     else:
-        halo = refs[1]
         total = partial[...] + came[:n].astype(F32)
         start = n
         if step >= 3:
             total = total + came[n : 2 * n].astype(F32)
             start = 2 * n
         got = came[start : start + m].astype(F32) + came[start + m : start + 2 * m].astype(F32)
-        start = start + 2 * m
-        gathered_next[a:] = came[start : start + a]
-        axis, turn = STEPS[step - 1]
-        if turn:
-            before = refs[2]
-            halo_next[...] = moved(
-                place, axis, halo[...], before[before.shape[0] - 2 * HW :], came[start + a :]
-            )
-        else:
-            halo_next[...] = halo[...]
+        more = came[start + 2 * m :] if step < 5 else None
     if sums_next.shape[0] == m:
         sums_next[...] = sums[...] + got
     else:
         sums_next[:m] = sums[...]
         sums_next[m:] = got
     keep[...] = total[: n // 2]
-    parts = [halo_next[...]]
     if step < 5:
-        parts = [gathered_next[...], *parts]
-    lay_out(payload, total[n // 2 :], step >= 2, sums_next[...], *parts)
+        a = gathered.shape[0]
+        gathered_next[:a] = gathered[...]
+        gathered_next[a:] = more
+    parts = [gathered if step == 5 else gathered_next] if step != 4 else []
+    lay_out(payload, total[n // 2 :], step >= 2, sums_next[...], *(part[...] for part in parts))
+
+
+def join_kernel(a, b, out):
+    n = a.shape[0]
+    out[:n] = a[...]
+    out[n:] = b[b.shape[0] - n :]
 
 
 def rows_of(blocks, c):
@@ -316,10 +296,13 @@
     sent[3 * HW :] = back[clusters + HW :].astype(BF)
 
 
-def near_kernel(columns, first, mright, mleft, blocks, back_outer, _, out, back):
+def near_kernel(
+    columns, first, mright, mleft, blocks, back_outer, halo, _, out, back, halo_on
+):
     clusters = mright.shape[0]
     slots = blocks.shape[1]
     back[...] = back_outer[...]
+    halo_on[...] = halo[...]
     for start in range(0, clusters, 4):
         group = range(start, start + 4)
         for c in group:
@@ -355,6 +338,11 @@
     halo[...] = pair[pl.ds(HW * core, HW)]
     edge(core == 1, columns, first, halo, blocks, out)
     back[...] = pair[pl.ds(2 * HW + HW * core, HW)].astype(F32)
+
+
+def edge_chain_kernel(place, columns, first, came, blocks, _, out, back):
+    edge((place[0] & 1) == 0, columns, first, came, blocks, out)
+    back[...] = came[HW:].astype(F32)
 
 
 def forward_kernel(place, count, parents, table, own, other, coupling, *rest):
@@ -382,8 +370,6 @@
 def down_kernel(
     place,
     points,
-    columns,
-    first,
     far_right,
     partial,
     sums,
@@ -396,15 +382,12 @@
     near_back,
     pair_out,
     pair_back,
-    held,
-    before,
-    blocks,
+    chain_out,
+    chain_back,
     product_hbm,
     adjoint_hbm,
     product,
     adjoint,
-    halo,
-    chain_out,
     done,
 ):
     clusters, rhs = near_out.shape[:2]
@@ -422,13 +405,6 @@
         jnp.concatenate([far_right[...], far_left], axis=0)
         + dot3(jnp.concatenate([top_right, top_left], axis=0), lift[0], NT)
     )
-
-    message = moved(
-        place, X, held[...], before[before.shape[0] - 2 * HW :], came[came.shape[0] - 2 * HW :]
-    )
-    halo[...] = message[:HW]
-    chain_back = message[HW:].astype(F32)
-    edge(core == 0, columns, first, halo, blocks, chain_out)
 
     pieces = done.shape[0] // 2
     per = clusters // pieces
@@ -584,18 +560,25 @@
     )
     pair = to_other_core(pair_sent)
 
-    def fold(step, came, partial, sums, gathered, *rest, after):
+    def fold(step, came, partial, sums, *rest, after):
         n = half >> step
         m = 2 if step == 0 or STEPS[step - 1][0] != X else 4
         a = 2 << step
-        size = n // 2 * (2 if step >= 2 else 1) + 2 * m + 2 * HW + (a if step < 5 else 0)
-        args = (place, came, partial, sums, gathered, *rest)
+        size = n // 2 * (2 if step >= 2 else 1) + 2 * m
+        size += (a, 0, half // 2)[max(step - 3, 0)]
+        args = (place, came, partial, sums, *rest)
         return call(
-            lambda *refs: fold_kernel(step, *refs[: len(args)], *refs[len(args) + 1 :]),
+            functools.partial(fold_kernel, step),
             "fold",
             (),
             [SMEM] + [VMEM] * (len(args) - 1) + [ANY],
-            [rows(size), rows(n // 2, F32), rows(m, F32), rows(a), rows(2 * HW)],
+            [
+                rows(size),
+                rows(n // 2, F32),
+                rows(m, F32),
+                *([rows(a)] if step < 5 else []),
+                *([rows(2 * HW)] if step == 0 else []),
+            ],
             (*args, after),
             us=0.3,
         )
@@ -604,22 +587,20 @@
         0, came, partial, sums, own, came_own, pair, after=back_outer
     )
     came = routed(payload, STEPS[0])
-    near_out, near_back = call(
+    near_out, near_back, halo = call(
         near_kernel,
         "near",
         (),
-        [SMEM] * 2 + [VMEM] * 4 + [ANY],
-        [rows(clusters, F32), rows(clusters + 2 * HW, F32)],
-        (columns, first, mright, mleft, near_blocks, back_outer, payload),
+        [SMEM] * 2 + [VMEM] * 5 + [ANY],
+        [rows(clusters, F32), rows(clusters + 2 * HW, F32), rows(2 * HW)],
+        (columns, first, mright, mleft, near_blocks, back_outer, halo, payload),
         us=4,
     )
+    halo_came = to_other_chips(halo)
     after = near_out
-    before = came
-    for step in range(1, len(STEPS)):
-        rest = (halo, before) if STEPS[step - 1][1] else (halo,)
-        before = came
-        payload, partial, sums, gathered, halo = fold(
-            step, came, partial, sums, gathered, *rest, after=after
+    for step in range(1, 5):
+        payload, partial, sums, gathered = fold(
+            step, came, partial, sums, gathered, after=after
         )
         came = routed(payload, STEPS[step])
         after = payload
@@ -635,6 +616,20 @@
                 scratch=[pltpu.VMEM((HW, *block), BF)],
             )
             after = pair_out
+    chain_out, chain_back = call(
+        edge_chain_kernel,
+        "edge_chain",
+        (),
+        [SMEM] * 3 + [VMEM] * 2 + [ANY],
+        [rows(HW, F32)] * 2,
+        (place, columns, first, halo_came, near_blocks, payload),
+        us=0.8,
+    )
+    payload, partial, sums = fold(5, came, partial, sums, gathered, after=chain_out)
+    came = routed(payload, STEPS[5])
+    (gathered,) = call(
+        join_kernel, "join", (), [VMEM] * 2, [rows(half)], (gathered, came), us=0.2
+    )
     gathered_other = to_other_core(gathered)
     (far_right,) = call(
         forward_kernel,
@@ -654,7 +649,7 @@
             slab_transfer,
             transfer,
             leaf_basis,
-            payload,
+            came,
         ),
         us=2.5,
         scratch=[pltpu.VMEM((devices, *block), BF)],
@@ -664,13 +659,11 @@
         down_kernel,
         "down",
         (),
-        [SMEM] * 4 + [VMEM] * 15,
+        [SMEM] * 2 + [VMEM] * 14,
         [(HBM, wide, F32)] * 2,
         (
             place,
             cluster_points,
-            columns,
-            first,
             far_right,
             partial,
             sums,
@@ -683,16 +676,13 @@
             near_back,
             pair_out,
             pair_back,
-            halo,
-            before,
-            near_blocks,
+            chain_out,
+            chain_back,
         ),
         us=4,
         scratch=[
             pltpu.VMEM(wide, F32),
             pltpu.VMEM(wide, F32),
-            pltpu.VMEM((HW, *block), BF),
-            pltpu.VMEM((HW, *block), F32),
             pltpu.SemaphoreType.DMA((8,)),
         ],
     )

time: 63.2 us -> 65.2 us (1.032); the launches traced: 63.1 us -> 64 us
  starting transfers between devices: 18.1 us -> 22 us
  waiting for transfers between devices: 25.8 us -> 22 us
  Pallas kernels: 17.4 us -> 18.2 us
    ppermute x7, waiting for transfers between devices: 25.8 us -> 20.1 us  [routed(): return lax.ppermute(block, AXES, route)]
    ppermute x7, starting transfers between devices: 17.5 us -> 19.5 us  [routed(): return lax.ppermute(block, AXES, route)]
    ppermute x3, waiting for transfers between devices: 0.01 us -> 1.9 us  [to_other_core(): lax.ppermute(block, AXES, [(i, i ^ 1) for i in range(lax.axis_size(AXES))])]
    ppermute x0 -> x1, starting transfers between devices: none -> 1.69 us  [to_other_chips(): return lax.ppermute(block, AXES, [(i, j) for i, j in route if j in devices])]
    pallas_call x12 -> x14, Pallas kernels: 17.4 us -> 18.2 us  [call(): pl.pallas_call(kernel, grid=grid, out_shape=tuple((shape(dims, kind) for...]
  transfers between devices with their start and end apart: 10 -> 11, of which waited for: 7 -> 8; matrix products, arithmetic and copies ran while one was open for 0% -> 0% of each run, Pallas kernels for 13% -> 11%
where the time goes in v7:
time: 65.2 us; the launch traced here: 64 us
  starting transfers between devices  22 us (34%)
  waiting for transfers between devices  22 us (34%)
  Pallas kernels  18.2 us (28%)
  between operations  1.64 us (3%)
    ppermute x7, waiting for transfers between devices, routed(): return lax.ppermute(block, AXES, route)  20.1 us
    ppermute x7, starting transfers between devices, routed(): return lax.ppermute(block, AXES, route)  19.5 us
    pallas_call x14, Pallas kernels, call(): pl.pallas_call(kernel, grid=grid, out_shape=tuple((shape(dims, kind) for...  18.2 us
    ppermute x3, waiting for transfers between devices, to_other_core(): lax.ppermute(block, AXES, [(i, i ^ 1) for i in range(lax.axis_size(AXES))])  1.9 us
    ppermute x1, starting transfers between devices, to_other_chips(): return lax.ppermute(block, AXES, [(i, j) for i, j in route if j in devices])  1.69 us
  transfers between devices with their start and end apart: 11, of which 8 were waited for; matrix products, arithmetic and copies ran while one was open for 0% of the time, Pallas kernels for 11%

profile of v7, /device:TPU:0, one launch (start us, length us, event | category | flops | bytes accessed | tf_op | source)
XLA Modules:
  0.0 64.0 jit_solution(10723854140755387846)
XLA Ops:
  1.3 0.0 copy-start
  1.3 0.0 copy-start.5
  1.3 5.6 %rise.1 = (bf16[32,32,128]{2,1,0:T(8,128)(2,1)S(1)}, bf16[32,32,128]{2,1,0:T(8,128)(2,1)S(1)}, bf16[1,32,128]{2,1,0:T(8,128)(2,1)S(1)}, f32[65,32,128]{2,1,0:T(8...) custom-call(s32[1]{0:T(128)} %bitcast.place, s32[1]{0:T(128)S(6)} %copy.16.count, s32[32]{0:T(128)} %points.1, ...), custom_call_target="tpu_custom_call" | custom-call | flops 1000 | bytes 18000000 | tf_op jit(solution)/shard_map/rise/pallas_call | solution.py:460
  6.9 0.1 collective-permute-start
  7.0 0.2 copy-done
  7.2 0.0 copy-done.5
  7.2 1.1 %near_outer.1 = (f32[40,32,128]{2,1,0:T(8,128)S(1)}, bf16[16,32,128]{2,1,0:T(8,128)(2,1)S(1)}) custom-call(s32[8,32]{1,0:T(8,128)S(1)} %bitcast.4, s32[1]{0:T(128)S(6)} %sub.3.first, bf16[32,32,128]{2,1,0:T(8,128)(2,1)S(1)} %get-tuple-element.45.mright, bf16[32,32,128]{2,1,0:T(8,128)(2,1)S(1)} %get-tuple-element.46.mleft, bf16[32,8,128,128]{3,2,1,0:T(8,128)(2,1)S(1)} %copy-done), custom_call_target="tpu_custom_call" | custom-call | flops 1000 | bytes 3600000 | tf_op jit(solution)/shard_map/near_outer/pallas_call | solution.py:460
  8.3 0.4 collective-permute-start.2
  8.7 1.6 %collective-permute-start.1 = (bf16[1,32,128]{2,1,0:T(8,128)(2,1)S(1)}, bf16[1,32,128]{2,1,0:T(8,128)(2,1)S(1)}, u32[]{:S(2)}, u32[]{:S(2)}) collective-permute-start(bf16[1,32,128]{2,1,0:T(8,128)(2,1)S(1)} %get-tuple-element.44.refs_0_), channel_id=1, source_target_pairs={{0,32},{1,97},{2,34},{3,99},{4,36},{5,101},{6,38},{7,103},{8,40},{... | collective-permute-start | bytes 24584 | tf_op jit(solution)/shard_map/ppermute | solution.py:29
  10.3 2.1 %collective-permute-done.1.refs_1_ = bf16[1,32,128]{2,1,0:T(8,128)(2,1)S(1)} collective-permute-done((bf16[1,32,128]{2,1,0:T(8,128)(2,1)S(1)}, bf16[1,32,128]{2,1,0:T(8,128)(2,1)S(1)}, u32[]{:S(2)}, u32[]{:S(2)}) %collective-permute-start.1) | collective-permute-done | bytes 8224 | tf_op jit(solution)/shard_map/ppermute | solution.py:29
  12.3 0.0 collective-permute-done.2.refs_2_.pair
  12.3 0.0 collective-permute-done.came
  12.3 0.2 fold.6
  12.5 1.7 %collective-permute-start.3 = (bf16[38,32,128]{2,1,0:T(8,128)(2,1)S(1)}, bf16[38,32,128]{2,1,0:T(8,128)(2,1)S(1)}, u32[]{:S(2)}, u32[]{:S(2)}) collective-permute-start(bf16[38,32,128]{2,1,0:T(8,128)(2,1)S(1)} %get-tuple-element.49._), channel_id=1, source_target_pairs={{0,8},{1,7},{2,10},{3,5},{4,12},{5,3},{6,14},{7,1},{8,0},{9,15},{1... | collective-permute-start | bytes 933896 | tf_op jit(solution)/shard_map/ppermute | solution.py:29
  14.3 3.9 %near.1 = (f32[32,32,128]{2,1,0:T(8,128)S(1)}, f32[40,32,128]{2,1,0:T(8,128)S(1)}, bf16[8,32,128]{2,1,0:T(8,128)(2,1)S(1)}) custom-call(s32[8,32]{1,0:T(8,128)S(1)} %bitcast.5, s32[1]{0:T(128)S(6)} %sub.3.first, bf16[32,32,128]{2,1,0:T(8,128)(2,1)S(1)} %get-tuple-element.45.mright, bf16[32,32,128]{2,1,0:T(8,128)(2,1)S(1)} %get-tuple-element.46.mleft, ...), custom_call_target="tpu_custom_call" | custom-call | flops 1000 | bytes 14400000 | tf_op jit(solution)/shard_map/near/pallas_call | solution.py:460
  18.1 1.4 %collective-permute-done.3.came = bf16[38,32,128]{2,1,0:T(8,128)(2,1)S(1)} collective-permute-done((bf16[38,32,128]{2,1,0:T(8,128)(2,1)S(1)}, bf16[38,32,128]{2,1,0:T(8,128)(2,1)S(1)}, u32[]{:S(2)}, u32[]{:S(2)}) %collective-permute-start.3) | collective-permute-done | bytes 311328 | tf_op jit(solution)/shard_map/ppermute | solution.py:29
  19.5 0.1 fold.7
  19.6 3.2 %collective-permute-start.4 = (bf16[24,32,128]{2,1,0:T(8,128)(2,1)S(1)}, bf16[24,32,128]{2,1,0:T(8,128)(2,1)S(1)}, u32[]{:S(2)}, u32[]{:S(2)}) collective-permute-start(bf16[24,32,128]{2,1,0:T(8,128)(2,1)S(1)} %get-tuple-element.55._), channel_id=1, source_target_pairs={{0,24},{1,3},{2,26},{3,1},{4,28},{5,7},{6,30},{7,5},{8,16},{9,11},... | collective-permute-start | bytes 589832 | tf_op jit(solution)/shard_map/ppermute | solution.py:29
  22.8 1.1 %edge_pair.1 = (f32[4,32,128]{2,1,0:T(8,128)S(1)}, f32[4,32,128]{2,1,0:T(8,128)S(1)}) custom-call(s32[1]{0:T(128)} %bitcast.place, s32[8,32]{1,0:T(8,128)S(1)} %bitcast.6, s32[1]{0:T(128)S(6)} %sub.3.first, bf16[16,32,128]{2,1,0:T(8,128)(2,1)S(1)} %collective-permute-done.2.refs_2_.pair, bf16[32,8,128,128]{3,2,1,0:T(8,128)(2,1)S(1)} %copy-done, ...), custom_call_target="tpu_custom_call" | custom-call | flops 1000 | bytes 2880000 | tf_op jit(solution)/shard_map/edge_pair/pallas_call | solution.py:460
  23.8 2.7 %collective-permute-done.4.came = bf16[24,32,128]{2,1,0:T(8,128)(2,1)S(1)} collective-permute-done((bf16[24,32,128]{2,1,0:T(8,128)(2,1)S(1)}, bf16[24,32,128]{2,1,0:T(8,128)(2,1)S(1)}, u32[]{:S(2)}, u32[]{:S(2)}) %collective-permute-start.4) | collective-permute-done | bytes 196640 | tf_op jit(solution)/shard_map/ppermute | solution.py:29
  26.6 0.1 fold.8
  26.6 2.1 %collective-permute-start.5 = (bf16[28,32,128]{2,1,0:T(8,128)(2,1)S(1)}, bf16[28,32,128]{2,1,0:T(8,128)(2,1)S(1)}, u32[]{:S(2)}, u32[]{:S(2)}) collective-permute-start(bf16[28,32,128]{2,1,0:T(8,128)(2,1)S(1)} %get-tuple-element.60.refs_1_), channel_id=1, source_target_pairs={{0,2},{1,25},{2,0},{3,27},{4,6},{5,29},{6,4},{7,31},{8,10},{9,17},... | collective-permute-start | bytes 688136 | tf_op jit(solution)/shard_map/ppermute | solution.py:29
  28.7 4.0 %collective-permute-done.5.came = bf16[28,32,128]{2,1,0:T(8,128)(2,1)S(1)} collective-permute-done((bf16[28,32,128]{2,1,0:T(8,128)(2,1)S(1)}, bf16[28,32,128]{2,1,0:T(8,128)(2,1)S(1)}, u32[]{:S(2)}, u32[]{:S(2)}) %collective-permute-start.5) | collective-permute-done | bytes 229408 | tf_op jit(solution)/shard_map/ppermute | solution.py:29
  32.8 4.2 %collective-permute-start.6 = (bf16[28,32,128]{2,1,0:T(8,128)(2,1)S(1)}, bf16[28,32,128]{2,1,0:T(8,128)(2,1)S(1)}, u32[]{:S(2)}, u32[]{:S(2)}) collective-permute-start(bf16[28,32,128]{2,1,0:T(8,128)(2,1)S(1)} %get-tuple-element.64.refs_1_), channel_id=1, source_target_pairs={{0,6},{1,9},{2,4},{3,11},{4,2},{5,13},{6,0},{7,15},{8,14},{9,1},{1... | collective-permute-start | bytes 688136 | tf_op jit(solution)/shard_map/ppermute | solution.py:29
  37.0 1.7 %collective-permute-start.8 = (bf16[8,32,128]{2,1,0:T(8,128)(2,1)S(1)}, bf16[8,32,128]{2,1,0:T(8,128)(2,1)S(1)}, u32[]{:S(2)}, u32[]{:S(2)}) collective-permute-start(bf16[8,32,128]{2,1,0:T(8,128)(2,1)S(1)} %get-tuple-element.72), channel_id=1, source_target_pairs={{0,2},{2,4},{3,1},{4,6},{5,3},{6,8},{7,5},{8,10},{9,7},{10,12},{11... | collective-permute-start | bytes 196616 | tf_op jit(solution)/shard_map/ppermute | solution.py:39
  38.7 2.5 %collective-permute-done.6.came = bf16[28,32,128]{2,1,0:T(8,128)(2,1)S(1)} collective-permute-done((bf16[28,32,128]{2,1,0:T(8,128)(2,1)S(1)}, bf16[28,32,128]{2,1,0:T(8,128)(2,1)S(1)}, u32[]{:S(2)}, u32[]{:S(2)}) %collective-permute-start.6) | collective-permute-done | bytes 229408 | tf_op jit(solution)/shard_map/ppermute | solution.py:29
  41.2 0.0 slice-start.1
  41.3 1.3 %collective-permute-start.7 = (bf16[8,32,128]{2,1,0:T(8,128)(2,1)S(1)}, bf16[8,32,128]{2,1,0:T(8,128)(2,1)S(1)}, u32[]{:S(2)}, u32[]{:S(2)}) collective-permute-start(bf16[8,32,128]{2,1,0:T(8,128)(2,1)S(1)} %get-tuple-element.69._), channel_id=1, source_target_pairs={{0,32},{1,97},{2,34},{3,99},{4,36},{5,101},{6,38},{7,103},{8,40},{... | collective-permute-start | bytes 196616 | tf_op jit(solution)/shard_map/ppermute | solution.py:29
  42.6 0.0 collective-permute-done.8.came
  42.6 1.1 %edge_chain.1 = (f32[4,32,128]{2,1,0:T(8,128)S(1)}, f32[4,32,128]{2,1,0:T(8,128)S(1)}) custom-call(s32[1]{0:T(128)} %bitcast.place, s32[8,32]{1,0:T(8,128)S(1)} %bitcast.7, s32[1]{0:T(128)S(6)} %sub.3.first, bf16[8,32,128]{2,1,0:T(8,128)(2,1)S(1)} %collective-permute-done.8.came, bf16[32,8,128,128]{3,2,1,0:T(8,128)(2,1)S(1)} %copy-done, ...), custom_call_target="tpu_custom_call" | custom-call | flops 1000 | bytes 2880000 | tf_op jit(solution)/shard_map/edge_chain/pallas_call | solution.py:460
  43.7 0.0 copy-start.2
  43.7 0.0 copy-start.6
  43.7 0.0 copy-start.8
  43.7 2.2 %collective-permute-done.7.came = bf16[8,32,128]{2,1,0:T(8,128)(2,1)S(1)} collective-permute-done((bf16[8,32,128]{2,1,0:T(8,128)(2,1)S(1)}, bf16[8,32,128]{2,1,0:T(8,128)(2,1)S(1)}, u32[]{:S(2)}, u32[]{:S(2)}) %collective-permute-start.7) | collective-permute-done | bytes 65568 | tf_op jit(solution)/shard_map/ppermute | solution.py:29
  45.9 5.4 %collective-permute-start.9 = (bf16[42,32,128]{2,1,0:T(8,128)(2,1)S(1)}, bf16[42,32,128]{2,1,0:T(8,128)(2,1)S(1)}, u32[]{:S(2)}, u32[]{:S(2)}) collective-permute-start(bf16[42,32,128]{2,1,0:T(8,128)(2,1)S(1)} %get-tuple-element.74), channel_id=1, source_target_pairs={{0,96},{1,33},{2,98},{3,35},{4,100},{5,37},{6,102},{7,39},{8,104},... | collective-permute-start | bytes 1032200 | tf_op jit(solution)/shard_map/ppermute | solution.py:29
  51.3 5.2 %collective-permute-done.9.b.rest_4_.came = bf16[42,32,128]{2,1,0:T(8,128)(2,1)S(1)} collective-permute-done((bf16[42,32,128]{2,1,0:T(8,128)(2,1)S(1)}, bf16[42,32,128]{2,1,0:T(8,128)(2,1)S(1)}, u32[]{:S(2)}, u32[]{:S(2)}) %collective-permute-start.9) | collective-permute-done | bytes 344096 | tf_op jit(solution)/shard_map/ppermute | solution.py:29
  56.6 0.0 copy-start.7
  56.6 0.3 collective-permute-start.10
  56.9 1.9 %collective-permute-done.10.other = bf16[64,32,128]{2,1,0:T(8,128)(2,1)S(1)} collective-permute-done((bf16[64,32,128]{2,1,0:T(8,128)(2,1)S(1)}, bf16[64,32,128]{2,1,0:T(8,128)(2,1)S(1)}, u32[]{:S(2)}, u32[]{:S(2)}) %collective-permute-start.10) | collective-permute-done | bytes 524320 | tf_op jit(solution)/shard_map/ppermute | solution.py:33
  58.8 0.0 slice-done
  58.8 0.0 slice-done.1
  58.8 0.0 copy-done.3
  58.8 0.0 copy-done.4
  58.8 0.0 copy-done.1
  58.8 0.0 copy-done.2
  58.8 0.0 copy-done.6
  58.9 2.4 %forward.1.far_right = f32[32,128]{1,0:T(8,128)S(1)} custom-call(s32[1]{0:T(128)} %bitcast.place, s32[1]{0:T(128)S(6)} %copy.16.count, s32[1,96]{1,0:T(1,128)S(1)} %copy-done.6, s32[256]{0:T(256)S(1)} %copy-done.8, bf16[64,32,128]{2,1,0:T(8,128)(2,1)S(1)} %join.1.own, bf16[64,32,128]{2,1,0:T(8,128)(2,1)S(1)} %collective-permute-done.10.other, ...), custom_call_target="tpu_custom_call" | custom-call | flops 1000 | bytes 9000000 | tf_op jit(solution)/shard_map/forward/pallas_call | solution.py:460
  61.3 2.6 %down.1 = (f32[32,4096]{1,0:T(8,128)}, f32[32,4096]{1,0:T(8,128)}) custom-call(s32[1]{0:T(128)} %bitcast.place, s32[32]{0:T(128)S(1)} %copy-done.7, f32[32,128]{1,0:T(8,128)S(1)} %forward.1.far_right, f32[1,32,128]{2,1,0:T(8,128)S(1)} %get-tuple-element.75.partial, f32[4,32,128]{2,1,0:T(8,128)S(1)} %get-tuple-element.76.sums, ...), custom_call_target="tpu_custom_call" | custom-call | flops 1000 | bytes 14400000 | tf_op jit(solution)/shard_map/down/pallas_call | solution.py:460
  (11 shorter events, 0.2 us)
Async XLA Ops:
  1.3 5.9 %copy-start = (bf16[32,8,128,128]{3,2,1,0:T(8,128)(2,1)S(1)}, bf16[32,8,128,128]{3,2,1,0:T(8,128)(2,1)}, u32[]{:S(2)}) copy-start(bf16[32,8,128,128]{3,2,1,0:T(8,128)(2,1)} %blocks.7) | copy-start | bytes 25165828
  1.3 5.9 %copy-start.5 = (s32[32,8]{0,1:T(8,128)S(1)}, s32[32,8]{0,1:T(8,128)}, u32[]{:S(2)}) copy-start(s32[32,8]{0,1:T(8,128)} %param.17) | copy-start | bytes 3076
  6.9 5.4 %collective-permute-start = (f32[67,32,128]{2,1,0:T(8,128)S(1)}, f32[67,32,128]{2,1,0:T(8,128)S(1)}, u32[]{:S(2)}, u32[]{:S(2)}) collective-permute-start(f32[67,32,128]{2,1,0:T(8,128)S(1)} %get-tuple-element.41), channel_id=1, source_target_pairs={{0,1},{1,0},{2,3},{3,2},{4,5},{5,4},{6,7},{7,6},{8,9},{9,8},{10,11... | collective-permute-start | bytes 3293192 | tf_op jit(solution)/shard_map/ppermute | solution.py:33
  8.3 4.1 %collective-permute-start.2 = (bf16[16,32,128]{2,1,0:T(8,128)(2,1)S(1)}, bf16[16,32,128]{2,1,0:T(8,128)(2,1)S(1)}, u32[]{:S(2)}, u32[]{:S(2)}) collective-permute-start(bf16[16,32,128]{2,1,0:T(8,128)(2,1)S(1)} %get-tuple-element.47), channel_id=1, source_target_pairs={{0,1},{1,0},{2,3},{3,2},{4,5},{5,4},{6,7},{7,6},{8,9},{9,8},{10,11... | collective-permute-start | bytes 393224 | tf_op jit(solution)/shard_map/ppermute | solution.py:33
  8.7 3.7 %collective-permute-start.1 = (bf16[1,32,128]{2,1,0:T(8,128)(2,1)S(1)}, bf16[1,32,128]{2,1,0:T(8,128)(2,1)S(1)}, u32[]{:S(2)}, u32[]{:S(2)}) collective-permute-start(bf16[1,32,128]{2,1,0:T(8,128)(2,1)S(1)} %get-tuple-element.44.refs_0_), channel_id=1, source_target_pairs={{0,32},{1,97},{2,34},{3,99},{4,36},{5,101},{6,38},{7,103},{8,40},{... | collective-permute-start | bytes 24584 | tf_op jit(solution)/shard_map/ppermute | solution.py:29
  12.5 7.0 %collective-permute-start.3 = (bf16[38,32,128]{2,1,0:T(8,128)(2,1)S(1)}, bf16[38,32,128]{2,1,0:T(8,128)(2,1)S(1)}, u32[]{:S(2)}, u32[]{:S(2)}) collective-permute-start(bf16[38,32,128]{2,1,0:T(8,128)(2,1)S(1)} %get-tuple-element.49._), channel_id=1, source_target_pairs={{0,8},{1,7},{2,10},{3,5},{4,12},{5,3},{6,14},{7,1},{8,0},{9,15},{1... | collective-permute-start | bytes 933896 | tf_op jit(solution)/shard_map/ppermute | solution.py:29
  19.6 7.0 %collective-permute-start.4 = (bf16[24,32,128]{2,1,0:T(8,128)(2,1)S(1)}, bf16[24,32,128]{2,1,0:T(8,128)(2,1)S(1)}, u32[]{:S(2)}, u32[]{:S(2)}) collective-permute-start(bf16[24,32,128]{2,1,0:T(8,128)(2,1)S(1)} %get-tuple-element.55._), channel_id=1, source_target_pairs={{0,24},{1,3},{2,26},{3,1},{4,28},{5,7},{6,30},{7,5},{8,16},{9,11},... | collective-permute-start | bytes 589832 | tf_op jit(solution)/shard_map/ppermute | solution.py:29
  26.6 6.1 %collective-permute-start.5 = (bf16[28,32,128]{2,1,0:T(8,128)(2,1)S(1)}, bf16[28,32,128]{2,1,0:T(8,128)(2,1)S(1)}, u32[]{:S(2)}, u32[]{:S(2)}) collective-permute-start(bf16[28,32,128]{2,1,0:T(8,128)(2,1)S(1)} %get-tuple-element.60.refs_1_), channel_id=1, source_target_pairs={{0,2},{1,25},{2,0},{3,27},{4,6},{5,29},{6,4},{7,31},{8,10},{9,17},... | collective-permute-start | bytes 688136 | tf_op jit(solution)/shard_map/ppermute | solution.py:29
  32.7 26.1 %slice-start = ((s8[6291456]{0:T(1024)(128)(4,1)}), s8[4194304]{0:T(1024)(128)(4,1)S(1)}, s32[]{:S(2)}) async-start(s8[6291456]{0:T(1024)(128)(4,1)} %bitcast.2), calls=%async_computation | async-start | bytes 8388608
  32.8 8.4 %collective-permute-start.6 = (bf16[28,32,128]{2,1,0:T(8,128)(2,1)S(1)}, bf16[28,32,128]{2,1,0:T(8,128)(2,1)S(1)}, u32[]{:S(2)}, u32[]{:S(2)}) collective-permute-start(bf16[28,32,128]{2,1,0:T(8,128)(2,1)S(1)} %get-tuple-element.64.refs_1_), channel_id=1, source_target_pairs={{0,6},{1,9},{2,4},{3,11},{4,2},{5,13},{6,0},{7,15},{8,14},{9,1},{1... | collective-permute-start | bytes 688136 | tf_op jit(solution)/shard_map/ppermute | solution.py:29
  37.0 5.6 %collective-permute-start.8 = (bf16[8,32,128]{2,1,0:T(8,128)(2,1)S(1)}, bf16[8,32,128]{2,1,0:T(8,128)(2,1)S(1)}, u32[]{:S(2)}, u32[]{:S(2)}) collective-permute-start(bf16[8,32,128]{2,1,0:T(8,128)(2,1)S(1)} %get-tuple-element.72), channel_id=1, source_target_pairs={{0,2},{2,4},{3,1},{4,6},{5,3},{6,8},{7,5},{8,10},{9,7},{10,12},{11... | collective-permute-start | bytes 196616 | tf_op jit(solution)/shard_map/ppermute | solution.py:39
  41.2 17.6 %slice-start.1 = ((s8[6291456]{0:T(1024)(128)(4,1)}), s8[2097152]{0:T(1024)(128)(4,1)S(1)}, s32[]{:S(2)}) async-start(s8[6291456]{0:T(1024)(128)(4,1)} %bitcast.2), calls=%async_computation.1 | async-start | bytes 4194304
  41.3 4.6 %collective-permute-start.7 = (bf16[8,32,128]{2,1,0:T(8,128)(2,1)S(1)}, bf16[8,32,128]{2,1,0:T(8,128)(2,1)S(1)}, u32[]{:S(2)}, u32[]{:S(2)}) collective-permute-start(bf16[8,32,128]{2,1,0:T(8,128)(2,1)S(1)} %get-tuple-element.69._), channel_id=1, source_target_pairs={{0,32},{1,97},{2,34},{3,99},{4,36},{5,101},{6,38},{7,103},{8,40},{... | collective-permute-start | bytes 196616 | tf_op jit(solution)/shard_map/ppermute | solution.py:29
  42.6 16.2 %copy-start.3 = (f32[4,4,128,128]{3,2,1,0:T(8,128)S(1)}, f32[4,4,128,128]{3,2,1,0:T(8,128)}, u32[]{:S(2)}) copy-start(f32[4,4,128,128]{3,2,1,0:T(8,128)} %apex.1) | copy-start | bytes 3145732
  42.6 16.2 %copy-start.4 = (f32[1,128,128]{2,1,0:T(8,128)S(1)}, f32[1,128,128]{2,1,0:T(8,128)}, u32[]{:S(2)}) copy-start(f32[1,128,128]{2,1,0:T(8,128)} %lift.1) | copy-start | bytes 196612
  43.7 15.2 %copy-start.1 = (f32[32,64,128]{2,1,0:T(8,128)S(1)}, f32[32,64,128]{2,1,0:T(8,128)}, u32[]{:S(2)}) copy-start(f32[32,64,128]{2,1,0:T(8,128)} %transfer.1) | copy-start | bytes 3145732
  43.7 15.2 %copy-start.2 = (bf16[32,64,128]{2,1,0:T(8,128)(2,1)S(1)}, bf16[32,64,128]{2,1,0:T(8,128)(2,1)}, u32[]{:S(2)}) copy-start(bf16[32,64,128]{2,1,0:T(8,128)(2,1)} %basis.1) | copy-start | bytes 1572868
  43.7 15.2 %copy-start.6 = (s32[1,96]{1,0:T(1,128)S(1)}, s32[1,96]{1,0:T(1,128)}, u32[]{:S(2)}) copy-start(s32[1,96]{1,0:T(1,128)} %parents.1) | copy-start | bytes 1156
  43.7 15.2 %copy-start.8 = (s32[256]{0:T(256)S(1)}, s32[256]{0:T(256)}, u32[]{:S(2)}) copy-start(s32[256]{0:T(256)} %constant.21.clone.table) | copy-start | bytes 3076
  45.9 10.7 %collective-permute-start.9 = (bf16[42,32,128]{2,1,0:T(8,128)(2,1)S(1)}, bf16[42,32,128]{2,1,0:T(8,128)(2,1)S(1)}, u32[]{:S(2)}, u32[]{:S(2)}) collective-permute-start(bf16[42,32,128]{2,1,0:T(8,128)(2,1)S(1)} %get-tuple-element.74), channel_id=1, source_target_pairs={{0,96},{1,33},{2,98},{3,35},{4,100},{5,37},{6,102},{7,39},{8,104},... | collective-permute-start | bytes 1032200 | tf_op jit(solution)/shard_map/ppermute | solution.py:29
  56.6 4.7 %copy-start.7 = (s32[32]{0:T(128)S(1)}, s32[32]{0:T(128)}, u32[]{:S(2)}) copy-start(s32[32]{0:T(128)} %points.1) | copy-start | bytes 388
  56.6 2.2 %collective-permute-start.10 = (bf16[64,32,128]{2,1,0:T(8,128)(2,1)S(1)}, bf16[64,32,128]{2,1,0:T(8,128)(2,1)S(1)}, u32[]{:S(2)}, u32[]{:S(2)}) collective-permute-start(bf16[64,32,128]{2,1,0:T(8,128)(2,1)S(1)} %join.1.own), channel_id=1, source_target_pairs={{0,1},{1,0},{2,3},{3,2},{4,5},{5,4},{6,7},{7,6},{8,9},{9,8},{10,11... | collective-permute-start | bytes 1572872 | tf_op jit(solution)/shard_map/ppermute | solution.py:33

commit v8 on v7

--- a/solution.py
+++ b/solution.py
@@ -17,7 +17,7 @@
 Z, Y, X = 1, 3, 5
 CORE_1 = {Y: Z, Z: Y, X: X}
 STEPS = ((Y, 0), (Y, 1), (Z, 0), (Z, 1), (X, 0), (X, 1))
-GATHER_STEPS = (STEPS[4], *STEPS[:4], STEPS[5])
+GATHER_STEPS = (STEPS[5], *STEPS[:5])
 
 
 def routed(block, step):
@@ -226,22 +226,15 @@
         start = start + part.shape[0]
 
 
-def fold_kernel(step, place, came, partial, sums, *refs):
-    if step == 0:
-        gathered, came_own, pair, _, payload, keep, sums_next, gathered_next, halo = refs
-    elif step < 5:
-        gathered, _, payload, keep, sums_next, gathered_next = refs
-    else:
-        gathered, _, payload, keep, sums_next = refs
+def fold_kernel(step, came, partial, sums, *refs):
+    gathered = refs[0]
+    payload, keep, sums_next, gathered_next = refs[-4:]
     n = 2 * keep.shape[0]
     m = sums.shape[0]
     if step == 0:
         total = partial[:n] + came[:n]
         got = came[n + 1 :]
-        other = HW * (1 - (place[0] & 1))
-        halo[:HW] = pair[pl.ds(other, HW)]
-        halo[HW:] = pair[pl.ds(2 * HW + other, HW)]
-        more = came_own[...]
+        more = refs[1][...]
     else:
         total = partial[...] + came[:n].astype(F32)
         start = n
@@ -249,25 +242,18 @@
             total = total + came[n : 2 * n].astype(F32)
             start = 2 * n
         got = came[start : start + m].astype(F32) + came[start + m : start + 2 * m].astype(F32)
-        more = came[start + 2 * m :] if step < 5 else None
+        more = came[start + 2 * m :]
     if sums_next.shape[0] == m:
         sums_next[...] = sums[...] + got
     else:
         sums_next[:m] = sums[...]
         sums_next[m:] = got
     keep[...] = total[: n // 2]
-    if step < 5:
-        a = gathered.shape[0]
-        gathered_next[:a] = gathered[...]
-        gathered_next[a:] = more
-    parts = [gathered if step == 5 else gathered_next] if step != 4 else []
-    lay_out(payload, total[n // 2 :], step >= 2, sums_next[...], *(part[...] for part in parts))
-
-
-def join_kernel(a, b, out):
-    n = a.shape[0]
-    out[:n] = a[...]
-    out[n:] = b[b.shape[0] - n :]
+    a = gathered.shape[0]
+    gathered_next[:a] = gathered[...]
+    gathered_next[a:] = more
+    parts = [gathered_next[...]] if step < 5 else []
+    lay_out(payload, total[n // 2 :], step >= 2, sums_next[...], *parts)
 
 
 def rows_of(blocks, c):
@@ -285,24 +271,10 @@
             back[place] = held[s] + value[:, s * B : (s + 1) * B]
 
 
-def near_outer_kernel(columns, first, mright, mleft, blocks, back, sent):
-    clusters = mleft.shape[0]
-    back[...] = jnp.zeros_like(back)
-    add_back(columns, first, mleft, blocks, range(HW), back)
-    add_back(columns, first, mleft, blocks, range(clusters - HW, clusters), back)
-    sent[:HW] = mright[:HW]
-    sent[HW : 2 * HW] = mright[clusters - HW :]
-    sent[2 * HW : 3 * HW] = back[:HW].astype(BF)
-    sent[3 * HW :] = back[clusters + HW :].astype(BF)
-
-
-def near_kernel(
-    columns, first, mright, mleft, blocks, back_outer, halo, _, out, back, halo_on
-):
+def near_kernel(columns, first, mright, mleft, blocks, _, out, back, sent):
     clusters = mright.shape[0]
     slots = blocks.shape[1]
-    back[...] = back_outer[...]
-    halo_on[...] = halo[...]
+    back[...] = jnp.zeros_like(back)
     for start in range(0, clusters, 4):
         group = range(start, start + 4)
         for c in group:
@@ -313,8 +285,11 @@
                 is_own = (own >= 0) & (own < clusters)
                 inside.append(jnp.where(is_own, value, jnp.zeros_like(value)))
             out[c] = dot(rows_of(blocks, c), jnp.concatenate(inside, axis=1), NT).T
-        if HW <= start < clusters - HW:
-            add_back(columns, first, mleft, blocks, group, back)
+        add_back(columns, first, mleft, blocks, group, back)
+    sent[:HW] = mright[:HW]
+    sent[HW : 2 * HW] = mright[clusters - HW :]
+    sent[2 * HW : 3 * HW] = back[:HW].astype(BF)
+    sent[3 * HW :] = back[clusters + HW :].astype(BF)
 
 
 def edge(low, columns, first, halo, blocks, out):
@@ -333,8 +308,10 @@
         out[g] = dot(rows_of(blocks, c), jnp.concatenate(values, axis=1), NT).T
 
 
-def edge_pair_kernel(place, columns, first, pair, blocks, _, out, back, halo):
+def edge_pair_kernel(place, columns, first, pair, blocks, _, out, back, message, halo):
     core = place[0] & 1
+    message[:HW] = pair[pl.ds(HW * (1 - core), HW)]
+    message[HW:] = pair[pl.ds(2 * HW + HW * (1 - core), HW)]
     halo[...] = pair[pl.ds(HW * core, HW)]
     edge(core == 1, columns, first, halo, blocks, out)
     back[...] = pair[pl.ds(2 * HW + HW * core, HW)].astype(F32)
@@ -549,87 +526,65 @@
     )
     came = to_other_core(sent)
     came_own = routed(own, GATHER_STEPS[0])
-    back_outer, pair_sent = call(
-        near_outer_kernel,
-        "near_outer",
-        (),
-        [SMEM] * 2 + [VMEM] * 3,
-        [rows(clusters + 2 * HW, F32), rows(4 * HW)],
-        (columns, first, mright, mleft, near_blocks),
-        us=1,
-    )
-    pair = to_other_core(pair_sent)
-
     def fold(step, came, partial, sums, *rest, after):
         n = half >> step
         m = 2 if step == 0 or STEPS[step - 1][0] != X else 4
         a = 2 << step
-        size = n // 2 * (2 if step >= 2 else 1) + 2 * m
-        size += (a, 0, half // 2)[max(step - 3, 0)]
-        args = (place, came, partial, sums, *rest)
+        size = n // 2 * (2 if step >= 2 else 1) + 2 * m + (a if step < 5 else 0)
+        args = (came, partial, sums, *rest)
         return call(
             functools.partial(fold_kernel, step),
             "fold",
             (),
-            [SMEM] + [VMEM] * (len(args) - 1) + [ANY],
-            [
-                rows(size),
-                rows(n // 2, F32),
-                rows(m, F32),
-                *([rows(a)] if step < 5 else []),
-                *([rows(2 * HW)] if step == 0 else []),
-            ],
+            [VMEM] * len(args) + [ANY],
+            [rows(size), rows(n // 2, F32), rows(m, F32), rows(a)],
             (*args, after),
             us=0.3,
         )
 
-    payload, partial, sums, gathered, halo = fold(
-        0, came, partial, sums, own, came_own, pair, after=back_outer
-    )
+    payload, partial, sums, gathered = fold(0, came, partial, sums, own, came_own, after=own)
     came = routed(payload, STEPS[0])
-    near_out, near_back, halo = call(
+    near_out, near_back, pair_sent = call(
         near_kernel,
         "near",
         (),
-        [SMEM] * 2 + [VMEM] * 5 + [ANY],
-        [rows(clusters, F32), rows(clusters + 2 * HW, F32), rows(2 * HW)],
-        (columns, first, mright, mleft, near_blocks, back_outer, halo, payload),
-        us=4,
+        [SMEM] * 2 + [VMEM] * 3 + [ANY],
+        [rows(clusters, F32), rows(clusters + 2 * HW, F32), rows(4 * HW)],
+        (columns, first, mright, mleft, near_blocks, payload),
+        us=5,
     )
-    halo_came = to_other_chips(halo)
+    pair = to_other_core(pair_sent)
     after = near_out
-    for step in range(1, 5):
+    for step in range(1, len(STEPS)):
         payload, partial, sums, gathered = fold(
             step, came, partial, sums, gathered, after=after
         )
         came = routed(payload, STEPS[step])
         after = payload
-        if step == 1:
-            pair_out, pair_back = call(
+        if step == 2:
+            pair_out, pair_back, message = call(
                 edge_pair_kernel,
                 "edge_pair",
                 (),
                 [SMEM] * 3 + [VMEM] * 2 + [ANY],
-                [rows(HW, F32)] * 2,
+                [rows(HW, F32)] * 2 + [rows(2 * HW)],
                 (place, columns, first, pair, near_blocks, payload),
                 us=0.8,
                 scratch=[pltpu.VMEM((HW, *block), BF)],
             )
             after = pair_out
-    chain_out, chain_back = call(
-        edge_chain_kernel,
-        "edge_chain",
-        (),
-        [SMEM] * 3 + [VMEM] * 2 + [ANY],
-        [rows(HW, F32)] * 2,
-        (place, columns, first, halo_came, near_blocks, payload),
-        us=0.8,
-    )
-    payload, partial, sums = fold(5, came, partial, sums, gathered, after=chain_out)
-    came = routed(payload, STEPS[5])
-    (gathered,) = call(
-        join_kernel, "join", (), [VMEM] * 2, [rows(half)], (gathered, came), us=0.2
-    )
+            halo_came = to_other_chips(message)
+        if step == 4:
+            chain_out, chain_back = call(
+                edge_chain_kernel,
+                "edge_chain",
+                (),
+                [SMEM] * 3 + [VMEM] * 2 + [ANY],
+                [rows(HW, F32)] * 2,
+                (place, columns, first, halo_came, near_blocks, payload),
+                us=0.8,
+            )
+            after = chain_out
     gathered_other = to_other_core(gathered)
     (far_right,) = call(
         forward_kernel,
@@ -649,7 +604,7 @@
             slab_transfer,
             transfer,
             leaf_basis,
-            came,
+            payload,
         ),
         us=2.5,
         scratch=[pltpu.VMEM((devices, *block), BF)],

time: 65.2 us -> 63.2 us (0.969); the launches traced: 64 us -> 62.8 us
  starting transfers between devices: 22 us -> 27.1 us
  waiting for transfers between devices: 22 us -> 17.3 us
  Pallas kernels: 18.2 us -> 16.7 us
    ppermute x7, waiting for transfers between devices: 20.1 us -> 14.1 us  [routed(): return lax.ppermute(block, AXES, route)]
    ppermute x7, starting transfers between devices: 19.5 us -> 24.5 us  [routed(): return lax.ppermute(block, AXES, route)]
    ppermute x1, waiting for transfers between devices: 0.01 us -> 1.88 us  [to_other_chips(): return lax.ppermute(block, AXES, [(i, j) for i, j in route if j in devices])]
    pallas_call x14 -> x12, Pallas kernels: 18.2 us -> 16.7 us  [call(): pl.pallas_call(kernel, grid=grid, out_shape=tuple((shape(dims, kind) for...]
    ppermute x1, starting transfers between devices: 1.69 us -> 2.44 us  [to_other_chips(): return lax.ppermute(block, AXES, [(i, j) for i, j in route if j in devices])]
  transfers between devices with their start and end apart: 11 -> 11, of which waited for: 8 -> 8; matrix products, arithmetic and copies ran while one was open for 0% -> 0% of each run, Pallas kernels for 11% -> 14%
where the time goes in v8:
time: 63.2 us; the launch traced here: 62.8 us
  starting transfers between devices  27.1 us (43%)
  waiting for transfers between devices  17.3 us (27%)
  Pallas kernels  16.7 us (26%)
  between operations  1.6 us (3%)
    ppermute x7, starting transfers between devices, routed(): return lax.ppermute(block, AXES, route)  24.5 us
    pallas_call x12, Pallas kernels, call(): pl.pallas_call(kernel, grid=grid, out_shape=tuple((shape(dims, kind) for...  16.7 us
    ppermute x7, waiting for transfers between devices, routed(): return lax.ppermute(block, AXES, route)  14.1 us
    ppermute x1, starting transfers between devices, to_other_chips(): return lax.ppermute(block, AXES, [(i, j) for i, j in route if j in devices])  2.44 us
    ppermute x1, waiting for transfers between devices, to_other_chips(): return lax.ppermute(block, AXES, [(i, j) for i, j in route if j in devices])  1.88 us
    ppermute x3, waiting for transfers between devices, to_other_core(): lax.ppermute(block, AXES, [(i, i ^ 1) for i in range(lax.axis_size(AXES))])  1.35 us
  transfers between devices with their start and end apart: 11, of which 8 were waited for; matrix products, arithmetic and copies ran while one was open for 0% of the time, Pallas kernels for 14%

profile of v8, /device:TPU:0, one launch (start us, length us, event | category | flops | bytes accessed | tf_op | source)
XLA Modules:
  0.0 62.8 jit_solution(10083751582910830309)
XLA Ops:
  1.3 0.0 copy-start
  1.3 5.1 %rise.1 = (bf16[32,32,128]{2,1,0:T(8,128)(2,1)S(1)}, bf16[32,32,128]{2,1,0:T(8,128)(2,1)S(1)}, bf16[1,32,128]{2,1,0:T(8,128)(2,1)S(1)}, f32[65,32,128]{2,1,0:T(8...) custom-call(s32[1]{0:T(128)} %bitcast.place, s32[1]{0:T(128)S(6)} %copy.16.count, s32[32]{0:T(128)} %points.1, ...), custom_call_target="tpu_custom_call" | custom-call | flops 1000 | bytes 18000000 | tf_op jit(solution)/shard_map/rise/pallas_call | solution.py:437
  6.4 0.1 collective-permute-start
  6.5 2.9 %collective-permute-start.1 = (bf16[1,32,128]{2,1,0:T(8,128)(2,1)S(1)}, bf16[1,32,128]{2,1,0:T(8,128)(2,1)S(1)}, u32[]{:S(2)}, u32[]{:S(2)}) collective-permute-start(bf16[1,32,128]{2,1,0:T(8,128)(2,1)S(1)} %get-tuple-element.43.refs_0_.refs_2_), channel_id=1, source_target_pairs={{0,96},{1,33},{2,98},{3,35},{4,100},{5,37},{6,102},{7,39},{8,104},... | collective-permute-start | bytes 24584 | tf_op jit(solution)/shard_map/ppermute | solution.py:29
  9.4 2.0 %collective-permute-done.1.refs_1_ = bf16[1,32,128]{2,1,0:T(8,128)(2,1)S(1)} collective-permute-done((bf16[1,32,128]{2,1,0:T(8,128)(2,1)S(1)}, bf16[1,32,128]{2,1,0:T(8,128)(2,1)S(1)}, u32[]{:S(2)}, u32[]{:S(2)}) %collective-permute-start.1) | collective-permute-done | bytes 8224 | tf_op jit(solution)/shard_map/ppermute | solution.py:29
  11.4 0.0 collective-permute-done.came
  11.4 0.0 copy-start.5
  11.4 0.1 fold.6
  11.5 1.7 %collective-permute-start.2 = (bf16[38,32,128]{2,1,0:T(8,128)(2,1)S(1)}, bf16[38,32,128]{2,1,0:T(8,128)(2,1)S(1)}, u32[]{:S(2)}, u32[]{:S(2)}) collective-permute-start(bf16[38,32,128]{2,1,0:T(8,128)(2,1)S(1)} %get-tuple-element.44._), channel_id=1, source_target_pairs={{0,8},{1,7},{2,10},{3,5},{4,12},{5,3},{6,14},{7,1},{8,0},{9,15},{1... | collective-permute-start | bytes 933896 | tf_op jit(solution)/shard_map/ppermute | solution.py:29
  13.3 0.0 copy-done
  13.3 0.0 copy-done.5
  13.3 4.1 %near.1 = (f32[32,32,128]{2,1,0:T(8,128)S(1)}, f32[40,32,128]{2,1,0:T(8,128)S(1)}, bf16[16,32,128]{2,1,0:T(8,128)(2,1)S(1)}) custom-call(s32[8,32]{1,0:T(8,128)S(1)} %bitcast.4, s32[1]{0:T(128)S(6)} %sub.3.first, bf16[32,32,128]{2,1,0:T(8,128)(2,1)S(1)} %get-tuple-element.48.mright, bf16[32,32,128]{2,1,0:T(8,128)(2,1)S(1)} %get-tuple-element.49.mleft, ...), custom_call_target="tpu_custom_call" | custom-call | flops 1000 | bytes 18000000 | tf_op jit(solution)/shard_map/near/pallas_call | solution.py:437
  17.4 1.2 %collective-permute-done.2.came = bf16[38,32,128]{2,1,0:T(8,128)(2,1)S(1)} collective-permute-done((bf16[38,32,128]{2,1,0:T(8,128)(2,1)S(1)}, bf16[38,32,128]{2,1,0:T(8,128)(2,1)S(1)}, u32[]{:S(2)}, u32[]{:S(2)}) %collective-permute-start.2) | collective-permute-done | bytes 311328 | tf_op jit(solution)/shard_map/ppermute | solution.py:29
  18.5 0.1 fold.7
  18.6 3.2 %collective-permute-start.3 = (bf16[24,32,128]{2,1,0:T(8,128)(2,1)S(1)}, bf16[24,32,128]{2,1,0:T(8,128)(2,1)S(1)}, u32[]{:S(2)}, u32[]{:S(2)}) collective-permute-start(bf16[24,32,128]{2,1,0:T(8,128)(2,1)S(1)} %get-tuple-element.51.refs_1_), channel_id=1, source_target_pairs={{0,24},{1,3},{2,26},{3,1},{4,28},{5,7},{6,30},{7,5},{8,16},{9,11},... | collective-permute-start | bytes 589832 | tf_op jit(solution)/shard_map/ppermute | solution.py:29
  21.8 3.8 %collective-permute-done.3.came = bf16[24,32,128]{2,1,0:T(8,128)(2,1)S(1)} collective-permute-done((bf16[24,32,128]{2,1,0:T(8,128)(2,1)S(1)}, bf16[24,32,128]{2,1,0:T(8,128)(2,1)S(1)}, u32[]{:S(2)}, u32[]{:S(2)}) %collective-permute-start.3) | collective-permute-done | bytes 196640 | tf_op jit(solution)/shard_map/ppermute | solution.py:29
  25.6 0.1 fold.8
  25.6 2.8 %collective-permute-start.4 = (bf16[28,32,128]{2,1,0:T(8,128)(2,1)S(1)}, bf16[28,32,128]{2,1,0:T(8,128)(2,1)S(1)}, u32[]{:S(2)}, u32[]{:S(2)}) collective-permute-start(bf16[28,32,128]{2,1,0:T(8,128)(2,1)S(1)} %get-tuple-element.55._), channel_id=1, source_target_pairs={{0,2},{1,25},{2,0},{3,27},{4,6},{5,29},{6,4},{7,31},{8,10},{9,17},... | collective-permute-start | bytes 688136 | tf_op jit(solution)/shard_map/ppermute | solution.py:29
  28.4 0.0 collective-permute-start.5
  28.4 1.3 %collective-permute-done.5.pair = bf16[16,32,128]{2,1,0:T(8,128)(2,1)S(1)} collective-permute-done((bf16[16,32,128]{2,1,0:T(8,128)(2,1)S(1)}, bf16[16,32,128]{2,1,0:T(8,128)(2,1)S(1)}, u32[]{:S(2)}, u32[]{:S(2)}) %collective-permute-start.5) | collective-permute-done | bytes 131104 | tf_op jit(solution)/shard_map/ppermute | solution.py:33
  29.8 0.0 slice-start
  29.8 1.1 %edge_pair.1 = (f32[4,32,128]{2,1,0:T(8,128)S(1)}, f32[4,32,128]{2,1,0:T(8,128)S(1)}, bf16[8,32,128]{2,1,0:T(8,128)(2,1)S(1)}) custom-call(s32[1]{0:T(128)} %bitcast.place, s32[8,32]{1,0:T(8,128)S(1)} %bitcast.5, s32[1]{0:T(128)S(6)} %sub.3.first, bf16[16,32,128]{2,1,0:T(8,128)(2,1)S(1)} %collective-permute-done.5.pair, ...), custom_call_target="tpu_custom_call" | custom-call | flops 1000 | bytes 2880000 | tf_op jit(solution)/shard_map/edge_pair/pallas_call | solution.py:437
  30.9 1.6 %collective-permute-done.4.came = bf16[28,32,128]{2,1,0:T(8,128)(2,1)S(1)} collective-permute-done((bf16[28,32,128]{2,1,0:T(8,128)(2,1)S(1)}, bf16[28,32,128]{2,1,0:T(8,128)(2,1)S(1)}, u32[]{:S(2)}, u32[]{:S(2)}) %collective-permute-start.4) | collective-permute-done | bytes 229408 | tf_op jit(solution)/shard_map/ppermute | solution.py:29
  32.5 3.7 %collective-permute-start.6 = (bf16[28,32,128]{2,1,0:T(8,128)(2,1)S(1)}, bf16[28,32,128]{2,1,0:T(8,128)(2,1)S(1)}, u32[]{:S(2)}, u32[]{:S(2)}) collective-permute-start(bf16[28,32,128]{2,1,0:T(8,128)(2,1)S(1)} %get-tuple-element.61.refs_1_), channel_id=1, source_target_pairs={{0,6},{1,9},{2,4},{3,11},{4,2},{5,13},{6,0},{7,15},{8,14},{9,1},{1... | collective-permute-start | bytes 688136 | tf_op jit(solution)/shard_map/ppermute | solution.py:29
  36.1 4.0 %collective-permute-done.6.came = bf16[28,32,128]{2,1,0:T(8,128)(2,1)S(1)} collective-permute-done((bf16[28,32,128]{2,1,0:T(8,128)(2,1)S(1)}, bf16[28,32,128]{2,1,0:T(8,128)(2,1)S(1)}, u32[]{:S(2)}, u32[]{:S(2)}) %collective-permute-start.6) | collective-permute-done | bytes 229408 | tf_op jit(solution)/shard_map/ppermute | solution.py:29
  40.1 0.1 fold.10
  40.2 0.2 collective-permute-start.7
  40.4 2.4 %collective-permute-start.8 = (bf16[8,32,128]{2,1,0:T(8,128)(2,1)S(1)}, bf16[8,32,128]{2,1,0:T(8,128)(2,1)S(1)}, u32[]{:S(2)}, u32[]{:S(2)}) collective-permute-start(bf16[8,32,128]{2,1,0:T(8,128)(2,1)S(1)} %get-tuple-element.69), channel_id=1, source_target_pairs={{0,2},{2,4},{3,1},{4,6},{5,3},{6,8},{7,5},{8,10},{9,7},{10,12},{11... | collective-permute-start | bytes 196616 | tf_op jit(solution)/shard_map/ppermute | solution.py:39
  42.9 1.9 %collective-permute-done.8.came = bf16[8,32,128]{2,1,0:T(8,128)(2,1)S(1)} collective-permute-done((bf16[8,32,128]{2,1,0:T(8,128)(2,1)S(1)}, bf16[8,32,128]{2,1,0:T(8,128)(2,1)S(1)}, u32[]{:S(2)}, u32[]{:S(2)}) %collective-permute-start.8) | collective-permute-done | bytes 65568 | tf_op jit(solution)/shard_map/ppermute | solution.py:39
  44.7 1.1 %edge_chain.1 = (f32[4,32,128]{2,1,0:T(8,128)S(1)}, f32[4,32,128]{2,1,0:T(8,128)S(1)}) custom-call(s32[1]{0:T(128)} %bitcast.place, s32[8,32]{1,0:T(8,128)S(1)} %bitcast.6, s32[1]{0:T(128)S(6)} %sub.3.first, bf16[8,32,128]{2,1,0:T(8,128)(2,1)S(1)} %collective-permute-done.8.came, bf16[32,8,128,128]{3,2,1,0:T(8,128)(2,1)S(1)} %copy-done, ...), custom_call_target="tpu_custom_call" | custom-call | flops 1000 | bytes 2880000 | tf_op jit(solution)/shard_map/edge_chain/pallas_call | solution.py:437
  45.8 1.5 %collective-permute-done.7.came = bf16[40,32,128]{2,1,0:T(8,128)(2,1)S(1)} collective-permute-done((bf16[40,32,128]{2,1,0:T(8,128)(2,1)S(1)}, bf16[40,32,128]{2,1,0:T(8,128)(2,1)S(1)}, u32[]{:S(2)}, u32[]{:S(2)}) %collective-permute-start.7) | collective-permute-done | bytes 327712 | tf_op jit(solution)/shard_map/ppermute | solution.py:29
  47.4 0.1 fold.11
  47.4 0.1 collective-permute-start.9
  47.5 0.0 copy-start.7
  47.5 10.0 %collective-permute-start.10 = (bf16[10,32,128]{2,1,0:T(8,128)(2,1)S(1)}, bf16[10,32,128]{2,1,0:T(8,128)(2,1)S(1)}, u32[]{:S(2)}, u32[]{:S(2)}) collective-permute-start(bf16[10,32,128]{2,1,0:T(8,128)(2,1)S(1)} %get-tuple-element.72.rest_4_), channel_id=1, source_target_pairs={{0,96},{1,33},{2,98},{3,35},{4,100},{5,37},{6,102},{7,39},{8,104},... | collective-permute-start | bytes 245768 | tf_op jit(solution)/shard_map/ppermute | solution.py:29
  57.5 0.0 collective-permute-done.9.other
  57.5 0.0 slice-done
  57.5 0.0 slice-done.1
  57.5 0.0 copy-done.2
  57.5 0.0 copy-done.4
  57.5 0.0 copy-done.6
  57.6 0.0 copy-done.8
  57.6 0.0 copy-done.1
  57.6 0.0 copy-done.3
  57.6 2.4 %forward.1.far_right = f32[32,128]{1,0:T(8,128)S(1)} custom-call(s32[1]{0:T(128)} %bitcast.place, s32[1]{0:T(128)S(6)} %copy.16.count, s32[1,96]{1,0:T(1,128)S(1)} %copy-done.6, s32[256]{0:T(256)S(1)} %copy-done.8, bf16[64,32,128]{2,1,0:T(8,128)(2,1)S(1)} %get-tuple-element.71.own, bf16[64,32,128]{2,1,0:T(8,128)(2,1)S(1)} %collective-permute-done.9.other, ...), custom_call_target="tpu_custom_call" | custom-call | flops 1000 | bytes 9000000 | tf_op jit(solution)/shard_map/forward/pallas_call | solution.py:437
  60.0 0.0 collective-permute-done.10.came
  60.0 0.0 copy-done.7
  60.0 2.6 %down.1 = (f32[32,4096]{1,0:T(8,128)}, f32[32,4096]{1,0:T(8,128)}) custom-call(s32[1]{0:T(128)} %bitcast.place, s32[32]{0:T(128)S(1)} %copy-done.7, f32[32,128]{1,0:T(8,128)S(1)} %forward.1.far_right, f32[1,32,128]{2,1,0:T(8,128)S(1)} %get-tuple-element.73.partial, f32[4,32,128]{2,1,0:T(8,128)S(1)} %get-tuple-element.74.sums, ...), custom_call_target="tpu_custom_call" | custom-call | flops 1000 | bytes 14400000 | tf_op jit(solution)/shard_map/down/pallas_call | solution.py:437
  (9 shorter events, 0.1 us)
Async XLA Ops:
  1.3 12.0 %copy-start = (bf16[32,8,128,128]{3,2,1,0:T(8,128)(2,1)S(1)}, bf16[32,8,128,128]{3,2,1,0:T(8,128)(2,1)}, u32[]{:S(2)}) copy-start(bf16[32,8,128,128]{3,2,1,0:T(8,128)(2,1)} %blocks.5) | copy-start | bytes 25165828
  6.4 5.0 %collective-permute-start = (f32[67,32,128]{2,1,0:T(8,128)S(1)}, f32[67,32,128]{2,1,0:T(8,128)S(1)}, u32[]{:S(2)}, u32[]{:S(2)}) collective-permute-start(f32[67,32,128]{2,1,0:T(8,128)S(1)} %get-tuple-element.40), channel_id=1, source_target_pairs={{0,1},{1,0},{2,3},{3,2},{4,5},{5,4},{6,7},{7,6},{8,9},{9,8},{10,11... | collective-permute-start | bytes 3293192 | tf_op jit(solution)/shard_map/ppermute | solution.py:33
  6.5 4.9 %collective-permute-start.1 = (bf16[1,32,128]{2,1,0:T(8,128)(2,1)S(1)}, bf16[1,32,128]{2,1,0:T(8,128)(2,1)S(1)}, u32[]{:S(2)}, u32[]{:S(2)}) collective-permute-start(bf16[1,32,128]{2,1,0:T(8,128)(2,1)S(1)} %get-tuple-element.43.refs_0_.refs_2_), channel_id=1, source_target_pairs={{0,96},{1,33},{2,98},{3,35},{4,100},{5,37},{6,102},{7,39},{8,104},... | collective-permute-start | bytes 24584 | tf_op jit(solution)/shard_map/ppermute | solution.py:29
  11.4 1.9 %copy-start.5 = (s32[32,8]{0,1:T(8,128)S(1)}, s32[32,8]{0,1:T(8,128)}, u32[]{:S(2)}) copy-start(s32[32,8]{0,1:T(8,128)} %param.17) | copy-start | bytes 3076
  11.5 7.0 %collective-permute-start.2 = (bf16[38,32,128]{2,1,0:T(8,128)(2,1)S(1)}, bf16[38,32,128]{2,1,0:T(8,128)(2,1)S(1)}, u32[]{:S(2)}, u32[]{:S(2)}) collective-permute-start(bf16[38,32,128]{2,1,0:T(8,128)(2,1)S(1)} %get-tuple-element.44._), channel_id=1, source_target_pairs={{0,8},{1,7},{2,10},{3,5},{4,12},{5,3},{6,14},{7,1},{8,0},{9,15},{1... | collective-permute-start | bytes 933896 | tf_op jit(solution)/shard_map/ppermute | solution.py:29
  18.6 7.0 %collective-permute-start.3 = (bf16[24,32,128]{2,1,0:T(8,128)(2,1)S(1)}, bf16[24,32,128]{2,1,0:T(8,128)(2,1)S(1)}, u32[]{:S(2)}, u32[]{:S(2)}) collective-permute-start(bf16[24,32,128]{2,1,0:T(8,128)(2,1)S(1)} %get-tuple-element.51.refs_1_), channel_id=1, source_target_pairs={{0,24},{1,3},{2,26},{3,1},{4,28},{5,7},{6,30},{7,5},{8,16},{9,11},... | collective-permute-start | bytes 589832 | tf_op jit(solution)/shard_map/ppermute | solution.py:29
  25.6 6.8 %collective-permute-start.4 = (bf16[28,32,128]{2,1,0:T(8,128)(2,1)S(1)}, bf16[28,32,128]{2,1,0:T(8,128)(2,1)S(1)}, u32[]{:S(2)}, u32[]{:S(2)}) collective-permute-start(bf16[28,32,128]{2,1,0:T(8,128)(2,1)S(1)} %get-tuple-element.55._), channel_id=1, source_target_pairs={{0,2},{1,25},{2,0},{3,27},{4,6},{5,29},{6,4},{7,31},{8,10},{9,17},... | collective-permute-start | bytes 688136 | tf_op jit(solution)/shard_map/ppermute | solution.py:29
  28.4 1.3 %collective-permute-start.5 = (bf16[16,32,128]{2,1,0:T(8,128)(2,1)S(1)}, bf16[16,32,128]{2,1,0:T(8,128)(2,1)S(1)}, u32[]{:S(2)}, u32[]{:S(2)}) collective-permute-start(bf16[16,32,128]{2,1,0:T(8,128)(2,1)S(1)} %get-tuple-element.59), channel_id=1, source_target_pairs={{0,1},{1,0},{2,3},{3,2},{4,5},{5,4},{6,7},{7,6},{8,9},{9,8},{10,11... | collective-permute-start | bytes 393224 | tf_op jit(solution)/shard_map/ppermute | solution.py:33
  29.8 27.7 %slice-start = ((s8[6291456]{0:T(1024)(128)(4,1)}), s8[4194304]{0:T(1024)(128)(4,1)S(1)}, s32[]{:S(2)}) async-start(s8[6291456]{0:T(1024)(128)(4,1)} %bitcast.2), calls=%async_computation | async-start | bytes 8388608
  32.5 7.7 %collective-permute-start.6 = (bf16[28,32,128]{2,1,0:T(8,128)(2,1)S(1)}, bf16[28,32,128]{2,1,0:T(8,128)(2,1)S(1)}, u32[]{:S(2)}, u32[]{:S(2)}) collective-permute-start(bf16[28,32,128]{2,1,0:T(8,128)(2,1)S(1)} %get-tuple-element.61.refs_1_), channel_id=1, source_target_pairs={{0,6},{1,9},{2,4},{3,11},{4,2},{5,13},{6,0},{7,15},{8,14},{9,1},{1... | collective-permute-start | bytes 688136 | tf_op jit(solution)/shard_map/ppermute | solution.py:29
  40.1 17.4 %slice-start.1 = ((s8[6291456]{0:T(1024)(128)(4,1)}), s8[2097152]{0:T(1024)(128)(4,1)S(1)}, s32[]{:S(2)}) async-start(s8[6291456]{0:T(1024)(128)(4,1)} %bitcast.2), calls=%async_computation.1 | async-start | bytes 4194304
  40.2 7.2 %collective-permute-start.7 = (bf16[40,32,128]{2,1,0:T(8,128)(2,1)S(1)}, bf16[40,32,128]{2,1,0:T(8,128)(2,1)S(1)}, u32[]{:S(2)}, u32[]{:S(2)}) collective-permute-start(bf16[40,32,128]{2,1,0:T(8,128)(2,1)S(1)} %get-tuple-element.65._), channel_id=1, source_target_pairs={{0,32},{1,97},{2,34},{3,99},{4,36},{5,101},{6,38},{7,103},{8,40},{... | collective-permute-start | bytes 983048 | tf_op jit(solution)/shard_map/ppermute | solution.py:29
  40.4 17.1 %copy-start.2 = (bf16[32,64,128]{2,1,0:T(8,128)(2,1)S(1)}, bf16[32,64,128]{2,1,0:T(8,128)(2,1)}, u32[]{:S(2)}) copy-start(bf16[32,64,128]{2,1,0:T(8,128)(2,1)} %basis.1) | copy-start | bytes 1572868
  40.4 17.1 %copy-start.4 = (f32[1,128,128]{2,1,0:T(8,128)S(1)}, f32[1,128,128]{2,1,0:T(8,128)}, u32[]{:S(2)}) copy-start(f32[1,128,128]{2,1,0:T(8,128)} %lift.1) | copy-start | bytes 196612
  40.4 17.1 %copy-start.6 = (s32[1,96]{1,0:T(1,128)S(1)}, s32[1,96]{1,0:T(1,128)}, u32[]{:S(2)}) copy-start(s32[1,96]{1,0:T(1,128)} %parents.1) | copy-start | bytes 1156
  40.4 17.2 %copy-start.8 = (s32[256]{0:T(256)S(1)}, s32[256]{0:T(256)}, u32[]{:S(2)}) copy-start(s32[256]{0:T(256)} %constant.21.clone.table) | copy-start | bytes 3076
  40.4 4.3 %collective-permute-start.8 = (bf16[8,32,128]{2,1,0:T(8,128)(2,1)S(1)}, bf16[8,32,128]{2,1,0:T(8,128)(2,1)S(1)}, u32[]{:S(2)}, u32[]{:S(2)}) collective-permute-start(bf16[8,32,128]{2,1,0:T(8,128)(2,1)S(1)} %get-tuple-element.69), channel_id=1, source_target_pairs={{0,2},{2,4},{3,1},{4,6},{5,3},{6,8},{7,5},{8,10},{9,7},{10,12},{11... | collective-permute-start | bytes 196616 | tf_op jit(solution)/shard_map/ppermute | solution.py:39
  44.7 12.8 %copy-start.1 = (f32[32,64,128]{2,1,0:T(8,128)S(1)}, f32[32,64,128]{2,1,0:T(8,128)}, u32[]{:S(2)}) copy-start(f32[32,64,128]{2,1,0:T(8,128)} %transfer.1) | copy-start | bytes 3145732
  44.7 12.8 %copy-start.3 = (f32[4,4,128,128]{3,2,1,0:T(8,128)S(1)}, f32[4,4,128,128]{3,2,1,0:T(8,128)}, u32[]{:S(2)}) copy-start(f32[4,4,128,128]{3,2,1,0:T(8,128)} %apex.1) | copy-start | bytes 3145732
  47.4 10.1 %collective-permute-start.9 = (bf16[64,32,128]{2,1,0:T(8,128)(2,1)S(1)}, bf16[64,32,128]{2,1,0:T(8,128)(2,1)S(1)}, u32[]{:S(2)}, u32[]{:S(2)}) collective-permute-start(bf16[64,32,128]{2,1,0:T(8,128)(2,1)S(1)} %get-tuple-element.71.own), channel_id=1, source_target_pairs={{0,1},{1,0},{2,3},{3,2},{4,5},{5,4},{6,7},{7,6},{8,9},{9,8},{10,11... | collective-permute-start | bytes 1572872 | tf_op jit(solution)/shard_map/ppermute | solution.py:33
  47.5 12.5 %copy-start.7 = (s32[32]{0:T(128)S(1)}, s32[32]{0:T(128)}, u32[]{:S(2)}) copy-start(s32[32]{0:T(128)} %points.1) | copy-start | bytes 388
  47.5 12.5 %collective-permute-start.10 = (bf16[10,32,128]{2,1,0:T(8,128)(2,1)S(1)}, bf16[10,32,128]{2,1,0:T(8,128)(2,1)S(1)}, u32[]{:S(2)}, u32[]{:S(2)}) collective-permute-start(bf16[10,32,128]{2,1,0:T(8,128)(2,1)S(1)} %get-tuple-element.72.rest_4_), channel_id=1, source_target_pairs={{0,96},{1,33},{2,98},{3,35},{4,100},{5,37},{6,102},{7,39},{8,104},... | collective-permute-start | bytes 245768 | tf_op jit(solution)/shard_map/ppermute | solution.py:29

commit v9 on v8

--- a/solution.py
+++ b/solution.py
@@ -35,7 +35,7 @@
 
 def to_other_chips(block):
     devices = range(lax.axis_size(AXES))
-    route = [(i, i + 2 - 4 * (i & 1)) for i in devices]
+    route = [(i, i - 1 + 2 * (i & 1)) for i in devices]
     return lax.ppermute(block, AXES, [(i, j) for i, j in route if j in devices])
 
 
@@ -271,7 +271,7 @@
             back[place] = held[s] + value[:, s * B : (s + 1) * B]
 
 
-def near_kernel(columns, first, mright, mleft, blocks, _, out, back, sent):
+def near_kernel(place, columns, first, mright, mleft, blocks, _, out, back, to_chip, to_core):
     clusters = mright.shape[0]
     slots = blocks.shape[1]
     back[...] = jnp.zeros_like(back)
@@ -286,10 +286,10 @@
                 inside.append(jnp.where(is_own, value, jnp.zeros_like(value)))
             out[c] = dot(rows_of(blocks, c), jnp.concatenate(inside, axis=1), NT).T
         add_back(columns, first, mleft, blocks, group, back)
-    sent[:HW] = mright[:HW]
-    sent[HW : 2 * HW] = mright[clusters - HW :]
-    sent[2 * HW : 3 * HW] = back[:HW].astype(BF)
-    sent[3 * HW :] = back[clusters + HW :].astype(BF)
+    core = place[0] & 1
+    for side, sent in ((core, to_chip), (1 - core, to_core)):
+        sent[:HW] = mright[pl.ds(side * (clusters - HW), HW)]
+        sent[HW:] = back[pl.ds(side * (clusters + HW), HW)].astype(BF)
 
 
 def edge(low, columns, first, halo, blocks, out):
@@ -308,17 +308,8 @@
         out[g] = dot(rows_of(blocks, c), jnp.concatenate(values, axis=1), NT).T
 
 
-def edge_pair_kernel(place, columns, first, pair, blocks, _, out, back, message, halo):
-    core = place[0] & 1
-    message[:HW] = pair[pl.ds(HW * (1 - core), HW)]
-    message[HW:] = pair[pl.ds(2 * HW + HW * (1 - core), HW)]
-    halo[...] = pair[pl.ds(HW * core, HW)]
-    edge(core == 1, columns, first, halo, blocks, out)
-    back[...] = pair[pl.ds(2 * HW + HW * core, HW)].astype(F32)
-
-
-def edge_chain_kernel(place, columns, first, came, blocks, _, out, back):
-    edge((place[0] & 1) == 0, columns, first, came, blocks, out)
+def edge_kernel(low_core, place, columns, first, came, blocks, _, out, back):
+    edge((place[0] & 1) == low_core, columns, first, came, blocks, out)
     back[...] = came[HW:].astype(F32)
 
 
@@ -544,16 +535,29 @@
 
     payload, partial, sums, gathered = fold(0, came, partial, sums, own, came_own, after=own)
     came = routed(payload, STEPS[0])
-    near_out, near_back, pair_sent = call(
+    near_out, near_back, to_chip, to_core = call(
         near_kernel,
         "near",
         (),
-        [SMEM] * 2 + [VMEM] * 3 + [ANY],
-        [rows(clusters, F32), rows(clusters + 2 * HW, F32), rows(4 * HW)],
-        (columns, first, mright, mleft, near_blocks, payload),
+        [SMEM] * 3 + [VMEM] * 3 + [ANY],
+        [rows(clusters, F32), rows(clusters + 2 * HW, F32), rows(2 * HW), rows(2 * HW)],
+        (place, columns, first, mright, mleft, near_blocks, payload),
         us=5,
     )
-    pair = to_other_core(pair_sent)
+    chip_came = to_other_chips(to_chip)
+    core_came = to_other_core(to_core)
+
+    def edges(low_core, came, after):
+        return call(
+            functools.partial(edge_kernel, low_core),
+            "edge",
+            (),
+            [SMEM] * 3 + [VMEM] * 2 + [ANY],
+            [rows(HW, F32)] * 2,
+            (place, columns, first, came, near_blocks, after),
+            us=0.8,
+        )
+
     after = near_out
     for step in range(1, len(STEPS)):
         payload, partial, sums, gathered = fold(
@@ -561,30 +565,12 @@
         )
         came = routed(payload, STEPS[step])
         after = payload
+        if step == 1:
+            chain_out, chain_back = edges(0, chip_came, payload)
+            after = chain_out
         if step == 2:
-            pair_out, pair_back, message = call(
-                edge_pair_kernel,
-                "edge_pair",
-                (),
-                [SMEM] * 3 + [VMEM] * 2 + [ANY],
-                [rows(HW, F32)] * 2 + [rows(2 * HW)],
-                (place, columns, first, pair, near_blocks, payload),
-                us=0.8,
-                scratch=[pltpu.VMEM((HW, *block), BF)],
-            )
+            pair_out, pair_back = edges(1, core_came, payload)
             after = pair_out
-            halo_came = to_other_chips(message)
-        if step == 4:
-            chain_out, chain_back = call(
-                edge_chain_kernel,
-                "edge_chain",
-                (),
-                [SMEM] * 3 + [VMEM] * 2 + [ANY],
-                [rows(HW, F32)] * 2,
-                (place, columns, first, halo_came, near_blocks, payload),
-                us=0.8,
-            )
-            after = chain_out
     gathered_other = to_other_core(gathered)
     (far_right,) = call(
         forward_kernel,

time: 63.2 us -> 62.3 us (0.986)
  starting transfers between devices: 27.1 us -> 26.3 us
    ppermute x1, waiting for transfers between devices: 1.88 us -> 0.01 us  [to_other_chips(): return lax.ppermute(block, AXES, [(i, j) for i, j in route if j in devices])]
    ppermute x7, waiting for transfers between devices: 14.1 us -> 15.9 us  [routed(): return lax.ppermute(block, AXES, route)]
    ppermute x1, starting transfers between devices: 2.44 us -> 0.65 us  [to_other_chips(): return lax.ppermute(block, AXES, [(i, j) for i, j in route if j in devices])]
    ppermute x7, starting transfers between devices: 24.5 us -> 25.5 us  [routed(): return lax.ppermute(block, AXES, route)]
  transfers between devices with their start and end apart: 11 -> 11, of which waited for: 8 -> 7; matrix products, arithmetic and copies ran while one was open for 0% -> 0% of each run, Pallas kernels for 14% -> 14%
where the time goes in v9:
time: 62.3 us; the launch traced here: 61.9 us
  starting transfers between devices  26.3 us (42%)
  waiting for transfers between devices  17.2 us (28%)
  Pallas kernels  16.7 us (27%)
  between operations  1.62 us (3%)
    ppermute x7, starting transfers between devices, routed(): return lax.ppermute(block, AXES, route)  25.5 us
    pallas_call x12, Pallas kernels, call(): pl.pallas_call(kernel, grid=grid, out_shape=tuple((shape(dims, kind) for...  16.7 us
    ppermute x7, waiting for transfers between devices, routed(): return lax.ppermute(block, AXES, route)  15.9 us
    ppermute x3, waiting for transfers between devices, to_other_core(): lax.ppermute(block, AXES, [(i, i ^ 1) for i in range(lax.axis_size(AXES))])  1.26 us
  transfers between devices with their start and end apart: 11, of which 7 were waited for; matrix products, arithmetic and copies ran while one was open for 0% of the time, Pallas kernels for 14%

profile of v9, /device:TPU:0, one launch (start us, length us, event | category | flops | bytes accessed | tf_op | source)
XLA Modules:
  0.0 61.9 jit_solution(12397362028242415195)
XLA Ops:
  1.3 0.0 copy-start
  1.3 5.1 %rise.1 = (bf16[32,32,128]{2,1,0:T(8,128)(2,1)S(1)}, bf16[32,32,128]{2,1,0:T(8,128)(2,1)S(1)}, bf16[1,32,128]{2,1,0:T(8,128)(2,1)S(1)}, f32[65,32,128]{2,1,0:T(8...) custom-call(s32[1]{0:T(128)} %bitcast.place, s32[1]{0:T(128)S(6)} %copy.16.count, s32[32]{0:T(128)} %points.1, ...), custom_call_target="tpu_custom_call" | custom-call | flops 1000 | bytes 18000000 | tf_op jit(solution)/shard_map/rise/pallas_call | solution.py:428
  6.4 0.1 collective-permute-start
  6.5 2.9 %collective-permute-start.1 = (bf16[1,32,128]{2,1,0:T(8,128)(2,1)S(1)}, bf16[1,32,128]{2,1,0:T(8,128)(2,1)S(1)}, u32[]{:S(2)}, u32[]{:S(2)}) collective-permute-start(bf16[1,32,128]{2,1,0:T(8,128)(2,1)S(1)} %get-tuple-element.43.refs_0_.refs_2_), channel_id=1, source_target_pairs={{0,96},{1,33},{2,98},{3,35},{4,100},{5,37},{6,102},{7,39},{8,104},... | collective-permute-start | bytes 24584 | tf_op jit(solution)/shard_map/ppermute | solution.py:29
  9.4 2.0 %collective-permute-done.1.refs_1_ = bf16[1,32,128]{2,1,0:T(8,128)(2,1)S(1)} collective-permute-done((bf16[1,32,128]{2,1,0:T(8,128)(2,1)S(1)}, bf16[1,32,128]{2,1,0:T(8,128)(2,1)S(1)}, u32[]{:S(2)}, u32[]{:S(2)}) %collective-permute-start.1) | collective-permute-done | bytes 8224 | tf_op jit(solution)/shard_map/ppermute | solution.py:29
  11.4 0.0 collective-permute-done.came
  11.4 0.0 copy-start.5
  11.4 0.1 fold.6
  11.5 1.7 %collective-permute-start.2 = (bf16[38,32,128]{2,1,0:T(8,128)(2,1)S(1)}, bf16[38,32,128]{2,1,0:T(8,128)(2,1)S(1)}, u32[]{:S(2)}, u32[]{:S(2)}) collective-permute-start(bf16[38,32,128]{2,1,0:T(8,128)(2,1)S(1)} %get-tuple-element.44._), channel_id=1, source_target_pairs={{0,8},{1,7},{2,10},{3,5},{4,12},{5,3},{6,14},{7,1},{8,0},{9,15},{1... | collective-permute-start | bytes 933896 | tf_op jit(solution)/shard_map/ppermute | solution.py:29
  13.3 0.0 copy-done
  13.3 0.0 copy-done.5
  13.3 4.1 %near.1 = (f32[32,32,128]{2,1,0:T(8,128)S(1)}, f32[40,32,128]{2,1,0:T(8,128)S(1)}, bf16[8,32,128]{2,1,0:T(8,128)(2,1)S(1)}, bf16[8,32,128]{2,1,0:T(8,128)(2,1)S(1)}) custom-call(s32[1]{0:T(128)} %bitcast.place, s32[8,32]{1,0:T(8,128)S(1)} %bitcast.4, s32[1]{0:T(128)S(6)} %sub.3.first, bf16[32,32,128]{2,1,0:T(8,128)(2,1)S(1)} %get-tuple-element.48.mright, ...), custom_call_target="tpu_custom_call" | custom-call | flops 1000 | bytes 18000000 | tf_op jit(solution)/shard_map/near/pallas_call | solution.py:428
  17.4 1.2 %collective-permute-done.2.came = bf16[38,32,128]{2,1,0:T(8,128)(2,1)S(1)} collective-permute-done((bf16[38,32,128]{2,1,0:T(8,128)(2,1)S(1)}, bf16[38,32,128]{2,1,0:T(8,128)(2,1)S(1)}, u32[]{:S(2)}, u32[]{:S(2)}) %collective-permute-start.2) | collective-permute-done | bytes 311328 | tf_op jit(solution)/shard_map/ppermute | solution.py:29
  18.5 0.1 fold.7
  18.6 3.2 %collective-permute-start.3 = (bf16[24,32,128]{2,1,0:T(8,128)(2,1)S(1)}, bf16[24,32,128]{2,1,0:T(8,128)(2,1)S(1)}, u32[]{:S(2)}, u32[]{:S(2)}) collective-permute-start(bf16[24,32,128]{2,1,0:T(8,128)(2,1)S(1)} %get-tuple-element.51._), channel_id=1, source_target_pairs={{0,24},{1,3},{2,26},{3,1},{4,28},{5,7},{6,30},{7,5},{8,16},{9,11},... | collective-permute-start | bytes 589832 | tf_op jit(solution)/shard_map/ppermute | solution.py:29
  21.8 0.7 %collective-permute-start.4 = (bf16[8,32,128]{2,1,0:T(8,128)(2,1)S(1)}, bf16[8,32,128]{2,1,0:T(8,128)(2,1)S(1)}, u32[]{:S(2)}, u32[]{:S(2)}) collective-permute-start(bf16[8,32,128]{2,1,0:T(8,128)(2,1)S(1)} %get-tuple-element.55), channel_id=1, source_target_pairs={{1,2},{2,1},{3,4},{4,3},{5,6},{6,5},{7,8},{8,7},{9,10},{10,9},{11,... | collective-permute-start | bytes 196616 | tf_op jit(solution)/shard_map/ppermute | solution.py:39
  22.4 0.0 collective-permute-done.4.came
  22.5 1.1 %edge.2 = (f32[4,32,128]{2,1,0:T(8,128)S(1)}, f32[4,32,128]{2,1,0:T(8,128)S(1)}) custom-call(s32[1]{0:T(128)} %bitcast.place, s32[8,32]{1,0:T(8,128)S(1)} %bitcast.5, s32[1]{0:T(128)S(6)} %sub.3.first, bf16[8,32,128]{2,1,0:T(8,128)(2,1)S(1)} %collective-permute-done.4.came, bf16[32,8,128,128]{3,2,1,0:T(8,128)(2,1)S(1)} %copy-done, ...), custom_call_target="tpu_custom_call" | custom-call | flops 1000 | bytes 2880000 | tf_op jit(solution)/shard_map/edge/pallas_call | solution.py:428
  23.5 2.0 %collective-permute-done.3.came = bf16[24,32,128]{2,1,0:T(8,128)(2,1)S(1)} collective-permute-done((bf16[24,32,128]{2,1,0:T(8,128)(2,1)S(1)}, bf16[24,32,128]{2,1,0:T(8,128)(2,1)S(1)}, u32[]{:S(2)}, u32[]{:S(2)}) %collective-permute-start.3) | collective-permute-done | bytes 196640 | tf_op jit(solution)/shard_map/ppermute | solution.py:29
  25.6 0.0 slice-start
  25.6 0.1 fold.8
  25.6 4.9 %collective-permute-start.5 = (bf16[28,32,128]{2,1,0:T(8,128)(2,1)S(1)}, bf16[28,32,128]{2,1,0:T(8,128)(2,1)S(1)}, u32[]{:S(2)}, u32[]{:S(2)}) collective-permute-start(bf16[28,32,128]{2,1,0:T(8,128)(2,1)S(1)} %get-tuple-element.57._), channel_id=1, source_target_pairs={{0,2},{1,25},{2,0},{3,27},{4,6},{5,29},{6,4},{7,31},{8,10},{9,17},... | collective-permute-start | bytes 688136 | tf_op jit(solution)/shard_map/ppermute | solution.py:29
  30.5 0.0 collective-permute-start.6
  30.5 1.3 %collective-permute-done.6.came = bf16[8,32,128]{2,1,0:T(8,128)(2,1)S(1)} collective-permute-done((bf16[8,32,128]{2,1,0:T(8,128)(2,1)S(1)}, bf16[8,32,128]{2,1,0:T(8,128)(2,1)S(1)}, u32[]{:S(2)}, u32[]{:S(2)}) %collective-permute-start.6) | collective-permute-done | bytes 65568 | tf_op jit(solution)/shard_map/ppermute | solution.py:33
  31.8 1.1 %edge.3 = (f32[4,32,128]{2,1,0:T(8,128)S(1)}, f32[4,32,128]{2,1,0:T(8,128)S(1)}) custom-call(s32[1]{0:T(128)} %bitcast.place, s32[8,32]{1,0:T(8,128)S(1)} %bitcast.6, s32[1]{0:T(128)S(6)} %sub.3.first, bf16[8,32,128]{2,1,0:T(8,128)(2,1)S(1)} %collective-permute-done.6.came, bf16[32,8,128,128]{3,2,1,0:T(8,128)(2,1)S(1)} %copy-done, ...), custom_call_target="tpu_custom_call" | custom-call | flops 1000 | bytes 2880000 | tf_op jit(solution)/shard_map/edge/pallas_call | solution.py:428
  32.9 1.7 %collective-permute-done.5.came = bf16[28,32,128]{2,1,0:T(8,128)(2,1)S(1)} collective-permute-done((bf16[28,32,128]{2,1,0:T(8,128)(2,1)S(1)}, bf16[28,32,128]{2,1,0:T(8,128)(2,1)S(1)}, u32[]{:S(2)}, u32[]{:S(2)}) %collective-permute-start.5) | collective-permute-done | bytes 229408 | tf_op jit(solution)/shard_map/ppermute | solution.py:29
  34.5 0.0 copy-start.8
  34.6 4.2 %collective-permute-start.7 = (bf16[28,32,128]{2,1,0:T(8,128)(2,1)S(1)}, bf16[28,32,128]{2,1,0:T(8,128)(2,1)S(1)}, u32[]{:S(2)}, u32[]{:S(2)}) collective-permute-start(bf16[28,32,128]{2,1,0:T(8,128)(2,1)S(1)} %get-tuple-element.63.refs_1_), channel_id=1, source_target_pairs={{0,6},{1,9},{2,4},{3,11},{4,2},{5,13},{6,0},{7,15},{8,14},{9,1},{1... | collective-permute-start | bytes 688136 | tf_op jit(solution)/shard_map/ppermute | solution.py:29
  38.8 4.0 %collective-permute-done.7.came = bf16[28,32,128]{2,1,0:T(8,128)(2,1)S(1)} collective-permute-done((bf16[28,32,128]{2,1,0:T(8,128)(2,1)S(1)}, bf16[28,32,128]{2,1,0:T(8,128)(2,1)S(1)}, u32[]{:S(2)}, u32[]{:S(2)}) %collective-permute-start.7) | collective-permute-done | bytes 229408 | tf_op jit(solution)/shard_map/ppermute | solution.py:29
  42.8 0.1 fold.10
  42.9 3.8 %collective-permute-start.8 = (bf16[40,32,128]{2,1,0:T(8,128)(2,1)S(1)}, bf16[40,32,128]{2,1,0:T(8,128)(2,1)S(1)}, u32[]{:S(2)}, u32[]{:S(2)}) collective-permute-start(bf16[40,32,128]{2,1,0:T(8,128)(2,1)S(1)} %get-tuple-element.67.refs_1_), channel_id=1, source_target_pairs={{0,32},{1,97},{2,34},{3,99},{4,36},{5,101},{6,38},{7,103},{8,40},{... | collective-permute-start | bytes 983048 | tf_op jit(solution)/shard_map/ppermute | solution.py:29
  46.7 5.1 %collective-permute-done.8.came = bf16[40,32,128]{2,1,0:T(8,128)(2,1)S(1)} collective-permute-done((bf16[40,32,128]{2,1,0:T(8,128)(2,1)S(1)}, bf16[40,32,128]{2,1,0:T(8,128)(2,1)S(1)}, u32[]{:S(2)}, u32[]{:S(2)}) %collective-permute-start.8) | collective-permute-done | bytes 327712 | tf_op jit(solution)/shard_map/ppermute | solution.py:29
  51.8 0.1 collective-permute-start.9
  51.9 0.0 copy-start.7
  51.9 4.8 %collective-permute-start.10 = (bf16[10,32,128]{2,1,0:T(8,128)(2,1)S(1)}, bf16[10,32,128]{2,1,0:T(8,128)(2,1)S(1)}, u32[]{:S(2)}, u32[]{:S(2)}) collective-permute-start(bf16[10,32,128]{2,1,0:T(8,128)(2,1)S(1)} %get-tuple-element.72.rest_4_), channel_id=1, source_target_pairs={{0,96},{1,33},{2,98},{3,35},{4,100},{5,37},{6,102},{7,39},{8,104},... | collective-permute-start | bytes 245768 | tf_op jit(solution)/shard_map/ppermute | solution.py:29
  56.6 0.0 collective-permute-done.9.other
  56.6 0.0 slice-done
  56.6 0.0 slice-done.1
  56.6 0.0 copy-done.3
  56.6 0.0 copy-done.1
  56.7 0.0 copy-done.2
  56.7 0.0 copy-done.4
  56.7 0.0 copy-done.6
  56.7 0.0 copy-done.8
  56.7 2.4 %forward.1.far_right = f32[32,128]{1,0:T(8,128)S(1)} custom-call(s32[1]{0:T(128)} %bitcast.place, s32[1]{0:T(128)S(6)} %copy.16.count, s32[1,96]{1,0:T(1,128)S(1)} %copy-done.6, s32[256]{0:T(256)S(1)} %copy-done.8, bf16[64,32,128]{2,1,0:T(8,128)(2,1)S(1)} %get-tuple-element.71.own, bf16[64,32,128]{2,1,0:T(8,128)(2,1)S(1)} %collective-permute-done.9.other, ...), custom_call_target="tpu_custom_call" | custom-call | flops 1000 | bytes 9000000 | tf_op jit(solution)/shard_map/forward/pallas_call | solution.py:428
  59.1 0.0 collective-permute-done.10.came
  59.1 0.0 copy-done.7
  59.1 2.6 %down.1 = (f32[32,4096]{1,0:T(8,128)}, f32[32,4096]{1,0:T(8,128)}) custom-call(s32[1]{0:T(128)} %bitcast.place, s32[32]{0:T(128)S(1)} %copy-done.7, f32[32,128]{1,0:T(8,128)S(1)} %forward.1.far_right, f32[1,32,128]{2,1,0:T(8,128)S(1)} %get-tuple-element.73.partial, f32[4,32,128]{2,1,0:T(8,128)S(1)} %get-tuple-element.74.sums, ...), custom_call_target="tpu_custom_call" | custom-call | flops 1000 | bytes 14400000 | tf_op jit(solution)/shard_map/down/pallas_call | solution.py:428
  (9 shorter events, 0.1 us)
Async XLA Ops:
  1.3 12.0 %copy-start = (bf16[32,8,128,128]{3,2,1,0:T(8,128)(2,1)S(1)}, bf16[32,8,128,128]{3,2,1,0:T(8,128)(2,1)}, u32[]{:S(2)}) copy-start(bf16[32,8,128,128]{3,2,1,0:T(8,128)(2,1)} %blocks.5) | copy-start | bytes 25165828
  6.4 5.0 %collective-permute-start = (f32[67,32,128]{2,1,0:T(8,128)S(1)}, f32[67,32,128]{2,1,0:T(8,128)S(1)}, u32[]{:S(2)}, u32[]{:S(2)}) collective-permute-start(f32[67,32,128]{2,1,0:T(8,128)S(1)} %get-tuple-element.40), channel_id=1, source_target_pairs={{0,1},{1,0},{2,3},{3,2},{4,5},{5,4},{6,7},{7,6},{8,9},{9,8},{10,11... | collective-permute-start | bytes 3293192 | tf_op jit(solution)/shard_map/ppermute | solution.py:33
  6.5 4.9 %collective-permute-start.1 = (bf16[1,32,128]{2,1,0:T(8,128)(2,1)S(1)}, bf16[1,32,128]{2,1,0:T(8,128)(2,1)S(1)}, u32[]{:S(2)}, u32[]{:S(2)}) collective-permute-start(bf16[1,32,128]{2,1,0:T(8,128)(2,1)S(1)} %get-tuple-element.43.refs_0_.refs_2_), channel_id=1, source_target_pairs={{0,96},{1,33},{2,98},{3,35},{4,100},{5,37},{6,102},{7,39},{8,104},... | collective-permute-start | bytes 24584 | tf_op jit(solution)/shard_map/ppermute | solution.py:29
  11.4 1.9 %copy-start.5 = (s32[32,8]{0,1:T(8,128)S(1)}, s32[32,8]{0,1:T(8,128)}, u32[]{:S(2)}) copy-start(s32[32,8]{0,1:T(8,128)} %param.17) | copy-start | bytes 3076
  11.5 7.0 %collective-permute-start.2 = (bf16[38,32,128]{2,1,0:T(8,128)(2,1)S(1)}, bf16[38,32,128]{2,1,0:T(8,128)(2,1)S(1)}, u32[]{:S(2)}, u32[]{:S(2)}) collective-permute-start(bf16[38,32,128]{2,1,0:T(8,128)(2,1)S(1)} %get-tuple-element.44._), channel_id=1, source_target_pairs={{0,8},{1,7},{2,10},{3,5},{4,12},{5,3},{6,14},{7,1},{8,0},{9,15},{1... | collective-permute-start | bytes 933896 | tf_op jit(solution)/shard_map/ppermute | solution.py:29
  18.6 7.0 %collective-permute-start.3 = (bf16[24,32,128]{2,1,0:T(8,128)(2,1)S(1)}, bf16[24,32,128]{2,1,0:T(8,128)(2,1)S(1)}, u32[]{:S(2)}, u32[]{:S(2)}) collective-permute-start(bf16[24,32,128]{2,1,0:T(8,128)(2,1)S(1)} %get-tuple-element.51._), channel_id=1, source_target_pairs={{0,24},{1,3},{2,26},{3,1},{4,28},{5,7},{6,30},{7,5},{8,16},{9,11},... | collective-permute-start | bytes 589832 | tf_op jit(solution)/shard_map/ppermute | solution.py:29
  21.8 0.7 %collective-permute-start.4 = (bf16[8,32,128]{2,1,0:T(8,128)(2,1)S(1)}, bf16[8,32,128]{2,1,0:T(8,128)(2,1)S(1)}, u32[]{:S(2)}, u32[]{:S(2)}) collective-permute-start(bf16[8,32,128]{2,1,0:T(8,128)(2,1)S(1)} %get-tuple-element.55), channel_id=1, source_target_pairs={{1,2},{2,1},{3,4},{4,3},{5,6},{6,5},{7,8},{8,7},{9,10},{10,9},{11,... | collective-permute-start | bytes 196616 | tf_op jit(solution)/shard_map/ppermute | solution.py:39
  25.6 31.1 %slice-start = ((s8[6291456]{0:T(1024)(128)(4,1)}), s8[4194304]{0:T(1024)(128)(4,1)S(1)}, s32[]{:S(2)}) async-start(s8[6291456]{0:T(1024)(128)(4,1)} %bitcast.2), calls=%async_computation | async-start | bytes 8388608
  25.6 8.9 %collective-permute-start.5 = (bf16[28,32,128]{2,1,0:T(8,128)(2,1)S(1)}, bf16[28,32,128]{2,1,0:T(8,128)(2,1)S(1)}, u32[]{:S(2)}, u32[]{:S(2)}) collective-permute-start(bf16[28,32,128]{2,1,0:T(8,128)(2,1)S(1)} %get-tuple-element.57._), channel_id=1, source_target_pairs={{0,2},{1,25},{2,0},{3,27},{4,6},{5,29},{6,4},{7,31},{8,10},{9,17},... | collective-permute-start | bytes 688136 | tf_op jit(solution)/shard_map/ppermute | solution.py:29
  30.5 26.1 %slice-start.1 = ((s8[6291456]{0:T(1024)(128)(4,1)}), s8[2097152]{0:T(1024)(128)(4,1)S(1)}, s32[]{:S(2)}) async-start(s8[6291456]{0:T(1024)(128)(4,1)} %bitcast.2), calls=%async_computation.1 | async-start | bytes 4194304
  30.5 1.3 %collective-permute-start.6 = (bf16[8,32,128]{2,1,0:T(8,128)(2,1)S(1)}, bf16[8,32,128]{2,1,0:T(8,128)(2,1)S(1)}, u32[]{:S(2)}, u32[]{:S(2)}) collective-permute-start(bf16[8,32,128]{2,1,0:T(8,128)(2,1)S(1)} %get-tuple-element.61), channel_id=1, source_target_pairs={{0,1},{1,0},{2,3},{3,2},{4,5},{5,4},{6,7},{7,6},{8,9},{9,8},{10,11... | collective-permute-start | bytes 196616 | tf_op jit(solution)/shard_map/ppermute | solution.py:33
  31.8 24.9 %copy-start.3 = (f32[4,4,128,128]{3,2,1,0:T(8,128)S(1)}, f32[4,4,128,128]{3,2,1,0:T(8,128)}, u32[]{:S(2)}) copy-start(f32[4,4,128,128]{3,2,1,0:T(8,128)} %apex.1) | copy-start | bytes 3145732
  34.5 22.1 %copy-start.1 = (f32[32,64,128]{2,1,0:T(8,128)S(1)}, f32[32,64,128]{2,1,0:T(8,128)}, u32[]{:S(2)}) copy-start(f32[32,64,128]{2,1,0:T(8,128)} %transfer.1) | copy-start | bytes 3145732
  34.5 22.1 %copy-start.2 = (bf16[32,64,128]{2,1,0:T(8,128)(2,1)S(1)}, bf16[32,64,128]{2,1,0:T(8,128)(2,1)}, u32[]{:S(2)}) copy-start(bf16[32,64,128]{2,1,0:T(8,128)(2,1)} %basis.1) | copy-start | bytes 1572868
  34.5 22.1 %copy-start.4 = (f32[1,128,128]{2,1,0:T(8,128)S(1)}, f32[1,128,128]{2,1,0:T(8,128)}, u32[]{:S(2)}) copy-start(f32[1,128,128]{2,1,0:T(8,128)} %lift.1) | copy-start | bytes 196612
  34.5 22.1 %copy-start.6 = (s32[1,96]{1,0:T(1,128)S(1)}, s32[1,96]{1,0:T(1,128)}, u32[]{:S(2)}) copy-start(s32[1,96]{1,0:T(1,128)} %parents.1) | copy-start | bytes 1156
  34.5 22.2 %copy-start.8 = (s32[256]{0:T(256)S(1)}, s32[256]{0:T(256)}, u32[]{:S(2)}) copy-start(s32[256]{0:T(256)} %constant.21.clone.table) | copy-start | bytes 3076
  34.6 8.2 %collective-permute-start.7 = (bf16[28,32,128]{2,1,0:T(8,128)(2,1)S(1)}, bf16[28,32,128]{2,1,0:T(8,128)(2,1)S(1)}, u32[]{:S(2)}, u32[]{:S(2)}) collective-permute-start(bf16[28,32,128]{2,1,0:T(8,128)(2,1)S(1)} %get-tuple-element.63.refs_1_), channel_id=1, source_target_pairs={{0,6},{1,9},{2,4},{3,11},{4,2},{5,13},{6,0},{7,15},{8,14},{9,1},{1... | collective-permute-start | bytes 688136 | tf_op jit(solution)/shard_map/ppermute | solution.py:29
  42.9 8.8 %collective-permute-start.8 = (bf16[40,32,128]{2,1,0:T(8,128)(2,1)S(1)}, bf16[40,32,128]{2,1,0:T(8,128)(2,1)S(1)}, u32[]{:S(2)}, u32[]{:S(2)}) collective-permute-start(bf16[40,32,128]{2,1,0:T(8,128)(2,1)S(1)} %get-tuple-element.67.refs_1_), channel_id=1, source_target_pairs={{0,32},{1,97},{2,34},{3,99},{4,36},{5,101},{6,38},{7,103},{8,40},{... | collective-permute-start | bytes 983048 | tf_op jit(solution)/shard_map/ppermute | solution.py:29
  51.8 4.9 %collective-permute-start.9 = (bf16[64,32,128]{2,1,0:T(8,128)(2,1)S(1)}, bf16[64,32,128]{2,1,0:T(8,128)(2,1)S(1)}, u32[]{:S(2)}, u32[]{:S(2)}) collective-permute-start(bf16[64,32,128]{2,1,0:T(8,128)(2,1)S(1)} %get-tuple-element.71.own), channel_id=1, source_target_pairs={{0,1},{1,0},{2,3},{3,2},{4,5},{5,4},{6,7},{7,6},{8,9},{9,8},{10,11... | collective-permute-start | bytes 1572872 | tf_op jit(solution)/shard_map/ppermute | solution.py:33
  51.9 7.3 %copy-start.7 = (s32[32]{0:T(128)S(1)}, s32[32]{0:T(128)}, u32[]{:S(2)}) copy-start(s32[32]{0:T(128)} %points.1) | copy-start | bytes 388
  51.9 7.3 %collective-permute-start.10 = (bf16[10,32,128]{2,1,0:T(8,128)(2,1)S(1)}, bf16[10,32,128]{2,1,0:T(8,128)(2,1)S(1)}, u32[]{:S(2)}, u32[]{:S(2)}) collective-permute-start(bf16[10,32,128]{2,1,0:T(8,128)(2,1)S(1)} %get-tuple-element.72.rest_4_), channel_id=1, source_target_pairs={{0,96},{1,33},{2,98},{3,35},{4,100},{5,37},{6,102},{7,39},{8,104},... | collective-permute-start | bytes 245768 | tf_op jit(solution)/shard_map/ppermute | solution.py:29

commit v10 on v9

--- a/solution.py
+++ b/solution.py
@@ -566,11 +566,13 @@
         came = routed(payload, STEPS[step])
         after = payload
         if step == 1:
+            pair_out, pair_back = edges(1, core_came, payload)
+            after = pair_out
+        if step == 2:
+            after = chip_came
+        if step == 3:
             chain_out, chain_back = edges(0, chip_came, payload)
             after = chain_out
-        if step == 2:
-            pair_out, pair_back = edges(1, core_came, payload)
-            after = pair_out
     gathered_other = to_other_core(gathered)
     (far_right,) = call(
         forward_kernel,

time: 62.3 us -> 61 us (0.979)
  starting transfers between devices: 26.3 us -> 24.7 us
    ppermute x7, starting transfers between devices: 25.5 us -> 23.9 us  [routed(): return lax.ppermute(block, AXES, route)]
where the time goes in v10:
time: 61 us; the launch traced here: 60.5 us
  starting transfers between devices  24.7 us (40%)
  waiting for transfers between devices  17.4 us (29%)
  Pallas kernels  16.7 us (27%)
  between operations  1.64 us (3%)
    ppermute x7, starting transfers between devices, routed(): return lax.ppermute(block, AXES, route)  23.9 us
    pallas_call x12, Pallas kernels, call(): pl.pallas_call(kernel, grid=grid, out_shape=tuple((shape(dims, kind) for...  16.7 us
    ppermute x7, waiting for transfers between devices, routed(): return lax.ppermute(block, AXES, route)  16.1 us
    ppermute x3, waiting for transfers between devices, to_other_core(): lax.ppermute(block, AXES, [(i, i ^ 1) for i in range(lax.axis_size(AXES))])  1.26 us
  transfers between devices with their start and end apart: 11, of which 7 were waited for; matrix products, arithmetic and copies ran while one was open for 0% of the time, Pallas kernels for 14%

profile of v10, /device:TPU:0, one launch (start us, length us, event | category | flops | bytes accessed | tf_op | source)
XLA Modules:
  0.0 60.5 jit_solution(10283986552281838040)
XLA Ops:
  1.3 0.0 copy-start
  1.3 5.1 %rise.1 = (bf16[32,32,128]{2,1,0:T(8,128)(2,1)S(1)}, bf16[32,32,128]{2,1,0:T(8,128)(2,1)S(1)}, bf16[1,32,128]{2,1,0:T(8,128)(2,1)S(1)}, f32[65,32,128]{2,1,0:T(8...) custom-call(s32[1]{0:T(128)} %bitcast.place, s32[1]{0:T(128)S(6)} %copy.16.count, s32[32]{0:T(128)} %points.1, ...), custom_call_target="tpu_custom_call" | custom-call | flops 1000 | bytes 18000000 | tf_op jit(solution)/shard_map/rise/pallas_call | solution.py:428
  6.4 0.1 collective-permute-start
  6.5 2.9 %collective-permute-start.1 = (bf16[1,32,128]{2,1,0:T(8,128)(2,1)S(1)}, bf16[1,32,128]{2,1,0:T(8,128)(2,1)S(1)}, u32[]{:S(2)}, u32[]{:S(2)}) collective-permute-start(bf16[1,32,128]{2,1,0:T(8,128)(2,1)S(1)} %get-tuple-element.43.refs_0_.refs_2_), channel_id=1, source_target_pairs={{0,96},{1,33},{2,98},{3,35},{4,100},{5,37},{6,102},{7,39},{8,104},... | collective-permute-start | bytes 24584 | tf_op jit(solution)/shard_map/ppermute | solution.py:29
  9.4 2.0 %collective-permute-done.1.refs_1_ = bf16[1,32,128]{2,1,0:T(8,128)(2,1)S(1)} collective-permute-done((bf16[1,32,128]{2,1,0:T(8,128)(2,1)S(1)}, bf16[1,32,128]{2,1,0:T(8,128)(2,1)S(1)}, u32[]{:S(2)}, u32[]{:S(2)}) %collective-permute-start.1) | collective-permute-done | bytes 8224 | tf_op jit(solution)/shard_map/ppermute | solution.py:29
  11.4 0.0 collective-permute-done.came
  11.4 0.1 fold.6
  11.5 1.7 %collective-permute-start.2 = (bf16[38,32,128]{2,1,0:T(8,128)(2,1)S(1)}, bf16[38,32,128]{2,1,0:T(8,128)(2,1)S(1)}, u32[]{:S(2)}, u32[]{:S(2)}) collective-permute-start(bf16[38,32,128]{2,1,0:T(8,128)(2,1)S(1)} %get-tuple-element.44._), channel_id=1, source_target_pairs={{0,8},{1,7},{2,10},{3,5},{4,12},{5,3},{6,14},{7,1},{8,0},{9,15},{1... | collective-permute-start | bytes 933896 | tf_op jit(solution)/shard_map/ppermute | solution.py:29
  13.3 0.0 copy-done
  13.3 0.0 copy-done.5
  13.3 4.1 %near.1 = (f32[32,32,128]{2,1,0:T(8,128)S(1)}, f32[40,32,128]{2,1,0:T(8,128)S(1)}, bf16[8,32,128]{2,1,0:T(8,128)(2,1)S(1)}, bf16[8,32,128]{2,1,0:T(8,128)(2,1)S(1)}) custom-call(s32[1]{0:T(128)} %bitcast.place, s32[8,32]{1,0:T(8,128)S(1)} %bitcast.4, s32[1]{0:T(128)S(6)} %sub.3.first, bf16[32,32,128]{2,1,0:T(8,128)(2,1)S(1)} %get-tuple-element.48.mright, ...), custom_call_target="tpu_custom_call" | custom-call | flops 1000 | bytes 18000000 | tf_op jit(solution)/shard_map/near/pallas_call | solution.py:428
  17.4 1.2 %collective-permute-done.2.came = bf16[38,32,128]{2,1,0:T(8,128)(2,1)S(1)} collective-permute-done((bf16[38,32,128]{2,1,0:T(8,128)(2,1)S(1)}, bf16[38,32,128]{2,1,0:T(8,128)(2,1)S(1)}, u32[]{:S(2)}, u32[]{:S(2)}) %collective-permute-start.2) | collective-permute-done | bytes 311328 | tf_op jit(solution)/shard_map/ppermute | solution.py:29
  18.5 0.1 fold.7
  18.6 3.2 %collective-permute-start.3 = (bf16[24,32,128]{2,1,0:T(8,128)(2,1)S(1)}, bf16[24,32,128]{2,1,0:T(8,128)(2,1)S(1)}, u32[]{:S(2)}, u32[]{:S(2)}) collective-permute-start(bf16[24,32,128]{2,1,0:T(8,128)(2,1)S(1)} %get-tuple-element.51._), channel_id=1, source_target_pairs={{0,24},{1,3},{2,26},{3,1},{4,28},{5,7},{6,30},{7,5},{8,16},{9,11},... | collective-permute-start | bytes 589832 | tf_op jit(solution)/shard_map/ppermute | solution.py:29
  21.8 0.0 collective-permute-start.4
  21.8 1.3 %collective-permute-done.4.came = bf16[8,32,128]{2,1,0:T(8,128)(2,1)S(1)} collective-permute-done((bf16[8,32,128]{2,1,0:T(8,128)(2,1)S(1)}, bf16[8,32,128]{2,1,0:T(8,128)(2,1)S(1)}, u32[]{:S(2)}, u32[]{:S(2)}) %collective-permute-start.4) | collective-permute-done | bytes 65568 | tf_op jit(solution)/shard_map/ppermute | solution.py:33
  23.0 1.1 %edge.2 = (f32[4,32,128]{2,1,0:T(8,128)S(1)}, f32[4,32,128]{2,1,0:T(8,128)S(1)}) custom-call(s32[1]{0:T(128)} %bitcast.place, s32[8,32]{1,0:T(8,128)S(1)} %bitcast.5, s32[1]{0:T(128)S(6)} %sub.3.first, bf16[8,32,128]{2,1,0:T(8,128)(2,1)S(1)} %collective-permute-done.4.came, bf16[32,8,128,128]{3,2,1,0:T(8,128)(2,1)S(1)} %copy-done, ...), custom_call_target="tpu_custom_call" | custom-call | flops 1000 | bytes 2880000 | tf_op jit(solution)/shard_map/edge/pallas_call | solution.py:428
  24.1 1.4 %collective-permute-done.3.came = bf16[24,32,128]{2,1,0:T(8,128)(2,1)S(1)} collective-permute-done((bf16[24,32,128]{2,1,0:T(8,128)(2,1)S(1)}, bf16[24,32,128]{2,1,0:T(8,128)(2,1)S(1)}, u32[]{:S(2)}, u32[]{:S(2)}) %collective-permute-start.3) | collective-permute-done | bytes 196640 | tf_op jit(solution)/shard_map/ppermute | solution.py:29
  25.6 0.1 fold.8
  25.6 2.1 %collective-permute-start.5 = (bf16[28,32,128]{2,1,0:T(8,128)(2,1)S(1)}, bf16[28,32,128]{2,1,0:T(8,128)(2,1)S(1)}, u32[]{:S(2)}, u32[]{:S(2)}) collective-permute-start(bf16[28,32,128]{2,1,0:T(8,128)(2,1)S(1)} %get-tuple-element.57), channel_id=1, source_target_pairs={{0,2},{1,25},{2,0},{3,27},{4,6},{5,29},{6,4},{7,31},{8,10},{9,17},... | collective-permute-start | bytes 688136 | tf_op jit(solution)/shard_map/ppermute | solution.py:29
  27.7 0.7 %collective-permute-start.6 = (bf16[8,32,128]{2,1,0:T(8,128)(2,1)S(1)}, bf16[8,32,128]{2,1,0:T(8,128)(2,1)S(1)}, u32[]{:S(2)}, u32[]{:S(2)}) collective-permute-start(bf16[8,32,128]{2,1,0:T(8,128)(2,1)S(1)} %get-tuple-element.61), channel_id=1, source_target_pairs={{1,2},{2,1},{3,4},{4,3},{5,6},{6,5},{7,8},{8,7},{9,10},{10,9},{11,... | collective-permute-start | bytes 196616 | tf_op jit(solution)/shard_map/ppermute | solution.py:39
  28.4 0.0 collective-permute-done.6.refs_1_.came
  28.4 3.6 %collective-permute-done.5.came = bf16[28,32,128]{2,1,0:T(8,128)(2,1)S(1)} collective-permute-done((bf16[28,32,128]{2,1,0:T(8,128)(2,1)S(1)}, bf16[28,32,128]{2,1,0:T(8,128)(2,1)S(1)}, u32[]{:S(2)}, u32[]{:S(2)}) %collective-permute-start.5) | collective-permute-done | bytes 229408 | tf_op jit(solution)/shard_map/ppermute | solution.py:29
  32.0 0.0 slice-start.1
  32.0 4.7 %collective-permute-start.7 = (bf16[28,32,128]{2,1,0:T(8,128)(2,1)S(1)}, bf16[28,32,128]{2,1,0:T(8,128)(2,1)S(1)}, u32[]{:S(2)}, u32[]{:S(2)}) collective-permute-start(bf16[28,32,128]{2,1,0:T(8,128)(2,1)S(1)} %get-tuple-element.62._), channel_id=1, source_target_pairs={{0,6},{1,9},{2,4},{3,11},{4,2},{5,13},{6,0},{7,15},{8,14},{9,1},{1... | collective-permute-start | bytes 688136 | tf_op jit(solution)/shard_map/ppermute | solution.py:29
  36.7 1.1 %edge.3 = (f32[4,32,128]{2,1,0:T(8,128)S(1)}, f32[4,32,128]{2,1,0:T(8,128)S(1)}) custom-call(s32[1]{0:T(128)} %bitcast.place, s32[8,32]{1,0:T(8,128)S(1)} %bitcast.6, s32[1]{0:T(128)S(6)} %sub.3.first, bf16[8,32,128]{2,1,0:T(8,128)(2,1)S(1)} %collective-permute-done.6.refs_1_.came, bf16[32,8,128,128]{3,2,1,0:T(8,128)(2,1)S(1)} %copy-done, ...), custom_call_target="tpu_custom_call" | custom-call | flops 1000 | bytes 2880000 | tf_op jit(solution)/shard_map/edge/pallas_call | solution.py:428
  37.8 0.0 copy-start.4
  37.8 0.0 copy-start.6
  37.8 0.0 copy-start.8
  37.8 2.9 %collective-permute-done.7.came = bf16[28,32,128]{2,1,0:T(8,128)(2,1)S(1)} collective-permute-done((bf16[28,32,128]{2,1,0:T(8,128)(2,1)S(1)}, bf16[28,32,128]{2,1,0:T(8,128)(2,1)S(1)}, u32[]{:S(2)}, u32[]{:S(2)}) %collective-permute-start.7) | collective-permute-done | bytes 229408 | tf_op jit(solution)/shard_map/ppermute | solution.py:29
  40.7 0.1 fold.10
  40.8 4.5 %collective-permute-start.8 = (bf16[40,32,128]{2,1,0:T(8,128)(2,1)S(1)}, bf16[40,32,128]{2,1,0:T(8,128)(2,1)S(1)}, u32[]{:S(2)}, u32[]{:S(2)}) collective-permute-start(bf16[40,32,128]{2,1,0:T(8,128)(2,1)S(1)} %get-tuple-element.67.refs_1_), channel_id=1, source_target_pairs={{0,32},{1,97},{2,34},{3,99},{4,36},{5,101},{6,38},{7,103},{8,40},{... | collective-permute-start | bytes 983048 | tf_op jit(solution)/shard_map/ppermute | solution.py:29
  45.3 5.1 %collective-permute-done.8.came = bf16[40,32,128]{2,1,0:T(8,128)(2,1)S(1)} collective-permute-done((bf16[40,32,128]{2,1,0:T(8,128)(2,1)S(1)}, bf16[40,32,128]{2,1,0:T(8,128)(2,1)S(1)}, u32[]{:S(2)}, u32[]{:S(2)}) %collective-permute-start.8) | collective-permute-done | bytes 327712 | tf_op jit(solution)/shard_map/ppermute | solution.py:29
  50.4 0.1 collective-permute-start.9
  50.5 0.0 copy-start.7
  50.5 4.8 %collective-permute-start.10 = (bf16[10,32,128]{2,1,0:T(8,128)(2,1)S(1)}, bf16[10,32,128]{2,1,0:T(8,128)(2,1)S(1)}, u32[]{:S(2)}, u32[]{:S(2)}) collective-permute-start(bf16[10,32,128]{2,1,0:T(8,128)(2,1)S(1)} %get-tuple-element.72.rest_4_), channel_id=1, source_target_pairs={{0,96},{1,33},{2,98},{3,35},{4,100},{5,37},{6,102},{7,39},{8,104},... | collective-permute-start | bytes 245768 | tf_op jit(solution)/shard_map/ppermute | solution.py:29
  55.3 0.0 collective-permute-done.9.other
  55.3 0.0 slice-done
  55.3 0.0 slice-done.1
  55.3 0.0 copy-done.2
  55.3 0.0 copy-done.3
  55.3 0.0 copy-done.1
  55.3 0.0 copy-done.4
  55.3 0.0 copy-done.6
  55.3 2.4 %forward.1.far_right = f32[32,128]{1,0:T(8,128)S(1)} custom-call(s32[1]{0:T(128)} %bitcast.place, s32[1]{0:T(128)S(6)} %copy.16.count, s32[1,96]{1,0:T(1,128)S(1)} %copy-done.6, s32[256]{0:T(256)S(1)} %copy-done.8, bf16[64,32,128]{2,1,0:T(8,128)(2,1)S(1)} %get-tuple-element.71.own, bf16[64,32,128]{2,1,0:T(8,128)(2,1)S(1)} %collective-permute-done.9.other, ...), custom_call_target="tpu_custom_call" | custom-call | flops 1000 | bytes 9000000 | tf_op jit(solution)/shard_map/forward/pallas_call | solution.py:428
  57.8 0.0 collective-permute-done.10.came
  57.8 0.0 copy-done.7
  57.8 2.6 %down.1 = (f32[32,4096]{1,0:T(8,128)}, f32[32,4096]{1,0:T(8,128)}) custom-call(s32[1]{0:T(128)} %bitcast.place, s32[32]{0:T(128)S(1)} %copy-done.7, f32[32,128]{1,0:T(8,128)S(1)} %forward.1.far_right, f32[1,32,128]{2,1,0:T(8,128)S(1)} %get-tuple-element.73.partial, f32[4,32,128]{2,1,0:T(8,128)S(1)} %get-tuple-element.74.sums, ...), custom_call_target="tpu_custom_call" | custom-call | flops 1000 | bytes 14400000 | tf_op jit(solution)/shard_map/down/pallas_call | solution.py:428
  (9 shorter events, 0.1 us)
Async XLA Ops:
  1.3 12.0 %copy-start = (bf16[32,8,128,128]{3,2,1,0:T(8,128)(2,1)S(1)}, bf16[32,8,128,128]{3,2,1,0:T(8,128)(2,1)}, u32[]{:S(2)}) copy-start(bf16[32,8,128,128]{3,2,1,0:T(8,128)(2,1)} %blocks.5) | copy-start | bytes 25165828
  6.4 5.0 %collective-permute-start = (f32[67,32,128]{2,1,0:T(8,128)S(1)}, f32[67,32,128]{2,1,0:T(8,128)S(1)}, u32[]{:S(2)}, u32[]{:S(2)}) collective-permute-start(f32[67,32,128]{2,1,0:T(8,128)S(1)} %get-tuple-element.40), channel_id=1, source_target_pairs={{0,1},{1,0},{2,3},{3,2},{4,5},{5,4},{6,7},{7,6},{8,9},{9,8},{10,11... | collective-permute-start | bytes 3293192 | tf_op jit(solution)/shard_map/ppermute | solution.py:33
  6.5 4.9 %collective-permute-start.1 = (bf16[1,32,128]{2,1,0:T(8,128)(2,1)S(1)}, bf16[1,32,128]{2,1,0:T(8,128)(2,1)S(1)}, u32[]{:S(2)}, u32[]{:S(2)}) collective-permute-start(bf16[1,32,128]{2,1,0:T(8,128)(2,1)S(1)} %get-tuple-element.43.refs_0_.refs_2_), channel_id=1, source_target_pairs={{0,96},{1,33},{2,98},{3,35},{4,100},{5,37},{6,102},{7,39},{8,104},... | collective-permute-start | bytes 24584 | tf_op jit(solution)/shard_map/ppermute | solution.py:29
  11.4 1.9 %copy-start.5 = (s32[32,8]{0,1:T(8,128)S(1)}, s32[32,8]{0,1:T(8,128)}, u32[]{:S(2)}) copy-start(s32[32,8]{0,1:T(8,128)} %param.17) | copy-start | bytes 3076
  11.5 7.0 %collective-permute-start.2 = (bf16[38,32,128]{2,1,0:T(8,128)(2,1)S(1)}, bf16[38,32,128]{2,1,0:T(8,128)(2,1)S(1)}, u32[]{:S(2)}, u32[]{:S(2)}) collective-permute-start(bf16[38,32,128]{2,1,0:T(8,128)(2,1)S(1)} %get-tuple-element.44._), channel_id=1, source_target_pairs={{0,8},{1,7},{2,10},{3,5},{4,12},{5,3},{6,14},{7,1},{8,0},{9,15},{1... | collective-permute-start | bytes 933896 | tf_op jit(solution)/shard_map/ppermute | solution.py:29
  18.6 7.0 %collective-permute-start.3 = (bf16[24,32,128]{2,1,0:T(8,128)(2,1)S(1)}, bf16[24,32,128]{2,1,0:T(8,128)(2,1)S(1)}, u32[]{:S(2)}, u32[]{:S(2)}) collective-permute-start(bf16[24,32,128]{2,1,0:T(8,128)(2,1)S(1)} %get-tuple-element.51._), channel_id=1, source_target_pairs={{0,24},{1,3},{2,26},{3,1},{4,28},{5,7},{6,30},{7,5},{8,16},{9,11},... | collective-permute-start | bytes 589832 | tf_op jit(solution)/shard_map/ppermute | solution.py:29
  21.8 1.3 %collective-permute-start.4 = (bf16[8,32,128]{2,1,0:T(8,128)(2,1)S(1)}, bf16[8,32,128]{2,1,0:T(8,128)(2,1)S(1)}, u32[]{:S(2)}, u32[]{:S(2)}) collective-permute-start(bf16[8,32,128]{2,1,0:T(8,128)(2,1)S(1)} %get-tuple-element.55), channel_id=1, source_target_pairs={{0,1},{1,0},{2,3},{3,2},{4,5},{5,4},{6,7},{7,6},{8,9},{9,8},{10,11... | collective-permute-start | bytes 196616 | tf_op jit(solution)/shard_map/ppermute | solution.py:33
  25.6 29.7 %slice-start = ((s8[6291456]{0:T(1024)(128)(4,1)}), s8[4194304]{0:T(1024)(128)(4,1)S(1)}, s32[]{:S(2)}) async-start(s8[6291456]{0:T(1024)(128)(4,1)} %bitcast.2), calls=%async_computation | async-start | bytes 8388608
  25.6 6.3 %collective-permute-start.5 = (bf16[28,32,128]{2,1,0:T(8,128)(2,1)S(1)}, bf16[28,32,128]{2,1,0:T(8,128)(2,1)S(1)}, u32[]{:S(2)}, u32[]{:S(2)}) collective-permute-start(bf16[28,32,128]{2,1,0:T(8,128)(2,1)S(1)} %get-tuple-element.57), channel_id=1, source_target_pairs={{0,2},{1,25},{2,0},{3,27},{4,6},{5,29},{6,4},{7,31},{8,10},{9,17},... | collective-permute-start | bytes 688136 | tf_op jit(solution)/shard_map/ppermute | solution.py:29
  27.7 0.7 %collective-permute-start.6 = (bf16[8,32,128]{2,1,0:T(8,128)(2,1)S(1)}, bf16[8,32,128]{2,1,0:T(8,128)(2,1)S(1)}, u32[]{:S(2)}, u32[]{:S(2)}) collective-permute-start(bf16[8,32,128]{2,1,0:T(8,128)(2,1)S(1)} %get-tuple-element.61), channel_id=1, source_target_pairs={{1,2},{2,1},{3,4},{4,3},{5,6},{6,5},{7,8},{8,7},{9,10},{10,9},{11,... | collective-permute-start | bytes 196616 | tf_op jit(solution)/shard_map/ppermute | solution.py:39
  32.0 23.3 %slice-start.1 = ((s8[6291456]{0:T(1024)(128)(4,1)}), s8[2097152]{0:T(1024)(128)(4,1)S(1)}, s32[]{:S(2)}) async-start(s8[6291456]{0:T(1024)(128)(4,1)} %bitcast.2), calls=%async_computation.1 | async-start | bytes 4194304
  32.0 8.7 %collective-permute-start.7 = (bf16[28,32,128]{2,1,0:T(8,128)(2,1)S(1)}, bf16[28,32,128]{2,1,0:T(8,128)(2,1)S(1)}, u32[]{:S(2)}, u32[]{:S(2)}) collective-permute-start(bf16[28,32,128]{2,1,0:T(8,128)(2,1)S(1)} %get-tuple-element.62._), channel_id=1, source_target_pairs={{0,6},{1,9},{2,4},{3,11},{4,2},{5,13},{6,0},{7,15},{8,14},{9,1},{1... | collective-permute-start | bytes 688136 | tf_op jit(solution)/shard_map/ppermute | solution.py:29
  36.7 18.6 %copy-start.2 = (bf16[32,64,128]{2,1,0:T(8,128)(2,1)S(1)}, bf16[32,64,128]{2,1,0:T(8,128)(2,1)}, u32[]{:S(2)}) copy-start(bf16[32,64,128]{2,1,0:T(8,128)(2,1)} %basis.1) | copy-start | bytes 1572868
  36.7 18.6 %copy-start.3 = (f32[4,4,128,128]{3,2,1,0:T(8,128)S(1)}, f32[4,4,128,128]{3,2,1,0:T(8,128)}, u32[]{:S(2)}) copy-start(f32[4,4,128,128]{3,2,1,0:T(8,128)} %apex.1) | copy-start | bytes 3145732
  37.8 17.5 %copy-start.1 = (f32[32,64,128]{2,1,0:T(8,128)S(1)}, f32[32,64,128]{2,1,0:T(8,128)}, u32[]{:S(2)}) copy-start(f32[32,64,128]{2,1,0:T(8,128)} %transfer.1) | copy-start | bytes 3145732
  37.8 17.5 %copy-start.4 = (f32[1,128,128]{2,1,0:T(8,128)S(1)}, f32[1,128,128]{2,1,0:T(8,128)}, u32[]{:S(2)}) copy-start(f32[1,128,128]{2,1,0:T(8,128)} %lift.1) | copy-start | bytes 196612
  37.8 17.5 %copy-start.6 = (s32[1,96]{1,0:T(1,128)S(1)}, s32[1,96]{1,0:T(1,128)}, u32[]{:S(2)}) copy-start(s32[1,96]{1,0:T(1,128)} %parents.1) | copy-start | bytes 1156
  37.8 17.5 %copy-start.8 = (s32[256]{0:T(256)S(1)}, s32[256]{0:T(256)}, u32[]{:S(2)}) copy-start(s32[256]{0:T(256)} %constant.21.clone.table) | copy-start | bytes 3076
  40.8 9.6 %collective-permute-start.8 = (bf16[40,32,128]{2,1,0:T(8,128)(2,1)S(1)}, bf16[40,32,128]{2,1,0:T(8,128)(2,1)S(1)}, u32[]{:S(2)}, u32[]{:S(2)}) collective-permute-start(bf16[40,32,128]{2,1,0:T(8,128)(2,1)S(1)} %get-tuple-element.67.refs_1_), channel_id=1, source_target_pairs={{0,32},{1,97},{2,34},{3,99},{4,36},{5,101},{6,38},{7,103},{8,40},{... | collective-permute-start | bytes 983048 | tf_op jit(solution)/shard_map/ppermute | solution.py:29
  50.4 4.9 %collective-permute-start.9 = (bf16[64,32,128]{2,1,0:T(8,128)(2,1)S(1)}, bf16[64,32,128]{2,1,0:T(8,128)(2,1)S(1)}, u32[]{:S(2)}, u32[]{:S(2)}) collective-permute-start(bf16[64,32,128]{2,1,0:T(8,128)(2,1)S(1)} %get-tuple-element.71.own), channel_id=1, source_target_pairs={{0,1},{1,0},{2,3},{3,2},{4,5},{5,4},{6,7},{7,6},{8,9},{9,8},{10,11... | collective-permute-start | bytes 1572872 | tf_op jit(solution)/shard_map/ppermute | solution.py:33
  50.5 7.3 %copy-start.7 = (s32[32]{0:T(128)S(1)}, s32[32]{0:T(128)}, u32[]{:S(2)}) copy-start(s32[32]{0:T(128)} %points.1) | copy-start | bytes 388
  50.5 7.3 %collective-permute-start.10 = (bf16[10,32,128]{2,1,0:T(8,128)(2,1)S(1)}, bf16[10,32,128]{2,1,0:T(8,128)(2,1)S(1)}, u32[]{:S(2)}, u32[]{:S(2)}) collective-permute-start(bf16[10,32,128]{2,1,0:T(8,128)(2,1)S(1)} %get-tuple-element.72.rest_4_), channel_id=1, source_target_pairs={{0,96},{1,33},{2,98},{3,35},{4,100},{5,37},{6,102},{7,39},{8,104},... | collective-permute-start | bytes 245768 | tf_op jit(solution)/shard_map/ppermute | solution.py:29
